TPU v7x, 32 devices: a whole 2x2x4 slice. The times are simulated.
32 devices in a mesh: row: 8 (over z, x), col: 4 (over y, core).
Axes of the slice: x: 2, y: 2, z: 4, core: 2. Of those that a mesh axis runs over, the one named last changes fastest.
Arguments:
- block_input: bfloat16 [1, 64, 128, 512], P(None, 'row', 'col'), may hold values from -6 to 6
- kernel_three: float32 [7, 7, 512], replicated, may hold values from -0.875 to 0.875
- gain_three: float32 [512], replicated, may hold values from 0.1 to 1.9
- expand_weight: bfloat16 [512, 2048], replicated, may hold values from -0.25 to 0.25
- project_weight: bfloat16 [2048, 512], replicated, may hold values from -0.125 to 0.125
- layer_scale: float32 [512], replicated, may hold values from 0.1 to 1
- merge_gain: float32 [512], replicated, may hold values from 0.1 to 1.9
- patch_weight: bfloat16 [2048, 1024], replicated, may hold values from -0.125 to 0.125
- kernel_four: float32 [7, 7, 1024], replicated, may hold values from -0.875 to 0.875
- gain_four: float32 [1024], replicated, may hold values from 0.1 to 1.9
- normed_cotangent: bfloat16 [1, 32, 64, 1024], P(None, 'row', 'col'), may hold values from -6 to 6
- residual_cotangent: bfloat16 [1, 32, 64, 1024], P(None, 'row', 'col'), may hold values from -6 to 6
Outputs:
- input_grad: bfloat16 [1, 64, 128, 512], P(None, 'row', 'col')
- kernel_three_grad: float32 [7, 7, 512], replicated
- gain_three_grad: float32 [512], replicated
- expand_grad: float32 [512, 2048], P('row')
- project_grad: float32 [2048, 512], P('row')
- scale_grad: float32 [512], replicated
- merge_gain_grad: float32 [512], replicated
- patch_grad: float32 [2048, 1024], P('row')
- kernel_four_grad: float32 [7, 7, 1024], replicated
- gain_four_grad: float32 [1024], replicated
All inputs are finite; a program needn't handle non-finite values.
Results may differ from a plain program's by a relative error of at most 0.03.
Values may be sent and summed in bfloat16 or wider, within the bound.
No kernel may reach another device: no remote copies, remote signals or barrier semaphores. Data moves between devices by JAX's collectives and lax.ppermute only.
A program may use at most 128 MiB of HBM per device.

v0:
```python
import functools
import math

import jax
import jax.numpy as jnp
from jax import lax
from jax.experimental import pallas as pl
from jax.experimental.pallas import tpu as pltpu
from jax.sharding import PartitionSpec as P

EPSILON = 1e-06
BF = jnp.bfloat16
F32 = jnp.float32
MIB = 1 << 20
PAD = 8
CHUNK = 256


def shape_of(*dims, dtype=F32):
    return jax.ShapeDtypeStruct(dims, dtype)


def run(kernel, name, args, outs, scratch=(), remote=(), limit=24, flops=10**7):
    inside = pl.BlockSpec(memory_space=pltpu.VMEM)
    outside = pl.BlockSpec(memory_space=pl.ANY)
    moved = sum(a.size * a.dtype.itemsize for a in args)
    moved += sum(math.prod(o.shape) * o.dtype.itemsize for o in outs)
    return pl.pallas_call(
        kernel,
        name=name,
        out_shape=outs,
        in_specs=[outside if i in remote else inside for i in range(len(args))],
        out_specs=[inside] * len(outs),
        scratch_shapes=list(scratch),
        compiler_params=pltpu.CompilerParams(vmem_limit_bytes=limit * MIB),
        cost_estimate=pl.CostEstimate(flops=flops, bytes_accessed=moved, transcendentals=0),
    )(*args)


def swap(values, axis, bit):
    return lax.ppermute(values, axis, [(i, i ^ bit) for i in range(lax.axis_size(axis))])


def axis_bits(axis):
    return [1 << k for k in range((lax.axis_size(axis) - 1).bit_length())]


def own_bit(axis, bit):
    return (lax.axis_index(axis) // bit) % 2


def pick(values, which, dim):
    return lax.dynamic_index_in_dim(values, which, dim, keepdims=False)


def scatter(values, axis, bits):
    for bit in bits:
        mine = own_bit(axis, bit)
        values = values.reshape(values.shape[0] // 2, 2, *values.shape[1:])
        values = pick(values, mine, 1) + swap(pick(values, 1 - mine, 1), axis, bit)
    return values[0]


def gather(values, axis, bits):
    values = values[None]
    for bit in reversed(bits):
        other = swap(values, axis, bit)
        mine = own_bit(axis, bit)
        low = jnp.where(mine == 0, values, other)
        high = jnp.where(mine == 0, other, values)
        values = jnp.stack([low, high], axis=1).reshape(-1, *values.shape[1:])
    return values


def neighbours(first, last, axis):
    count = lax.axis_size(axis)
    forward = [(i, i + 1) for i in range(count - 1)]
    backward = [(i + 1, i) for i in range(count - 1)]
    return lax.ppermute(last, axis, forward), lax.ppermute(first, axis, backward)


def strip_kernel(center, top, bottom, first, last):
    height, breadth = center.shape[:2]
    for source, start in ((top, 0), (center, 3), (bottom, 3 + height)):
        values = source[...].astype(F32)
        rows = slice(start, start + source.shape[0])
        first[rows] = values[:, :PAD].astype(BF)
        last[rows] = values[:, breadth - PAD :].astype(BF)


def halo(center, first_rows, last_rows, name):
    height, _, channels = center.shape
    top, bottom = neighbours(first_rows, last_rows, "row")
    strip = shape_of(height + 6, PAD, channels, dtype=BF)
    first, last = run(strip_kernel, name, (center, top, bottom), (strip, strip), limit=8)
    left, right = neighbours(first, last, "col")
    return center, top, bottom, left, right


def fill_frame(frame, parts):
    center, top, bottom, left, right = parts
    height, breadth = center.shape[:2]
    middle = slice(PAD, PAD + breadth)
    frame[0:3, middle] = top[...].astype(F32)
    frame[3 : 3 + height, middle] = center[...].astype(F32)
    frame[3 + height :, middle] = bottom[...].astype(F32)
    frame[:, :PAD] = left[...].astype(F32)
    frame[:, PAD + breadth :] = right[...].astype(F32)


def frame_scratch(center):
    height, breadth, channels = center.shape
    return pltpu.VMEM((height + 6, breadth + 2 * PAD, channels), F32)


def lane_tiles(channels):
    def over(step):
        def wrapped(index, carry):
            step(pl.ds(pl.multiple_of(index * 128, 128), 128))
            return carry

        lax.fori_loop(0, channels // 128, wrapped, 0)

    return over


def convolve(frame, taps, flip, out):
    height, breadth, channels = out.shape

    @lane_tiles(channels)
    def _(lanes):
        for column in range(0, breadth, 8):
            total = jnp.zeros((height, 8, 128), F32)
            for q in range(7):
                rows = frame[:, pl.ds(column + PAD - 3 + q, 8), lanes]
                for p in range(7):
                    a, b = (6 - p, 6 - q) if flip else (p, q)
                    total = total + rows[p : p + height] * taps[a, pl.ds(b, 1), lanes]
            out[:, pl.ds(column, 8), lanes] = total


def weight_sums(frame, grads, scale, out):
    height, breadth, channels = grads.shape

    @lane_tiles(channels)
    def _(lanes):
        for q in range(7):
            totals = [jnp.zeros((8, 128), F32)] * 7
            for column in range(0, breadth, 8):
                rows = frame[:, pl.ds(column + PAD - 3 + q, 8), lanes]
                grad = grads[:, pl.ds(column, 8), lanes]
                for p in range(7):
                    totals[p] = totals[p] + jnp.sum(rows[p : p + height] * grad, axis=0)
            for p in range(7):
                out[pl.ds(7 * p + q, 1), lanes] = scale * jnp.sum(totals[p], axis=0, keepdims=True)


def mean(values):
    return jnp.mean(values, axis=-1, keepdims=True)


def normalize(values):
    level = mean(values)
    inverse = lax.rsqrt(mean(values * values) - level * level + EPSILON)
    return (values - level) * inverse, inverse


def normalize_back(grads, unit_values, inverse):
    return (grads - mean(grads) - unit_values * mean(grads * unit_values)) * inverse


def dot(left, right):
    return jnp.dot(left, right, preferred_element_type=F32)


def dot_last(left, right):
    return lax.dot_general(left, right, (((1,), (1,)), ((), ())), preferred_element_type=F32)


def dot_first(left, right):
    return lax.dot_general(left, right, (((0,), (0,)), ((), ())), preferred_element_type=F32)


def over_rows(count, size):
    def over(step):
        def wrapped(index, carry):
            step(index, pl.ds(pl.multiple_of(index * size, size), size))
            return carry

        lax.fori_loop(0, count, wrapped, 0)

    return over


def fetch(sources, targets, semaphores):
    copies = [
        pltpu.make_async_copy(source, target, semaphores.at[i])
        for i, (source, target) in enumerate(zip(sources, targets))
    ]
    for copy in copies:
        copy.start()
    return copies


def front_kernel(
    center, top, bottom, left, right, taps, gain, expand, project, layer_scale, merge_gain, patch,
    early, unit_mixed, inverse_mixed, slope, branch, unit_summed, inverse_summed, section, first, last,
    frame, image, pairs, expand_here, project_here, patch_here, upward, semaphores,
):
    height, breadth, channels = center.shape
    hidden_width = expand.shape[1]
    pixels = height * breadth
    copies = fetch(
        (expand, project, patch), (expand_here, project_here, patch_here), semaphores
    )
    fill_frame(frame, (center, top, bottom, left, right))
    convolve(frame, taps, False, image)
    at_normed = slice(hidden_width, hidden_width + channels)
    at_patches = slice(hidden_width + channels, hidden_width + 2 * channels)

    @over_rows(height, breadth)
    def _(y, rows):
        unit, inverse = normalize(image[y])
        unit_mixed[rows] = unit
        inverse_mixed[rows] = inverse
        early[rows, at_normed] = (unit * gain[...]).astype(BF)

    copies[0].wait()

    def chunk(index, carry):
        lanes = pl.ds(pl.multiple_of(index * CHUNK, CHUNK), CHUNK)
        upward[...] = dot(early[:, at_normed], expand_here[:, lanes])
        for start in range(0, pixels, 64):
            rows = slice(start, start + 64)
            value = upward[rows]
            cumulative = 0.5 + 0.5 * lax.erf(value * (1.0 / math.sqrt(2.0)))
            density = jnp.exp(-0.5 * value * value) * (1.0 / math.sqrt(2.0 * math.pi))
            early[rows, lanes] = (value * cumulative).astype(BF)
            slope[rows, lanes] = (cumulative + value * density).astype(BF)
        return carry

    lax.fori_loop(0, hidden_width // CHUNK, chunk, 0)
    copies[1].wait()
    branch[...] = dot(early[:, :hidden_width], project_here[...])

    @over_rows(height, breadth)
    def _(y, rows):
        summed = center[y].astype(F32) + layer_scale[...] * branch[rows]
        unit, inverse = normalize(summed)
        unit_summed[rows] = unit
        inverse_summed[rows] = inverse
        merged = unit * merge_gain[...]
        for k in range(channels // 128):
            pairs[k, y] = merged[:, k * 128 : (k + 1) * 128]

    quarter = pixels // 4
    for dy in range(2):
        for dx in range(2):
            j = 2 * dy + dx
            for y in range(height // 2):
                start = j * quarter + y * (breadth // 2)
                for k in range(channels // 128):
                    piece = pairs[k, 2 * y + dy, pl.ds(dx, breadth // 2, stride=2), :]
                    lane = hidden_width + channels + k * 128
                    early[start : start + breadth // 2, lane : lane + 128] = piece.astype(BF)
    copies[2].wait()
    total = dot(early[:quarter, at_patches], patch_here[:channels])
    for j in range(1, 4):
        total = total + dot(
            early[j * quarter : (j + 1) * quarter, at_patches],
            patch_here[j * channels : (j + 1) * channels],
        )
    total = total.reshape(section.shape)
    section[...] = total.astype(BF)
    first[...] = total[:3].astype(BF)
    last[...] = total[height // 2 - 3 :].astype(BF)


def mixer_kernel(
    center, top, bottom, left, right, taps, gain, cotangent,
    grad, grad_half, first, last, gain_part,
    frame, image,
):
    height, breadth, channels = center.shape
    fill_frame(frame, (center, top, bottom, left, right))
    convolve(frame, taps, False, image)
    part = jnp.zeros((1, channels), F32)
    for y in range(height):
        unit, inverse = normalize(image[y])
        cot = cotangent[y].astype(F32)
        part = part + jnp.sum(cot * unit, axis=0, keepdims=True)
        value = normalize_back(cot * gain[...], unit, inverse)
        grad[y] = value
        narrow = value.astype(BF)
        grad_half[y] = narrow
        if y < 3:
            first[y] = narrow
        if y >= height - 3:
            last[y - (height - 3)] = narrow
    gain_part[...] = part


def weight_kernel(scale, center, top, bottom, left, right, grads, out, frame):
    fill_frame(frame, (center, top, bottom, left, right))
    weight_sums(frame, grads, scale, out)


def weight_pack_kernel(
    scale, scale_wide, center, top, bottom, left, right, grads,
    gain_part, layer_part, merge_part, wide_part, wide_gain,
    keep, send, frame, wide_grads, packed,
):
    channels = center.shape[2]
    half = channels // 2
    fill_frame(frame, (center, top, bottom, left, right))
    wide_grads[...] = grads[...].astype(F32)
    packed[...] = jnp.zeros(packed.shape, F32)
    weight_sums(frame, wide_grads, scale, packed)
    for i, part in enumerate((gain_part, layer_part, merge_part)):
        packed[49 + i : 50 + i] = scale * part[...]
    for i in range(2):
        columns = slice(i * channels, (i + 1) * channels)
        packed[52 + 49 * i : 101 + 49 * i] = wide_part[:, columns]
        packed[150 + i : 151 + i] = scale_wide * wide_gain[:, columns]
    values = packed[...].astype(BF)
    core = lax.axis_index("col") % 2
    for i in range(2):

        @pl.when(core == i)
        def _():
            keep[...] = values[:, i * half : (i + 1) * half]
            send[...] = values[:, (1 - i) * half : (2 - i) * half]


def section_kernel(
    center, top, bottom, left, right, taps, residual,
    flat, keep, send,
    frame, image,
):
    height, breadth, channels = center.shape
    fill_frame(frame, (center, top, bottom, left, right))
    convolve(frame, taps, True, image)
    value = (image[...] + residual[...].astype(F32)).reshape(flat.shape).astype(BF)
    flat[...] = value
    blocks, _, width = keep.shape
    core = lax.axis_index("col") % 2
    for i in range(2):

        @pl.when(core == i)
        def _():
            for m in range(blocks):
                mine, other = (2 * m + i) * width, (2 * m + 1 - i) * width
                keep[m] = value[:, mine : mine + width]
                send[m] = value[:, other : other + width]


def merge_kernel(
    flat, patch, unit_summed, inverse_summed, merge_gain, branch, layer_scale,
    grad_summed, grad_branch, keep, send, merge_part, layer_part,
    patch_here, pairs, semaphores,
):
    tiles, height, breadth, _ = pairs.shape
    channels = 128 * tiles
    (copy,) = fetch((patch,), (patch_here,), semaphores)
    value = flat[...]
    copy.wait()
    for dy in range(2):
        for dx in range(2):
            j = 2 * dy + dx
            part = dot_last(value, patch_here[j * channels : (j + 1) * channels])
            part = part.reshape(height // 2, breadth // 2, channels)
            for y in range(height // 2):
                for k in range(channels // 128):
                    piece = part[y, :, k * 128 : (k + 1) * 128]
                    pairs[k, 2 * y + dy, pl.ds(dx, breadth // 2, stride=2), :] = piece
    merge_part[...] = jnp.zeros(merge_part.shape, F32)
    layer_part[...] = jnp.zeros(layer_part.shape, F32)
    core = lax.axis_index("col") % 2
    half = channels // 2

    @over_rows(height, breadth)
    def _(y, rows):
        merged = jnp.concatenate([pairs[k, y] for k in range(tiles)], axis=1)
        unit = unit_summed[rows]
        merge_part[...] += jnp.sum(merged * unit, axis=0, keepdims=True)
        grad = normalize_back(merged * merge_gain[...], unit, inverse_summed[rows])
        grad_summed[rows] = grad
        layer_part[...] += jnp.sum(grad * branch[rows], axis=0, keepdims=True)
        narrow = (layer_scale[...] * grad).astype(BF)
        grad_branch[rows] = narrow
        for i in range(2):

            @pl.when(core == i)
            def _():
                keep[rows] = narrow[:, i * half : (i + 1) * half]
                send[rows] = narrow[:, (1 - i) * half : (2 - i) * half]


def back_kernel(
    grad_branch, project, slope, expand, unit_mixed, inverse_mixed, gain,
    keep, send, grad_mixed, first, last, gain_part,
    project_here, expand_here, hidden, upward, normed, semaphores,
):
    height, breadth, channels = grad_mixed.shape
    pixels, hidden_width = slope.shape
    copies = fetch((project, expand), (project_here, expand_here), semaphores)
    copies[0].wait()

    def chunk(index, carry):
        span = pl.ds(pl.multiple_of(index * CHUNK, CHUNK), CHUNK)
        hidden[...] = dot_last(grad_branch[...], project_here[span])
        for start in range(0, pixels, 64):
            rows = slice(start, start + 64)
            upward[rows, span] = (hidden[rows] * slope[rows, span].astype(F32)).astype(BF)
        return carry

    lax.fori_loop(0, hidden_width // CHUNK, chunk, 0)
    copies[1].wait()
    normed[...] = dot_last(upward[...], expand_here[...])
    half = hidden_width // 2
    core = lax.axis_index("col") % 2
    for i in range(2):

        @pl.when(core == i)
        def _():
            keep[...] = upward[:, i * half : (i + 1) * half]
            send[...] = upward[:, (1 - i) * half : (2 - i) * half]

    part = jnp.zeros((1, channels), F32)
    for y in range(height):
        rows = slice(y * breadth, (y + 1) * breadth)
        value = normed[rows]
        unit = unit_mixed[rows]
        part = part + jnp.sum(value * unit, axis=0, keepdims=True)
        narrow = normalize_back(value * gain[...], unit, inverse_mixed[rows]).astype(BF)
        grad_mixed[y] = narrow
        if y < 3:
            first[y] = narrow
        if y >= height - 3:
            last[y - (height - 3)] = narrow
    gain_part[...] = part


def patch_product_kernel(factor, early, early_other, own, other, keep, send):
    _, rows, width = keep.shape
    blocks = own.shape[0]
    channels = rows // 4
    quarter = own.shape[1]
    at_patches = early.shape[1] - channels
    bit = (lax.axis_index("col") // 2) % 2
    for j in range(4):
        span = slice(j * quarter, (j + 1) * quarter)
        left = jnp.concatenate([early[span, at_patches:], early_other[span, at_patches:]], axis=0)
        for m in range(blocks):
            right = jnp.concatenate([own[m], other[m]], axis=0)
            value = (factor * dot_first(left, right)).astype(BF)
            target = slice(j * channels, (j + 1) * channels)
            for i in range(2):

                @pl.when(bit == i)
                def _():
                    if m % 2 == i:
                        keep[m // 2, target] = value
                    else:
                        send[m // 2, target] = value


def share_product_kernel(
    factor, early, early_other, branch_own, branch_other, upward_own, upward_other,
    small_own, small_other, keep, send,
):
    slices = 2 * keep.shape[0]
    width = keep.shape[2]
    channels = 2 * width
    hidden_width = early.shape[1] - 2 * channels
    deep, shallow = hidden_width // slices, channels // slices
    blocks = upward_own.shape[1] // width
    per = small_own.shape[0] // slices
    bit = lax.axis_index("row") % 2

    def store(value, start, rows):
        begin, offset = start
        for i in range(2):

            @pl.when(bit == i)
            def _():
                for k in range(value.shape[0] // rows):
                    r = begin + k
                    target = keep if r % 2 == i else send
                    target[r // 2, offset : offset + rows] = value[k * rows : (k + 1) * rows]

    right = jnp.concatenate([branch_own[...], branch_other[...]], axis=0)
    step = max(CHUNK, deep)
    for start in range(0, hidden_width, step):
        columns = slice(start, start + step)
        left = jnp.concatenate([early[:, columns], early_other[:, columns]], axis=0)
        store((factor * dot_first(left, right)).astype(BF), (start // deep, 0), deep)
    columns = slice(hidden_width, hidden_width + channels)
    left = jnp.concatenate([early[:, columns], early_other[:, columns]], axis=0)
    for k in range(blocks):
        columns = slice(k * width, (k + 1) * width)
        right = jnp.concatenate([upward_own[:, columns], upward_other[:, columns]], axis=0)
        store((factor * dot_first(left, right)).astype(BF), (0, deep + k * shallow), shallow)
    small = (small_own[...].astype(F32) + small_other[...].astype(F32)).astype(BF)
    store(small, (0, deep + blocks * shallow), per)


def input_kernel(center, top, bottom, left, right, taps, grad_summed, out, frame, image):
    fill_frame(frame, (center, top, bottom, left, right))
    convolve(frame, taps, True, image)
    out[...] = (image[...] + grad_summed[...].reshape(image.shape)).astype(BF)


def body(
    block_input,
    kernel_three,
    gain_three,
    expand_weight,
    project_weight,
    layer_scale,
    merge_gain,
    patch_weight,
    kernel_four,
    gain_four,
    normed_cotangent,
    residual_cotangent,
):
    _, height, breadth, channels = block_input.shape
    hidden_width = expand_weight.shape[1]
    wide = patch_weight.shape[1]
    pixels = height * breadth
    quarter = pixels // 4
    rows4, cols4 = height // 2, breadth // 2
    row_count = lax.axis_size("row")
    col_count = lax.axis_size("col")
    scale_three = 1.0 / math.sqrt(pixels * row_count * col_count)
    scale_four = 1.0 / math.sqrt(quarter * row_count * col_count)
    center = block_input[0]
    cotangent = normed_cotangent[0]
    residual = residual_cotangent[0]
    gain_three, layer_scale, merge_gain, gain_four = (
        v[None] for v in (gain_three, layer_scale, merge_gain, gain_four)
    )
    dma = pltpu.SemaphoreType.DMA
    half = channels // 2

    framed = halo(center, center[:3], center[height - 3 :], "strips_input")
    (
        early, unit_mixed, inverse_mixed, slope, branch, unit_summed, inverse_summed,
        section, first, last,
    ) = run(
        front_kernel,
        "front",
        (*framed, kernel_three, gain_three, expand_weight, project_weight, layer_scale, merge_gain, patch_weight),
        (
            shape_of(pixels, hidden_width + 2 * channels, dtype=BF),
            shape_of(pixels, channels),
            shape_of(pixels, 1),
            shape_of(pixels, hidden_width, dtype=BF),
            shape_of(pixels, channels),
            shape_of(pixels, channels),
            shape_of(pixels, 1),
            shape_of(rows4, cols4, wide, dtype=BF),
            shape_of(3, cols4, wide, dtype=BF),
            shape_of(3, cols4, wide, dtype=BF),
        ),
        scratch=(
            frame_scratch(center),
            pltpu.VMEM((height, breadth, channels), F32),
            pltpu.VMEM((channels // 128, height, breadth, 128), F32),
            pltpu.VMEM(expand_weight.shape, BF),
            pltpu.VMEM(project_weight.shape, BF),
            pltpu.VMEM(patch_weight.shape, BF),
            pltpu.VMEM((pixels, CHUNK), F32),
            dma((3,)),
        ),
        remote=(7, 8, 11),
        limit=28,
        flops=2 * 10**9,
    )

    framed_four = halo(section, first, last, "strips_section")
    early_other = swap(early, "col", 1)
    mixer_image = pltpu.VMEM((rows4, cols4, wide), F32)
    grad_four, grad_four_half, first, last, gain_four_part = run(
        mixer_kernel,
        "mixer",
        (*framed_four, kernel_four, gain_four, cotangent),
        (
            shape_of(rows4, cols4, wide),
            shape_of(rows4, cols4, wide, dtype=BF),
            shape_of(3, cols4, wide, dtype=BF),
            shape_of(3, cols4, wide, dtype=BF),
            shape_of(1, wide),
        ),
        scratch=(frame_scratch(section), mixer_image),
        limit=12,
    )
    framed_grad = halo(grad_four_half, first, last, "strips_mixer")
    (kernel_four_part,) = run(
        functools.partial(weight_kernel, scale_four),
        "mixer_weights",
        (*framed_four, grad_four),
        (shape_of(49, wide),),
        scratch=(frame_scratch(section),),
        limit=12,
    )
    block_count = col_count // 2
    block = wide // col_count
    blocked = shape_of(block_count, quarter, block, dtype=BF)
    flat, flat_keep, flat_send = run(
        section_kernel,
        "section_grad",
        (*framed_grad, kernel_four, residual),
        (shape_of(quarter, wide, dtype=BF), blocked, blocked),
        scratch=(frame_scratch(section), mixer_image),
        limit=12,
    )

    flat_other = swap(flat_send, "col", 1)
    grad_summed, grad_branch, branch_keep, branch_send, merge_part, layer_part = run(
        merge_kernel,
        "merge_back",
        (flat, patch_weight, unit_summed, inverse_summed, merge_gain, branch, layer_scale),
        (
            shape_of(pixels, channels),
            shape_of(pixels, channels, dtype=BF),
            shape_of(pixels, half, dtype=BF),
            shape_of(pixels, half, dtype=BF),
            shape_of(1, channels),
            shape_of(1, channels),
        ),
        scratch=(
            pltpu.VMEM(patch_weight.shape, BF),
            pltpu.VMEM((channels // 128, height, breadth, 128), F32),
            dma((1,)),
        ),
        remote=(1,),
        limit=16,
        flops=5 * 10**8,
    )
    patch_half = shape_of(block_count // 2, 4 * channels, block, dtype=BF)
    patch_keep, patch_send = run(
        functools.partial(patch_product_kernel, scale_four),
        "patch_product",
        (early, early_other, flat_keep, flat_other),
        (patch_half, patch_half),
        limit=16,
        flops=5 * 10**8,
    )
    branch_other = swap(branch_send, "col", 1)
    upward_keep, upward_send, grad_mixed, first, last, gain_part = run(
        back_kernel,
        "mlp_back",
        (grad_branch, project_weight, slope, expand_weight, unit_mixed, inverse_mixed, gain_three),
        (
            shape_of(pixels, hidden_width // 2, dtype=BF),
            shape_of(pixels, hidden_width // 2, dtype=BF),
            shape_of(height, breadth, channels, dtype=BF),
            shape_of(3, breadth, channels, dtype=BF),
            shape_of(3, breadth, channels, dtype=BF),
            shape_of(1, channels),
        ),
        scratch=(
            pltpu.VMEM(project_weight.shape, BF),
            pltpu.VMEM(expand_weight.shape, BF),
            pltpu.VMEM((pixels, CHUNK), F32),
            pltpu.VMEM((pixels, hidden_width), BF),
            pltpu.VMEM((pixels, channels), F32),
            dma((2,)),
        ),
        remote=(1, 3),
        limit=16,
        flops=2 * 10**9,
    )
    upward_other = swap(upward_send, "col", 1)
    framed_back = halo(grad_mixed, first, last, "strips_back")
    per = -(-152 // (16 * row_count)) * 16
    small_half = shape_of(row_count * per, half, dtype=BF)
    small_keep, small_send = run(
        functools.partial(weight_pack_kernel, scale_three, scale_four),
        "block_weights",
        (*framed, grad_mixed, gain_part, layer_part, merge_part, kernel_four_part, gain_four_part),
        (small_half, small_half),
        scratch=(
            frame_scratch(center),
            pltpu.VMEM((height, breadth, channels), F32),
            pltpu.VMEM((row_count * per, channels), F32),
        ),
        limit=12,
    )
    small_other = swap(small_send, "col", 1)
    deep, shallow = hidden_width // row_count, channels // row_count
    groups = hidden_width // channels
    share_half = shape_of(row_count // 2, deep + groups * shallow + per, half, dtype=BF)
    share_keep, share_send = run(
        functools.partial(share_product_kernel, scale_three),
        "share_product",
        (early, early_other, branch_keep, branch_other, upward_keep, upward_other, small_keep, small_other),
        (share_half, share_half),
        limit=16,
        flops=2 * 10**9,
    )
    (input_grad,) = run(
        input_kernel,
        "input_grad",
        (*framed_back, kernel_three, grad_summed),
        (shape_of(height, breadth, channels, dtype=BF),),
        scratch=(frame_scratch(center), pltpu.VMEM((height, breadth, channels), F32)),
        limit=12,
    )

    row_bits, col_bits = axis_bits("row"), axis_bits("col")
    patch_sum = patch_keep + swap(patch_send, "col", 2)
    patch_sum = scatter(patch_sum, "col", col_bits[2:])
    patch_sum = scatter(patch_sum.reshape(row_count, -1, block), "row", row_bits)
    share = share_keep + swap(share_send, "row", 1)
    share = scatter(share, "row", row_bits[1:])
    for bit in col_bits[1:]:
        share = share + swap(share, "col", bit)

    patch_sum = gather(patch_sum, "col", col_bits)
    patch_grad = patch_sum.transpose(1, 0, 2).reshape(-1, wide).astype(F32)
    share = gather(share, "col", col_bits[:1])
    project_grad = share[:, :deep].transpose(1, 0, 2).reshape(deep, channels).astype(F32)
    expand_grad = share[:, deep : deep + groups * shallow].reshape(2 * groups, shallow, half)
    expand_grad = expand_grad.transpose(1, 0, 2).reshape(shallow, hidden_width).astype(F32)
    small = share[:, deep + groups * shallow :].transpose(1, 0, 2).reshape(per, channels)
    small = gather(small, "row", row_bits).reshape(row_count * per, channels).astype(F32)
    wide_rows = small[52:150].reshape(2, 49, channels).transpose(1, 0, 2).reshape(7, 7, wide)
    return (
        input_grad[None],
        small[:49].reshape(7, 7, channels),
        small[49],
        expand_grad,
        project_grad,
        small[50],
        small[51],
        patch_grad,
        wide_rows,
        small[150:152].reshape(wide),
    )


def solution(mesh):
    pixels = P(None, "row", "col", None)
    return jax.shard_map(
        body,
        mesh=mesh,
        in_specs=(pixels,) + (P(),) * 9 + (pixels, pixels),
        out_specs=(pixels, P(), P(), P("row", None), P("row", None), P(), P(), P("row", None), P(), P()),
        check_vma=False,
    )
```

profile of v0, /device:TPU:0, one launch (start us, length us, event | category | flops | bytes accessed | tf_op | source)
XLA Modules:
  0.0 218.6 jit_solution(610495006637081607)
XLA Ops:
  1.6 4.8 %collective-permute-start = (bf16[3,32,512]{2,1,0:T(8,128)(2,1)S(1)}, bf16[3,32,512]{2,1,0:T(8,128)(2,1)S(1)}, u32[]{:S(2)}, u32[]{:S(2)}) collective-permute-start(bf16[3,32,512]{2,1,0:T(8,128)(2,1)S(1)} %get-tuple-element.132), channel_id=1, source_target_pairs={{0,4},{4,8},{8,12},{12,16},{16,20},{20,24},{24,28},{1,5},{5,9},{9,... | collective-permute-start | bytes 294920 | tf_op jit(solution)/shard_map/ppermute | solution.py:79
  6.5 1.3 collective-permute-start.1
  8.6 4.3 %collective-permute-done.1.bottom = bf16[3,32,512]{2,1,0:T(8,128)(2,1)S(1)} collective-permute-done((bf16[3,32,512]{2,1,0:T(8,128)(2,1)S(1)}, bf16[3,32,512]{2,1,0:T(8,128)(2,1)S(1)}, u32[]{:S(2)}, u32[]{:S(2)}) %collective-permute-start.1) | collective-permute-done | bytes 98336 | tf_op jit(solution)/shard_map/ppermute | solution.py:79
  13.9 1.3 collective-permute-start.2
  15.2 1.3 collective-permute-start.3
  16.6 3.7 %collective-permute-done.3.right = bf16[14,8,512]{2,1,0:T(8,128)(2,1)S(1)} collective-permute-done((bf16[14,8,512]{2,1,0:T(8,128)(2,1)S(1)}, bf16[14,8,512]{2,1,0:T(8,128)(2,1)S(1)}, u32[]{:S(2)}, u32[]{:S(2)}) %collective-permute-start.3) | collective-permute-done | bytes 114720 | tf_op jit(solution)/shard_map/ppermute | solution.py:79
  20.2 2.2 %copy-done = bf16[2048,1024]{1,0:T(8,128)(2,1)S(1)} copy-done((bf16[2048,1024]{1,0:T(8,128)(2,1)S(1)}, bf16[2048,1024]{1,0:T(8,128)(2,1)}, u32[]{:S(2)}) %copy-start) | copy-done | bytes 4194328
  23.4 1.6 copy-done.3
  24.9 1.6 copy-done.4
  29.5 12.1 %front.1 = (bf16[256,3072]{1,0:T(8,128)(2,1)S(1)}, f32[256,512]{1,0:T(8,128)S(1)}, f32[256,1]{1,0:T(8,128)S(1)}, bf16[256,2048]{1,0:T(8,128)(2,1)S(1)}, f32[256,...) custom-call(bf16[8,32,512]{2,1,0:T(8,128)(2,1)S(1)} %bitcast.96, ...), custom_call_target="tpu_custom_call" | custom-call | flops 2000000000 | bytes 13707264 | tf_op jit(solution)/shard_map/front/pallas_call | solution.py:28
  41.6 3.5 %collective-permute-start.16 = (bf16[256,3072]{1,0:T(8,128)(2,1)S(1)}, bf16[256,3072]{1,0:T(8,128)(2,1)S(1)}, u32[]{:S(2)}, u32[]{:S(2)}) collective-permute-start(bf16[256,3072]{1,0:T(8,128)(2,1)S(1)} %get-tuple-element.80.early), channel_id=1, source_target_pairs={{0,1},{1,0},{2,3},{3,2},{4,5},{5,4},{6,7},{7,6},{8,9},{9,8},{10,11... | collective-permute-start | bytes 4718600 | tf_op jit(solution)/shard_map/ppermute | solution.py:41
  45.1 4.3 %collective-permute-start.4 = (bf16[3,16,1024]{2,1,0:T(8,128)(2,1)S(1)}, bf16[3,16,1024]{2,1,0:T(8,128)(2,1)S(1)}, u32[]{:S(2)}, u32[]{:S(2)}) collective-permute-start(bf16[3,16,1024]{2,1,0:T(8,128)(2,1)S(1)} %get-tuple-element.57), channel_id=1, source_target_pairs={{0,4},{4,8},{8,12},{12,16},{16,20},{20,24},{24,28},{1,5},{5,9},{9,... | collective-permute-start | bytes 294920 | tf_op jit(solution)/shard_map/ppermute | solution.py:79
  49.4 1.3 collective-permute-start.5
  51.6 4.3 %collective-permute-done.5.bottom = bf16[3,16,1024]{2,1,0:T(8,128)(2,1)S(1)} collective-permute-done((bf16[3,16,1024]{2,1,0:T(8,128)(2,1)S(1)}, bf16[3,16,1024]{2,1,0:T(8,128)(2,1)S(1)}, u32[]{:S(2)}, u32[]{:S(2)}) %collective-permute-start.5) | collective-permute-done | bytes 98336 | tf_op jit(solution)/shard_map/ppermute | solution.py:79
  55.9 1.3 collective-permute-start.6
  57.3 1.3 collective-permute-start.7
  58.6 2.3 %collective-permute-done.7.right = bf16[10,8,1024]{2,1,0:T(8,128)(2,1)S(1)} collective-permute-done((bf16[10,8,1024]{2,1,0:T(8,128)(2,1)S(1)}, bf16[10,8,1024]{2,1,0:T(8,128)(2,1)S(1)}, u32[]{:S(2)}, u32[]{:S(2)}) %collective-permute-start.7) | collective-permute-done | bytes 163872 | tf_op jit(solution)/shard_map/ppermute | solution.py:79
  60.9 3.3 %mixer.1 = (f32[4,16,1024]{2,1,0:T(8,128)S(1)}, bf16[4,16,1024]{2,1,0:T(8,128)(2,1)S(1)}, bf16[3,16,1024]{2,1,0:T(8,128)(2,1)S(1)}, bf16[3,16,1024]{2,1,0:T(8,128)(2,1)S(1)}, f32[1,1024]{1,0:T(1,128)S(1)}) custom-call(bf16[4,16,1024]{2,1,0:T(8,128)(2,1)S(1)} %get-tuple-element.56.center, bf16[3,16,1024]{2,1,0:T(8,128)(2,1)S(1)} %collective-permute-done.4.top, ...), custom_call_target="tpu_custom_call" | custom-call | flops 10000000 | bytes 1585152 | tf_op jit(solution)/shard_map/mixer/pallas_call | solution.py:28
  64.2 3.4 %collective-permute-start.8 = (bf16[3,16,1024]{2,1,0:T(8,128)(2,1)S(1)}, bf16[3,16,1024]{2,1,0:T(8,128)(2,1)S(1)}, u32[]{:S(2)}, u32[]{:S(2)}) collective-permute-start(bf16[3,16,1024]{2,1,0:T(8,128)(2,1)S(1)} %get-tuple-element.62), channel_id=1, source_target_pairs={{0,4},{4,8},{8,12},{12,16},{16,20},{20,24},{24,28},{1,5},{5,9},{9,... | collective-permute-start | bytes 294920 | tf_op jit(solution)/shard_map/ppermute | solution.py:79
  67.6 1.3 collective-permute-start.9
  69.8 4.3 %collective-permute-done.9.bottom = bf16[3,16,1024]{2,1,0:T(8,128)(2,1)S(1)} collective-permute-done((bf16[3,16,1024]{2,1,0:T(8,128)(2,1)S(1)}, bf16[3,16,1024]{2,1,0:T(8,128)(2,1)S(1)}, u32[]{:S(2)}, u32[]{:S(2)}) %collective-permute-start.9) | collective-permute-done | bytes 98336 | tf_op jit(solution)/shard_map/ppermute | solution.py:79
  74.2 4.3 %collective-permute-start.10 = (bf16[10,8,1024]{2,1,0:T(8,128)(2,1)S(1)}, bf16[10,8,1024]{2,1,0:T(8,128)(2,1)S(1)}, u32[]{:S(2)}, u32[]{:S(2)}) collective-permute-start(bf16[10,8,1024]{2,1,0:T(8,128)(2,1)S(1)} %get-tuple-element.64), channel_id=1, source_target_pairs={{0,1},{1,2},{2,3},{4,5},{5,6},{6,7},{8,9},{9,10},{10,11},{12,13},{... | collective-permute-start | bytes 491528 | tf_op jit(solution)/shard_map/ppermute | solution.py:79
  78.5 1.3 collective-permute-start.11
  79.8 2.7 %collective-permute-done.11.right = bf16[10,8,1024]{2,1,0:T(8,128)(2,1)S(1)} collective-permute-done((bf16[10,8,1024]{2,1,0:T(8,128)(2,1)S(1)}, bf16[10,8,1024]{2,1,0:T(8,128)(2,1)S(1)}, u32[]{:S(2)}, u32[]{:S(2)}) %collective-permute-start.11) | collective-permute-done | bytes 163872 | tf_op jit(solution)/shard_map/ppermute | solution.py:79
  82.6 3.1 %section_grad.1 = (bf16[64,1024]{1,0:T(8,128)(2,1)S(1)}, bf16[2,64,256]{2,1,0:T(8,128)(2,1)S(1)}, bf16[2,64,256]{2,1,0:T(8,128)(2,1)S(1)}) custom-call(bf16[4,16,1024]{2,1,0:T(8,128)(2,1)S(1)} %get-tuple-element.61.center, bf16[3,16,1024]{2,1,0:T(8,128)(2,1)S(1)} %collective-permute-done.8.top, bf16[3,16,1024]{2,1,0:T(8,128)(2,1)S(1)} %collective-permute-done.9.bottom, ...), custom_call_target="tpu_custom_call" | custom-call | flops 10000000 | bytes 1249280 | tf_op jit(solution)/shard_map/section_grad/pallas_call | solution.py:28
  85.7 2.8 %merge_back.1 = (f32[256,512]{1,0:T(8,128)S(1)}, bf16[256,512]{1,0:T(8,128)(2,1)S(1)}, bf16[256,256]{1,0:T(8,128)(2,1)S(1)}, bf16[256,256]{1,0:T(8,128)(2,1)S(1)...) custom-call(bf16[64,1024]{1,0:T(8,128)(2,1)S(1)} %get-tuple-element.66.flat, bf16[2048,1024]{1,0:T(8,128)(2,1)S(1)} %copy-done, ...), custom_call_target="tpu_custom_call" | custom-call | flops 500000000 | bytes 6431744 | tf_op jit(solution)/shard_map/merge_back/pallas_call | solution.py:28
  88.4 3.5 %mlp_back.1 = (bf16[256,1024]{1,0:T(8,128)(2,1)S(1)}, bf16[256,1024]{1,0:T(8,128)(2,1)S(1)}, bf16[8,32,512]{2,1,0:T(8,128)(2,1)S(1)}, bf16[3,32,512]{2,1,0:T(8,1...) custom-call(bf16[256,512]{1,0:T(8,128)(2,1)S(1)} %get-tuple-element.70.grad_branch, ...), custom_call_target="tpu_custom_call" | custom-call | flops 2000000000 | bytes 7541760 | tf_op jit(solution)/shard_map/mlp_back/pallas_call | solution.py:28
  91.9 3.9 %collective-permute-start.18 = (bf16[256,1024]{1,0:T(8,128)(2,1)S(1)}, bf16[256,1024]{1,0:T(8,128)(2,1)S(1)}, u32[]{:S(2)}, u32[]{:S(2)}) collective-permute-start(bf16[256,1024]{1,0:T(8,128)(2,1)S(1)} %get-tuple-element.84), channel_id=1, source_target_pairs={{0,1},{1,0},{2,3},{3,2},{4,5},{5,4},{6,7},{7,6},{8,9},{9,8},{10,11... | collective-permute-start | bytes 1572872 | tf_op jit(solution)/shard_map/ppermute | solution.py:41
  95.9 2.9 %mixer_weights.1.wide_part = f32[49,1024]{1,0:T(8,128)S(1)} custom-call(bf16[4,16,1024]{2,1,0:T(8,128)(2,1)S(1)} %get-tuple-element.56.center, bf16[3,16,1024]{2,1,0:T(8,128)(2,1)S(1)} %collective-permute-done.4.top, bf16[3,16,1024]{2,1,0:T(8,128)(2,1)S(1)} %collective-permute-done.5.bottom, bf16[10,8,1024]{2,1,0:T(8,128)(2,1)S(1)} %collective-permute-done.6.left, ...), custom_call_target="tpu_custom_call" | custom-call | flops 10000000 | bytes 1118208 | tf_op jit(solution)/shard_map/mixer_weights/pallas_call | solution.py:28
  99.3 5.4 %block_weights.1 = (bf16[256,256]{1,0:T(8,128)(2,1)S(1)}, bf16[256,256]{1,0:T(8,128)(2,1)S(1)}) custom-call(bf16[8,32,512]{2,1,0:T(8,128)(2,1)S(1)} %bitcast.97, bf16[3,32,512]{2,1,0:T(8,128)(2,1)S(1)} %collective-permute-done.top, bf16[3,32,512]{2,1,0:T(8,128)(2,1)S(1)} %collective-permute-done.1.bottom, ...), custom_call_target="tpu_custom_call" | custom-call | flops 10000000 | bytes 1423360 | tf_op jit(solution)/shard_map/block_weights/pallas_call | solution.py:28
  104.9 3.5 %patch_product.1 = (bf16[1,2048,256]{2,1,0:T(8,128)(2,1)S(1)}, bf16[1,2048,256]{2,1,0:T(8,128)(2,1)}) custom-call(bf16[256,3072]{1,0:T(8,128)(2,1)S(1)} %get-tuple-element.80.early, bf16[256,3072]{1,0:T(8,128)(2,1)S(1)} %collective-permute-done.16.early_other, bf16[2,64,256]{2,1,0:T(8,128)(2,1)S(1)} %get-tuple-element.94.own, ...), custom_call_target="tpu_custom_call" | custom-call | flops 500000000 | bytes 5373952 | tf_op jit(solution)/shard_map/patch_product/pallas_call | solution.py:28
  108.6 5.7 %share_product.1 = (bf16[4,544,256]{2,1,0:T(8,128)(2,1)S(1)}, bf16[4,544,256]{2,1,0:T(8,128)(2,1)}) custom-call(bf16[256,3072]{1,0:T(8,128)(2,1)S(1)} %get-tuple-element.80.early, bf16[256,3072]{1,0:T(8,128)(2,1)S(1)} %collective-permute-done.16.early_other, bf16[256,256]{1,0:T(8,128)(2,1)S(1)} %get-tuple-element.81.branch_own, ...), custom_call_target="tpu_custom_call" | custom-call | flops 2000000000 | bytes 6946816 | tf_op jit(solution)/shard_map/share_product/pallas_call | solution.py:28
  114.3 2.5 %collective-permute-start.20 = (bf16[4,544,256]{2,1,0:T(8,128)(2,1)}, bf16[4,544,256]{2,1,0:T(8,128)(2,1)}, u32[]{:S(2)}, u32[]{:S(2)}) collective-permute-start(bf16[4,544,256]{2,1,0:T(8,128)(2,1)} %get-tuple-element.93), channel_id=1, source_target_pairs={{0,4},{4,0},{8,12},{12,8},{16,20},{20,16},{24,28},{28,24},{1,5},{5... | collective-permute-start | bytes 3342344 | tf_op jit(solution)/shard_map/ppermute | solution.py:41
  116.8 17.4 %collective-permute-done.29 = bf16[1,2048,256]{2,1,0:T(8,128)(2,1)} collective-permute-done((bf16[1,2048,256]{2,1,0:T(8,128)(2,1)}, bf16[1,2048,256]{2,1,0:T(8,128)(2,1)}, u32[]{:S(2)}, u32[]{:S(2)}) %collective-permute-start.29) | collective-permute-done | bytes 1048608 | tf_op jit(solution)/shard_map/ppermute | solution.py:41
  134.2 1.5 add.94
  137.5 2.4 %collective-permute-start.30 = (bf16[4,256,256]{2,1,0:T(8,128)(2,1)}, bf16[4,256,256]{2,1,0:T(8,128)(2,1)}, u32[]{:S(2)}, u32[]{:S(2)}) collective-permute-start(bf16[4,256,256]{2,1,0:T(8,128)(2,1)} %dynamic-slice_bitcast_fusion.1), channel_id=1, source_target_pairs={{0,4},{4,0},{8,12},{12,8},{16,20},{20,16},{24,28},{28,24},{1,5},{5... | collective-permute-start | bytes 1572872 | tf_op jit(solution)/shard_map/ppermute | solution.py:41
  140.0 2.5 %collective-permute-done.20 = bf16[4,544,256]{2,1,0:T(8,128)(2,1)} collective-permute-done((bf16[4,544,256]{2,1,0:T(8,128)(2,1)}, bf16[4,544,256]{2,1,0:T(8,128)(2,1)}, u32[]{:S(2)}, u32[]{:S(2)}) %collective-permute-start.20) | collective-permute-done | bytes 1114144 | tf_op jit(solution)/shard_map/ppermute | solution.py:41
  142.5 1.5 add.85
  144.0 1.0 copy-done.14
  145.8 1.6 collective-permute-start.21
  147.4 5.9 %collective-permute-done.30 = bf16[4,256,256]{2,1,0:T(8,128)(2,1)} collective-permute-done((bf16[4,256,256]{2,1,0:T(8,128)(2,1)}, bf16[4,256,256]{2,1,0:T(8,128)(2,1)}, u32[]{:S(2)}, u32[]{:S(2)}) %collective-permute-start.30) | collective-permute-done | bytes 524320 | tf_op jit(solution)/shard_map/ppermute | solution.py:41
  153.4 1.1 bitcast_add_fusion.1
  156.0 1.6 collective-permute-start.31
  157.6 3.6 %collective-permute-start.12 = (bf16[3,32,512]{2,1,0:T(8,128)(2,1)S(1)}, bf16[3,32,512]{2,1,0:T(8,128)(2,1)S(1)}, u32[]{:S(2)}, u32[]{:S(2)}) collective-permute-start(bf16[3,32,512]{2,1,0:T(8,128)(2,1)S(1)} %get-tuple-element.75), channel_id=1, source_target_pairs={{0,4},{4,8},{8,12},{12,16},{16,20},{20,24},{24,28},{1,5},{5,9},{9,... | collective-permute-start | bytes 294920 | tf_op jit(solution)/shard_map/ppermute | solution.py:79
  161.2 1.3 collective-permute-start.13
  162.5 1.1 bitcast_add_fusion
  163.6 3.1 %collective-permute-done.31 = bf16[2,256,256]{2,1,0:T(8,128)(2,1)} collective-permute-done((bf16[2,256,256]{2,1,0:T(8,128)(2,1)}, bf16[2,256,256]{2,1,0:T(8,128)(2,1)}, u32[]{:S(2)}, u32[]{:S(2)}) %collective-permute-start.31) | collective-permute-done | bytes 262176 | tf_op jit(solution)/shard_map/ppermute | solution.py:41
  166.8 1.0 bitcast_add_fusion.2
  167.8 1.6 collective-permute-start.32
  169.4 1.5 collective-permute-start.22
  170.9 1.3 collective-permute-start.14
  172.2 1.3 collective-permute-start.15
  173.5 8.3 %collective-permute-done.32 = bf16[1,256,256]{2,1,0:T(8,128)(2,1)S(1)} collective-permute-done((bf16[1,256,256]{2,1,0:T(8,128)(2,1)S(1)}, bf16[1,256,256]{2,1,0:T(8,128)(2,1)S(1)}, u32[]{:S(2)}, u32[]{:S(2)}) %collective-permute-start.32) | collective-permute-done | bytes 131104 | tf_op jit(solution)/shard_map/ppermute | solution.py:41
  181.8 1.7 collective-permute-start.33
  183.5 3.1 %collective-permute-done.22 = bf16[1,544,256]{2,1,0:T(8,128)(2,1)S(1)} collective-permute-done((bf16[1,544,256]{2,1,0:T(8,128)(2,1)S(1)}, bf16[1,544,256]{2,1,0:T(8,128)(2,1)S(1)}, u32[]{:S(2)}, u32[]{:S(2)}) %collective-permute-start.22) | collective-permute-done | bytes 278560 | tf_op jit(solution)/shard_map/ppermute | solution.py:41
  186.6 1.7 collective-permute-start.23
  188.5 5.7 %collective-permute-done.23 = bf16[544,256]{1,0:T(8,128)(2,1)S(1)} collective-permute-done((bf16[544,256]{1,0:T(8,128)(2,1)S(1)}, bf16[544,256]{1,0:T(8,128)(2,1)S(1)}, u32[]{:S(2)}, u32[]{:S(2)}) %collective-permute-start.23) | collective-permute-done | bytes 278560 | tf_op jit(solution)/shard_map/ppermute | solution.py:41
  194.4 6.6 %input_grad.1 = bf16[8,32,512]{2,1,0:T(8,128)(2,1)} custom-call(bf16[8,32,512]{2,1,0:T(8,128)(2,1)S(1)} %get-tuple-element.74.center.grads, bf16[3,32,512]{2,1,0:T(8,128)(2,1)S(1)} %collective-permute-done.12.top, bf16[3,32,512]{2,1,0:T(8,128)(2,1)S(1)} %collective-permute-done.13.bottom, bf16[14,8,512]{2,1,0:T(8,128)(2,1)S(1)} %collective-permute-done.14.left, ...), custom_call_target="tpu_custom_call" | custom-call | flops 10000000 | bytes 1574912 | tf_op jit(solution)/shard_map/input_grad/pallas_call | solution.py:28
  201.8 1.3 copy.44
  203.1 3.0 %collective-permute-done.25 = bf16[1,32,512]{2,1,0:T(8,128)(2,1)S(1)} collective-permute-done((bf16[1,32,512]{2,1,0:T(8,128)(2,1)S(1)}, bf16[1,32,512]{2,1,0:T(8,128)(2,1)S(1)}, u32[]{:S(2)}, u32[]{:S(2)}) %collective-permute-start.25) | collective-permute-done | bytes 32800 | tf_op jit(solution)/shard_map/ppermute | solution.py:41
  206.2 4.2 %collective-permute-done.26 = bf16[2,32,512]{2,1,0:T(8,128)(2,1)S(1)} collective-permute-done((bf16[2,32,512]{2,1,0:T(8,128)(2,1)S(1)}, bf16[2,32,512]{2,1,0:T(8,128)(2,1)S(1)}, u32[]{:S(2)}, u32[]{:S(2)}) %collective-permute-start.26) | collective-permute-done | bytes 65568 | tf_op jit(solution)/shard_map/ppermute | solution.py:41
  210.5 1.5 collective-permute-start.27
  213.1 1.0 copy.43
  214.1 1.5 collective-permute-done.27
  (108 shorter events, 19.0 us)
Async XLA Ops:
  1.6 7.0 %collective-permute-start = (bf16[3,32,512]{2,1,0:T(8,128)(2,1)S(1)}, bf16[3,32,512]{2,1,0:T(8,128)(2,1)S(1)}, u32[]{:S(2)}, u32[]{:S(2)}) collective-permute-start(bf16[3,32,512]{2,1,0:T(8,128)(2,1)S(1)} %get-tuple-element.132), channel_id=1, source_target_pairs={{0,4},{4,8},{8,12},{12,16},{16,20},{20,24},{24,28},{1,5},{5,9},{9,... | collective-permute-start | bytes 294920 | tf_op jit(solution)/shard_map/ppermute | solution.py:79
  6.5 6.5 %collective-permute-start.1 = (bf16[3,32,512]{2,1,0:T(8,128)(2,1)S(1)}, bf16[3,32,512]{2,1,0:T(8,128)(2,1)S(1)}, u32[]{:S(2)}, u32[]{:S(2)}) collective-permute-start(bf16[3,32,512]{2,1,0:T(8,128)(2,1)S(1)} %get-tuple-element.131), channel_id=1, source_target_pairs={{4,0},{8,4},{12,8},{16,12},{20,16},{24,20},{28,24},{5,1},{9,5},{13... | collective-permute-start | bytes 294920 | tf_op jit(solution)/shard_map/ppermute | solution.py:79
  13.0 1.0 copy-start.1
  13.9 2.6 %collective-permute-start.2 = (bf16[14,8,512]{2,1,0:T(8,128)(2,1)S(1)}, bf16[14,8,512]{2,1,0:T(8,128)(2,1)S(1)}, u32[]{:S(2)}, u32[]{:S(2)}) collective-permute-start(bf16[14,8,512]{2,1,0:T(8,128)(2,1)S(1)} %get-tuple-element.54), channel_id=1, source_target_pairs={{0,1},{1,2},{2,3},{4,5},{5,6},{6,7},{8,9},{9,10},{10,11},{12,13},{... | collective-permute-start | bytes 344072 | tf_op jit(solution)/shard_map/ppermute | solution.py:79
  15.2 5.0 %collective-permute-start.3 = (bf16[14,8,512]{2,1,0:T(8,128)(2,1)S(1)}, bf16[14,8,512]{2,1,0:T(8,128)(2,1)S(1)}, u32[]{:S(2)}, u32[]{:S(2)}) collective-permute-start(bf16[14,8,512]{2,1,0:T(8,128)(2,1)S(1)} %get-tuple-element.55), channel_id=1, source_target_pairs={{1,0},{2,1},{3,2},{5,4},{6,5},{7,6},{9,8},{10,9},{11,10},{13,12},{... | collective-permute-start | bytes 344072 | tf_op jit(solution)/shard_map/ppermute | solution.py:79
  20.2 2.2 %copy-start = (bf16[2048,1024]{1,0:T(8,128)(2,1)S(1)}, bf16[2048,1024]{1,0:T(8,128)(2,1)}, u32[]{:S(2)}) copy-start(bf16[2048,1024]{1,0:T(8,128)(2,1)} %patch.3) | copy-start | bytes 12582916
  22.4 0.9 copy-start.2
  23.3 1.6 copy-start.3
  24.9 1.6 copy-start.4
  26.5 0.9 copy-start.6
  27.4 0.7 copy-start.10
  28.1 0.7 copy-start.11
  28.8 0.7 copy-start.13
  29.5 31.4 %copy-start.5 = (f32[7,7,1024]{2,1,0:T(8,128)S(1)}, f32[7,7,1024]{2,1,0:T(8,128)}, u32[]{:S(2)}) copy-start(f32[7,7,1024]{2,1,0:T(8,128)} %taps.6) | copy-start | bytes 602116
  29.5 31.4 %copy-start.8 = (bf16[1,4,16,1024]{3,2,1,0:T(8,128)(2,1)S(1)}, bf16[1,4,16,1024]{3,2,1,0:T(8,128)(2,1)}, u32[]{:S(2)}) copy-start(bf16[1,4,16,1024]{3,2,1,0:T(8,128)(2,1)} %param.22) | copy-start | bytes 393220
  29.5 31.4 %copy-start.12 = (f32[1024]{0:T(1024)S(1)}, f32[1024]{0:T(1024)}, u32[]{:S(2)}) copy-start(f32[1024]{0:T(1024)} %param.21) | copy-start | bytes 12292
  41.6 41.0 %copy-start.9 = (bf16[1,4,16,1024]{3,2,1,0:T(8,128)(2,1)S(1)}, bf16[1,4,16,1024]{3,2,1,0:T(8,128)(2,1)}, u32[]{:S(2)}) copy-start(bf16[1,4,16,1024]{3,2,1,0:T(8,128)(2,1)} %param.23) | copy-start | bytes 393220
  41.6 63.3 %collective-permute-start.16 = (bf16[256,3072]{1,0:T(8,128)(2,1)S(1)}, bf16[256,3072]{1,0:T(8,128)(2,1)S(1)}, u32[]{:S(2)}, u32[]{:S(2)}) collective-permute-start(bf16[256,3072]{1,0:T(8,128)(2,1)S(1)} %get-tuple-element.80.early), channel_id=1, source_target_pairs={{0,1},{1,0},{2,3},{3,2},{4,5},{5,4},{6,7},{7,6},{8,9},{9,8},{10,11... | collective-permute-start | bytes 4718600 | tf_op jit(solution)/shard_map/ppermute | solution.py:41
  45.1 6.6 %collective-permute-start.4 = (bf16[3,16,1024]{2,1,0:T(8,128)(2,1)S(1)}, bf16[3,16,1024]{2,1,0:T(8,128)(2,1)S(1)}, u32[]{:S(2)}, u32[]{:S(2)}) collective-permute-start(bf16[3,16,1024]{2,1,0:T(8,128)(2,1)S(1)} %get-tuple-element.57), channel_id=1, source_target_pairs={{0,4},{4,8},{8,12},{12,16},{16,20},{20,24},{24,28},{1,5},{5,9},{9,... | collective-permute-start | bytes 294920 | tf_op jit(solution)/shard_map/ppermute | solution.py:79
  49.4 6.5 %collective-permute-start.5 = (bf16[3,16,1024]{2,1,0:T(8,128)(2,1)S(1)}, bf16[3,16,1024]{2,1,0:T(8,128)(2,1)S(1)}, u32[]{:S(2)}, u32[]{:S(2)}) collective-permute-start(bf16[3,16,1024]{2,1,0:T(8,128)(2,1)S(1)} %get-tuple-element.58), channel_id=1, source_target_pairs={{4,0},{8,4},{12,8},{16,12},{20,16},{24,20},{28,24},{5,1},{9,5},{13... | collective-permute-start | bytes 294920 | tf_op jit(solution)/shard_map/ppermute | solution.py:79
  55.9 2.6 %collective-permute-start.6 = (bf16[10,8,1024]{2,1,0:T(8,128)(2,1)S(1)}, bf16[10,8,1024]{2,1,0:T(8,128)(2,1)S(1)}, u32[]{:S(2)}, u32[]{:S(2)}) collective-permute-start(bf16[10,8,1024]{2,1,0:T(8,128)(2,1)S(1)} %get-tuple-element.59), channel_id=1, source_target_pairs={{0,1},{1,2},{2,3},{4,5},{5,6},{6,7},{8,9},{9,10},{10,11},{12,13},{... | collective-permute-start | bytes 491528 | tf_op jit(solution)/shard_map/ppermute | solution.py:79
  57.3 3.6 %collective-permute-start.7 = (bf16[10,8,1024]{2,1,0:T(8,128)(2,1)S(1)}, bf16[10,8,1024]{2,1,0:T(8,128)(2,1)S(1)}, u32[]{:S(2)}, u32[]{:S(2)}) collective-permute-start(bf16[10,8,1024]{2,1,0:T(8,128)(2,1)S(1)} %get-tuple-element.60), channel_id=1, source_target_pairs={{1,0},{2,1},{3,2},{5,4},{6,5},{7,6},{9,8},{10,9},{11,10},{13,12},{... | collective-permute-start | bytes 491528 | tf_op jit(solution)/shard_map/ppermute | solution.py:79
  64.2 5.6 %collective-permute-start.8 = (bf16[3,16,1024]{2,1,0:T(8,128)(2,1)S(1)}, bf16[3,16,1024]{2,1,0:T(8,128)(2,1)S(1)}, u32[]{:S(2)}, u32[]{:S(2)}) collective-permute-start(bf16[3,16,1024]{2,1,0:T(8,128)(2,1)S(1)} %get-tuple-element.62), channel_id=1, source_target_pairs={{0,4},{4,8},{8,12},{12,16},{16,20},{20,24},{24,28},{1,5},{5,9},{9,... | collective-permute-start | bytes 294920 | tf_op jit(solution)/shard_map/ppermute | solution.py:79
  67.6 6.5 %collective-permute-start.9 = (bf16[3,16,1024]{2,1,0:T(8,128)(2,1)S(1)}, bf16[3,16,1024]{2,1,0:T(8,128)(2,1)S(1)}, u32[]{:S(2)}, u32[]{:S(2)}) collective-permute-start(bf16[3,16,1024]{2,1,0:T(8,128)(2,1)S(1)} %get-tuple-element.63), channel_id=1, source_target_pairs={{4,0},{8,4},{12,8},{16,12},{20,16},{24,20},{28,24},{5,1},{9,5},{13... | collective-permute-start | bytes 294920 | tf_op jit(solution)/shard_map/ppermute | solution.py:79
  74.2 5.6 %collective-permute-start.10 = (bf16[10,8,1024]{2,1,0:T(8,128)(2,1)S(1)}, bf16[10,8,1024]{2,1,0:T(8,128)(2,1)S(1)}, u32[]{:S(2)}, u32[]{:S(2)}) collective-permute-start(bf16[10,8,1024]{2,1,0:T(8,128)(2,1)S(1)} %get-tuple-element.64), channel_id=1, source_target_pairs={{0,1},{1,2},{2,3},{4,5},{5,6},{6,7},{8,9},{9,10},{10,11},{12,13},{... | collective-permute-start | bytes 491528 | tf_op jit(solution)/shard_map/ppermute | solution.py:79
  78.5 4.0 %collective-permute-start.11 = (bf16[10,8,1024]{2,1,0:T(8,128)(2,1)S(1)}, bf16[10,8,1024]{2,1,0:T(8,128)(2,1)S(1)}, u32[]{:S(2)}, u32[]{:S(2)}) collective-permute-start(bf16[10,8,1024]{2,1,0:T(8,128)(2,1)S(1)} %get-tuple-element.65), channel_id=1, source_target_pairs={{1,0},{2,1},{3,2},{5,4},{6,5},{7,6},{9,8},{10,9},{11,10},{13,12},{... | collective-permute-start | bytes 491528 | tf_op jit(solution)/shard_map/ppermute | solution.py:79
  91.9 16.7 %collective-permute-start.18 = (bf16[256,1024]{1,0:T(8,128)(2,1)S(1)}, bf16[256,1024]{1,0:T(8,128)(2,1)S(1)}, u32[]{:S(2)}, u32[]{:S(2)}) collective-permute-start(bf16[256,1024]{1,0:T(8,128)(2,1)S(1)} %get-tuple-element.84), channel_id=1, source_target_pairs={{0,1},{1,0},{2,3},{3,2},{4,5},{5,4},{6,7},{7,6},{8,9},{9,8},{10,11... | collective-permute-start | bytes 1572872 | tf_op jit(solution)/shard_map/ppermute | solution.py:41
  95.8 9.1 %collective-permute-start.28 = (bf16[2,64,256]{2,1,0:T(8,128)(2,1)S(1)}, bf16[2,64,256]{2,1,0:T(8,128)(2,1)S(1)}, u32[]{:S(2)}, u32[]{:S(2)}) collective-permute-start(bf16[2,64,256]{2,1,0:T(8,128)(2,1)S(1)} %get-tuple-element.95), channel_id=1, source_target_pairs={{0,1},{1,0},{2,3},{3,2},{4,5},{5,4},{6,7},{7,6},{8,9},{9,8},{10,11... | collective-permute-start | bytes 196616 | tf_op jit(solution)/shard_map/ppermute | solution.py:41
  98.8 9.8 %collective-permute-start.17 = (bf16[256,256]{1,0:T(8,128)(2,1)S(1)}, bf16[256,256]{1,0:T(8,128)(2,1)S(1)}, u32[]{:S(2)}, u32[]{:S(2)}) collective-permute-start(bf16[256,256]{1,0:T(8,128)(2,1)S(1)} %get-tuple-element.82), channel_id=1, source_target_pairs={{0,1},{1,0},{2,3},{3,2},{4,5},{5,4},{6,7},{7,6},{8,9},{9,8},{10,11... | collective-permute-start | bytes 393224 | tf_op jit(solution)/shard_map/ppermute | solution.py:41
  104.7 3.9 %collective-permute-start.19 = (bf16[256,256]{1,0:T(8,128)(2,1)S(1)}, bf16[256,256]{1,0:T(8,128)(2,1)S(1)}, u32[]{:S(2)}, u32[]{:S(2)}) collective-permute-start(bf16[256,256]{1,0:T(8,128)(2,1)S(1)} %get-tuple-element.91), channel_id=1, source_target_pairs={{0,1},{1,0},{2,3},{3,2},{4,5},{5,4},{6,7},{7,6},{8,9},{9,8},{10,11... | collective-permute-start | bytes 393224 | tf_op jit(solution)/shard_map/ppermute | solution.py:41
  108.4 25.8 %collective-permute-start.29 = (bf16[1,2048,256]{2,1,0:T(8,128)(2,1)}, bf16[1,2048,256]{2,1,0:T(8,128)(2,1)}, u32[]{:S(2)}, u32[]{:S(2)}) collective-permute-start(bf16[1,2048,256]{2,1,0:T(8,128)(2,1)} %get-tuple-element.97), channel_id=1, source_target_pairs={{0,2},{1,3},{2,0},{3,1},{4,6},{5,7},{6,4},{7,5},{8,10},{9,11},{10,... | collective-permute-start | bytes 3145736 | tf_op jit(solution)/shard_map/ppermute | solution.py:41
  114.3 28.1 %collective-permute-start.20 = (bf16[4,544,256]{2,1,0:T(8,128)(2,1)}, bf16[4,544,256]{2,1,0:T(8,128)(2,1)}, u32[]{:S(2)}, u32[]{:S(2)}) collective-permute-start(bf16[4,544,256]{2,1,0:T(8,128)(2,1)} %get-tuple-element.93), channel_id=1, source_target_pairs={{0,4},{4,0},{8,12},{12,8},{16,20},{20,16},{24,28},{28,24},{1,5},{5... | collective-permute-start | bytes 3342344 | tf_op jit(solution)/shard_map/ppermute | solution.py:41
  135.7 1.0 copy-start.16
  137.5 15.8 %collective-permute-start.30 = (bf16[4,256,256]{2,1,0:T(8,128)(2,1)}, bf16[4,256,256]{2,1,0:T(8,128)(2,1)}, u32[]{:S(2)}, u32[]{:S(2)}) collective-permute-start(bf16[4,256,256]{2,1,0:T(8,128)(2,1)} %dynamic-slice_bitcast_fusion.1), channel_id=1, source_target_pairs={{0,4},{4,0},{8,12},{12,8},{16,20},{20,16},{24,28},{28,24},{1,5},{5... | collective-permute-start | bytes 1572872 | tf_op jit(solution)/shard_map/ppermute | solution.py:41
  144.0 1.0 copy-start.14
  144.0 9.4 %copy-start.17 = (bf16[1,2048,256]{2,1,0:T(8,128)(2,1)S(1)}, bf16[1,2048,256]{2,1,0:T(8,128)(2,1)}, u32[]{:S(2)}) copy-start(bf16[1,2048,256]{2,1,0:T(8,128)(2,1)} %copy-done.16) | copy-start | bytes 3145732
  145.8 16.7 %copy-start.15 = (bf16[4,544,256]{2,1,0:T(8,128)(2,1)S(1)}, bf16[4,544,256]{2,1,0:T(8,128)(2,1)}, u32[]{:S(2)}) copy-start(bf16[4,544,256]{2,1,0:T(8,128)(2,1)} %copy-done.14) | copy-start | bytes 3342340
  145.8 16.7 %collective-permute-start.21 = (bf16[2,544,256]{2,1,0:T(8,128)(2,1)}, bf16[2,544,256]{2,1,0:T(8,128)(2,1)}, u32[]{:S(2)}, u32[]{:S(2)}) collective-permute-start(bf16[2,544,256]{2,1,0:T(8,128)(2,1)} %dynamic-slice_bitcast_fusion), channel_id=1, source_target_pairs={{0,8},{4,12},{8,0},{12,4},{16,24},{20,28},{24,16},{28,20},{1,9},{5... | collective-permute-start | bytes 1671176 | tf_op jit(solution)/shard_map/ppermute | solution.py:41
  154.5 0.8 copy-start.18
  156.0 10.8 %copy-start.19 = (bf16[4,256,256]{2,1,0:T(8,128)(2,1)S(1)}, bf16[4,256,256]{2,1,0:T(8,128)(2,1)}, u32[]{:S(2)}) copy-start(bf16[4,256,256]{2,1,0:T(8,128)(2,1)} %copy-done.18) | copy-start | bytes 1572868
  156.0 10.8 %collective-permute-start.31 = (bf16[2,256,256]{2,1,0:T(8,128)(2,1)}, bf16[2,256,256]{2,1,0:T(8,128)(2,1)}, u32[]{:S(2)}, u32[]{:S(2)}) collective-permute-start(bf16[2,256,256]{2,1,0:T(8,128)(2,1)} %dynamic-slice_bitcast_fusion.2), channel_id=1, source_target_pairs={{0,8},{4,12},{8,0},{12,4},{16,24},{20,28},{24,16},{28,20},{1,9},{5... | collective-permute-start | bytes 786440 | tf_op jit(solution)/shard_map/ppermute | solution.py:41
  157.6 13.3 %collective-permute-start.12 = (bf16[3,32,512]{2,1,0:T(8,128)(2,1)S(1)}, bf16[3,32,512]{2,1,0:T(8,128)(2,1)S(1)}, u32[]{:S(2)}, u32[]{:S(2)}) collective-permute-start(bf16[3,32,512]{2,1,0:T(8,128)(2,1)S(1)} %get-tuple-element.75), channel_id=1, source_target_pairs={{0,4},{4,8},{8,12},{12,16},{16,20},{20,24},{24,28},{1,5},{5,9},{9,... | collective-permute-start | bytes 294920 | tf_op jit(solution)/shard_map/ppermute | solution.py:79
  161.2 9.7 %collective-permute-start.13 = (bf16[3,32,512]{2,1,0:T(8,128)(2,1)S(1)}, bf16[3,32,512]{2,1,0:T(8,128)(2,1)S(1)}, u32[]{:S(2)}, u32[]{:S(2)}) collective-permute-start(bf16[3,32,512]{2,1,0:T(8,128)(2,1)S(1)} %get-tuple-element.76), channel_id=1, source_target_pairs={{4,0},{8,4},{12,8},{16,12},{20,16},{24,20},{28,24},{5,1},{9,5},{13... | collective-permute-start | bytes 294920 | tf_op jit(solution)/shard_map/ppermute | solution.py:79
  167.8 14.0 %collective-permute-start.32 = (bf16[1,256,256]{2,1,0:T(8,128)(2,1)S(1)}, bf16[1,256,256]{2,1,0:T(8,128)(2,1)S(1)}, u32[]{:S(2)}, u32[]{:S(2)}) collective-permute-start(bf16[1,256,256]{2,1,0:T(8,128)(2,1)S(1)} %constant_dynamic-slice_fusion), channel_id=1, source_target_pairs={{0,16},{4,20},{8,24},{12,28},{16,0},{20,4},{24,8},{28,12},{1,17},{... | collective-permute-start | bytes 393224 | tf_op jit(solution)/shard_map/ppermute | solution.py:41
  169.4 17.2 %collective-permute-start.22 = (bf16[1,544,256]{2,1,0:T(8,128)(2,1)S(1)}, bf16[1,544,256]{2,1,0:T(8,128)(2,1)S(1)}, u32[]{:S(2)}, u32[]{:S(2)}) collective-permute-start(bf16[1,544,256]{2,1,0:T(8,128)(2,1)S(1)} %constant_dynamic-slice_fusion.1), channel_id=1, source_target_pairs={{0,16},{4,20},{8,24},{12,28},{16,0},{20,4},{24,8},{28,12},{1,17},{... | collective-permute-start | bytes 835592 | tf_op jit(solution)/shard_map/ppermute | solution.py:41
  170.9 23.4 %collective-permute-start.14 = (bf16[14,8,512]{2,1,0:T(8,128)(2,1)S(1)}, bf16[14,8,512]{2,1,0:T(8,128)(2,1)S(1)}, u32[]{:S(2)}, u32[]{:S(2)}) collective-permute-start(bf16[14,8,512]{2,1,0:T(8,128)(2,1)S(1)} %get-tuple-element.77), channel_id=1, source_target_pairs={{0,1},{1,2},{2,3},{4,5},{5,6},{6,7},{8,9},{9,10},{10,11},{12,13},{... | collective-permute-start | bytes 344072 | tf_op jit(solution)/shard_map/ppermute | solution.py:79
  172.2 22.1 %collective-permute-start.15 = (bf16[14,8,512]{2,1,0:T(8,128)(2,1)S(1)}, bf16[14,8,512]{2,1,0:T(8,128)(2,1)S(1)}, u32[]{:S(2)}, u32[]{:S(2)}) collective-permute-start(bf16[14,8,512]{2,1,0:T(8,128)(2,1)S(1)} %get-tuple-element.78), channel_id=1, source_target_pairs={{1,0},{2,1},{3,2},{5,4},{6,5},{7,6},{9,8},{10,9},{11,10},{13,12},{... | collective-permute-start | bytes 344072 | tf_op jit(solution)/shard_map/ppermute | solution.py:79
  181.8 6.5 %collective-permute-start.33 = (bf16[1,256,256]{2,1,0:T(8,128)(2,1)S(1)}, bf16[1,256,256]{2,1,0:T(8,128)(2,1)S(1)}, u32[]{:S(2)}, u32[]{:S(2)}) collective-permute-start(bf16[1,256,256]{2,1,0:T(8,128)(2,1)S(1)} %dynamic-slice_add_fusion), channel_id=1, source_target_pairs={{0,2},{1,3},{2,0},{3,1},{4,6},{5,7},{6,4},{7,5},{8,10},{9,11},{10,... | collective-permute-start | bytes 393224 | tf_op jit(solution)/shard_map/ppermute | solution.py:41
  186.6 7.7 %copy-start.7 = (f32[7,7,512]{2,1,0:T(8,128)S(1)}, f32[7,7,512]{2,1,0:T(8,128)}, u32[]{:S(2)}) copy-start(f32[7,7,512]{2,1,0:T(8,128)} %taps.7) | copy-start | bytes 301060
  186.6 7.6 %collective-permute-start.23 = (bf16[544,256]{1,0:T(8,128)(2,1)S(1)}, bf16[544,256]{1,0:T(8,128)(2,1)S(1)}, u32[]{:S(2)}, u32[]{:S(2)}) collective-permute-start(bf16[544,256]{1,0:T(8,128)(2,1)S(1)} %add_bitcast_fusion.1), channel_id=1, source_target_pairs={{0,2},{1,3},{2,0},{3,1},{4,6},{5,7},{6,4},{7,5},{8,10},{9,11},{10,... | collective-permute-start | bytes 835592 | tf_op jit(solution)/shard_map/ppermute | solution.py:41
  188.4 12.5 %collective-permute-start.34 = (bf16[2,256,256]{2,1,0:T(8,128)(2,1)S(1)}, bf16[2,256,256]{2,1,0:T(8,128)(2,1)S(1)}, u32[]{:S(2)}, u32[]{:S(2)}) collective-permute-start(bf16[2,256,256]{2,1,0:T(8,128)(2,1)S(1)} %maximum_bitcast_fusion.1), channel_id=1, source_target_pairs={{0,1},{1,0},{2,3},{3,2},{4,5},{5,4},{6,7},{7,6},{8,9},{9,8},{10,11... | collective-permute-start | bytes 786440 | tf_op jit(solution)/shard_map/ppermute | solution.py:41
  194.2 6.8 %collective-permute-start.24 = (bf16[1,544,256]{2,1,0:T(8,128)(2,1)S(1)}, bf16[1,544,256]{2,1,0:T(8,128)(2,1)S(1)}, u32[]{:S(2)}, u32[]{:S(2)}) collective-permute-start(bf16[1,544,256]{2,1,0:T(8,128)(2,1)S(1)} %add_bitcast_fusion), channel_id=1, source_target_pairs={{0,1},{1,0},{2,3},{3,2},{4,5},{5,4},{6,7},{7,6},{8,9},{9,8},{10,11... | collective-permute-start | bytes 835592 | tf_op jit(solution)/shard_map/ppermute | solution.py:41
  201.2 4.9 %collective-permute-start.25 = (bf16[1,32,512]{2,1,0:T(8,128)(2,1)S(1)}, bf16[1,32,512]{2,1,0:T(8,128)(2,1)S(1)}, u32[]{:S(2)}, u32[]{:S(2)}) collective-permute-start(bf16[1,32,512]{2,1,0:T(8,128)(2,1)S(1)} %broadcast_in_dim_reshape.3), channel_id=1, source_target_pairs={{0,16},{4,20},{8,24},{12,28},{16,0},{20,4},{24,8},{28,12},{1,17},{... | collective-permute-start | bytes 98312 | tf_op jit(solution)/shard_map/ppermute | solution.py:41
  206.1 4.3 %collective-permute-start.26 = (bf16[2,32,512]{2,1,0:T(8,128)(2,1)S(1)}, bf16[2,32,512]{2,1,0:T(8,128)(2,1)S(1)}, u32[]{:S(2)}, u32[]{:S(2)}) collective-permute-start(bf16[2,32,512]{2,1,0:T(8,128)(2,1)S(1)} %maximum_bitcast_fusion.2), channel_id=1, source_target_pairs={{0,8},{4,12},{8,0},{12,4},{16,24},{20,28},{24,16},{28,20},{1,9},{5... | collective-permute-start | bytes 196616 | tf_op jit(solution)/shard_map/ppermute | solution.py:41
  210.5 5.0 %collective-permute-start.27 = (bf16[4,32,512]{2,1,0:T(8,128)(2,1)S(1)}, bf16[4,32,512]{2,1,0:T(8,128)(2,1)S(1)}, u32[]{:S(2)}, u32[]{:S(2)}) collective-permute-start(bf16[4,32,512]{2,1,0:T(8,128)(2,1)S(1)} %bitcast.122), channel_id=1, source_target_pairs={{0,4},{4,0},{8,12},{12,8},{16,20},{20,16},{24,28},{28,24},{1,5},{5... | collective-permute-start | bytes 393224 | tf_op jit(solution)/shard_map/ppermute | solution.py:41
where the time goes:
time: 220 us; the launch traced here: 219 us
  waiting for transfers between devices  79.1 us (36%)
  starting transfers between devices  59.4 us (27%)
  Pallas kernels  49 us (22%)
  local copies, waits for them, and re-layouts  23.2 us (11%)
  other arithmetic  6.73 us (3%)
    ppermute x19, waiting for transfers between devices, swap(): lax.ppermute(values, axis, [(i, i ^ bit) for i in range(lax.axis_size(axi...  54.7 us
    pallas_call x14, Pallas kernels, run(): pl.pallas_call(kernel, name=name, out_shape=outs, in_specs=[outside if i...  49 us
    ppermute x19, starting transfers between devices, swap(): lax.ppermute(values, axis, [(i, i ^ bit) for i in range(lax.axis_size(axi...  24.6 us
    ppermute x8, starting transfers between devices, neighbours(): lax.ppermute(last, axis, forward)  24.4 us
    ppermute x8, waiting for transfers between devices, neighbours(): lax.ppermute(first, axis, backward)  21.6 us
    unnamed x44, local copies, waits for them, and re-layouts  15.9 us
    ppermute x8, starting transfers between devices, neighbours(): lax.ppermute(first, axis, backward)  10.3 us
  transfers between devices with their start and end apart: 35, of which 19 were waited for; matrix products, arithmetic and copies ran while one was open for 6% of the time, Pallas kernels for 17%

commit v1 on v0

v1 whole, which is shorter than its diff:
```python
import functools
import math

import jax
import jax.numpy as jnp
from jax import lax
from jax.experimental import pallas as pl
from jax.experimental.pallas import tpu as pltpu
from jax.sharding import PartitionSpec as P

EPSILON = 1e-06
BF = jnp.bfloat16
F32 = jnp.float32
MIB = 1 << 20
PAD = 8
CHUNK = 256


def shape_of(*dims, dtype=F32):
    return jax.ShapeDtypeStruct(dims, dtype)


def run(kernel, name, args, outs, scratch=(), spaces=None, after=(), aliases=None, limit=24, us=1.0):
    spaces = spaces or {}
    count, extra = len(args), len(after)
    moved = sum(a.size * a.dtype.itemsize for a in args)
    moved += sum(math.prod(o.shape) * o.dtype.itemsize for o in outs)

    def spec(place):
        return pl.BlockSpec(memory_space=spaces.get(place, pltpu.VMEM))

    def inner(*refs):
        kernel(*refs[:count], *refs[count + extra :])

    return pl.pallas_call(
        inner,
        name=name,
        out_shape=outs,
        in_specs=[spec(i) for i in range(count)] + [pl.BlockSpec(memory_space=pl.ANY)] * extra,
        out_specs=[spec(("out", i)) for i in range(len(outs))],
        scratch_shapes=list(scratch),
        input_output_aliases=aliases or {},
        compiler_params=pltpu.CompilerParams(vmem_limit_bytes=limit * MIB),
        cost_estimate=pl.CostEstimate(flops=int(us * 1.1e9), bytes_accessed=moved, transcendentals=0),
    )(*args, *after)


def swap(values, axis, bit):
    return lax.ppermute(values, axis, [(i, i ^ bit) for i in range(lax.axis_size(axis))])


def axis_bits(axis):
    return [1 << k for k in range((lax.axis_size(axis) - 1).bit_length())]


def own_bit(axis, bit):
    return (lax.axis_index(axis) // bit) % 2


def chain(keep, send, order, count, rows, extra=()):
    for place, (axis, bit, _) in enumerate(order):
        received = swap(send, axis, bit)
        if place + 1 == len(order):
            return keep + received
        axis, bit, position = order[place + 1]
        grown = extra if place == 0 else ()
        count //= 2
        tail = keep.shape[0] - count * rows + (grown[0].shape[0] if grown else 0)
        out = shape_of(count // 2 * rows + tail, keep.shape[1], dtype=BF)
        keep, send = run(
            functools.partial(step_kernel, axis, bit, position, count, rows),
            "sum_step",
            (keep, received, *grown),
            (out, out),
            limit=8,
        )


def step_kernel(axis, bit, position, count, rows, keep, received, *refs):
    *grown, next_keep, next_send = refs
    mine = (lax.axis_index(axis) // bit) % 2
    low = (1 << position) - 1
    for i in range(2):

        @pl.when(mine == i)
        def _():
            for s in range(count):
                span = slice(s * rows, (s + 1) * rows)
                at = ((s >> (position + 1)) << position | (s & low)) * rows
                target = next_keep if (s >> position) & 1 == i else next_send
                target[at : at + rows] = (keep[span].astype(F32) + received[span].astype(F32)).astype(BF)

    tails = []
    if keep.shape[0] > count * rows:
        tails.append(keep[count * rows :].astype(F32) + received[count * rows :].astype(F32))
    if grown:
        tails.append(sum(g[...].astype(F32) for g in grown))
    at = count // 2 * rows
    for tail in tails:
        for target in (next_keep, next_send):
            target[at : at + tail.shape[0]] = tail.astype(BF)
        at += tail.shape[0]


def gather(values, axis, bits):
    values = values[None]
    for bit in reversed(bits):
        other = swap(values, axis, bit)
        mine = own_bit(axis, bit)
        low = jnp.where(mine == 0, values, other)
        high = jnp.where(mine == 0, other, values)
        values = jnp.stack([low, high], axis=1).reshape(-1, *values.shape[1:])
    return values


def neighbours(first, last, axis):
    count = lax.axis_size(axis)
    forward = [(i, i + 1) for i in range(count - 1)]
    backward = [(i + 1, i) for i in range(count - 1)]
    return lax.ppermute(last, axis, forward), lax.ppermute(first, axis, backward)


def strip_kernel(center, top, bottom, first, last):
    height, breadth = center.shape[:2]
    for source, start in ((top, 0), (center, 3), (bottom, 3 + height)):
        values = source[...].astype(F32)
        rows = slice(start, start + source.shape[0])
        first[rows] = values[:, :PAD].astype(BF)
        last[rows] = values[:, breadth - PAD :].astype(BF)


def halo(center, rows, name, after=()):
    height, _, channels = center.shape
    top, bottom = rows
    strip = shape_of(height + 6, PAD, channels, dtype=BF)
    first, last = run(strip_kernel, name, (center, top, bottom), (strip, strip), after=after, limit=8)
    left, right = neighbours(first, last, "col")
    return center, top, bottom, left, right


def fill_frame(frame, parts):
    center, top, bottom, left, right = parts
    height, breadth = center.shape[:2]
    middle = slice(PAD, PAD + breadth)
    frame[0:3, middle] = top[...].astype(F32)
    frame[3 : 3 + height, middle] = center[...].astype(F32)
    frame[3 + height :, middle] = bottom[...].astype(F32)
    frame[:, :PAD] = left[...].astype(F32)
    frame[:, PAD + breadth :] = right[...].astype(F32)


def frame_scratch(center):
    height, breadth, channels = center.shape
    return pltpu.VMEM((height + 6, breadth + 2 * PAD, channels), F32)


def lane_tiles(channels):
    def over(step):
        def wrapped(index, carry):
            step(pl.ds(pl.multiple_of(index * 128, 128), 128))
            return carry

        lax.fori_loop(0, channels // 128, wrapped, 0)

    return over


def convolve(frame, taps, flip, out):
    height, breadth, channels = out.shape

    @lane_tiles(channels)
    def _(lanes):
        for column in range(0, breadth, 8):
            total = jnp.zeros((height, 8, 128), F32)
            for q in range(7):
                rows = frame[:, pl.ds(column + PAD - 3 + q, 8), lanes]
                for p in range(7):
                    a, b = (6 - p, 6 - q) if flip else (p, q)
                    total = total + rows[p : p + height] * taps[a, pl.ds(b, 1), lanes]
            out[:, pl.ds(column, 8), lanes] = total


def weight_sums(frame, grads, scale, out):
    height, breadth, channels = grads.shape

    @lane_tiles(channels)
    def _(lanes):
        for q in range(7):
            totals = [jnp.zeros((8, 128), F32)] * 7
            for column in range(0, breadth, 8):
                rows = frame[:, pl.ds(column + PAD - 3 + q, 8), lanes]
                grad = grads[:, pl.ds(column, 8), lanes]
                for p in range(7):
                    totals[p] = totals[p] + jnp.sum(rows[p : p + height] * grad, axis=0)
            for p in range(7):
                out[pl.ds(7 * p + q, 1), lanes] = scale * jnp.sum(totals[p], axis=0, keepdims=True)


def mean(values):
    return jnp.mean(values, axis=-1, keepdims=True)


def normalize(values):
    level = mean(values)
    inverse = lax.rsqrt(mean(values * values) - level * level + EPSILON)
    return (values - level) * inverse, inverse


def normalize_back(grads, unit_values, inverse):
    return (grads - mean(grads) - unit_values * mean(grads * unit_values)) * inverse


def dot(left, right):
    return jnp.dot(left, right, preferred_element_type=F32)


def dot_last(left, right):
    return lax.dot_general(left, right, (((1,), (1,)), ((), ())), preferred_element_type=F32)


def dot_first(left, right):
    return lax.dot_general(left, right, (((0,), (0,)), ((), ())), preferred_element_type=F32)


def over_rows(count, size):
    def over(step):
        def wrapped(index, carry):
            step(index, pl.ds(pl.multiple_of(index * size, size), size))
            return carry

        lax.fori_loop(0, count, wrapped, 0)

    return over


def fetch(sources, targets, semaphores):
    copies = [
        pltpu.make_async_copy(source, target, semaphores.at[i])
        for i, (source, target) in enumerate(zip(sources, targets))
    ]
    for copy in copies:
        copy.start()
    return copies


def load_kernel(center, taps, gain, layer, merge, *refs):
    *outs, semaphores = refs
    height = center.shape[0]
    sources = (center.at[pl.ds(0, 3)], center.at[pl.ds(height - 3, 3)], center, taps, gain, layer, merge)
    for copy in fetch(sources, outs, semaphores):
        copy.wait()


def front_kernel(
    center, top, bottom, left, right, taps, gain, layer_scale, merge_gain,
    expand, project, patch, wide_taps, wide_gain, cotangent, residual,
    early, unit_mixed, inverse_mixed, slope, branch, unit_summed, inverse_summed, section, first, last,
    expand_here, project_here, patch_here, wide_taps_here, wide_gain_here, cotangent_here, residual_here,
    frame, image, pairs, upward, semaphores,
):
    height, breadth, channels = center.shape
    hidden_width = expand.shape[1]
    pixels = height * breadth
    copies = fetch(
        (expand, project, patch, wide_taps, wide_gain, cotangent, residual),
        (expand_here, project_here, patch_here, wide_taps_here, wide_gain_here, cotangent_here, residual_here),
        semaphores,
    )
    fill_frame(frame, (center, top, bottom, left, right))
    convolve(frame, taps, False, image)
    at_normed = slice(hidden_width, hidden_width + channels)
    at_patches = slice(hidden_width + channels, hidden_width + 2 * channels)

    @over_rows(height, breadth)
    def _(y, rows):
        unit, inverse = normalize(image[y])
        unit_mixed[rows] = unit
        inverse_mixed[rows] = inverse
        early[rows, at_normed] = (unit * gain[...]).astype(BF)

    copies[0].wait()

    def chunk(index, carry):
        lanes = pl.ds(pl.multiple_of(index * CHUNK, CHUNK), CHUNK)
        upward[...] = dot(early[:, at_normed], expand_here[:, lanes])
        for start in range(0, pixels, 64):
            rows = slice(start, start + 64)
            value = upward[rows]
            cumulative = 0.5 + 0.5 * lax.erf(value * (1.0 / math.sqrt(2.0)))
            density = jnp.exp(-0.5 * value * value) * (1.0 / math.sqrt(2.0 * math.pi))
            early[rows, lanes] = (value * cumulative).astype(BF)
            slope[rows, lanes] = (cumulative + value * density).astype(BF)
        return carry

    lax.fori_loop(0, hidden_width // CHUNK, chunk, 0)
    copies[1].wait()
    branch[...] = dot(early[:, :hidden_width], project_here[...])

    @over_rows(height, breadth)
    def _(y, rows):
        summed = center[y].astype(F32) + layer_scale[...] * branch[rows]
        unit, inverse = normalize(summed)
        unit_summed[rows] = unit
        inverse_summed[rows] = inverse
        merged = unit * merge_gain[...]
        for k in range(channels // 128):
            pairs[k, y] = merged[:, k * 128 : (k + 1) * 128]

    quarter = pixels // 4
    for dy in range(2):
        for dx in range(2):
            j = 2 * dy + dx
            for y in range(height // 2):
                start = j * quarter + y * (breadth // 2)
                for k in range(channels // 128):
                    piece = pairs[k, 2 * y + dy, pl.ds(dx, breadth // 2, stride=2), :]
                    lane = hidden_width + channels + k * 128
                    early[start : start + breadth // 2, lane : lane + 128] = piece.astype(BF)
    copies[2].wait()
    total = dot(early[:quarter, at_patches], patch_here[:channels])
    for j in range(1, 4):
        total = total + dot(
            early[j * quarter : (j + 1) * quarter, at_patches],
            patch_here[j * channels : (j + 1) * channels],
        )
    total = total.reshape(section.shape)
    section[...] = total.astype(BF)
    first[...] = total[:3].astype(BF)
    last[...] = total[height // 2 - 3 :].astype(BF)
    for copy in copies[3:]:
        copy.wait()


def mixer_kernel(
    center, top, bottom, left, right, taps, gain, cotangent,
    grad, grad_half, first, last, gain_part,
    frame, image,
):
    height, breadth, channels = center.shape
    fill_frame(frame, (center, top, bottom, left, right))
    convolve(frame, taps, False, image)
    part = jnp.zeros((1, channels), F32)
    for y in range(height):
        unit, inverse = normalize(image[y])
        cot = cotangent[y].astype(F32)
        part = part + jnp.sum(cot * unit, axis=0, keepdims=True)
        value = normalize_back(cot * gain[...], unit, inverse)
        grad[y] = value
        narrow = value.astype(BF)
        grad_half[y] = narrow
        if y < 3:
            first[y] = narrow
        if y >= height - 3:
            last[y - (height - 3)] = narrow
    gain_part[...] = part


def weight_kernel(scale, center, top, bottom, left, right, grads, _, out, __, frame):
    fill_frame(frame, (center, top, bottom, left, right))
    weight_sums(frame, grads, scale, out)


def split_halves(values, start, keep, send):
    half = values.shape[1] // 2
    rows = slice(start, start + values.shape[0])
    core = lax.axis_index("col") % 2
    for i in range(2):

        @pl.when(core == i)
        def _():
            keep[rows] = values[:, i * half : (i + 1) * half]
            send[rows] = values[:, (1 - i) * half : (2 - i) * half]


def weight_pack_kernel(
    scale, center, top, bottom, left, right, grads, gain_part,
    keep, send, frame, wide_grads, packed,
):
    fill_frame(frame, (center, top, bottom, left, right))
    wide_grads[...] = grads[...].astype(F32)
    packed[...] = jnp.zeros(packed.shape, F32)
    weight_sums(frame, wide_grads, scale, packed)
    packed[49:50] = scale * gain_part[...]
    split_halves(packed[...].astype(BF), 0, keep, send)


def section_kernel(
    center, top, bottom, left, right, taps, residual,
    flat, keep, send,
    frame, image,
):
    height, breadth, channels = center.shape
    fill_frame(frame, (center, top, bottom, left, right))
    convolve(frame, taps, True, image)
    value = (image[...] + residual[...].astype(F32)).reshape(flat.shape).astype(BF)
    flat[...] = value
    blocks, _, width = keep.shape
    core = lax.axis_index("col") % 2
    for i in range(2):

        @pl.when(core == i)
        def _():
            for m in range(blocks):
                mine, other = (2 * m + i) * width, (2 * m + 1 - i) * width
                keep[m] = value[:, mine : mine + width]
                send[m] = value[:, other : other + width]


def merge_kernel(
    scale, scale_wide,
    flat, patch, unit_summed, inverse_summed, merge_gain, branch, layer_scale, wide_part, wide_gain,
    grad_summed, grad_branch, keep, send,
    pairs, packed, sums,
):
    tiles, height, breadth, _ = pairs.shape
    channels = 128 * tiles
    value = flat[...]
    for dy in range(2):
        for dx in range(2):
            j = 2 * dy + dx
            part = dot_last(value, patch[j * channels : (j + 1) * channels])
            part = part.reshape(height // 2, breadth // 2, channels)
            for y in range(height // 2):
                for k in range(tiles):
                    piece = part[y, :, k * 128 : (k + 1) * 128]
                    pairs[k, 2 * y + dy, pl.ds(dx, breadth // 2, stride=2), :] = piece
    sums[...] = jnp.zeros(sums.shape, F32)

    @over_rows(height, breadth)
    def _(y, rows):
        merged = jnp.concatenate([pairs[k, y] for k in range(tiles)], axis=1)
        unit = unit_summed[rows]
        sums[0:1] += jnp.sum(merged * unit, axis=0, keepdims=True)
        grad = normalize_back(merged * merge_gain[...], unit, inverse_summed[rows])
        grad_summed[rows] = grad
        sums[1:2] += jnp.sum(grad * branch[rows], axis=0, keepdims=True)
        grad_branch[rows] = (layer_scale[...] * grad).astype(BF)

    split_halves(grad_branch[...], 0, keep, send)
    packed[...] = jnp.zeros(packed.shape, F32)
    for i in range(2):
        columns = slice(i * channels, (i + 1) * channels)
        packed[49 * i : 49 + 49 * i] = wide_part[:, columns]
        packed[98 + i : 99 + i] = scale_wide * wide_gain[:, columns]
        packed[100 + i : 101 + i] = scale * sums[i : i + 1]
    split_halves(packed[...].astype(BF), grad_branch.shape[0], keep, send)


def back_kernel(
    grad_branch, project, slope, expand, unit_mixed, inverse_mixed, gain,
    keep, send, grad_mixed, first, last, gain_part,
    hidden, upward, normed,
):
    height, breadth, channels = grad_mixed.shape
    pixels, hidden_width = slope.shape

    def chunk(index, carry):
        span = pl.ds(pl.multiple_of(index * CHUNK, CHUNK), CHUNK)
        hidden[...] = dot_last(grad_branch[...], project[span])
        for start in range(0, pixels, 64):
            rows = slice(start, start + 64)
            upward[rows, span] = (hidden[rows] * slope[rows, span].astype(F32)).astype(BF)
        return carry

    lax.fori_loop(0, hidden_width // CHUNK, chunk, 0)
    normed[...] = dot_last(upward[...], expand[...])
    split_halves(upward[...], 0, keep, send)
    part = jnp.zeros((1, channels), F32)
    for y in range(height):
        rows = slice(y * breadth, (y + 1) * breadth)
        value = normed[rows]
        unit = unit_mixed[rows]
        part = part + jnp.sum(value * unit, axis=0, keepdims=True)
        narrow = normalize_back(value * gain[...], unit, inverse_mixed[rows]).astype(BF)
        grad_mixed[y] = narrow
        if y < 3:
            first[y] = narrow
        if y >= height - 3:
            last[y - (height - 3)] = narrow
    gain_part[...] = part


def patch_product_kernel(factor, early, early_other, own, other, keep, send):
    blocks, quarter, _ = own.shape
    rows = keep.shape[0] // max(blocks // 2, 1)
    channels = rows // 4
    at_patches = early.shape[1] - channels
    bit = (lax.axis_index("col") // 2) % 2
    for j in range(4):
        span = slice(j * quarter, (j + 1) * quarter)
        left = jnp.concatenate([early[span, at_patches:], early_other[span, at_patches:]], axis=0)
        for m in range(blocks):
            right = jnp.concatenate([own[m], other[m]], axis=0)
            value = (factor * dot_first(left, right)).astype(BF)
            at = m // 2 * rows + j * channels
            for i in range(2):

                @pl.when(bit == i)
                def _():
                    target = keep if m % 2 == i else send
                    target[at : at + channels] = value


def store_slices(value, begin, offset, rows, pitch, keep, send):
    bit = lax.axis_index("row") % 2
    for i in range(2):

        @pl.when(bit == i)
        def _():
            for k in range(value.shape[0] // rows):
                r = begin + k
                target = keep if r % 2 == i else send
                at = r // 2 * pitch + offset
                target[at : at + rows] = value[k * rows : (k + 1) * rows]


def project_product_kernel(factor, slices, early, early_other, own, other, keep, send):
    width = keep.shape[1]
    hidden_width = early.shape[1] - 4 * width
    pixels = early.shape[0]
    deep = hidden_width // slices
    right = jnp.concatenate([own[:pixels], other[:pixels]], axis=0)
    step = max(CHUNK, deep)
    for start in range(0, hidden_width, step):
        columns = slice(start, start + step)
        left = jnp.concatenate([early[:, columns], early_other[:, columns]], axis=0)
        value = (factor * dot_first(left, right)).astype(BF)
        store_slices(value, start // deep, 0, deep, deep, keep, send)
    tail = (own[pixels:].astype(F32) + other[pixels:].astype(F32)).astype(BF)
    at = slices // 2 * deep
    keep[at:] = tail
    send[at:] = tail


def expand_product_kernel(factor, slices, early, early_other, own, other, keep, send):
    width = keep.shape[1]
    channels = 2 * width
    hidden_width = early.shape[1] - 2 * channels
    shallow = channels // slices
    blocks = own.shape[1] // width
    columns = slice(hidden_width, hidden_width + channels)
    left = jnp.concatenate([early[:, columns], early_other[:, columns]], axis=0)
    for k in range(blocks):
        columns = slice(k * width, (k + 1) * width)
        right = jnp.concatenate([own[:, columns], other[:, columns]], axis=0)
        value = (factor * dot_first(left, right)).astype(BF)
        store_slices(value, 0, k * shallow, shallow, blocks * shallow, keep, send)


def finish_patch_kernel(own, other, out):
    blocks, _, width = own.shape
    core = lax.axis_index("col") % 2
    for i in range(2):

        @pl.when(core == i)
        def _():
            for m in range(blocks):
                a, b = (2 * m + i) * width, (2 * m + 1 - i) * width
                out[:, a : a + width] = own[m].astype(F32)
                out[:, b : b + width] = other[m].astype(F32)


def join_halves(own, other, start, out):
    half = own.shape[1]
    rows = slice(start, start + out.shape[0])
    core = lax.axis_index("col") % 2
    for i in range(2):

        @pl.when(core == i)
        def _():
            out[:, i * half : (i + 1) * half] = own[rows].astype(F32)
            out[:, (1 - i) * half : (2 - i) * half] = other[rows].astype(F32)


def finish_project_kernel(own, other, project, wide_taps, wide_gain, merge, layer, small):
    deep, channels = project.shape
    join_halves(own, other, 0, project)
    join_halves(own, other, deep, small)
    for i in range(2):
        columns = slice(i * channels, (i + 1) * channels)
        for p in range(7):
            start = 49 * i + 7 * p
            wide_taps[p, :, columns] = small[start : start + 7]
        wide_gain[:, columns] = small[98 + i : 99 + i]
    merge[...] = small[100:101]
    layer[...] = small[101:102]


def finish_expand_kernel(own, other, expand, taps, gain, small):
    shallow, hidden_width = expand.shape
    width = own.shape[1]
    blocks = hidden_width // (2 * width)
    core = lax.axis_index("col") % 2
    for i in range(2):

        @pl.when(core == i)
        def _():
            for k in range(blocks):
                rows = slice(k * shallow, (k + 1) * shallow)
                a, b = (i * blocks + k) * width, ((1 - i) * blocks + k) * width
                expand[:, a : a + width] = own[rows].astype(F32)
                expand[:, b : b + width] = other[rows].astype(F32)

    join_halves(own, other, blocks * shallow, small)
    for p in range(7):
        taps[p] = small[7 * p : 7 * p + 7]
    gain[...] = small[49:50]


def input_kernel(center, top, bottom, left, right, taps, grad_summed, out, frame, image):
    fill_frame(frame, (center, top, bottom, left, right))
    convolve(frame, taps, True, image)
    out[...] = (image[...] + grad_summed[...].reshape(image.shape)).astype(BF)


def body(
    block_input,
    kernel_three,
    gain_three,
    expand_weight,
    project_weight,
    layer_scale,
    merge_gain,
    patch_weight,
    kernel_four,
    gain_four,
    normed_cotangent,
    residual_cotangent,
):
    _, height, breadth, channels = block_input.shape
    hidden_width = expand_weight.shape[1]
    wide = patch_weight.shape[1]
    pixels = height * breadth
    quarter = pixels // 4
    rows4, cols4 = height // 2, breadth // 2
    row_count = lax.axis_size("row")
    col_count = lax.axis_size("col")
    scale_three = 1.0 / math.sqrt(pixels * row_count * col_count)
    scale_four = 1.0 / math.sqrt(quarter * row_count * col_count)
    center = block_input[0]
    gain_three, layer_scale, merge_gain, gain_four = (
        v[None] for v in (gain_three, layer_scale, merge_gain, gain_four)
    )
    dma = pltpu.SemaphoreType.DMA
    half = channels // 2
    hbm = pltpu.HBM

    def like(array):
        return shape_of(*array.shape, dtype=array.dtype)

    edge = shape_of(3, breadth, channels, dtype=BF)
    inputs = (center, kernel_three, gain_three, layer_scale, merge_gain)
    first, last, *inputs = run(
        load_kernel,
        "load",
        inputs,
        (edge, edge, *map(like, inputs)),
        scratch=(dma((7,)),),
        spaces=dict.fromkeys(range(5), hbm),
        limit=4,
        us=2,
    )
    center, taps_three, gain_three, layer_scale, merge_gain = inputs
    framed = halo(center, neighbours(first, last, "row"), "strips_input")
    inputs = (
        expand_weight, project_weight, patch_weight, kernel_four, gain_four,
        normed_cotangent[0], residual_cotangent[0],
    )
    edge_four = shape_of(3, cols4, wide, dtype=BF)
    (
        early, unit_mixed, inverse_mixed, slope, branch, unit_summed, inverse_summed,
        section, first, last,
        expand_weight, project_weight, patch_weight, taps_four, gain_four, cotangent, residual,
    ) = run(
        front_kernel,
        "front",
        (*framed, taps_three, gain_three, layer_scale, merge_gain, *inputs),
        (
            shape_of(pixels, hidden_width + 2 * channels, dtype=BF),
            shape_of(pixels, channels),
            shape_of(pixels, 1),
            shape_of(pixels, hidden_width, dtype=BF),
            shape_of(pixels, channels),
            shape_of(pixels, channels),
            shape_of(pixels, 1),
            shape_of(rows4, cols4, wide, dtype=BF),
            edge_four,
            edge_four,
            *map(like, inputs),
        ),
        scratch=(
            frame_scratch(center),
            pltpu.VMEM((height, breadth, channels), F32),
            pltpu.VMEM((channels // 128, height, breadth, 128), F32),
            pltpu.VMEM((pixels, CHUNK), F32),
            dma((7,)),
        ),
        spaces=dict.fromkeys(range(9, 16), hbm),
        limit=28,
        us=12,
    )

    framed_four = halo(section, neighbours(first, last, "row"), "strips_section")
    mixer_image = pltpu.VMEM((rows4, cols4, wide), F32)
    grad_four, grad_four_half, first, last, gain_four_part = run(
        mixer_kernel,
        "mixer",
        (*framed_four, taps_four, gain_four, cotangent),
        (
            shape_of(rows4, cols4, wide),
            shape_of(rows4, cols4, wide, dtype=BF),
            edge_four,
            edge_four,
            shape_of(1, wide),
        ),
        scratch=(frame_scratch(section), mixer_image),
        limit=12,
        us=3,
    )
    rows_grad = neighbours(first, last, "row")
    kernel_four_part, early = run(
        functools.partial(weight_kernel, scale_four),
        "mixer_weights",
        (*framed_four, grad_four, early),
        (shape_of(49, wide), like(early)),
        scratch=(frame_scratch(section),),
        spaces={6: pl.ANY, ("out", 1): pl.ANY},
        aliases={6: 1},
        limit=12,
        us=3,
    )
    framed_grad = halo(grad_four_half, rows_grad, "strips_mixer", after=(kernel_four_part,))
    early_other = swap(early, "col", 1)
    block_count = col_count // 2
    block = wide // col_count
    blocked = shape_of(block_count, quarter, block, dtype=BF)
    flat, flat_keep, flat_send = run(
        section_kernel,
        "section_grad",
        (*framed_grad, taps_four, residual),
        (shape_of(quarter, wide, dtype=BF), blocked, blocked),
        scratch=(frame_scratch(section), mixer_image),
        limit=12,
        us=3,
    )

    flat_other = swap(flat_send, "col", 1)
    split = shape_of(pixels + 112, half, dtype=BF)
    grad_summed, grad_branch, branch_keep, branch_send = run(
        functools.partial(merge_kernel, scale_three, scale_four),
        "merge_back",
        (
            flat, patch_weight, unit_summed, inverse_summed, merge_gain, branch, layer_scale,
            kernel_four_part, gain_four_part,
        ),
        (shape_of(pixels, channels), shape_of(pixels, channels, dtype=BF), split, split),
        scratch=(
            pltpu.VMEM((channels // 128, height, breadth, 128), F32),
            pltpu.VMEM((112, channels), F32),
            pltpu.VMEM((8, channels), F32),
        ),
        limit=16,
        us=3,
    )
    branch_other = swap(branch_send, "col", 1)
    patch_half = shape_of(block_count // 2 * 4 * channels, block, dtype=BF)
    patch_keep, patch_send = run(
        functools.partial(patch_product_kernel, scale_four),
        "patch_product",
        (early, early_other, flat_keep, flat_other),
        (patch_half, patch_half),
        limit=16,
        us=3,
    )
    deep, shallow = hidden_width // row_count, channels // row_count
    groups = hidden_width // channels
    project_half = shape_of(row_count // 2 * deep + 112, half, dtype=BF)
    project_keep, project_send = run(
        functools.partial(project_product_kernel, scale_three, row_count),
        "project_product",
        (early, early_other, branch_keep, branch_other),
        (project_half, project_half),
        after=(patch_send,),
        limit=16,
        us=3,
    )
    upward_half = shape_of(pixels, hidden_width // 2, dtype=BF)
    upward_keep, upward_send, grad_mixed, first, last, gain_part = run(
        back_kernel,
        "mlp_back",
        (grad_branch, project_weight, slope, expand_weight, unit_mixed, inverse_mixed, gain_three),
        (
            upward_half,
            upward_half,
            shape_of(height, breadth, channels, dtype=BF),
            edge,
            edge,
            shape_of(1, channels),
        ),
        scratch=(
            pltpu.VMEM((pixels, CHUNK), F32),
            pltpu.VMEM((pixels, hidden_width), BF),
            pltpu.VMEM((pixels, channels), F32),
        ),
        after=(project_send,),
        limit=16,
        us=4,
    )
    rows_back = neighbours(first, last, "row")
    upward_other = swap(upward_send, "col", 1)
    expand_half = shape_of(row_count // 2 * groups * shallow, half, dtype=BF)
    expand_keep, expand_send = run(
        functools.partial(expand_product_kernel, scale_three, row_count),
        "expand_product",
        (early, early_other, upward_keep, upward_other),
        (expand_half, expand_half),
        limit=16,
        us=3,
    )
    framed_back = halo(grad_mixed, rows_back, "strips_back", after=(expand_send,))
    small_half = shape_of(64, half, dtype=BF)
    small_keep, small_send = run(
        functools.partial(weight_pack_kernel, scale_three),
        "block_weights",
        (*framed, grad_mixed, gain_part),
        (small_half, small_half),
        scratch=(
            frame_scratch(center),
            pltpu.VMEM((height, breadth, channels), F32),
            pltpu.VMEM((64, channels), F32),
        ),
        after=framed_back[1:3],
        limit=12,
        us=5,
    )
    (input_grad,) = run(
        input_kernel,
        "input_grad",
        (*framed_back, taps_three, grad_summed),
        (shape_of(height, breadth, channels, dtype=BF),),
        scratch=(frame_scratch(center), pltpu.VMEM((height, breadth, channels), F32)),
        after=(small_keep,),
        limit=12,
        us=5,
    )

    row_bits, col_bits = axis_bits("row"), axis_bits("col")
    outer = len(row_bits)
    low_first = [("row", bit, 0) for bit in row_bits]
    patch_order = [("col", bit, outer) for bit in col_bits[1:]]
    patch_order += [("row", bit, 1) for bit in row_bits[1:]] + [("row", 1, 0)]
    patch_sum = chain(patch_keep, patch_send, patch_order, block_count * row_count, 4 * channels // row_count)
    patch_sum = gather(patch_sum, "col", col_bits[1:])
    (patch_grad,) = run(
        finish_patch_kernel,
        "finish_patch",
        (patch_sum, swap(patch_sum, "col", 1)),
        (shape_of(4 * channels // row_count, wide),),
        limit=8,
    )

    def share(keep, send, rows, extra=()):
        total = chain(keep, send, low_first, row_count, rows, extra)
        for bit in col_bits[1:]:
            total = total + swap(total, "col", bit)
        return total, swap(total, "col", 1)

    vector, wide_vector = shape_of(1, channels), shape_of(1, wide)
    project_grad, wide_taps, wide_gain, merge_sum, layer_sum = run(
        finish_project_kernel,
        "finish_project",
        share(project_keep, project_send, deep),
        (shape_of(deep, channels), shape_of(7, 7, wide), wide_vector, vector, vector),
        scratch=(pltpu.VMEM((112, channels), F32),),
        limit=8,
    )
    small = small_keep + swap(small_send, "col", 1)
    expand_grad, taps_sum, gain_sum = run(
        finish_expand_kernel,
        "finish_expand",
        share(expand_keep, expand_send, groups * shallow, (small, swap(small, "row", 1))),
        (shape_of(shallow, hidden_width), shape_of(7, 7, channels), vector),
        scratch=(pltpu.VMEM((64, channels), F32),),
        limit=8,
    )
    return (
        input_grad[None],
        taps_sum,
        gain_sum[0],
        expand_grad,
        project_grad,
        layer_sum[0],
        merge_sum[0],
        patch_grad,
        wide_taps,
        wide_gain[0],
    )


def solution(mesh):
    pixels = P(None, "row", "col", None)
    return jax.shard_map(
        body,
        mesh=mesh,
        in_specs=(pixels,) + (P(),) * 9 + (pixels, pixels),
        out_specs=(pixels, P(), P(), P("row", None), P("row", None), P(), P(), P("row", None), P(), P()),
        check_vma=False,
    )
```

time: 220 us -> 187 us (0.85)
  local copies, waits for them, and re-layouts: 23.2 us -> 3.92 us
  waiting for transfers between devices: 79.1 us -> 64.2 us
  other arithmetic: 6.73 us -> 0.28 us
  starting transfers between devices: 59.4 us -> 65 us
    ppermute x19 -> x22, waiting for transfers between devices: 54.7 us -> 39.8 us  [swap(): lax.ppermute(values, axis, [(i, i ^ bit) for i in range(lax.axis_size(axi...]
    unnamed x44 -> x24, local copies, waits for them, and re-layouts: 15.9 us -> 3.92 us
    ppermute x19 -> x22, starting transfers between devices: 24.6 us -> 31.9 us  [swap(): lax.ppermute(values, axis, [(i, i ^ bit) for i in range(lax.axis_size(axi...]
    add x6 -> x5, other arithmetic: 6.2 us -> 0.21 us  [the longest x2 0.1 us: share(): total = total + swap(total, 'col', bit)]
    squeeze x5 -> x0, local copies, waits for them, and re-layouts: 2.42 us -> none  [pick(): return lax.dynamic_index_in_dim(values, which, dim, keepdims=False)]
    pallas_call x14 -> x26, Pallas kernels: 49 us -> 51.1 us  [run(): pl.pallas_call(inner, name=name, out_shape=outs, in_specs=[spec(i) for i...]
  transfers between devices with their start and end apart: 35 -> 38, of which waited for: 19 -> 18; matrix products, arithmetic and copies ran while one was open for 6% -> 0% of each run, Pallas kernels for 17% -> 16%
where the time goes in v1:
time: 187 us; the launch traced here: 186 us
  starting transfers between devices  65 us (35%)
  waiting for transfers between devices  64.2 us (34%)
  Pallas kernels  51.1 us (27%)
  local copies, waits for them, and re-layouts  3.92 us (2%)
    pallas_call x26, Pallas kernels, run(): pl.pallas_call(inner, name=name, out_shape=outs, in_specs=[spec(i) for i...  51.1 us
    ppermute x22, waiting for transfers between devices, swap(): lax.ppermute(values, axis, [(i, i ^ bit) for i in range(lax.axis_size(axi...  39.8 us
    ppermute x22, starting transfers between devices, swap(): lax.ppermute(values, axis, [(i, i ^ bit) for i in range(lax.axis_size(axi...  31.9 us
    ppermute x8, starting transfers between devices, neighbours(): lax.ppermute(last, axis, forward)  22.5 us
    ppermute x8, waiting for transfers between devices, neighbours(): lax.ppermute(first, axis, backward)  21.6 us
    ppermute x8, starting transfers between devices, neighbours(): lax.ppermute(first, axis, backward)  10.5 us
    unnamed x24, local copies, waits for them, and re-layouts  3.92 us
  transfers between devices with their start and end apart: 38, of which 18 were waited for; matrix products, arithmetic and copies ran while one was open for 0% of the time, Pallas kernels for 16%

profile of v1, /device:TPU:0, one launch (start us, length us, event | category | flops | bytes accessed | tf_op | source)
XLA Modules:
  0.0 185.6 jit_solution(16965868431473807917)
XLA Ops:
  0.7 0.9 copy-done.3
  1.6 0.9 copy-done.7
  2.5 0.7 copy-done.9
  3.9 0.7 copy-done.11
  5.1 5.1 %collective-permute-start = (bf16[3,32,512]{2,1,0:T(8,128)(2,1)S(1)}, bf16[3,32,512]{2,1,0:T(8,128)(2,1)S(1)}, u32[]{:S(2)}, u32[]{:S(2)}) collective-permute-start(bf16[3,32,512]{2,1,0:T(8,128)(2,1)S(1)} %get-tuple-element.93), channel_id=1, source_target_pairs={{0,4},{4,8},{8,12},{12,16},{16,20},{20,24},{24,28},{1,5},{5,9},{9,... | collective-permute-start | bytes 294920 | tf_op jit(solution)/shard_map/ppermute | solution.py:120
  10.2 1.3 collective-permute-start.1
  11.5 0.9 collective-permute-done.refs_1_
  12.4 4.3 %collective-permute-done.1.refs_2_ = bf16[3,32,512]{2,1,0:T(8,128)(2,1)S(1)} collective-permute-done((bf16[3,32,512]{2,1,0:T(8,128)(2,1)S(1)}, bf16[3,32,512]{2,1,0:T(8,128)(2,1)S(1)}, u32[]{:S(2)}, u32[]{:S(2)}) %collective-permute-start.1) | collective-permute-done | bytes 98336 | tf_op jit(solution)/shard_map/ppermute | solution.py:120
  16.7 1.3 collective-permute-start.2
  18.0 1.3 collective-permute-start.3
  19.4 3.7 %collective-permute-done.3.refs_4_ = bf16[14,8,512]{2,1,0:T(8,128)(2,1)S(1)} collective-permute-done((bf16[14,8,512]{2,1,0:T(8,128)(2,1)S(1)}, bf16[14,8,512]{2,1,0:T(8,128)(2,1)S(1)}, u32[]{:S(2)}, u32[]{:S(2)}) %collective-permute-start.3) | collective-permute-done | bytes 114720 | tf_op jit(solution)/shard_map/ppermute | solution.py:120
  23.1 12.8 %front.1 = (bf16[256,3072]{1,0:T(8,128)(2,1)S(1)}, f32[256,512]{1,0:T(8,128)S(1)}, f32[256,1]{1,0:T(8,128)S(1)}, bf16[256,2048]{1,0:T(8,128)(2,1)S(1)}, f32[256,...) custom-call(bf16[8,32,512]{2,1,0:T(8,128)(2,1)S(1)} %get-tuple-eleme, ...), custom_call_target="tpu_custom_call" | custom-call | flops 13200000000 | bytes 23029760 | tf_op jit(solution)/shard_map/front/pallas_call | solution.py:35
  35.9 4.4 %collective-permute-start.4 = (bf16[3,16,1024]{2,1,0:T(8,128)(2,1)S(1)}, bf16[3,16,1024]{2,1,0:T(8,128)(2,1)S(1)}, u32[]{:S(2)}, u32[]{:S(2)}) collective-permute-start(bf16[3,16,1024]{2,1,0:T(8,128)(2,1)S(1)} %get-tuple-element.102), channel_id=1, source_target_pairs={{0,4},{4,8},{8,12},{12,16},{16,20},{20,24},{24,28},{1,5},{5,9},{9,... | collective-permute-start | bytes 294920 | tf_op jit(solution)/shard_map/ppermute | solution.py:120
  40.2 1.3 collective-permute-start.5
  41.5 0.9 collective-permute-done.4.refs_1_
  42.4 4.3 %collective-permute-done.5.refs_2_ = bf16[3,16,1024]{2,1,0:T(8,128)(2,1)S(1)} collective-permute-done((bf16[3,16,1024]{2,1,0:T(8,128)(2,1)S(1)}, bf16[3,16,1024]{2,1,0:T(8,128)(2,1)S(1)}, u32[]{:S(2)}, u32[]{:S(2)}) %collective-permute-start.5) | collective-permute-done | bytes 98336 | tf_op jit(solution)/shard_map/ppermute | solution.py:120
  46.8 3.9 %collective-permute-start.6 = (bf16[10,8,1024]{2,1,0:T(8,128)(2,1)S(1)}, bf16[10,8,1024]{2,1,0:T(8,128)(2,1)S(1)}, u32[]{:S(2)}, u32[]{:S(2)}) collective-permute-start(bf16[10,8,1024]{2,1,0:T(8,128)(2,1)S(1)} %get-tuple-element.104), channel_id=1, source_target_pairs={{0,1},{1,2},{2,3},{4,5},{5,6},{6,7},{8,9},{9,10},{10,11},{12,13},{... | collective-permute-start | bytes 491528 | tf_op jit(solution)/shard_map/ppermute | solution.py:120
  50.7 1.3 collective-permute-start.7
  52.0 2.8 %collective-permute-done.7.refs_4_ = bf16[10,8,1024]{2,1,0:T(8,128)(2,1)S(1)} collective-permute-done((bf16[10,8,1024]{2,1,0:T(8,128)(2,1)S(1)}, bf16[10,8,1024]{2,1,0:T(8,128)(2,1)S(1)}, u32[]{:S(2)}, u32[]{:S(2)}) %collective-permute-start.7) | collective-permute-done | bytes 163872 | tf_op jit(solution)/shard_map/ppermute | solution.py:120
  54.8 3.3 %mixer.1 = (f32[4,16,1024]{2,1,0:T(8,128)S(1)}, bf16[4,16,1024]{2,1,0:T(8,128)(2,1)S(1)}, bf16[3,16,1024]{2,1,0:T(8,128)(2,1)S(1)}, bf16[3,16,1024]{2,1,0:T(8,128)(2,1)S(1)}, f32[1,1024]{1,0:T(1,128)S(1)}) custom-call(bf16[4,16,1024]{2,1,0:T(8,128)(2,1)S(1)} %get-tuple-element.101.refs_0_, bf16[3,16,1024]{2,1,0:T(8,128)(2,1)S(1)} %collective-permute-done.4.refs_1_, ...), custom_call_target="tpu_custom_call" | custom-call | flops 3300000000 | bytes 1585152 | tf_op jit(solution)/shard_map/mixer/pallas_call | solution.py:35
  58.1 2.9 %mixer_weights.1 = (f32[49,1024]{1,0:T(8,128)S(1)}, bf16[256,3072]{1,0:T(8,128)(2,1)S(1)}) custom-call(bf16[4,16,1024]{2,1,0:T(8,128)(2,1)S(1)} %get-tuple-element.101.refs_0_, bf16[3,16,1024]{2,1,0:T(8,128)(2,1)S(1)} %collective-permute-done.4.refs_1_, bf16[3,16,1024]{2,1,0:T(8,128)(2,1)S(1)} %collective-permute-done.5.refs_2_, ...), custom_call_target="tpu_custom_call", output_to_operand_aliasing={{1}: (6, {})} | custom-call | flops 3300000000 | bytes 4263936 | tf_op jit(solution)/shard_map/mixer_weights/pallas_call | solution.py:35
  61.0 3.9 %collective-permute-start.12 = (bf16[256,3072]{1,0:T(8,128)(2,1)S(1)}, bf16[256,3072]{1,0:T(8,128)(2,1)S(1)}, u32[]{:S(2)}, u32[]{:S(2)}) collective-permute-start(bf16[256,3072]{1,0:T(8,128)(2,1)S(1)} %get-tuple-element.130.refs_0_), channel_id=1, source_target_pairs={{0,1},{1,0},{2,3},{3,2},{4,5},{5,4},{6,7},{7,6},{8,9},{9,8},{10,11... | collective-permute-start | bytes 4718600 | tf_op jit(solution)/shard_map/ppermute | solution.py:49
  64.9 3.4 %collective-permute-start.8 = (bf16[3,16,1024]{2,1,0:T(8,128)(2,1)S(1)}, bf16[3,16,1024]{2,1,0:T(8,128)(2,1)S(1)}, u32[]{:S(2)}, u32[]{:S(2)}) collective-permute-start(bf16[3,16,1024]{2,1,0:T(8,128)(2,1)S(1)} %get-tuple-element.110), channel_id=1, source_target_pairs={{0,4},{4,8},{8,12},{12,16},{16,20},{20,24},{24,28},{1,5},{5,9},{9,... | collective-permute-start | bytes 294920 | tf_op jit(solution)/shard_map/ppermute | solution.py:120
  68.3 1.3 collective-permute-start.9
  69.6 0.9 collective-permute-done.8.refs_1_
  70.5 4.3 %collective-permute-done.9.refs_2_ = bf16[3,16,1024]{2,1,0:T(8,128)(2,1)S(1)} collective-permute-done((bf16[3,16,1024]{2,1,0:T(8,128)(2,1)S(1)}, bf16[3,16,1024]{2,1,0:T(8,128)(2,1)S(1)}, u32[]{:S(2)}, u32[]{:S(2)}) %collective-permute-start.9) | collective-permute-done | bytes 98336 | tf_op jit(solution)/shard_map/ppermute | solution.py:120
  74.8 1.3 collective-permute-start.10
  76.2 1.3 collective-permute-start.11
  77.5 2.2 %collective-permute-done.11.refs_4_ = bf16[10,8,1024]{2,1,0:T(8,128)(2,1)S(1)} collective-permute-done((bf16[10,8,1024]{2,1,0:T(8,128)(2,1)S(1)}, bf16[10,8,1024]{2,1,0:T(8,128)(2,1)S(1)}, u32[]{:S(2)}, u32[]{:S(2)}) %collective-permute-start.11) | collective-permute-done | bytes 163872 | tf_op jit(solution)/shard_map/ppermute | solution.py:120
  79.7 3.1 %section_grad.1 = (bf16[64,1024]{1,0:T(8,128)(2,1)S(1)}, bf16[2,64,256]{2,1,0:T(8,128)(2,1)S(1)}, bf16[2,64,256]{2,1,0:T(8,128)(2,1)S(1)}) custom-call(bf16[4,16,1024]{2,1,0:T(8,128)(2,1)S(1)} %get-tuple-element.109.refs_0_, bf16[3,16,1024]{2,1,0:T(8,128)(2,1)S(1)} %collective-permute-done.8.refs_1_, ...), custom_call_target="tpu_custom_call" | custom-call | flops 3300000000 | bytes 1249280 | tf_op jit(solution)/shard_map/section_grad/pallas_call | solution.py:35
  82.8 3.9 %collective-permute-start.14 = (bf16[2,64,256]{2,1,0:T(8,128)(2,1)S(1)}, bf16[2,64,256]{2,1,0:T(8,128)(2,1)S(1)}, u32[]{:S(2)}, u32[]{:S(2)}) collective-permute-start(bf16[2,64,256]{2,1,0:T(8,128)(2,1)S(1)} %get-tuple-element.134), channel_id=1, source_target_pairs={{0,1},{1,0},{2,3},{3,2},{4,5},{5,4},{6,7},{7,6},{8,9},{9,8},{10,11... | collective-permute-start | bytes 196616 | tf_op jit(solution)/shard_map/ppermute | solution.py:49
  86.7 2.5 %merge_back.1 = (f32[256,512]{1,0:T(8,128)S(1)}, bf16[256,512]{1,0:T(8,128)(2,1)S(1)}, bf16[368,256]{1,0:T(8,128)(2,1)S(1)}, bf16[368,256]{1,0:T(8,128)(2,1)S(1)}) custom-call(bf16[64,1024]{1,0:T(8,128)(2,1)S(1)} %get-tuple-element.118.refs_0_, bf16[2048,1024]{1,0:T(8,128)(2,1)S(1)} %get-tuple-element.119.refs_1_, ...), custom_call_target="tpu_custom_call" | custom-call | flops 3300000000 | bytes 6747136 | tf_op jit(solution)/shard_map/merge_back/pallas_call | solution.py:35
  89.3 2.6 %patch_product.1 = (bf16[2048,256]{1,0:T(8,128)(2,1)S(1)}, bf16[2048,256]{1,0:T(8,128)(2,1)S(1)}) custom-call(bf16[256,3072]{1,0:T(8,128)(2,1)S(1)} %get-tuple-element.130.refs_0_, bf16[256,3072]{1,0:T(8,128)(2,1)S(1)} %collective-permute-done.12.refs_1_, bf16[2,64,256]{2,1,0:T(8,128)(2,1)S(1)} %get-tuple-element.133.refs_2_, ...), custom_call_target="tpu_custom_call" | custom-call | flops 3300000000 | bytes 5373952 | tf_op jit(solution)/shard_map/patch_product/pallas_call | solution.py:35
  92.2 2.6 %project_product.1 = (bf16[1136,256]{1,0:T(8,128)(2,1)S(1)}, bf16[1136,256]{1,0:T(8,128)(2,1)S(1)}) custom-call(bf16[256,3072]{1,0:T(8,128)(2,1)S(1)} %get-tuple-element.130.refs_0_, bf16[256,3072]{1,0:T(8,128)(2,1)S(1)} %collective-permute-done.12.refs_1_, bf16[368,256]{1,0:T(8,128)(2,1)S(1)} %get-tuple-element.131.refs_2_, ...), custom_call_target="tpu_custom_call" | custom-call | flops 3300000000 | bytes 4685824 | tf_op jit(solution)/shard_map/project_product/pallas_call | solution.py:35
  94.8 3.2 %mlp_back.1 = (bf16[256,1024]{1,0:T(8,128)(2,1)S(1)}, bf16[256,1024]{1,0:T(8,128)(2,1)S(1)}, bf16[8,32,512]{2,1,0:T(8,128)(2,1)S(1)}, bf16[3,32,512]{2,1,0:T(8,1...) custom-call(bf16[256,512]{1,0:T(8,128)(2,1)S(1)} %get-tuple-element.124.refs_0_, ...), custom_call_target="tpu_custom_call" | custom-call | flops 4400000000 | bytes 7541760 | tf_op jit(solution)/shard_map/mlp_back/pallas_call | solution.py:35
  98.3 2.5 %collective-permute-start.27 = (bf16[1136,256]{1,0:T(8,128)(2,1)S(1)}, bf16[1136,256]{1,0:T(8,128)(2,1)S(1)}, u32[]{:S(2)}, u32[]{:S(2)}) collective-permute-start(bf16[1136,256]{1,0:T(8,128)(2,1)S(1)} %get-tuple-element.136.refs_7_), channel_id=1, source_target_pairs={{0,4},{4,0},{8,12},{12,8},{16,20},{20,16},{24,28},{28,24},{1,5},{5... | collective-permute-start | bytes 1744904 | tf_op jit(solution)/shard_map/ppermute | solution.py:49
  100.8 1.9 %collective-permute-start.15 = (bf16[3,32,512]{2,1,0:T(8,128)(2,1)S(1)}, bf16[3,32,512]{2,1,0:T(8,128)(2,1)S(1)}, u32[]{:S(2)}, u32[]{:S(2)}) collective-permute-start(bf16[3,32,512]{2,1,0:T(8,128)(2,1)S(1)} %get-tuple-element.138), channel_id=1, source_target_pairs={{0,4},{4,8},{8,12},{12,16},{16,20},{20,24},{24,28},{1,5},{5,9},{9,... | collective-permute-start | bytes 294920 | tf_op jit(solution)/shard_map/ppermute | solution.py:120
  102.7 1.5 collective-permute-start.16
  104.2 1.9 %expand_product.1 = (bf16[1024,256]{1,0:T(8,128)(2,1)S(1)}, bf16[1024,256]{1,0:T(8,128)(2,1)S(1)}) custom-call(bf16[256,3072]{1,0:T(8,128)(2,1)S(1)} %get-tuple-element.130.refs_0_, bf16[256,3072]{1,0:T(8,128)(2,1)S(1)} %collective-permute-done.12.refs_1_, bf16[256,1024]{1,0:T(8,128)(2,1)S(1)} %get-tuple-element.140.refs_2_, ...), custom_call_target="tpu_custom_call" | custom-call | flops 3300000000 | bytes 5242880 | tf_op jit(solution)/shard_map/expand_product/pallas_call | solution.py:35
  106.0 3.7 %collective-permute-start.20 = (bf16[1024,256]{1,0:T(8,128)(2,1)S(1)}, bf16[1024,256]{1,0:T(8,128)(2,1)S(1)}, u32[]{:S(2)}, u32[]{:S(2)}) collective-permute-start(bf16[1024,256]{1,0:T(8,128)(2,1)S(1)} %get-tuple-element.142.refs_3_), channel_id=1, source_target_pairs={{0,4},{4,0},{8,12},{12,8},{16,20},{20,16},{24,28},{28,24},{1,5},{5... | collective-permute-start | bytes 1572872 | tf_op jit(solution)/shard_map/ppermute | solution.py:49
  109.8 7.7 %collective-permute-done.32.refs_1_ = bf16[2048,256]{1,0:T(8,128)(2,1)S(1)} collective-permute-done((bf16[2048,256]{1,0:T(8,128)(2,1)S(1)}, bf16[2048,256]{1,0:T(8,128)(2,1)S(1)}, u32[]{:S(2)}, u32[]{:S(2)}) %collective-permute-start.32) | collective-permute-done | bytes 1048608 | tf_op jit(solution)/shard_map/ppermute | solution.py:49
  117.8 1.6 collective-permute-start.33
  119.4 5.4 %block_weights.1 = (bf16[64,256]{1,0:T(8,128)(2,1)S(1)}, bf16[64,256]{1,0:T(8,128)(2,1)S(1)}) custom-call(bf16[8,32,512]{2,1,0:T(8,128)(2,1)S(1)} %get-tuple-element.92.refs_0_, bf16[3,32,512]{2,1,0:T(8,128)(2,1)S(1)} %collective-permute-done.refs_1_, bf16[3,32,512]{2,1,0:T(8,128)(2,1)S(1)} %collective-permute-done.1.refs_2_, ...), custom_call_target="tpu_custom_call" | custom-call | flops 5500000256 | bytes 1017856 | tf_op jit(solution)/shard_map/block_weights/pallas_call | solution.py:35
  124.8 1.2 collective-permute-done.21
  126.1 2.5 %collective-permute-start.22 = (bf16[64,256]{1,0:T(8,128)(2,1)S(1)}, bf16[64,256]{1,0:T(8,128)(2,1)S(1)}, u32[]{:S(2)}, u32[]{:S(2)}) collective-permute-start(bf16[64,256]{1,0:T(8,128)(2,1)S(1)} %add.23.refs_2_), channel_id=1, source_target_pairs={{0,4},{4,0},{8,12},{12,8},{16,20},{20,16},{24,28},{28,24},{1,5},{5... | collective-permute-start | bytes 98312 | tf_op jit(solution)/shard_map/ppermute | solution.py:49
  128.7 0.8 collective-permute-start.28
  129.5 1.0 collective-permute-done.22.refs_3_
  130.6 1.7 collective-permute-start.23
  132.4 3.0 %collective-permute-start.34 = (bf16[512,256]{1,0:T(8,128)(2,1)S(1)}, bf16[512,256]{1,0:T(8,128)(2,1)S(1)}, u32[]{:S(2)}, u32[]{:S(2)}) collective-permute-start(bf16[512,256]{1,0:T(8,128)(2,1)S(1)} %get-tuple-element.169), channel_id=1, source_target_pairs={{0,16},{4,20},{8,24},{12,28},{16,0},{20,4},{24,8},{28,12},{1,17},{... | collective-permute-start | bytes 786440 | tf_op jit(solution)/shard_map/ppermute | solution.py:49
  135.4 9.4 %collective-permute-done.28.refs_1_ = bf16[624,256]{1,0:T(8,128)(2,1)S(1)} collective-permute-done((bf16[624,256]{1,0:T(8,128)(2,1)S(1)}, bf16[624,256]{1,0:T(8,128)(2,1)S(1)}, u32[]{:S(2)}, u32[]{:S(2)}) %collective-permute-start.28) | collective-permute-done | bytes 319520 | tf_op jit(solution)/shard_map/ppermute | solution.py:49
  145.5 5.4 %collective-permute-done.23.refs_1_ = bf16[576,256]{1,0:T(8,128)(2,1)S(1)} collective-permute-done((bf16[576,256]{1,0:T(8,128)(2,1)S(1)}, bf16[576,256]{1,0:T(8,128)(2,1)S(1)}, u32[]{:S(2)}, u32[]{:S(2)}) %collective-permute-start.23) | collective-permute-done | bytes 294944 | tf_op jit(solution)/shard_map/ppermute | solution.py:49
  151.1 2.0 %collective-permute-start.35 = (bf16[256,256]{1,0:T(8,128)(2,1)S(1)}, bf16[256,256]{1,0:T(8,128)(2,1)S(1)}, u32[]{:S(2)}, u32[]{:S(2)}) collective-permute-start(bf16[256,256]{1,0:T(8,128)(2,1)S(1)} %get-tuple-element.171), channel_id=1, source_target_pairs={{0,4},{4,0},{8,12},{12,8},{16,20},{20,16},{24,28},{28,24},{1,5},{5... | collective-permute-start | bytes 393224 | tf_op jit(solution)/shard_map/ppermute | solution.py:49
  153.2 10.7 %collective-permute-done.29 = bf16[368,256]{1,0:T(8,128)(2,1)S(1)} collective-permute-done((bf16[368,256]{1,0:T(8,128)(2,1)S(1)}, bf16[368,256]{1,0:T(8,128)(2,1)S(1)}, u32[]{:S(2)}, u32[]{:S(2)}) %collective-permute-start.29) | collective-permute-done | bytes 188448 | tf_op jit(solution)/shard_map/ppermute | solution.py:49
  164.3 2.3 %collective-permute-done.24 = bf16[320,256]{1,0:T(8,128)(2,1)S(1)} collective-permute-done((bf16[320,256]{1,0:T(8,128)(2,1)S(1)}, bf16[320,256]{1,0:T(8,128)(2,1)S(1)}, u32[]{:S(2)}, u32[]{:S(2)}) %collective-permute-start.24) | collective-permute-done | bytes 163872 | tf_op jit(solution)/shard_map/ppermute | solution.py:49
  166.7 0.9 collective-permute-start.25
  167.6 1.3 collective-permute-start.36
  168.9 1.3 collective-permute-start.18
  170.2 1.3 collective-permute-start.19
  171.5 2.2 %collective-permute-start.31 = (bf16[368,256]{1,0:T(8,128)(2,1)S(1)}, bf16[368,256]{1,0:T(8,128)(2,1)S(1)}, u32[]{:S(2)}, u32[]{:S(2)}) collective-permute-start(bf16[368,256]{1,0:T(8,128)(2,1)S(1)} %add.27.refs_0_), channel_id=1, source_target_pairs={{0,1},{1,0},{2,3},{3,2},{4,5},{5,4},{6,7},{7,6},{8,9},{9,8},{10,11... | collective-permute-start | bytes 565256 | tf_op jit(solution)/shard_map/ppermute | solution.py:49
  174.2 1.7 collective-permute-done.36
  176.1 6.6 %input_grad.1 = bf16[8,32,512]{2,1,0:T(8,128)(2,1)} custom-call(bf16[8,32,512]{2,1,0:T(8,128)(2,1)S(1)} %get-tuple-element.137.refs_0_.refs_5_, bf16[3,32,512]{2,1,0:T(8,128)(2,1)S(1)} %collective-permute-done.15.refs_1_.refs_7_, bf16[3,32,512]{2,1,0:T(8,128)(2,1)S(1)} %collective-permute-done.16.refs_2_.refs_8_, ...), custom_call_target="tpu_custom_call" | custom-call | flops 5500000256 | bytes 1574912 | tf_op jit(solution)/shard_map/input_grad/pallas_call | solution.py:35
  182.7 1.0 finish_project.1
  183.6 0.9 finish_expand.1
  184.5 1.0 finish_patch.1
  (70 shorter events, 4.7 us)
Async XLA Ops:
  0.6 1.0 copy-start.3
  1.6 0.9 copy-start.7
  2.5 0.7 copy-start.9
  3.2 0.7 copy-start.10
  3.9 0.7 copy-start.11
  4.5 18.5 %copy-start = (bf16[2048,1024]{1,0:T(8,128)(2,1)S(1)}, bf16[2048,1024]{1,0:T(8,128)(2,1)}, u32[]{:S(2)}) copy-start(bf16[2048,1024]{1,0:T(8,128)(2,1)} %refs_11_.1) | copy-start | bytes 12582916
  4.5 18.5 %copy-start.2 = (bf16[2048,512]{1,0:T(8,128)(2,1)S(1)}, bf16[2048,512]{1,0:T(8,128)(2,1)}, u32[]{:S(2)}) copy-start(bf16[2048,512]{1,0:T(8,128)(2,1)} %refs_10_.1) | copy-start | bytes 6291460
  5.0 18.0 %copy-start.1 = (bf16[512,2048]{1,0:T(8,128)(2,1)S(1)}, bf16[512,2048]{1,0:T(8,128)(2,1)}, u32[]{:S(2)}) copy-start(bf16[512,2048]{1,0:T(8,128)(2,1)} %refs_9_.1) | copy-start | bytes 6291460
  5.0 18.0 %copy-start.4 = (f32[7,7,1024]{2,1,0:T(8,128)S(1)}, f32[7,7,1024]{2,1,0:T(8,128)}, u32[]{:S(2)}) copy-start(f32[7,7,1024]{2,1,0:T(8,128)} %refs_12_.1) | copy-start | bytes 602116
  5.1 18.0 %copy-start.5 = (bf16[1,4,16,1024]{3,2,1,0:T(8,128)(2,1)S(1)}, bf16[1,4,16,1024]{3,2,1,0:T(8,128)(2,1)}, u32[]{:S(2)}) copy-start(bf16[1,4,16,1024]{3,2,1,0:T(8,128)(2,1)} %param.22) | copy-start | bytes 393220
  5.1 18.0 %copy-start.6 = (bf16[1,4,16,1024]{3,2,1,0:T(8,128)(2,1)S(1)}, bf16[1,4,16,1024]{3,2,1,0:T(8,128)(2,1)}, u32[]{:S(2)}) copy-start(bf16[1,4,16,1024]{3,2,1,0:T(8,128)(2,1)} %param.23) | copy-start | bytes 393220
  5.1 18.0 %copy-start.8 = (f32[1024]{0:T(1024)S(1)}, f32[1024]{0:T(1024)}, u32[]{:S(2)}) copy-start(f32[1024]{0:T(1024)} %param.21) | copy-start | bytes 12292
  5.1 7.3 %collective-permute-start = (bf16[3,32,512]{2,1,0:T(8,128)(2,1)S(1)}, bf16[3,32,512]{2,1,0:T(8,128)(2,1)S(1)}, u32[]{:S(2)}, u32[]{:S(2)}) collective-permute-start(bf16[3,32,512]{2,1,0:T(8,128)(2,1)S(1)} %get-tuple-element.93), channel_id=1, source_target_pairs={{0,4},{4,8},{8,12},{12,16},{16,20},{20,24},{24,28},{1,5},{5,9},{9,... | collective-permute-start | bytes 294920 | tf_op jit(solution)/shard_map/ppermute | solution.py:120
  10.2 6.5 %collective-permute-start.1 = (bf16[3,32,512]{2,1,0:T(8,128)(2,1)S(1)}, bf16[3,32,512]{2,1,0:T(8,128)(2,1)S(1)}, u32[]{:S(2)}, u32[]{:S(2)}) collective-permute-start(bf16[3,32,512]{2,1,0:T(8,128)(2,1)S(1)} %get-tuple-element.94), channel_id=1, source_target_pairs={{4,0},{8,4},{12,8},{16,12},{20,16},{24,20},{28,24},{5,1},{9,5},{13... | collective-permute-start | bytes 294920 | tf_op jit(solution)/shard_map/ppermute | solution.py:120
  16.7 2.6 %collective-permute-start.2 = (bf16[14,8,512]{2,1,0:T(8,128)(2,1)S(1)}, bf16[14,8,512]{2,1,0:T(8,128)(2,1)S(1)}, u32[]{:S(2)}, u32[]{:S(2)}) collective-permute-start(bf16[14,8,512]{2,1,0:T(8,128)(2,1)S(1)} %get-tuple-element.95), channel_id=1, source_target_pairs={{0,1},{1,2},{2,3},{4,5},{5,6},{6,7},{8,9},{9,10},{10,11},{12,13},{... | collective-permute-start | bytes 344072 | tf_op jit(solution)/shard_map/ppermute | solution.py:120
  18.0 5.0 %collective-permute-start.3 = (bf16[14,8,512]{2,1,0:T(8,128)(2,1)S(1)}, bf16[14,8,512]{2,1,0:T(8,128)(2,1)S(1)}, u32[]{:S(2)}, u32[]{:S(2)}) collective-permute-start(bf16[14,8,512]{2,1,0:T(8,128)(2,1)S(1)} %get-tuple-element.96), channel_id=1, source_target_pairs={{1,0},{2,1},{3,2},{5,4},{6,5},{7,6},{9,8},{10,9},{11,10},{13,12},{... | collective-permute-start | bytes 344072 | tf_op jit(solution)/shard_map/ppermute | solution.py:120
  35.9 6.6 %collective-permute-start.4 = (bf16[3,16,1024]{2,1,0:T(8,128)(2,1)S(1)}, bf16[3,16,1024]{2,1,0:T(8,128)(2,1)S(1)}, u32[]{:S(2)}, u32[]{:S(2)}) collective-permute-start(bf16[3,16,1024]{2,1,0:T(8,128)(2,1)S(1)} %get-tuple-element.102), channel_id=1, source_target_pairs={{0,4},{4,8},{8,12},{12,16},{16,20},{20,24},{24,28},{1,5},{5,9},{9,... | collective-permute-start | bytes 294920 | tf_op jit(solution)/shard_map/ppermute | solution.py:120
  40.2 6.5 %collective-permute-start.5 = (bf16[3,16,1024]{2,1,0:T(8,128)(2,1)S(1)}, bf16[3,16,1024]{2,1,0:T(8,128)(2,1)S(1)}, u32[]{:S(2)}, u32[]{:S(2)}) collective-permute-start(bf16[3,16,1024]{2,1,0:T(8,128)(2,1)S(1)} %get-tuple-element.103), channel_id=1, source_target_pairs={{4,0},{8,4},{12,8},{16,12},{20,16},{24,20},{28,24},{5,1},{9,5},{13... | collective-permute-start | bytes 294920 | tf_op jit(solution)/shard_map/ppermute | solution.py:120
  46.8 5.2 %collective-permute-start.6 = (bf16[10,8,1024]{2,1,0:T(8,128)(2,1)S(1)}, bf16[10,8,1024]{2,1,0:T(8,128)(2,1)S(1)}, u32[]{:S(2)}, u32[]{:S(2)}) collective-permute-start(bf16[10,8,1024]{2,1,0:T(8,128)(2,1)S(1)} %get-tuple-element.104), channel_id=1, source_target_pairs={{0,1},{1,2},{2,3},{4,5},{5,6},{6,7},{8,9},{9,10},{10,11},{12,13},{... | collective-permute-start | bytes 491528 | tf_op jit(solution)/shard_map/ppermute | solution.py:120
  50.7 4.1 %collective-permute-start.7 = (bf16[10,8,1024]{2,1,0:T(8,128)(2,1)S(1)}, bf16[10,8,1024]{2,1,0:T(8,128)(2,1)S(1)}, u32[]{:S(2)}, u32[]{:S(2)}) collective-permute-start(bf16[10,8,1024]{2,1,0:T(8,128)(2,1)S(1)} %get-tuple-element.105), channel_id=1, source_target_pairs={{1,0},{2,1},{3,2},{5,4},{6,5},{7,6},{9,8},{10,9},{11,10},{13,12},{... | collective-permute-start | bytes 491528 | tf_op jit(solution)/shard_map/ppermute | solution.py:120
  61.0 28.3 %collective-permute-start.12 = (bf16[256,3072]{1,0:T(8,128)(2,1)S(1)}, bf16[256,3072]{1,0:T(8,128)(2,1)S(1)}, u32[]{:S(2)}, u32[]{:S(2)}) collective-permute-start(bf16[256,3072]{1,0:T(8,128)(2,1)S(1)} %get-tuple-element.130.refs_0_), channel_id=1, source_target_pairs={{0,1},{1,0},{2,3},{3,2},{4,5},{5,4},{6,7},{7,6},{8,9},{9,8},{10,11... | collective-permute-start | bytes 4718600 | tf_op jit(solution)/shard_map/ppermute | solution.py:49
  64.9 5.6 %collective-permute-start.8 = (bf16[3,16,1024]{2,1,0:T(8,128)(2,1)S(1)}, bf16[3,16,1024]{2,1,0:T(8,128)(2,1)S(1)}, u32[]{:S(2)}, u32[]{:S(2)}) collective-permute-start(bf16[3,16,1024]{2,1,0:T(8,128)(2,1)S(1)} %get-tuple-element.110), channel_id=1, source_target_pairs={{0,4},{4,8},{8,12},{12,16},{16,20},{20,24},{24,28},{1,5},{5,9},{9,... | collective-permute-start | bytes 294920 | tf_op jit(solution)/shard_map/ppermute | solution.py:120
  68.3 6.5 %collective-permute-start.9 = (bf16[3,16,1024]{2,1,0:T(8,128)(2,1)S(1)}, bf16[3,16,1024]{2,1,0:T(8,128)(2,1)S(1)}, u32[]{:S(2)}, u32[]{:S(2)}) collective-permute-start(bf16[3,16,1024]{2,1,0:T(8,128)(2,1)S(1)} %get-tuple-element.111), channel_id=1, source_target_pairs={{4,0},{8,4},{12,8},{16,12},{20,16},{24,20},{28,24},{5,1},{9,5},{13... | collective-permute-start | bytes 294920 | tf_op jit(solution)/shard_map/ppermute | solution.py:120
  74.8 2.6 %collective-permute-start.10 = (bf16[10,8,1024]{2,1,0:T(8,128)(2,1)S(1)}, bf16[10,8,1024]{2,1,0:T(8,128)(2,1)S(1)}, u32[]{:S(2)}, u32[]{:S(2)}) collective-permute-start(bf16[10,8,1024]{2,1,0:T(8,128)(2,1)S(1)} %get-tuple-element.115), channel_id=1, source_target_pairs={{0,1},{1,2},{2,3},{4,5},{5,6},{6,7},{8,9},{9,10},{10,11},{12,13},{... | collective-permute-start | bytes 491528 | tf_op jit(solution)/shard_map/ppermute | solution.py:120
  76.2 3.6 %collective-permute-start.11 = (bf16[10,8,1024]{2,1,0:T(8,128)(2,1)S(1)}, bf16[10,8,1024]{2,1,0:T(8,128)(2,1)S(1)}, u32[]{:S(2)}, u32[]{:S(2)}) collective-permute-start(bf16[10,8,1024]{2,1,0:T(8,128)(2,1)S(1)} %get-tuple-element.116), channel_id=1, source_target_pairs={{1,0},{2,1},{3,2},{5,4},{6,5},{7,6},{9,8},{10,9},{11,10},{13,12},{... | collective-permute-start | bytes 491528 | tf_op jit(solution)/shard_map/ppermute | solution.py:120
  82.8 6.5 %collective-permute-start.14 = (bf16[2,64,256]{2,1,0:T(8,128)(2,1)S(1)}, bf16[2,64,256]{2,1,0:T(8,128)(2,1)S(1)}, u32[]{:S(2)}, u32[]{:S(2)}) collective-permute-start(bf16[2,64,256]{2,1,0:T(8,128)(2,1)S(1)} %get-tuple-element.134), channel_id=1, source_target_pairs={{0,1},{1,0},{2,3},{3,2},{4,5},{5,4},{6,7},{7,6},{8,9},{9,8},{10,11... | collective-permute-start | bytes 196616 | tf_op jit(solution)/shard_map/ppermute | solution.py:49
  89.2 3.0 %collective-permute-start.13 = (bf16[368,256]{1,0:T(8,128)(2,1)S(1)}, bf16[368,256]{1,0:T(8,128)(2,1)S(1)}, u32[]{:S(2)}, u32[]{:S(2)}) collective-permute-start(bf16[368,256]{1,0:T(8,128)(2,1)S(1)} %get-tuple-element.132), channel_id=1, source_target_pairs={{0,1},{1,0},{2,3},{3,2},{4,5},{5,4},{6,7},{7,6},{8,9},{9,8},{10,11... | collective-permute-start | bytes 565256 | tf_op jit(solution)/shard_map/ppermute | solution.py:49
  91.9 25.6 %collective-permute-start.32 = (bf16[2048,256]{1,0:T(8,128)(2,1)S(1)}, bf16[2048,256]{1,0:T(8,128)(2,1)S(1)}, u32[]{:S(2)}, u32[]{:S(2)}) collective-permute-start(bf16[2048,256]{1,0:T(8,128)(2,1)S(1)} %get-tuple-element.135.refs_4_), channel_id=1, source_target_pairs={{0,2},{1,3},{2,0},{3,1},{4,6},{5,7},{6,4},{7,5},{8,10},{9,11},{10,... | collective-permute-start | bytes 3145736 | tf_op jit(solution)/shard_map/ppermute | solution.py:49
  98.0 6.2 %collective-permute-start.17 = (bf16[256,1024]{1,0:T(8,128)(2,1)S(1)}, bf16[256,1024]{1,0:T(8,128)(2,1)S(1)}, u32[]{:S(2)}, u32[]{:S(2)}) collective-permute-start(bf16[256,1024]{1,0:T(8,128)(2,1)S(1)} %get-tuple-element.141), channel_id=1, source_target_pairs={{0,1},{1,0},{2,3},{3,2},{4,5},{5,4},{6,7},{7,6},{8,9},{9,8},{10,11... | collective-permute-start | bytes 1572872 | tf_op jit(solution)/shard_map/ppermute | solution.py:49
  98.3 30.3 %collective-permute-start.27 = (bf16[1136,256]{1,0:T(8,128)(2,1)S(1)}, bf16[1136,256]{1,0:T(8,128)(2,1)S(1)}, u32[]{:S(2)}, u32[]{:S(2)}) collective-permute-start(bf16[1136,256]{1,0:T(8,128)(2,1)S(1)} %get-tuple-element.136.refs_7_), channel_id=1, source_target_pairs={{0,4},{4,0},{8,12},{12,8},{16,20},{20,16},{24,28},{28,24},{1,5},{5... | collective-permute-start | bytes 1744904 | tf_op jit(solution)/shard_map/ppermute | solution.py:49
  100.8 18.6 %collective-permute-start.15 = (bf16[3,32,512]{2,1,0:T(8,128)(2,1)S(1)}, bf16[3,32,512]{2,1,0:T(8,128)(2,1)S(1)}, u32[]{:S(2)}, u32[]{:S(2)}) collective-permute-start(bf16[3,32,512]{2,1,0:T(8,128)(2,1)S(1)} %get-tuple-element.138), channel_id=1, source_target_pairs={{0,4},{4,8},{8,12},{12,16},{16,20},{20,24},{24,28},{1,5},{5,9},{9,... | collective-permute-start | bytes 294920 | tf_op jit(solution)/shard_map/ppermute | solution.py:120
  102.7 16.7 %collective-permute-start.16 = (bf16[3,32,512]{2,1,0:T(8,128)(2,1)S(1)}, bf16[3,32,512]{2,1,0:T(8,128)(2,1)S(1)}, u32[]{:S(2)}, u32[]{:S(2)}) collective-permute-start(bf16[3,32,512]{2,1,0:T(8,128)(2,1)S(1)} %get-tuple-element.139), channel_id=1, source_target_pairs={{4,0},{8,4},{12,8},{16,12},{20,16},{24,20},{28,24},{5,1},{9,5},{13... | collective-permute-start | bytes 294920 | tf_op jit(solution)/shard_map/ppermute | solution.py:120
  106.0 24.4 %collective-permute-start.20 = (bf16[1024,256]{1,0:T(8,128)(2,1)S(1)}, bf16[1024,256]{1,0:T(8,128)(2,1)S(1)}, u32[]{:S(2)}, u32[]{:S(2)}) collective-permute-start(bf16[1024,256]{1,0:T(8,128)(2,1)S(1)} %get-tuple-element.142.refs_3_), channel_id=1, source_target_pairs={{0,4},{4,0},{8,12},{12,8},{16,20},{20,16},{24,28},{28,24},{1,5},{5... | collective-permute-start | bytes 1572872 | tf_op jit(solution)/shard_map/ppermute | solution.py:49
  117.8 14.5 %collective-permute-start.33 = (bf16[1024,256]{1,0:T(8,128)(2,1)S(1)}, bf16[1024,256]{1,0:T(8,128)(2,1)S(1)}, u32[]{:S(2)}, u32[]{:S(2)}) collective-permute-start(bf16[1024,256]{1,0:T(8,128)(2,1)S(1)} %get-tuple-element.167), channel_id=1, source_target_pairs={{0,8},{4,12},{8,0},{12,4},{16,24},{20,28},{24,16},{28,20},{1,9},{5... | collective-permute-start | bytes 1572872 | tf_op jit(solution)/shard_map/ppermute | solution.py:49
  124.8 1.3 collective-permute-start.21
  126.1 4.4 %collective-permute-start.22 = (bf16[64,256]{1,0:T(8,128)(2,1)S(1)}, bf16[64,256]{1,0:T(8,128)(2,1)S(1)}, u32[]{:S(2)}, u32[]{:S(2)}) collective-permute-start(bf16[64,256]{1,0:T(8,128)(2,1)S(1)} %add.23.refs_2_), channel_id=1, source_target_pairs={{0,4},{4,0},{8,12},{12,8},{16,20},{20,16},{24,28},{28,24},{1,5},{5... | collective-permute-start | bytes 98312 | tf_op jit(solution)/shard_map/ppermute | solution.py:49
  128.7 16.1 %collective-permute-start.28 = (bf16[624,256]{1,0:T(8,128)(2,1)S(1)}, bf16[624,256]{1,0:T(8,128)(2,1)S(1)}, u32[]{:S(2)}, u32[]{:S(2)}) collective-permute-start(bf16[624,256]{1,0:T(8,128)(2,1)S(1)} %get-tuple-element.159), channel_id=1, source_target_pairs={{0,8},{4,12},{8,0},{12,4},{16,24},{20,28},{24,16},{28,20},{1,9},{5... | collective-permute-start | bytes 958472 | tf_op jit(solution)/shard_map/ppermute | solution.py:49
  130.6 20.3 %collective-permute-start.23 = (bf16[576,256]{1,0:T(8,128)(2,1)S(1)}, bf16[576,256]{1,0:T(8,128)(2,1)S(1)}, u32[]{:S(2)}, u32[]{:S(2)}) collective-permute-start(bf16[576,256]{1,0:T(8,128)(2,1)S(1)} %get-tuple-element.151), channel_id=1, source_target_pairs={{0,8},{4,12},{8,0},{12,4},{16,24},{20,28},{24,16},{28,20},{1,9},{5... | collective-permute-start | bytes 884744 | tf_op jit(solution)/shard_map/ppermute | solution.py:49
  132.4 18.6 %collective-permute-start.34 = (bf16[512,256]{1,0:T(8,128)(2,1)S(1)}, bf16[512,256]{1,0:T(8,128)(2,1)S(1)}, u32[]{:S(2)}, u32[]{:S(2)}) collective-permute-start(bf16[512,256]{1,0:T(8,128)(2,1)S(1)} %get-tuple-element.169), channel_id=1, source_target_pairs={{0,16},{4,20},{8,24},{12,28},{16,0},{20,4},{24,8},{28,12},{1,17},{... | collective-permute-start | bytes 786440 | tf_op jit(solution)/shard_map/ppermute | solution.py:49
  144.9 19.0 %collective-permute-start.29 = (bf16[368,256]{1,0:T(8,128)(2,1)S(1)}, bf16[368,256]{1,0:T(8,128)(2,1)S(1)}, u32[]{:S(2)}, u32[]{:S(2)}) collective-permute-start(bf16[368,256]{1,0:T(8,128)(2,1)S(1)} %get-tuple-element.161), channel_id=1, source_target_pairs={{0,16},{4,20},{8,24},{12,28},{16,0},{20,4},{24,8},{28,12},{1,17},{... | collective-permute-start | bytes 565256 | tf_op jit(solution)/shard_map/ppermute | solution.py:49
  150.9 15.7 %collective-permute-start.24 = (bf16[320,256]{1,0:T(8,128)(2,1)S(1)}, bf16[320,256]{1,0:T(8,128)(2,1)S(1)}, u32[]{:S(2)}, u32[]{:S(2)}) collective-permute-start(bf16[320,256]{1,0:T(8,128)(2,1)S(1)} %get-tuple-element.153), channel_id=1, source_target_pairs={{0,16},{4,20},{8,24},{12,28},{16,0},{20,4},{24,8},{28,12},{1,17},{... | collective-permute-start | bytes 491528 | tf_op jit(solution)/shard_map/ppermute | solution.py:49
  151.1 16.4 %collective-permute-start.35 = (bf16[256,256]{1,0:T(8,128)(2,1)S(1)}, bf16[256,256]{1,0:T(8,128)(2,1)S(1)}, u32[]{:S(2)}, u32[]{:S(2)}) collective-permute-start(bf16[256,256]{1,0:T(8,128)(2,1)S(1)} %get-tuple-element.171), channel_id=1, source_target_pairs={{0,4},{4,0},{8,12},{12,8},{16,20},{20,16},{24,28},{28,24},{1,5},{5... | collective-permute-start | bytes 393224 | tf_op jit(solution)/shard_map/ppermute | solution.py:49
  164.0 7.5 %collective-permute-start.30 = (bf16[368,256]{1,0:T(8,128)(2,1)S(1)}, bf16[368,256]{1,0:T(8,128)(2,1)S(1)}, u32[]{:S(2)}, u32[]{:S(2)}) collective-permute-start(bf16[368,256]{1,0:T(8,128)(2,1)S(1)} %add.26), channel_id=1, source_target_pairs={{0,2},{1,3},{2,0},{3,1},{4,6},{5,7},{6,4},{7,5},{8,10},{9,11},{10,... | collective-permute-start | bytes 565256 | tf_op jit(solution)/shard_map/ppermute | solution.py:49
  166.7 7.4 %collective-permute-start.25 = (bf16[320,256]{1,0:T(8,128)(2,1)S(1)}, bf16[320,256]{1,0:T(8,128)(2,1)S(1)}, u32[]{:S(2)}, u32[]{:S(2)}) collective-permute-start(bf16[320,256]{1,0:T(8,128)(2,1)S(1)} %add.24), channel_id=1, source_target_pairs={{0,2},{1,3},{2,0},{3,1},{4,6},{5,7},{6,4},{7,5},{8,10},{9,11},{10,... | collective-permute-start | bytes 491528 | tf_op jit(solution)/shard_map/ppermute | solution.py:49
  167.6 8.4 %collective-permute-start.36 = (bf16[1,256,256]{2,1,0:T(8,128)(2,1)S(1)}, bf16[1,256,256]{2,1,0:T(8,128)(2,1)S(1)}, u32[]{:S(2)}, u32[]{:S(2)}) collective-permute-start(bf16[1,256,256]{2,1,0:T(8,128)(2,1)S(1)} %add_bitcast_fusion), channel_id=1, source_target_pairs={{0,2},{1,3},{2,0},{3,1},{4,6},{5,7},{6,4},{7,5},{8,10},{9,11},{10,... | collective-permute-start | bytes 393224 | tf_op jit(solution)/shard_map/ppermute | solution.py:49
  168.9 7.2 %collective-permute-start.18 = (bf16[14,8,512]{2,1,0:T(8,128)(2,1)S(1)}, bf16[14,8,512]{2,1,0:T(8,128)(2,1)S(1)}, u32[]{:S(2)}, u32[]{:S(2)}) collective-permute-start(bf16[14,8,512]{2,1,0:T(8,128)(2,1)S(1)} %get-tuple-element.143), channel_id=1, source_target_pairs={{0,1},{1,2},{2,3},{4,5},{5,6},{6,7},{8,9},{9,10},{10,11},{12,13},{... | collective-permute-start | bytes 344072 | tf_op jit(solution)/shard_map/ppermute | solution.py:120
  170.2 5.9 %collective-permute-start.19 = (bf16[14,8,512]{2,1,0:T(8,128)(2,1)S(1)}, bf16[14,8,512]{2,1,0:T(8,128)(2,1)S(1)}, u32[]{:S(2)}, u32[]{:S(2)}) collective-permute-start(bf16[14,8,512]{2,1,0:T(8,128)(2,1)S(1)} %get-tuple-element.144), channel_id=1, source_target_pairs={{1,0},{2,1},{3,2},{5,4},{6,5},{7,6},{9,8},{10,9},{11,10},{13,12},{... | collective-permute-start | bytes 344072 | tf_op jit(solution)/shard_map/ppermute | solution.py:120
  171.5 11.1 %collective-permute-start.31 = (bf16[368,256]{1,0:T(8,128)(2,1)S(1)}, bf16[368,256]{1,0:T(8,128)(2,1)S(1)}, u32[]{:S(2)}, u32[]{:S(2)}) collective-permute-start(bf16[368,256]{1,0:T(8,128)(2,1)S(1)} %add.27.refs_0_), channel_id=1, source_target_pairs={{0,1},{1,0},{2,3},{3,2},{4,5},{5,4},{6,7},{7,6},{8,9},{9,8},{10,11... | collective-permute-start | bytes 565256 | tf_op jit(solution)/shard_map/ppermute | solution.py:49
  174.1 9.5 %collective-permute-start.26 = (bf16[320,256]{1,0:T(8,128)(2,1)S(1)}, bf16[320,256]{1,0:T(8,128)(2,1)S(1)}, u32[]{:S(2)}, u32[]{:S(2)}) collective-permute-start(bf16[320,256]{1,0:T(8,128)(2,1)S(1)} %add.25.refs_0_), channel_id=1, source_target_pairs={{0,1},{1,0},{2,3},{3,2},{4,5},{5,4},{6,7},{7,6},{8,9},{9,8},{10,11... | collective-permute-start | bytes 491528 | tf_op jit(solution)/shard_map/ppermute | solution.py:49
  176.0 8.5 %collective-permute-start.37 = (bf16[2,256,256]{2,1,0:T(8,128)(2,1)S(1)}, bf16[2,256,256]{2,1,0:T(8,128)(2,1)S(1)}, u32[]{:S(2)}, u32[]{:S(2)}) collective-permute-start(bf16[2,256,256]{2,1,0:T(8,128)(2,1)S(1)} %maximum_bitcast_fusion.refs_0_), channel_id=1, source_target_pairs={{0,1},{1,0},{2,3},{3,2},{4,5},{5,4},{6,7},{7,6},{8,9},{9,8},{10,11... | collective-permute-start | bytes 786440 | tf_op jit(solution)/shard_map/ppermute | solution.py:49

commit v2 on v1

--- a/solution.py
+++ b/solution.py
@@ -57,7 +57,7 @@
     return (lax.axis_index(axis) // bit) % 2
 
 
-def chain(keep, send, order, count, rows, extra=()):
+def chain(keep, send, order, count, rows, extra=(), after=()):
     for place, (axis, bit, _) in enumerate(order):
         received = swap(send, axis, bit)
         if place + 1 == len(order):
@@ -72,6 +72,7 @@
             "sum_step",
             (keep, received, *grown),
             (out, out),
+            after=after if place == 0 else (),
             limit=8,
         )
 
@@ -136,6 +137,23 @@
     first, last = run(strip_kernel, name, (center, top, bottom), (strip, strip), after=after, limit=8)
     left, right = neighbours(first, last, "col")
     return center, top, bottom, left, right
+
+
+def hold(kernel, name, args, outs, carried, **options):
+    count = len(args)
+
+    def inner(*refs):
+        kernel(*refs[:count], *refs[count + 1 : count + 1 + len(outs)], *refs[count + 2 + len(outs) :])
+
+    return run(
+        inner,
+        name,
+        (*args, carried),
+        (*outs, shape_of(*carried.shape, dtype=carried.dtype)),
+        spaces={count: pl.ANY, ("out", len(outs)): pl.ANY},
+        aliases={count: len(outs)},
+        **options,
+    )
 
 
 def fill_frame(frame, parts):
@@ -243,11 +261,10 @@
     return copies
 
 
-def load_kernel(center, taps, gain, layer, merge, *refs):
-    *outs, semaphores = refs
-    height = center.shape[0]
-    sources = (center.at[pl.ds(0, 3)], center.at[pl.ds(height - 3, 3)], center, taps, gain, layer, merge)
-    for copy in fetch(sources, outs, semaphores):
+def load_kernel(*refs):
+    *arrays, semaphores = refs
+    count = len(arrays) // 2
+    for copy in fetch(arrays[:count], arrays[count:], semaphores):
         copy.wait()
 
 
@@ -355,7 +372,7 @@
     gain_part[...] = part
 
 
-def weight_kernel(scale, center, top, bottom, left, right, grads, _, out, __, frame):
+def weight_kernel(scale, center, top, bottom, left, right, grads, out, frame):
     fill_frame(frame, (center, top, bottom, left, right))
     weight_sums(frame, grads, scale, out)
 
@@ -649,19 +666,20 @@
         return shape_of(*array.shape, dtype=array.dtype)
 
     edge = shape_of(3, breadth, channels, dtype=BF)
+    rows_input = neighbours(center[:3], center[height - 3 :], "row")
     inputs = (center, kernel_three, gain_three, layer_scale, merge_gain)
-    first, last, *inputs = run(
+    center, taps_three, gain_three, layer_scale, merge_gain = run(
         load_kernel,
         "load",
         inputs,
-        (edge, edge, *map(like, inputs)),
-        scratch=(dma((7,)),),
+        tuple(map(like, inputs)),
+        scratch=(dma((5,)),),
         spaces=dict.fromkeys(range(5), hbm),
+        after=rows_input[:1],
         limit=4,
         us=2,
     )
-    center, taps_three, gain_three, layer_scale, merge_gain = inputs
-    framed = halo(center, neighbours(first, last, "row"), "strips_input")
+    framed = halo(center, rows_input, "strips_input")
     inputs = (
         expand_weight, project_weight, patch_weight, kernel_four, gain_four,
         normed_cotangent[0], residual_cotangent[0],
@@ -718,33 +736,33 @@
         us=3,
     )
     rows_grad = neighbours(first, last, "row")
-    kernel_four_part, early = run(
+    (kernel_four_part,) = run(
         functools.partial(weight_kernel, scale_four),
         "mixer_weights",
-        (*framed_four, grad_four, early),
-        (shape_of(49, wide), like(early)),
+        (*framed_four, grad_four),
+        (shape_of(49, wide),),
         scratch=(frame_scratch(section),),
-        spaces={6: pl.ANY, ("out", 1): pl.ANY},
-        aliases={6: 1},
+        after=rows_grad[:1],
         limit=12,
         us=3,
     )
     framed_grad = halo(grad_four_half, rows_grad, "strips_mixer", after=(kernel_four_part,))
-    early_other = swap(early, "col", 1)
     block_count = col_count // 2
     block = wide // col_count
     blocked = shape_of(block_count, quarter, block, dtype=BF)
-    flat, flat_keep, flat_send = run(
+    flat, flat_keep, flat_send, early = hold(
         section_kernel,
         "section_grad",
         (*framed_grad, taps_four, residual),
         (shape_of(quarter, wide, dtype=BF), blocked, blocked),
+        early,
         scratch=(frame_scratch(section), mixer_image),
         limit=12,
         us=3,
     )
 
     flat_other = swap(flat_send, "col", 1)
+    early_other = swap(early, "col", 1)
     split = shape_of(pixels + 112, half, dtype=BF)
     grad_summed, grad_branch, branch_keep, branch_send = run(
         functools.partial(merge_kernel, scale_three, scale_four),
@@ -847,9 +865,11 @@
     row_bits, col_bits = axis_bits("row"), axis_bits("col")
     outer = len(row_bits)
     low_first = [("row", bit, 0) for bit in row_bits]
-    patch_order = [("col", bit, outer) for bit in col_bits[1:]]
-    patch_order += [("row", bit, 1) for bit in row_bits[1:]] + [("row", 1, 0)]
-    patch_sum = chain(patch_keep, patch_send, patch_order, block_count * row_count, 4 * channels // row_count)
+    patch_order = [("col", bit, outer) for bit in col_bits[1:]] + low_first
+    patch_sum = chain(
+        patch_keep, patch_send, patch_order, block_count * row_count, 4 * channels // row_count,
+        after=(small_keep,),
+    )
     patch_sum = gather(patch_sum, "col", col_bits[1:])
     (patch_grad,) = run(
         finish_patch_kernel,
@@ -859,8 +879,8 @@
         limit=8,
     )
 
-    def share(keep, send, rows, extra=()):
-        total = chain(keep, send, low_first, row_count, rows, extra)
+    def share(keep, send, rows, extra=(), after=()):
+        total = chain(keep, send, low_first, row_count, rows, extra, after)
         for bit in col_bits[1:]:
             total = total + swap(total, "col", bit)
         return total, swap(total, "col", 1)
@@ -878,7 +898,7 @@
     expand_grad, taps_sum, gain_sum = run(
         finish_expand_kernel,
         "finish_expand",
-        share(expand_keep, expand_send, groups * shallow, (small, swap(small, "row", 1))),
+        share(expand_keep, expand_send, groups * shallow, (small, swap(small, "row", 1)), (input_grad,)),
         (shape_of(shallow, hidden_width), shape_of(7, 7, channels), vector),
         scratch=(pltpu.VMEM((64, channels), F32),),
         limit=8,

time: 187 us -> 175 us (0.936)
  waiting for transfers between devices: 64.2 us -> 57.5 us
  starting transfers between devices: 65 us -> 58.6 us
  local copies, waits for them, and re-layouts: 3.92 us -> 5.83 us
    ppermute x22, starting transfers between devices: 31.9 us -> 19.1 us  [swap(): lax.ppermute(values, axis, [(i, i ^ bit) for i in range(lax.axis_size(axi...]
    ppermute x8, starting transfers between devices: 22.5 us -> 28.9 us  [neighbours(): lax.ppermute(last, axis, forward)]
    ppermute x8, waiting for transfers between devices: 21.6 us -> 18 us  [neighbours(): lax.ppermute(first, axis, backward)]
    ppermute x22, waiting for transfers between devices: 39.8 us -> 36.8 us  [swap(): lax.ppermute(values, axis, [(i, i ^ bit) for i in range(lax.axis_size(axi...]
    unnamed x24 -> x26, local copies, waits for them, and re-layouts: 3.92 us -> 4.88 us
  transfers between devices with their start and end apart: 38 -> 38, of which waited for: 18 -> 20; matrix products, arithmetic and copies ran while one was open for 0% -> 0% of each run, Pallas kernels for 16% -> 14%
where the time goes in v2:
time: 175 us; the launch traced here: 174 us
  starting transfers between devices  58.6 us (33%)
  waiting for transfers between devices  57.5 us (33%)
  Pallas kernels  50.9 us (29%)
  local copies, waits for them, and re-layouts  5.83 us (3%)
    pallas_call x26, Pallas kernels, run(): pl.pallas_call(inner, name=name, out_shape=outs, in_specs=[spec(i) for i...  50.9 us
    ppermute x22, waiting for transfers between devices, swap(): lax.ppermute(values, axis, [(i, i ^ bit) for i in range(lax.axis_size(axi...  36.8 us
    ppermute x8, starting transfers between devices, neighbours(): lax.ppermute(last, axis, forward)  28.9 us
    ppermute x22, starting transfers between devices, swap(): lax.ppermute(values, axis, [(i, i ^ bit) for i in range(lax.axis_size(axi...  19.1 us
    ppermute x8, waiting for transfers between devices, neighbours(): lax.ppermute(first, axis, backward)  18 us
    ppermute x8, starting transfers between devices, neighbours(): lax.ppermute(first, axis, backward)  10.6 us
    unnamed x26, local copies, waits for them, and re-layouts  4.88 us
  transfers between devices with their start and end apart: 38, of which 20 were waited for; matrix products, arithmetic and copies ran while one was open for 0% of the time, Pallas kernels for 14%

profile of v2, /device:TPU:0, one launch (start us, length us, event | category | flops | bytes accessed | tf_op | source)
XLA Modules:
  0.0 174.3 jit_solution(14251065110219047502)
XLA Ops:
  0.6 1.0 slice_bitcast_fusion
  1.6 4.8 %collective-permute-start = (bf16[3,32,512]{2,1,0:T(8,128)(2,1)S(1)}, bf16[3,32,512]{2,1,0:T(8,128)(2,1)S(1)}, u32[]{:S(2)}, u32[]{:S(2)}) collective-permute-start(bf16[3,32,512]{2,1,0:T(8,128)(2,1)S(1)} %get-tuple-element.171), channel_id=1, source_target_pairs={{0,4},{4,8},{8,12},{12,16},{16,20},{20,24},{24,28},{1,5},{5,9},{9,... | collective-permute-start | bytes 294920 | tf_op jit(solution)/shard_map/ppermute | solution.py:121
  6.5 1.3 collective-permute-start.1
  7.8 0.9 collective-permute-done.refs_5_.refs_1_
  8.6 0.9 copy-done
  9.6 0.9 copy-done.7
  10.5 0.7 copy-done.9
  11.2 0.7 copy-done.10
  11.9 0.7 copy-done.11
  13.0 1.6 collective-permute-start.2
  14.6 1.4 collective-permute-start.3
  16.0 3.5 %collective-permute-done.3.refs_4_ = bf16[14,8,512]{2,1,0:T(8,128)(2,1)S(1)} collective-permute-done((bf16[14,8,512]{2,1,0:T(8,128)(2,1)S(1)}, bf16[14,8,512]{2,1,0:T(8,128)(2,1)S(1)}, u32[]{:S(2)}, u32[]{:S(2)}) %collective-permute-start.3) | collective-permute-done | bytes 114720 | tf_op jit(solution)/shard_map/ppermute | solution.py:121
  19.6 12.8 %front.1 = (bf16[256,3072]{1,0:T(8,128)(2,1)S(1)}, f32[256,512]{1,0:T(8,128)S(1)}, f32[256,1]{1,0:T(8,128)S(1)}, bf16[256,2048]{1,0:T(8,128)(2,1)S(1)}, f32[256,...) custom-call(bf16[8,32,512]{2,1,0:T(8,128)(2,1)S(1)} %get-tuple-eleme, ...), custom_call_target="tpu_custom_call" | custom-call | flops 13200000000 | bytes 23029760 | tf_op jit(solution)/shard_map/front/pallas_call | solution.py:35
  32.4 4.3 %collective-permute-start.4 = (bf16[3,16,1024]{2,1,0:T(8,128)(2,1)S(1)}, bf16[3,16,1024]{2,1,0:T(8,128)(2,1)S(1)}, u32[]{:S(2)}, u32[]{:S(2)}) collective-permute-start(bf16[3,16,1024]{2,1,0:T(8,128)(2,1)S(1)} %get-tuple-element.97), channel_id=1, source_target_pairs={{0,4},{4,8},{8,12},{12,16},{16,20},{20,24},{24,28},{1,5},{5,9},{9,... | collective-permute-start | bytes 294920 | tf_op jit(solution)/shard_map/ppermute | solution.py:121
  36.7 1.3 collective-permute-start.5
  38.0 0.9 collective-permute-done.4.refs_1_
  38.9 4.6 %collective-permute-done.5.refs_2_ = bf16[3,16,1024]{2,1,0:T(8,128)(2,1)S(1)} collective-permute-done((bf16[3,16,1024]{2,1,0:T(8,128)(2,1)S(1)}, bf16[3,16,1024]{2,1,0:T(8,128)(2,1)S(1)}, u32[]{:S(2)}, u32[]{:S(2)}) %collective-permute-start.5) | collective-permute-done | bytes 98336 | tf_op jit(solution)/shard_map/ppermute | solution.py:121
  43.6 4.2 %collective-permute-start.6 = (bf16[10,8,1024]{2,1,0:T(8,128)(2,1)S(1)}, bf16[10,8,1024]{2,1,0:T(8,128)(2,1)S(1)}, u32[]{:S(2)}, u32[]{:S(2)}) collective-permute-start(bf16[10,8,1024]{2,1,0:T(8,128)(2,1)S(1)} %get-tuple-element.99), channel_id=1, source_target_pairs={{0,1},{1,2},{2,3},{4,5},{5,6},{6,7},{8,9},{9,10},{10,11},{12,13},{... | collective-permute-start | bytes 491528 | tf_op jit(solution)/shard_map/ppermute | solution.py:121
  47.7 1.3 collective-permute-start.7
  49.0 2.5 %collective-permute-done.7.refs_4_ = bf16[10,8,1024]{2,1,0:T(8,128)(2,1)S(1)} collective-permute-done((bf16[10,8,1024]{2,1,0:T(8,128)(2,1)S(1)}, bf16[10,8,1024]{2,1,0:T(8,128)(2,1)S(1)}, u32[]{:S(2)}, u32[]{:S(2)}) %collective-permute-start.7) | collective-permute-done | bytes 163872 | tf_op jit(solution)/shard_map/ppermute | solution.py:121
  51.5 3.3 %mixer.1 = (f32[4,16,1024]{2,1,0:T(8,128)S(1)}, bf16[4,16,1024]{2,1,0:T(8,128)(2,1)S(1)}, bf16[3,16,1024]{2,1,0:T(8,128)(2,1)S(1)}, bf16[3,16,1024]{2,1,0:T(8,128)(2,1)S(1)}, f32[1,1024]{1,0:T(1,128)S(1)}) custom-call(bf16[4,16,1024]{2,1,0:T(8,128)(2,1)S(1)} %get-tuple-element.96.refs_0_, bf16[3,16,1024]{2,1,0:T(8,128)(2,1)S(1)} %collective-permute-done.4.refs_1_, ...), custom_call_target="tpu_custom_call" | custom-call | flops 3300000000 | bytes 1585152 | tf_op jit(solution)/shard_map/mixer/pallas_call | solution.py:35
  54.9 4.8 %collective-permute-start.8 = (bf16[3,16,1024]{2,1,0:T(8,128)(2,1)S(1)}, bf16[3,16,1024]{2,1,0:T(8,128)(2,1)S(1)}, u32[]{:S(2)}, u32[]{:S(2)}) collective-permute-start(bf16[3,16,1024]{2,1,0:T(8,128)(2,1)S(1)} %get-tuple-element.105), channel_id=1, source_target_pairs={{0,4},{4,8},{8,12},{12,16},{16,20},{20,24},{24,28},{1,5},{5,9},{9,... | collective-permute-start | bytes 294920 | tf_op jit(solution)/shard_map/ppermute | solution.py:121
  59.7 1.3 collective-permute-start.9
  61.0 0.9 collective-permute-done.8.refs_6_.refs_1_
  61.9 2.9 %mixer_weights.1.refs_3_.refs_7_ = f32[49,1024]{1,0:T(8,128)S(1)} custom-call(bf16[4,16,1024]{2,1,0:T(8,128)(2,1)S(1)} %get-tuple-element.96.refs_0_, bf16[3,16,1024]{2,1,0:T(8,128)(2,1)S(1)} %collective-permute-done.4.refs_1_, bf16[3,16,1024]{2,1,0:T(8,128)(2,1)S(1)} %collective-permute-done.5.refs_2_, ...), custom_call_target="tpu_custom_call" | custom-call | flops 3300000000 | bytes 1118208 | tf_op jit(solution)/shard_map/mixer_weights/pallas_call | solution.py:35
  64.8 1.4 collective-permute-done.9.refs_2_
  66.2 4.5 %collective-permute-start.10 = (bf16[10,8,1024]{2,1,0:T(8,128)(2,1)S(1)}, bf16[10,8,1024]{2,1,0:T(8,128)(2,1)S(1)}, u32[]{:S(2)}, u32[]{:S(2)}) collective-permute-start(bf16[10,8,1024]{2,1,0:T(8,128)(2,1)S(1)} %get-tuple-element.108), channel_id=1, source_target_pairs={{0,1},{1,2},{2,3},{4,5},{5,6},{6,7},{8,9},{9,10},{10,11},{12,13},{... | collective-permute-start | bytes 491528 | tf_op jit(solution)/shard_map/ppermute | solution.py:121
  70.7 1.3 collective-permute-start.11
  72.0 2.6 %collective-permute-done.11.refs_4_ = bf16[10,8,1024]{2,1,0:T(8,128)(2,1)S(1)} collective-permute-done((bf16[10,8,1024]{2,1,0:T(8,128)(2,1)S(1)}, bf16[10,8,1024]{2,1,0:T(8,128)(2,1)S(1)}, u32[]{:S(2)}, u32[]{:S(2)}) %collective-permute-start.11) | collective-permute-done | bytes 163872 | tf_op jit(solution)/shard_map/ppermute | solution.py:121
  74.6 3.1 %section_grad.1 = (bf16[64,1024]{1,0:T(8,128)(2,1)S(1)}, bf16[2,64,256]{2,1,0:T(8,128)(2,1)S(1)}, bf16[2,64,256]{2,1,0:T(8,128)(2,1)S(1)}, bf16[256,3072]{1,0:T(8,128)(2,1)S(1)}) custom-call(bf16[4,16,1024]{2,1,0:T(8,128)(2,1)S(1)} %get-tuple-element.104.refs_0_, ...), custom_call_target="tpu_custom_call", output_to_operand_aliasing={{3}: (7, {})} | custom-call | flops 3300000000 | bytes 4395008 | tf_op jit(solution)/shard_map/section_grad/pallas_call | solution.py:35
  77.7 3.9 %collective-permute-start.12 = (bf16[256,3072]{1,0:T(8,128)(2,1)S(1)}, bf16[256,3072]{1,0:T(8,128)(2,1)S(1)}, u32[]{:S(2)}, u32[]{:S(2)}) collective-permute-start(bf16[256,3072]{1,0:T(8,128)(2,1)S(1)} %get-tuple-element.124.refs_0_), channel_id=1, source_target_pairs={{0,1},{1,0},{2,3},{3,2},{4,5},{5,4},{6,7},{7,6},{8,9},{9,8},{10,11... | collective-permute-start | bytes 4718600 | tf_op jit(solution)/shard_map/ppermute | solution.py:49
  81.7 2.5 %merge_back.1 = (f32[256,512]{1,0:T(8,128)S(1)}, bf16[256,512]{1,0:T(8,128)(2,1)S(1)}, bf16[368,256]{1,0:T(8,128)(2,1)S(1)}, bf16[368,256]{1,0:T(8,128)(2,1)S(1)}) custom-call(bf16[64,1024]{1,0:T(8,128)(2,1)S(1)} %get-tuple-element.112.refs_0_, bf16[2048,1024]{1,0:T(8,128)(2,1)S(1)} %get-tuple-element.113.refs_1_, ...), custom_call_target="tpu_custom_call" | custom-call | flops 3300000000 | bytes 6747136 | tf_op jit(solution)/shard_map/merge_back/pallas_call | solution.py:35
  84.8 2.6 %patch_product.1 = (bf16[2048,256]{1,0:T(8,128)(2,1)S(1)}, bf16[2048,256]{1,0:T(8,128)(2,1)S(1)}) custom-call(bf16[256,3072]{1,0:T(8,128)(2,1)S(1)} %get-tuple-element.124.refs_0_, bf16[256,3072]{1,0:T(8,128)(2,1)S(1)} %collective-permute-done.12.refs_1_, bf16[2,64,256]{2,1,0:T(8,128)(2,1)S(1)} %get-tuple-element.127.refs_2_, ...), custom_call_target="tpu_custom_call" | custom-call | flops 3300000000 | bytes 5373952 | tf_op jit(solution)/shard_map/patch_product/pallas_call | solution.py:35
  87.4 2.6 %project_product.1 = (bf16[1136,256]{1,0:T(8,128)(2,1)S(1)}, bf16[1136,256]{1,0:T(8,128)(2,1)S(1)}) custom-call(bf16[256,3072]{1,0:T(8,128)(2,1)S(1)} %get-tuple-element.124.refs_0_, bf16[256,3072]{1,0:T(8,128)(2,1)S(1)} %collective-permute-done.12.refs_1_, bf16[368,256]{1,0:T(8,128)(2,1)S(1)} %get-tuple-element.125.refs_2_, ...), custom_call_target="tpu_custom_call" | custom-call | flops 3300000000 | bytes 4685824 | tf_op jit(solution)/shard_map/project_product/pallas_call | solution.py:35
  90.0 3.2 %mlp_back.1 = (bf16[256,1024]{1,0:T(8,128)(2,1)S(1)}, bf16[256,1024]{1,0:T(8,128)(2,1)S(1)}, bf16[8,32,512]{2,1,0:T(8,128)(2,1)S(1)}, bf16[3,32,512]{2,1,0:T(8,1...) custom-call(bf16[256,512]{1,0:T(8,128)(2,1)S(1)} %get-tuple-element.118.refs_0_, ...), custom_call_target="tpu_custom_call" | custom-call | flops 4400000000 | bytes 7541760 | tf_op jit(solution)/shard_map/mlp_back/pallas_call | solution.py:35
  93.2 2.9 %collective-permute-start.15 = (bf16[3,32,512]{2,1,0:T(8,128)(2,1)S(1)}, bf16[3,32,512]{2,1,0:T(8,128)(2,1)S(1)}, u32[]{:S(2)}, u32[]{:S(2)}) collective-permute-start(bf16[3,32,512]{2,1,0:T(8,128)(2,1)S(1)} %get-tuple-element.132), channel_id=1, source_target_pairs={{0,4},{4,8},{8,12},{12,16},{16,20},{20,24},{24,28},{1,5},{5,9},{9,... | collective-permute-start | bytes 294920 | tf_op jit(solution)/shard_map/ppermute | solution.py:121
  96.2 1.5 collective-permute-start.16
  97.7 2.7 %collective-permute-start.27 = (bf16[1136,256]{1,0:T(8,128)(2,1)S(1)}, bf16[1136,256]{1,0:T(8,128)(2,1)S(1)}, u32[]{:S(2)}, u32[]{:S(2)}) collective-permute-start(bf16[1136,256]{1,0:T(8,128)(2,1)S(1)} %get-tuple-element.130.refs_7_), channel_id=1, source_target_pairs={{0,4},{4,0},{8,12},{12,8},{16,20},{20,16},{24,28},{28,24},{1,5},{5... | collective-permute-start | bytes 1744904 | tf_op jit(solution)/shard_map/ppermute | solution.py:49
  100.5 3.2 %collective-permute-done.16.refs_2_.refs_8_ = bf16[3,32,512]{2,1,0:T(8,128)(2,1)S(1)} collective-permute-done((bf16[3,32,512]{2,1,0:T(8,128)(2,1)S(1)}, bf16[3,32,512]{2,1,0:T(8,128)(2,1)S(1)}, u32[]{:S(2)}, u32[]{:S(2)}) %collective-permute-start.16) | collective-permute-done | bytes 98336 | tf_op jit(solution)/shard_map/ppermute | solution.py:121
  103.7 5.4 %block_weights.1 = (bf16[64,256]{1,0:T(8,128)(2,1)S(1)}, bf16[64,256]{1,0:T(8,128)(2,1)S(1)}) custom-call(bf16[8,32,512]{2,1,0:T(8,128)(2,1)S(1)} %get-tuple-element.89.refs_0_, bf16[3,32,512]{2,1,0:T(8,128)(2,1)S(1)} %collective-permute-done.refs_5_.refs_1_, bf16[3,32,512]{2,1,0:T(8,128)(2,1)S(1)} %collective-permute-done.1.refs_2_, ...), custom_call_target="tpu_custom_call" | custom-call | flops 5500000256 | bytes 1017856 | tf_op jit(solution)/shard_map/block_weights/pallas_call | solution.py:35
  109.1 1.2 collective-permute-done.21
  110.4 2.2 %collective-permute-start.22 = (bf16[64,256]{1,0:T(8,128)(2,1)S(1)}, bf16[64,256]{1,0:T(8,128)(2,1)S(1)}, u32[]{:S(2)}, u32[]{:S(2)}) collective-permute-start(bf16[64,256]{1,0:T(8,128)(2,1)S(1)} %add.23.refs_2_), channel_id=1, source_target_pairs={{0,4},{4,0},{8,12},{12,8},{16,20},{20,16},{24,28},{28,24},{1,5},{5... | collective-permute-start | bytes 98312 | tf_op jit(solution)/shard_map/ppermute | solution.py:49
  112.5 1.9 %expand_product.1 = (bf16[1024,256]{1,0:T(8,128)(2,1)S(1)}, bf16[1024,256]{1,0:T(8,128)(2,1)S(1)}) custom-call(bf16[256,3072]{1,0:T(8,128)(2,1)S(1)} %get-tuple-element.124.refs_0_, bf16[256,3072]{1,0:T(8,128)(2,1)S(1)} %collective-permute-done.12.refs_1_, bf16[256,1024]{1,0:T(8,128)(2,1)S(1)} %get-tuple-element.134.refs_2_, ...), custom_call_target="tpu_custom_call" | custom-call | flops 3300000000 | bytes 5242880 | tf_op jit(solution)/shard_map/expand_product/pallas_call | solution.py:35
  114.5 1.8 %collective-permute-start.18 = (bf16[14,8,512]{2,1,0:T(8,128)(2,1)S(1)}, bf16[14,8,512]{2,1,0:T(8,128)(2,1)S(1)}, u32[]{:S(2)}, u32[]{:S(2)}) collective-permute-start(bf16[14,8,512]{2,1,0:T(8,128)(2,1)S(1)} %get-tuple-element.137), channel_id=1, source_target_pairs={{0,1},{1,2},{2,3},{4,5},{5,6},{6,7},{8,9},{9,10},{10,11},{12,13},{... | collective-permute-start | bytes 344072 | tf_op jit(solution)/shard_map/ppermute | solution.py:121
  116.3 1.3 collective-permute-start.19
  117.8 7.4 %collective-permute-done.32.refs_1_ = bf16[2048,256]{1,0:T(8,128)(2,1)S(1)} collective-permute-done((bf16[2048,256]{1,0:T(8,128)(2,1)S(1)}, bf16[2048,256]{1,0:T(8,128)(2,1)S(1)}, u32[]{:S(2)}, u32[]{:S(2)}) %collective-permute-start.32) | collective-permute-done | bytes 1048608 | tf_op jit(solution)/shard_map/ppermute | solution.py:49
  125.2 1.6 collective-permute-start.28
  127.0 1.7 collective-permute-start.33
  128.7 6.6 %input_grad.1.refs_4_ = bf16[8,32,512]{2,1,0:T(8,128)(2,1)} custom-call(bf16[8,32,512]{2,1,0:T(8,128)(2,1)S(1)} %get-tuple-element.131.refs_0_.refs_5_, bf16[3,32,512]{2,1,0:T(8,128)(2,1)S(1)} %collective-permute-done.15.refs_1_.refs_7_, bf16[3,32,512]{2,1,0:T(8,128)(2,1)S(1)} %collective-permute-done.16.refs_2_.refs_8_, ...), custom_call_target="tpu_custom_call" | custom-call | flops 5500000256 | bytes 1574912 | tf_op jit(solution)/shard_map/input_grad/pallas_call | solution.py:35
  135.3 0.9 copy-done.12
  136.5 3.0 %collective-permute-done.33.refs_1_ = bf16[1024,256]{1,0:T(8,128)(2,1)S(1)} collective-permute-done((bf16[1024,256]{1,0:T(8,128)(2,1)S(1)}, bf16[1024,256]{1,0:T(8,128)(2,1)S(1)}, u32[]{:S(2)}, u32[]{:S(2)}) %collective-permute-start.33) | collective-permute-done | bytes 524320 | tf_op jit(solution)/shard_map/ppermute | solution.py:49
  139.6 1.6 collective-permute-start.34
  141.3 1.5 collective-permute-start.29
  142.8 9.1 %collective-permute-done.23.refs_1_ = bf16[576,256]{1,0:T(8,128)(2,1)S(1)} collective-permute-done((bf16[576,256]{1,0:T(8,128)(2,1)S(1)}, bf16[576,256]{1,0:T(8,128)(2,1)S(1)}, u32[]{:S(2)}, u32[]{:S(2)}) %collective-permute-start.23) | collective-permute-done | bytes 294944 | tf_op jit(solution)/shard_map/ppermute | solution.py:49
  152.0 0.7 collective-permute-start.24
  152.7 2.1 %collective-permute-done.34.refs_1_ = bf16[512,256]{1,0:T(8,128)(2,1)S(1)} collective-permute-done((bf16[512,256]{1,0:T(8,128)(2,1)S(1)}, bf16[512,256]{1,0:T(8,128)(2,1)S(1)}, u32[]{:S(2)}, u32[]{:S(2)}) %collective-permute-start.34) | collective-permute-done | bytes 262176 | tf_op jit(solution)/shard_map/ppermute | solution.py:49
  156.1 8.3 %collective-permute-done.24 = bf16[320,256]{1,0:T(8,128)(2,1)S(1)} collective-permute-done((bf16[320,256]{1,0:T(8,128)(2,1)S(1)}, bf16[320,256]{1,0:T(8,128)(2,1)S(1)}, u32[]{:S(2)}, u32[]{:S(2)}) %collective-permute-start.24) | collective-permute-done | bytes 163872 | tf_op jit(solution)/shard_map/ppermute | solution.py:49
  164.4 1.3 collective-permute-done.35
  165.7 0.8 collective-permute-start.36
  166.7 3.2 %collective-permute-done.25 = bf16[320,256]{1,0:T(8,128)(2,1)S(1)} collective-permute-done((bf16[320,256]{1,0:T(8,128)(2,1)S(1)}, bf16[320,256]{1,0:T(8,128)(2,1)S(1)}, u32[]{:S(2)}, u32[]{:S(2)}) %collective-permute-start.25) | collective-permute-done | bytes 163872 | tf_op jit(solution)/shard_map/ppermute | solution.py:49
  170.0 1.3 collective-permute-done.36
  171.4 1.0 finish_project.1
  172.4 0.9 finish_expand.1
  173.3 1.0 finish_patch.1
  (73 shorter events, 4.1 us)
Async XLA Ops:
  1.6 7.0 %collective-permute-start = (bf16[3,32,512]{2,1,0:T(8,128)(2,1)S(1)}, bf16[3,32,512]{2,1,0:T(8,128)(2,1)S(1)}, u32[]{:S(2)}, u32[]{:S(2)}) collective-permute-start(bf16[3,32,512]{2,1,0:T(8,128)(2,1)S(1)} %get-tuple-element.171), channel_id=1, source_target_pairs={{0,4},{4,8},{8,12},{12,16},{16,20},{20,24},{24,28},{1,5},{5,9},{9,... | collective-permute-start | bytes 294920 | tf_op jit(solution)/shard_map/ppermute | solution.py:121
  6.5 6.5 %collective-permute-start.1 = (bf16[3,32,512]{2,1,0:T(8,128)(2,1)S(1)}, bf16[3,32,512]{2,1,0:T(8,128)(2,1)S(1)}, u32[]{:S(2)}, u32[]{:S(2)}) collective-permute-start(bf16[3,32,512]{2,1,0:T(8,128)(2,1)S(1)} %get-tuple-element.170), channel_id=1, source_target_pairs={{4,0},{8,4},{12,8},{16,12},{20,16},{24,20},{28,24},{5,1},{9,5},{13... | collective-permute-start | bytes 294920 | tf_op jit(solution)/shard_map/ppermute | solution.py:121
  8.6 0.9 copy-start
  9.6 0.9 copy-start.7
  10.5 0.7 copy-start.9
  11.2 0.7 copy-start.10
  11.9 0.7 copy-start.11
  12.5 7.0 %copy-start.1 = (bf16[2048,1024]{1,0:T(8,128)(2,1)S(1)}, bf16[2048,1024]{1,0:T(8,128)(2,1)}, u32[]{:S(2)}) copy-start(bf16[2048,1024]{1,0:T(8,128)(2,1)} %refs_11_.1) | copy-start | bytes 12582916
  12.5 7.0 %copy-start.3 = (bf16[2048,512]{1,0:T(8,128)(2,1)S(1)}, bf16[2048,512]{1,0:T(8,128)(2,1)}, u32[]{:S(2)}) copy-start(bf16[2048,512]{1,0:T(8,128)(2,1)} %refs_10_.1) | copy-start | bytes 6291460
  12.8 6.8 %copy-start.2 = (bf16[512,2048]{1,0:T(8,128)(2,1)S(1)}, bf16[512,2048]{1,0:T(8,128)(2,1)}, u32[]{:S(2)}) copy-start(bf16[512,2048]{1,0:T(8,128)(2,1)} %refs_9_.1) | copy-start | bytes 6291460
  12.8 6.8 %copy-start.4 = (f32[7,7,1024]{2,1,0:T(8,128)S(1)}, f32[7,7,1024]{2,1,0:T(8,128)}, u32[]{:S(2)}) copy-start(f32[7,7,1024]{2,1,0:T(8,128)} %refs_12_.1) | copy-start | bytes 602116
  12.8 6.7 %copy-start.5 = (bf16[1,4,16,1024]{3,2,1,0:T(8,128)(2,1)S(1)}, bf16[1,4,16,1024]{3,2,1,0:T(8,128)(2,1)}, u32[]{:S(2)}) copy-start(bf16[1,4,16,1024]{3,2,1,0:T(8,128)(2,1)} %param.22) | copy-start | bytes 393220
  12.8 6.7 %copy-start.6 = (bf16[1,4,16,1024]{3,2,1,0:T(8,128)(2,1)S(1)}, bf16[1,4,16,1024]{3,2,1,0:T(8,128)(2,1)}, u32[]{:S(2)}) copy-start(bf16[1,4,16,1024]{3,2,1,0:T(8,128)(2,1)} %param.23) | copy-start | bytes 393220
  12.8 6.7 %copy-start.8 = (f32[1024]{0:T(1024)S(1)}, f32[1024]{0:T(1024)}, u32[]{:S(2)}) copy-start(f32[1024]{0:T(1024)} %param.21) | copy-start | bytes 12292
  13.0 3.0 %collective-permute-start.2 = (bf16[14,8,512]{2,1,0:T(8,128)(2,1)S(1)}, bf16[14,8,512]{2,1,0:T(8,128)(2,1)S(1)}, u32[]{:S(2)}, u32[]{:S(2)}) collective-permute-start(bf16[14,8,512]{2,1,0:T(8,128)(2,1)S(1)} %get-tuple-element.90), channel_id=1, source_target_pairs={{0,1},{1,2},{2,3},{4,5},{5,6},{6,7},{8,9},{9,10},{10,11},{12,13},{... | collective-permute-start | bytes 344072 | tf_op jit(solution)/shard_map/ppermute | solution.py:121
  14.6 5.0 %collective-permute-start.3 = (bf16[14,8,512]{2,1,0:T(8,128)(2,1)S(1)}, bf16[14,8,512]{2,1,0:T(8,128)(2,1)S(1)}, u32[]{:S(2)}, u32[]{:S(2)}) collective-permute-start(bf16[14,8,512]{2,1,0:T(8,128)(2,1)S(1)} %get-tuple-element.91), channel_id=1, source_target_pairs={{1,0},{2,1},{3,2},{5,4},{6,5},{7,6},{9,8},{10,9},{11,10},{13,12},{... | collective-permute-start | bytes 344072 | tf_op jit(solution)/shard_map/ppermute | solution.py:121
  32.4 6.5 %collective-permute-start.4 = (bf16[3,16,1024]{2,1,0:T(8,128)(2,1)S(1)}, bf16[3,16,1024]{2,1,0:T(8,128)(2,1)S(1)}, u32[]{:S(2)}, u32[]{:S(2)}) collective-permute-start(bf16[3,16,1024]{2,1,0:T(8,128)(2,1)S(1)} %get-tuple-element.97), channel_id=1, source_target_pairs={{0,4},{4,8},{8,12},{12,16},{16,20},{20,24},{24,28},{1,5},{5,9},{9,... | collective-permute-start | bytes 294920 | tf_op jit(solution)/shard_map/ppermute | solution.py:121
  36.7 6.8 %collective-permute-start.5 = (bf16[3,16,1024]{2,1,0:T(8,128)(2,1)S(1)}, bf16[3,16,1024]{2,1,0:T(8,128)(2,1)S(1)}, u32[]{:S(2)}, u32[]{:S(2)}) collective-permute-start(bf16[3,16,1024]{2,1,0:T(8,128)(2,1)S(1)} %get-tuple-element.98), channel_id=1, source_target_pairs={{4,0},{8,4},{12,8},{16,12},{20,16},{24,20},{28,24},{5,1},{9,5},{13... | collective-permute-start | bytes 294920 | tf_op jit(solution)/shard_map/ppermute | solution.py:121
  43.6 5.5 %collective-permute-start.6 = (bf16[10,8,1024]{2,1,0:T(8,128)(2,1)S(1)}, bf16[10,8,1024]{2,1,0:T(8,128)(2,1)S(1)}, u32[]{:S(2)}, u32[]{:S(2)}) collective-permute-start(bf16[10,8,1024]{2,1,0:T(8,128)(2,1)S(1)} %get-tuple-element.99), channel_id=1, source_target_pairs={{0,1},{1,2},{2,3},{4,5},{5,6},{6,7},{8,9},{9,10},{10,11},{12,13},{... | collective-permute-start | bytes 491528 | tf_op jit(solution)/shard_map/ppermute | solution.py:121
  47.7 3.8 %collective-permute-start.7 = (bf16[10,8,1024]{2,1,0:T(8,128)(2,1)S(1)}, bf16[10,8,1024]{2,1,0:T(8,128)(2,1)S(1)}, u32[]{:S(2)}, u32[]{:S(2)}) collective-permute-start(bf16[10,8,1024]{2,1,0:T(8,128)(2,1)S(1)} %get-tuple-element.100), channel_id=1, source_target_pairs={{1,0},{2,1},{3,2},{5,4},{6,5},{7,6},{9,8},{10,9},{11,10},{13,12},{... | collective-permute-start | bytes 491528 | tf_op jit(solution)/shard_map/ppermute | solution.py:121
  54.9 7.0 %collective-permute-start.8 = (bf16[3,16,1024]{2,1,0:T(8,128)(2,1)S(1)}, bf16[3,16,1024]{2,1,0:T(8,128)(2,1)S(1)}, u32[]{:S(2)}, u32[]{:S(2)}) collective-permute-start(bf16[3,16,1024]{2,1,0:T(8,128)(2,1)S(1)} %get-tuple-element.105), channel_id=1, source_target_pairs={{0,4},{4,8},{8,12},{12,16},{16,20},{20,24},{24,28},{1,5},{5,9},{9,... | collective-permute-start | bytes 294920 | tf_op jit(solution)/shard_map/ppermute | solution.py:121
  59.7 6.5 %collective-permute-start.9 = (bf16[3,16,1024]{2,1,0:T(8,128)(2,1)S(1)}, bf16[3,16,1024]{2,1,0:T(8,128)(2,1)S(1)}, u32[]{:S(2)}, u32[]{:S(2)}) collective-permute-start(bf16[3,16,1024]{2,1,0:T(8,128)(2,1)S(1)} %get-tuple-element.106), channel_id=1, source_target_pairs={{4,0},{8,4},{12,8},{16,12},{20,16},{24,20},{28,24},{5,1},{9,5},{13... | collective-permute-start | bytes 294920 | tf_op jit(solution)/shard_map/ppermute | solution.py:121
  66.2 5.8 %collective-permute-start.10 = (bf16[10,8,1024]{2,1,0:T(8,128)(2,1)S(1)}, bf16[10,8,1024]{2,1,0:T(8,128)(2,1)S(1)}, u32[]{:S(2)}, u32[]{:S(2)}) collective-permute-start(bf16[10,8,1024]{2,1,0:T(8,128)(2,1)S(1)} %get-tuple-element.108), channel_id=1, source_target_pairs={{0,1},{1,2},{2,3},{4,5},{5,6},{6,7},{8,9},{9,10},{10,11},{12,13},{... | collective-permute-start | bytes 491528 | tf_op jit(solution)/shard_map/ppermute | solution.py:121
  70.7 3.9 %collective-permute-start.11 = (bf16[10,8,1024]{2,1,0:T(8,128)(2,1)S(1)}, bf16[10,8,1024]{2,1,0:T(8,128)(2,1)S(1)}, u32[]{:S(2)}, u32[]{:S(2)}) collective-permute-start(bf16[10,8,1024]{2,1,0:T(8,128)(2,1)S(1)} %get-tuple-element.109), channel_id=1, source_target_pairs={{1,0},{2,1},{3,2},{5,4},{6,5},{7,6},{9,8},{10,9},{11,10},{13,12},{... | collective-permute-start | bytes 491528 | tf_op jit(solution)/shard_map/ppermute | solution.py:121
  77.7 7.0 %collective-permute-start.12 = (bf16[256,3072]{1,0:T(8,128)(2,1)S(1)}, bf16[256,3072]{1,0:T(8,128)(2,1)S(1)}, u32[]{:S(2)}, u32[]{:S(2)}) collective-permute-start(bf16[256,3072]{1,0:T(8,128)(2,1)S(1)} %get-tuple-element.124.refs_0_), channel_id=1, source_target_pairs={{0,1},{1,0},{2,3},{3,2},{4,5},{5,4},{6,7},{7,6},{8,9},{9,8},{10,11... | collective-permute-start | bytes 4718600 | tf_op jit(solution)/shard_map/ppermute | solution.py:49
  81.7 3.1 %collective-permute-start.14 = (bf16[2,64,256]{2,1,0:T(8,128)(2,1)S(1)}, bf16[2,64,256]{2,1,0:T(8,128)(2,1)S(1)}, u32[]{:S(2)}, u32[]{:S(2)}) collective-permute-start(bf16[2,64,256]{2,1,0:T(8,128)(2,1)S(1)} %get-tuple-element.128), channel_id=1, source_target_pairs={{0,1},{1,0},{2,3},{3,2},{4,5},{5,4},{6,7},{7,6},{8,9},{9,8},{10,11... | collective-permute-start | bytes 196616 | tf_op jit(solution)/shard_map/ppermute | solution.py:49
  84.2 3.2 %collective-permute-start.13 = (bf16[368,256]{1,0:T(8,128)(2,1)S(1)}, bf16[368,256]{1,0:T(8,128)(2,1)S(1)}, u32[]{:S(2)}, u32[]{:S(2)}) collective-permute-start(bf16[368,256]{1,0:T(8,128)(2,1)S(1)} %get-tuple-element.126), channel_id=1, source_target_pairs={{0,1},{1,0},{2,3},{3,2},{4,5},{5,4},{6,7},{7,6},{8,9},{9,8},{10,11... | collective-permute-start | bytes 565256 | tf_op jit(solution)/shard_map/ppermute | solution.py:49
  93.2 7.3 %collective-permute-start.15 = (bf16[3,32,512]{2,1,0:T(8,128)(2,1)S(1)}, bf16[3,32,512]{2,1,0:T(8,128)(2,1)S(1)}, u32[]{:S(2)}, u32[]{:S(2)}) collective-permute-start(bf16[3,32,512]{2,1,0:T(8,128)(2,1)S(1)} %get-tuple-element.132), channel_id=1, source_target_pairs={{0,4},{4,8},{8,12},{12,16},{16,20},{20,24},{24,28},{1,5},{5,9},{9,... | collective-permute-start | bytes 294920 | tf_op jit(solution)/shard_map/ppermute | solution.py:121
  96.2 7.5 %collective-permute-start.16 = (bf16[3,32,512]{2,1,0:T(8,128)(2,1)S(1)}, bf16[3,32,512]{2,1,0:T(8,128)(2,1)S(1)}, u32[]{:S(2)}, u32[]{:S(2)}) collective-permute-start(bf16[3,32,512]{2,1,0:T(8,128)(2,1)S(1)} %get-tuple-element.133), channel_id=1, source_target_pairs={{4,0},{8,4},{12,8},{16,12},{20,16},{24,20},{28,24},{5,1},{9,5},{13... | collective-permute-start | bytes 294920 | tf_op jit(solution)/shard_map/ppermute | solution.py:121
  97.7 18.7 %collective-permute-start.27 = (bf16[1136,256]{1,0:T(8,128)(2,1)S(1)}, bf16[1136,256]{1,0:T(8,128)(2,1)S(1)}, u32[]{:S(2)}, u32[]{:S(2)}) collective-permute-start(bf16[1136,256]{1,0:T(8,128)(2,1)S(1)} %get-tuple-element.130.refs_7_), channel_id=1, source_target_pairs={{0,4},{4,0},{8,12},{12,8},{16,20},{20,16},{24,28},{28,24},{1,5},{5... | collective-permute-start | bytes 1744904 | tf_op jit(solution)/shard_map/ppermute | solution.py:49
  100.4 24.8 %collective-permute-start.32 = (bf16[2048,256]{1,0:T(8,128)(2,1)S(1)}, bf16[2048,256]{1,0:T(8,128)(2,1)S(1)}, u32[]{:S(2)}, u32[]{:S(2)}) collective-permute-start(bf16[2048,256]{1,0:T(8,128)(2,1)S(1)} %get-tuple-element.129.refs_4_), channel_id=1, source_target_pairs={{0,2},{1,3},{2,0},{3,1},{4,6},{5,7},{6,4},{7,5},{8,10},{9,11},{10,... | collective-permute-start | bytes 3145736 | tf_op jit(solution)/shard_map/ppermute | solution.py:49
  100.5 12.1 %collective-permute-start.17 = (bf16[256,1024]{1,0:T(8,128)(2,1)S(1)}, bf16[256,1024]{1,0:T(8,128)(2,1)S(1)}, u32[]{:S(2)}, u32[]{:S(2)}) collective-permute-start(bf16[256,1024]{1,0:T(8,128)(2,1)S(1)} %get-tuple-element.135), channel_id=1, source_target_pairs={{0,1},{1,0},{2,3},{3,2},{4,5},{5,4},{6,7},{7,6},{8,9},{9,8},{10,11... | collective-permute-start | bytes 1572872 | tf_op jit(solution)/shard_map/ppermute | solution.py:49
  109.1 1.3 collective-permute-start.21
  110.4 25.0 %collective-permute-start.22 = (bf16[64,256]{1,0:T(8,128)(2,1)S(1)}, bf16[64,256]{1,0:T(8,128)(2,1)S(1)}, u32[]{:S(2)}, u32[]{:S(2)}) collective-permute-start(bf16[64,256]{1,0:T(8,128)(2,1)S(1)} %add.23.refs_2_), channel_id=1, source_target_pairs={{0,4},{4,0},{8,12},{12,8},{16,20},{20,16},{24,28},{28,24},{1,5},{5... | collective-permute-start | bytes 98312 | tf_op jit(solution)/shard_map/ppermute | solution.py:49
  114.4 20.9 %collective-permute-start.20 = (bf16[1024,256]{1,0:T(8,128)(2,1)S(1)}, bf16[1024,256]{1,0:T(8,128)(2,1)S(1)}, u32[]{:S(2)}, u32[]{:S(2)}) collective-permute-start(bf16[1024,256]{1,0:T(8,128)(2,1)S(1)} %get-tuple-element.136.refs_3_), channel_id=1, source_target_pairs={{0,4},{4,0},{8,12},{12,8},{16,20},{20,16},{24,28},{28,24},{1,5},{5... | collective-permute-start | bytes 1572872 | tf_op jit(solution)/shard_map/ppermute | solution.py:49
  114.5 12.5 %collective-permute-start.18 = (bf16[14,8,512]{2,1,0:T(8,128)(2,1)S(1)}, bf16[14,8,512]{2,1,0:T(8,128)(2,1)S(1)}, u32[]{:S(2)}, u32[]{:S(2)}) collective-permute-start(bf16[14,8,512]{2,1,0:T(8,128)(2,1)S(1)} %get-tuple-element.137), channel_id=1, source_target_pairs={{0,1},{1,2},{2,3},{4,5},{5,6},{6,7},{8,9},{9,10},{10,11},{12,13},{... | collective-permute-start | bytes 344072 | tf_op jit(solution)/shard_map/ppermute | solution.py:121
  116.3 12.4 %collective-permute-start.19 = (bf16[14,8,512]{2,1,0:T(8,128)(2,1)S(1)}, bf16[14,8,512]{2,1,0:T(8,128)(2,1)S(1)}, u32[]{:S(2)}, u32[]{:S(2)}) collective-permute-start(bf16[14,8,512]{2,1,0:T(8,128)(2,1)S(1)} %get-tuple-element.138), channel_id=1, source_target_pairs={{1,0},{2,1},{3,2},{5,4},{6,5},{7,6},{9,8},{10,9},{11,10},{13,12},{... | collective-permute-start | bytes 344072 | tf_op jit(solution)/shard_map/ppermute | solution.py:121
  125.2 16.0 %collective-permute-start.28 = (bf16[624,256]{1,0:T(8,128)(2,1)S(1)}, bf16[624,256]{1,0:T(8,128)(2,1)S(1)}, u32[]{:S(2)}, u32[]{:S(2)}) collective-permute-start(bf16[624,256]{1,0:T(8,128)(2,1)S(1)} %get-tuple-element.153), channel_id=1, source_target_pairs={{0,8},{4,12},{8,0},{12,4},{16,24},{20,28},{24,16},{28,20},{1,9},{5... | collective-permute-start | bytes 958472 | tf_op jit(solution)/shard_map/ppermute | solution.py:49
  127.0 12.5 %collective-permute-start.33 = (bf16[1024,256]{1,0:T(8,128)(2,1)S(1)}, bf16[1024,256]{1,0:T(8,128)(2,1)S(1)}, u32[]{:S(2)}, u32[]{:S(2)}) collective-permute-start(bf16[1024,256]{1,0:T(8,128)(2,1)S(1)} %get-tuple-element.161), channel_id=1, source_target_pairs={{0,4},{4,0},{8,12},{12,8},{16,20},{20,16},{24,28},{28,24},{1,5},{5... | collective-permute-start | bytes 1572872 | tf_op jit(solution)/shard_map/ppermute | solution.py:49
  135.3 1.0 copy-start.12
  136.4 15.5 %collective-permute-start.23 = (bf16[576,256]{1,0:T(8,128)(2,1)S(1)}, bf16[576,256]{1,0:T(8,128)(2,1)S(1)}, u32[]{:S(2)}, u32[]{:S(2)}) collective-permute-start(bf16[576,256]{1,0:T(8,128)(2,1)S(1)} %get-tuple-element.145), channel_id=1, source_target_pairs={{0,8},{4,12},{8,0},{12,4},{16,24},{20,28},{24,16},{28,20},{1,9},{5... | collective-permute-start | bytes 884744 | tf_op jit(solution)/shard_map/ppermute | solution.py:49
  139.6 15.2 %collective-permute-start.34 = (bf16[512,256]{1,0:T(8,128)(2,1)S(1)}, bf16[512,256]{1,0:T(8,128)(2,1)S(1)}, u32[]{:S(2)}, u32[]{:S(2)}) collective-permute-start(bf16[512,256]{1,0:T(8,128)(2,1)S(1)} %get-tuple-element.163), channel_id=1, source_target_pairs={{0,8},{4,12},{8,0},{12,4},{16,24},{20,28},{24,16},{28,20},{1,9},{5... | collective-permute-start | bytes 786440 | tf_op jit(solution)/shard_map/ppermute | solution.py:49
  141.3 14.2 %collective-permute-start.29 = (bf16[368,256]{1,0:T(8,128)(2,1)S(1)}, bf16[368,256]{1,0:T(8,128)(2,1)S(1)}, u32[]{:S(2)}, u32[]{:S(2)}) collective-permute-start(bf16[368,256]{1,0:T(8,128)(2,1)S(1)} %get-tuple-element.155), channel_id=1, source_target_pairs={{0,16},{4,20},{8,24},{12,28},{16,0},{20,4},{24,8},{28,12},{1,17},{... | collective-permute-start | bytes 565256 | tf_op jit(solution)/shard_map/ppermute | solution.py:49
  152.0 12.3 %collective-permute-start.24 = (bf16[320,256]{1,0:T(8,128)(2,1)S(1)}, bf16[320,256]{1,0:T(8,128)(2,1)S(1)}, u32[]{:S(2)}, u32[]{:S(2)}) collective-permute-start(bf16[320,256]{1,0:T(8,128)(2,1)S(1)} %get-tuple-element.147), channel_id=1, source_target_pairs={{0,16},{4,20},{8,24},{12,28},{16,0},{20,4},{24,8},{28,12},{1,17},{... | collective-permute-start | bytes 491528 | tf_op jit(solution)/shard_map/ppermute | solution.py:49
  154.9 10.8 %collective-permute-start.35 = (bf16[256,256]{1,0:T(8,128)(2,1)S(1)}, bf16[256,256]{1,0:T(8,128)(2,1)S(1)}, u32[]{:S(2)}, u32[]{:S(2)}) collective-permute-start(bf16[256,256]{1,0:T(8,128)(2,1)S(1)} %get-tuple-element.165), channel_id=1, source_target_pairs={{0,16},{4,20},{8,24},{12,28},{16,0},{20,4},{24,8},{28,12},{1,17},{... | collective-permute-start | bytes 393224 | tf_op jit(solution)/shard_map/ppermute | solution.py:49
  155.6 11.0 %collective-permute-start.30 = (bf16[368,256]{1,0:T(8,128)(2,1)S(1)}, bf16[368,256]{1,0:T(8,128)(2,1)S(1)}, u32[]{:S(2)}, u32[]{:S(2)}) collective-permute-start(bf16[368,256]{1,0:T(8,128)(2,1)S(1)} %add.26), channel_id=1, source_target_pairs={{0,2},{1,3},{2,0},{3,1},{4,6},{5,7},{6,4},{7,5},{8,10},{9,11},{10,... | collective-permute-start | bytes 565256 | tf_op jit(solution)/shard_map/ppermute | solution.py:49
  164.4 5.5 %collective-permute-start.25 = (bf16[320,256]{1,0:T(8,128)(2,1)S(1)}, bf16[320,256]{1,0:T(8,128)(2,1)S(1)}, u32[]{:S(2)}, u32[]{:S(2)}) collective-permute-start(bf16[320,256]{1,0:T(8,128)(2,1)S(1)} %add.24), channel_id=1, source_target_pairs={{0,2},{1,3},{2,0},{3,1},{4,6},{5,7},{6,4},{7,5},{8,10},{9,11},{10,... | collective-permute-start | bytes 491528 | tf_op jit(solution)/shard_map/ppermute | solution.py:49
  165.7 5.5 %collective-permute-start.36 = (bf16[1,256,256]{2,1,0:T(8,128)(2,1)S(1)}, bf16[1,256,256]{2,1,0:T(8,128)(2,1)S(1)}, u32[]{:S(2)}, u32[]{:S(2)}) collective-permute-start(bf16[1,256,256]{2,1,0:T(8,128)(2,1)S(1)} %add_bitcast_fusion), channel_id=1, source_target_pairs={{0,2},{1,3},{2,0},{3,1},{4,6},{5,7},{6,4},{7,5},{8,10},{9,11},{10,... | collective-permute-start | bytes 393224 | tf_op jit(solution)/shard_map/ppermute | solution.py:49
  166.6 4.8 %collective-permute-start.31 = (bf16[368,256]{1,0:T(8,128)(2,1)S(1)}, bf16[368,256]{1,0:T(8,128)(2,1)S(1)}, u32[]{:S(2)}, u32[]{:S(2)}) collective-permute-start(bf16[368,256]{1,0:T(8,128)(2,1)S(1)} %add.27.refs_0_), channel_id=1, source_target_pairs={{0,1},{1,0},{2,3},{3,2},{4,5},{5,4},{6,7},{7,6},{8,9},{9,8},{10,11... | collective-permute-start | bytes 565256 | tf_op jit(solution)/shard_map/ppermute | solution.py:49
  169.9 2.5 %collective-permute-start.26 = (bf16[320,256]{1,0:T(8,128)(2,1)S(1)}, bf16[320,256]{1,0:T(8,128)(2,1)S(1)}, u32[]{:S(2)}, u32[]{:S(2)}) collective-permute-start(bf16[320,256]{1,0:T(8,128)(2,1)S(1)} %add.25.refs_0_), channel_id=1, source_target_pairs={{0,1},{1,0},{2,3},{3,2},{4,5},{5,4},{6,7},{7,6},{8,9},{9,8},{10,11... | collective-permute-start | bytes 491528 | tf_op jit(solution)/shard_map/ppermute | solution.py:49
  171.3 2.0 %collective-permute-start.37 = (bf16[2,256,256]{2,1,0:T(8,128)(2,1)S(1)}, bf16[2,256,256]{2,1,0:T(8,128)(2,1)S(1)}, u32[]{:S(2)}, u32[]{:S(2)}) collective-permute-start(bf16[2,256,256]{2,1,0:T(8,128)(2,1)S(1)} %maximum_bitcast_fusion.refs_0_), channel_id=1, source_target_pairs={{0,1},{1,0},{2,3},{3,2},{4,5},{5,4},{6,7},{7,6},{8,9},{9,8},{10,11... | collective-permute-start | bytes 786440 | tf_op jit(solution)/shard_map/ppermute | solution.py:49

commit v3 on v2

--- a/solution.py
+++ b/solution.py
@@ -20,11 +20,9 @@
     return jax.ShapeDtypeStruct(dims, dtype)
 
 
-def run(kernel, name, args, outs, scratch=(), spaces=None, after=(), aliases=None, limit=24, us=1.0):
+def run(kernel, name, args, outs, scratch=(), spaces=None, after=(), aliases=None, limit=24, us=0.0):
     spaces = spaces or {}
     count, extra = len(args), len(after)
-    moved = sum(a.size * a.dtype.itemsize for a in args)
-    moved += sum(math.prod(o.shape) * o.dtype.itemsize for o in outs)
 
     def spec(place):
         return pl.BlockSpec(memory_space=spaces.get(place, pltpu.VMEM))
@@ -41,7 +39,7 @@
         scratch_shapes=list(scratch),
         input_output_aliases=aliases or {},
         compiler_params=pltpu.CompilerParams(vmem_limit_bytes=limit * MIB),
-        cost_estimate=pl.CostEstimate(flops=int(us * 1.1e9), bytes_accessed=moved, transcendentals=0),
+        cost_estimate=pl.CostEstimate(flops=int(us * 1.1e9) + 1000, bytes_accessed=1000, transcendentals=0),
     )(*args, *after)
 
 
@@ -518,16 +516,17 @@
                     target[at : at + channels] = value
 
 
-def store_slices(value, begin, offset, rows, pitch, keep, send):
-    bit = lax.axis_index("row") % 2
+def store_slices(position, value, begin, offset, rows, pitch, keep, send):
+    bit = (lax.axis_index("row") >> position) % 2
+    low = (1 << position) - 1
     for i in range(2):
 
         @pl.when(bit == i)
         def _():
             for k in range(value.shape[0] // rows):
                 r = begin + k
-                target = keep if r % 2 == i else send
-                at = r // 2 * pitch + offset
+                target = keep if (r >> position) & 1 == i else send
+                at = ((r >> (position + 1)) << position | (r & low)) * pitch + offset
                 target[at : at + rows] = value[k * rows : (k + 1) * rows]
 
 
@@ -542,7 +541,7 @@
         columns = slice(start, start + step)
         left = jnp.concatenate([early[:, columns], early_other[:, columns]], axis=0)
         value = (factor * dot_first(left, right)).astype(BF)
-        store_slices(value, start // deep, 0, deep, deep, keep, send)
+        store_slices(1, value, start // deep, 0, deep, deep, keep, send)
     tail = (own[pixels:].astype(F32) + other[pixels:].astype(F32)).astype(BF)
     at = slices // 2 * deep
     keep[at:] = tail
@@ -561,7 +560,7 @@
         columns = slice(k * width, (k + 1) * width)
         right = jnp.concatenate([own[:, columns], other[:, columns]], axis=0)
         value = (factor * dot_first(left, right)).astype(BF)
-        store_slices(value, 0, k * shallow, shallow, blocks * shallow, keep, send)
+        store_slices(0, value, 0, k * shallow, shallow, blocks * shallow, keep, send)
 
 
 def finish_patch_kernel(own, other, out):
@@ -778,7 +777,6 @@
             pltpu.VMEM((8, channels), F32),
         ),
         limit=16,
-        us=3,
     )
     branch_other = swap(branch_send, "col", 1)
     patch_half = shape_of(block_count // 2 * 4 * channels, block, dtype=BF)
@@ -788,20 +786,10 @@
         (early, early_other, flat_keep, flat_other),
         (patch_half, patch_half),
         limit=16,
-        us=3,
     )
     deep, shallow = hidden_width // row_count, channels // row_count
     groups = hidden_width // channels
     project_half = shape_of(row_count // 2 * deep + 112, half, dtype=BF)
-    project_keep, project_send = run(
-        functools.partial(project_product_kernel, scale_three, row_count),
-        "project_product",
-        (early, early_other, branch_keep, branch_other),
-        (project_half, project_half),
-        after=(patch_send,),
-        limit=16,
-        us=3,
-    )
     upward_half = shape_of(pixels, hidden_width // 2, dtype=BF)
     upward_keep, upward_send, grad_mixed, first, last, gain_part = run(
         back_kernel,
@@ -820,20 +808,27 @@
             pltpu.VMEM((pixels, hidden_width), BF),
             pltpu.VMEM((pixels, channels), F32),
         ),
-        after=(project_send,),
+        after=(patch_send,),
         limit=16,
-        us=4,
     )
     rows_back = neighbours(first, last, "row")
     upward_other = swap(upward_send, "col", 1)
+    project_keep, project_send = run(
+        functools.partial(project_product_kernel, scale_three, row_count),
+        "project_product",
+        (early, early_other, branch_keep, branch_other),
+        (project_half, project_half),
+        after=(upward_send,),
+        limit=16,
+    )
     expand_half = shape_of(row_count // 2 * groups * shallow, half, dtype=BF)
     expand_keep, expand_send = run(
         functools.partial(expand_product_kernel, scale_three, row_count),
         "expand_product",
         (early, early_other, upward_keep, upward_other),
         (expand_half, expand_half),
+        after=(project_send,),
         limit=16,
-        us=3,
     )
     framed_back = halo(grad_mixed, rows_back, "strips_back", after=(expand_send,))
     small_half = shape_of(64, half, dtype=BF)
@@ -847,9 +842,8 @@
             pltpu.VMEM((height, breadth, channels), F32),
             pltpu.VMEM((64, channels), F32),
         ),
-        after=framed_back[1:3],
+        after=(*framed_back[1:3], expand_send),
         limit=12,
-        us=5,
     )
     (input_grad,) = run(
         input_kernel,
@@ -859,7 +853,6 @@
         scratch=(frame_scratch(center), pltpu.VMEM((height, breadth, channels), F32)),
         after=(small_keep,),
         limit=12,
-        us=5,
     )
 
     row_bits, col_bits = axis_bits("row"), axis_bits("col")
@@ -879,8 +872,8 @@
         limit=8,
     )
 
-    def share(keep, send, rows, extra=(), after=()):
-        total = chain(keep, send, low_first, row_count, rows, extra, after)
+    def share(keep, send, order, rows, extra=(), after=()):
+        total = chain(keep, send, order, row_count, rows, extra, after)
         for bit in col_bits[1:]:
             total = total + swap(total, "col", bit)
         return total, swap(total, "col", 1)
@@ -889,7 +882,7 @@
     project_grad, wide_taps, wide_gain, merge_sum, layer_sum = run(
         finish_project_kernel,
         "finish_project",
-        share(project_keep, project_send, deep),
+        share(project_keep, project_send, [("row", row_bits[1], 1), low_first[0], *low_first[2:]], deep),
         (shape_of(deep, channels), shape_of(7, 7, wide), wide_vector, vector, vector),
         scratch=(pltpu.VMEM((112, channels), F32),),
         limit=8,
@@ -898,7 +891,7 @@
     expand_grad, taps_sum, gain_sum = run(
         finish_expand_kernel,
         "finish_expand",
-        share(expand_keep, expand_send, groups * shallow, (small, swap(small, "row", 1)), (input_grad,)),
+        share(expand_keep, expand_send, low_first, groups * shallow, (small, swap(small, "row", 1)), (input_grad,)),
         (shape_of(shallow, hidden_width), shape_of(7, 7, channels), vector),
         scratch=(pltpu.VMEM((64, channels), F32),),
         limit=8,

time: 175 us -> 177 us (1.011)
    ppermute x22, waiting for transfers between devices: 36.8 us -> 40.5 us  [swap(): lax.ppermute(values, axis, [(i, i ^ bit) for i in range(lax.axis_size(axi...]
    ppermute x8, waiting for transfers between devices: 18 us -> 15.5 us  [neighbours(): lax.ppermute(first, axis, backward)]
  transfers between devices with their start and end apart: 38 -> 38, of which waited for: 20 -> 20; matrix products, arithmetic and copies ran while one was open for 0% -> 0% of each run, Pallas kernels for 14% -> 16%
where the time goes in v3:
time: 177 us
  starting transfers between devices  59.5 us (34%)
  waiting for transfers between devices  58.8 us (33%)
  Pallas kernels  51 us (29%)
  local copies, waits for them, and re-layouts  5.87 us (3%)
    pallas_call x26, Pallas kernels, run(): pl.pallas_call(inner, name=name, out_shape=outs, in_specs=[spec(i) for i...  51 us
    ppermute x22, waiting for transfers between devices, swap(): lax.ppermute(values, axis, [(i, i ^ bit) for i in range(lax.axis_size(axi...  40.5 us
    ppermute x8, starting transfers between devices, neighbours(): lax.ppermute(last, axis, forward)  28.5 us
    ppermute x22, starting transfers between devices, swap(): lax.ppermute(values, axis, [(i, i ^ bit) for i in range(lax.axis_size(axi...  20.5 us
    ppermute x8, waiting for transfers between devices, neighbours(): lax.ppermute(first, axis, backward)  15.5 us
    ppermute x8, starting transfers between devices, neighbours(): lax.ppermute(first, axis, backward)  10.5 us
    unnamed x26, local copies, waits for them, and re-layouts  4.87 us
  transfers between devices with their start and end apart: 38, of which 20 were waited for; matrix products, arithmetic and copies ran while one was open for 0% of the time, Pallas kernels for 16%

profile of v3, /device:TPU:0, one launch (start us, length us, event | category | flops | bytes accessed | tf_op | source)
XLA Modules:
  0.0 176.6 jit_solution(452087416139627442)
XLA Ops:
  0.7 1.0 slice_bitcast_fusion
  1.7 4.8 %collective-permute-start = (bf16[3,32,512]{2,1,0:T(8,128)(2,1)S(1)}, bf16[3,32,512]{2,1,0:T(8,128)(2,1)S(1)}, u32[]{:S(2)}, u32[]{:S(2)}) collective-permute-start(bf16[3,32,512]{2,1,0:T(8,128)(2,1)S(1)} %get-tuple-element.171), channel_id=1, source_target_pairs={{0,4},{4,8},{8,12},{12,16},{16,20},{20,24},{24,28},{1,5},{5,9},{9,... | collective-permute-start | bytes 294920 | tf_op jit(solution)/shard_map/ppermute | solution.py:119
  6.5 1.3 collective-permute-start.1
  7.8 0.9 collective-permute-done.refs_5_.refs_1_
  8.7 0.9 copy-done.1
  9.7 0.9 copy-done.8
  13.1 1.6 collective-permute-start.2
  14.6 1.4 collective-permute-start.3
  16.1 3.5 %collective-permute-done.3.refs_4_ = bf16[14,8,512]{2,1,0:T(8,128)(2,1)S(1)} collective-permute-done((bf16[14,8,512]{2,1,0:T(8,128)(2,1)S(1)}, bf16[14,8,512]{2,1,0:T(8,128)(2,1)S(1)}, u32[]{:S(2)}, u32[]{:S(2)}) %collective-permute-start.3) | collective-permute-done | bytes 114720 | tf_op jit(solution)/shard_map/ppermute | solution.py:119
  19.6 12.8 %front.1 = (bf16[256,3072]{1,0:T(8,128)(2,1)S(1)}, f32[256,512]{1,0:T(8,128)S(1)}, f32[256,1]{1,0:T(8,128)S(1)}, bf16[256,2048]{1,0:T(8,128)(2,1)S(1)}, f32[256,...) custom-call(bf16[8,32,512]{2,1,0:T(8,128)(2,1)S(1)} %get-tuple-eleme, ...), custom_call_target="tpu_custom_call" | custom-call | flops 13200001024 | bytes 1000 | tf_op jit(solution)/shard_map/front/pallas_call | solution.py:33
  32.5 4.4 %collective-permute-start.4 = (bf16[3,16,1024]{2,1,0:T(8,128)(2,1)S(1)}, bf16[3,16,1024]{2,1,0:T(8,128)(2,1)S(1)}, u32[]{:S(2)}, u32[]{:S(2)}) collective-permute-start(bf16[3,16,1024]{2,1,0:T(8,128)(2,1)S(1)} %get-tuple-element.97), channel_id=1, source_target_pairs={{0,4},{4,8},{8,12},{12,16},{16,20},{20,24},{24,28},{1,5},{5,9},{9,... | collective-permute-start | bytes 294920 | tf_op jit(solution)/shard_map/ppermute | solution.py:119
  36.8 1.3 collective-permute-start.5
  38.1 0.9 collective-permute-done.4.refs_1_
  39.0 4.5 %collective-permute-done.5.refs_2_ = bf16[3,16,1024]{2,1,0:T(8,128)(2,1)S(1)} collective-permute-done((bf16[3,16,1024]{2,1,0:T(8,128)(2,1)S(1)}, bf16[3,16,1024]{2,1,0:T(8,128)(2,1)S(1)}, u32[]{:S(2)}, u32[]{:S(2)}) %collective-permute-start.5) | collective-permute-done | bytes 98336 | tf_op jit(solution)/shard_map/ppermute | solution.py:119
  43.6 4.2 %collective-permute-start.6 = (bf16[10,8,1024]{2,1,0:T(8,128)(2,1)S(1)}, bf16[10,8,1024]{2,1,0:T(8,128)(2,1)S(1)}, u32[]{:S(2)}, u32[]{:S(2)}) collective-permute-start(bf16[10,8,1024]{2,1,0:T(8,128)(2,1)S(1)} %get-tuple-element.99), channel_id=1, source_target_pairs={{0,1},{1,2},{2,3},{4,5},{5,6},{6,7},{8,9},{9,10},{10,11},{12,13},{... | collective-permute-start | bytes 491528 | tf_op jit(solution)/shard_map/ppermute | solution.py:119
  47.8 1.3 collective-permute-start.7
  49.1 2.5 %collective-permute-done.7.refs_4_ = bf16[10,8,1024]{2,1,0:T(8,128)(2,1)S(1)} collective-permute-done((bf16[10,8,1024]{2,1,0:T(8,128)(2,1)S(1)}, bf16[10,8,1024]{2,1,0:T(8,128)(2,1)S(1)}, u32[]{:S(2)}, u32[]{:S(2)}) %collective-permute-start.7) | collective-permute-done | bytes 163872 | tf_op jit(solution)/shard_map/ppermute | solution.py:119
  51.6 3.3 %mixer.1 = (f32[4,16,1024]{2,1,0:T(8,128)S(1)}, bf16[4,16,1024]{2,1,0:T(8,128)(2,1)S(1)}, bf16[3,16,1024]{2,1,0:T(8,128)(2,1)S(1)}, bf16[3,16,1024]{2,1,0:T(8,128)(2,1)S(1)}, f32[1,1024]{1,0:T(1,128)S(1)}) custom-call(bf16[4,16,1024]{2,1,0:T(8,128)(2,1)S(1)} %get-tuple-element.96.refs_0_, bf16[3,16,1024]{2,1,0:T(8,128)(2,1)S(1)} %collective-permute-done.4.refs_1_, ...), custom_call_target="tpu_custom_call" | custom-call | flops 3300001024 | bytes 1000 | tf_op jit(solution)/shard_map/mixer/pallas_call | solution.py:33
  54.9 4.8 %collective-permute-start.8 = (bf16[3,16,1024]{2,1,0:T(8,128)(2,1)S(1)}, bf16[3,16,1024]{2,1,0:T(8,128)(2,1)S(1)}, u32[]{:S(2)}, u32[]{:S(2)}) collective-permute-start(bf16[3,16,1024]{2,1,0:T(8,128)(2,1)S(1)} %get-tuple-element.105), channel_id=1, source_target_pairs={{0,4},{4,8},{8,12},{12,16},{16,20},{20,24},{24,28},{1,5},{5,9},{9,... | collective-permute-start | bytes 294920 | tf_op jit(solution)/shard_map/ppermute | solution.py:119
  59.7 1.3 collective-permute-start.9
  61.0 0.9 collective-permute-done.8.refs_6_.refs_1_
  61.9 2.9 %mixer_weights.1.refs_3_.refs_7_ = f32[49,1024]{1,0:T(8,128)S(1)} custom-call(bf16[4,16,1024]{2,1,0:T(8,128)(2,1)S(1)} %get-tuple-element.96.refs_0_, bf16[3,16,1024]{2,1,0:T(8,128)(2,1)S(1)} %collective-permute-done.4.refs_1_, bf16[3,16,1024]{2,1,0:T(8,128)(2,1)S(1)} %collective-permute-done.5.refs_2_, ...), custom_call_target="tpu_custom_call" | custom-call | flops 3300001024 | bytes 1000 | tf_op jit(solution)/shard_map/mixer_weights/pallas_call | solution.py:33
  64.8 1.4 collective-permute-done.9.refs_2_
  66.3 4.5 %collective-permute-start.10 = (bf16[10,8,1024]{2,1,0:T(8,128)(2,1)S(1)}, bf16[10,8,1024]{2,1,0:T(8,128)(2,1)S(1)}, u32[]{:S(2)}, u32[]{:S(2)}) collective-permute-start(bf16[10,8,1024]{2,1,0:T(8,128)(2,1)S(1)} %get-tuple-element.108), channel_id=1, source_target_pairs={{0,1},{1,2},{2,3},{4,5},{5,6},{6,7},{8,9},{9,10},{10,11},{12,13},{... | collective-permute-start | bytes 491528 | tf_op jit(solution)/shard_map/ppermute | solution.py:119
  70.8 1.3 collective-permute-start.11
  72.1 2.6 %collective-permute-done.11.refs_4_ = bf16[10,8,1024]{2,1,0:T(8,128)(2,1)S(1)} collective-permute-done((bf16[10,8,1024]{2,1,0:T(8,128)(2,1)S(1)}, bf16[10,8,1024]{2,1,0:T(8,128)(2,1)S(1)}, u32[]{:S(2)}, u32[]{:S(2)}) %collective-permute-start.11) | collective-permute-done | bytes 163872 | tf_op jit(solution)/shard_map/ppermute | solution.py:119
  74.7 3.1 %section_grad.1 = (bf16[64,1024]{1,0:T(8,128)(2,1)S(1)}, bf16[2,64,256]{2,1,0:T(8,128)(2,1)S(1)}, bf16[2,64,256]{2,1,0:T(8,128)(2,1)S(1)}, bf16[256,3072]{1,0:T(8,128)(2,1)S(1)}) custom-call(bf16[4,16,1024]{2,1,0:T(8,128)(2,1)S(1)} %get-tuple-element.104.refs_0_, ...), custom_call_target="tpu_custom_call", output_to_operand_aliasing={{3}: (7, {})} | custom-call | flops 3300001024 | bytes 1000 | tf_op jit(solution)/shard_map/section_grad/pallas_call | solution.py:33
  77.8 3.9 %collective-permute-start.12 = (bf16[256,3072]{1,0:T(8,128)(2,1)S(1)}, bf16[256,3072]{1,0:T(8,128)(2,1)S(1)}, u32[]{:S(2)}, u32[]{:S(2)}) collective-permute-start(bf16[256,3072]{1,0:T(8,128)(2,1)S(1)} %get-tuple-element.124.refs_0_), channel_id=1, source_target_pairs={{0,1},{1,0},{2,3},{3,2},{4,5},{5,4},{6,7},{7,6},{8,9},{9,8},{10,11... | collective-permute-start | bytes 4718600 | tf_op jit(solution)/shard_map/ppermute | solution.py:47
  81.8 3.1 %collective-permute-done.13.refs_3_ = bf16[2,64,256]{2,1,0:T(8,128)(2,1)S(1)} collective-permute-done((bf16[2,64,256]{2,1,0:T(8,128)(2,1)S(1)}, bf16[2,64,256]{2,1,0:T(8,128)(2,1)S(1)}, u32[]{:S(2)}, u32[]{:S(2)}) %collective-permute-start.13) | collective-permute-done | bytes 65568 | tf_op jit(solution)/shard_map/ppermute | solution.py:47
  84.8 2.6 %patch_product.1 = (bf16[2048,256]{1,0:T(8,128)(2,1)S(1)}, bf16[2048,256]{1,0:T(8,128)(2,1)S(1)}) custom-call(bf16[256,3072]{1,0:T(8,128)(2,1)S(1)} %get-tuple-element.124.refs_0_, bf16[256,3072]{1,0:T(8,128)(2,1)S(1)} %collective-permute-done.12.refs_1_, bf16[2,64,256]{2,1,0:T(8,128)(2,1)S(1)} %get-tuple-element.125.refs_2_, ...), custom_call_target="tpu_custom_call" | custom-call | flops 1000 | bytes 1000 | tf_op jit(solution)/shard_map/patch_product/pallas_call | solution.py:33
  87.6 2.5 %merge_back.1 = (f32[256,512]{1,0:T(8,128)S(1)}, bf16[256,512]{1,0:T(8,128)(2,1)S(1)}, bf16[368,256]{1,0:T(8,128)(2,1)S(1)}, bf16[368,256]{1,0:T(8,128)(2,1)S(1)}) custom-call(bf16[64,1024]{1,0:T(8,128)(2,1)S(1)} %get-tuple-element.112.refs_0_, bf16[2048,1024]{1,0:T(8,128)(2,1)S(1)} %get-tuple-element.113.refs_1_, ...), custom_call_target="tpu_custom_call" | custom-call | flops 1000 | bytes 1000 | tf_op jit(solution)/shard_map/merge_back/pallas_call | solution.py:33
  90.1 3.2 %mlp_back.1 = (bf16[256,1024]{1,0:T(8,128)(2,1)S(1)}, bf16[256,1024]{1,0:T(8,128)(2,1)S(1)}, bf16[8,32,512]{2,1,0:T(8,128)(2,1)S(1)}, bf16[3,32,512]{2,1,0:T(8,1...) custom-call(bf16[256,512]{1,0:T(8,128)(2,1)S(1)} %get-tuple-element.118.refs_0_, ...), custom_call_target="tpu_custom_call" | custom-call | flops 1000 | bytes 1000 | tf_op jit(solution)/shard_map/mlp_back/pallas_call | solution.py:33
  93.8 3.0 %collective-permute-start.14 = (bf16[3,32,512]{2,1,0:T(8,128)(2,1)S(1)}, bf16[3,32,512]{2,1,0:T(8,128)(2,1)S(1)}, u32[]{:S(2)}, u32[]{:S(2)}) collective-permute-start(bf16[3,32,512]{2,1,0:T(8,128)(2,1)S(1)} %get-tuple-element.129), channel_id=1, source_target_pairs={{0,4},{4,8},{8,12},{12,16},{16,20},{20,24},{24,28},{1,5},{5,9},{9,... | collective-permute-start | bytes 294920 | tf_op jit(solution)/shard_map/ppermute | solution.py:119
  96.9 1.3 collective-permute-start.15
  98.2 2.8 %project_product.1 = (bf16[1136,256]{1,0:T(8,128)(2,1)S(1)}, bf16[1136,256]{1,0:T(8,128)(2,1)S(1)}) custom-call(bf16[256,3072]{1,0:T(8,128)(2,1)S(1)} %get-tuple-element.124.refs_0_, bf16[256,3072]{1,0:T(8,128)(2,1)S(1)} %collective-permute-done.12.refs_1_, bf16[368,256]{1,0:T(8,128)(2,1)S(1)} %get-tuple-element.133.refs_2_, ...), custom_call_target="tpu_custom_call" | custom-call | flops 1000 | bytes 1000 | tf_op jit(solution)/shard_map/project_product/pallas_call | solution.py:33
  101.0 1.9 %expand_product.1 = (bf16[1024,256]{1,0:T(8,128)(2,1)S(1)}, bf16[1024,256]{1,0:T(8,128)(2,1)S(1)}) custom-call(bf16[256,3072]{1,0:T(8,128)(2,1)S(1)} %get-tuple-element.124.refs_0_, bf16[256,3072]{1,0:T(8,128)(2,1)S(1)} %collective-permute-done.12.refs_1_, bf16[256,1024]{1,0:T(8,128)(2,1)S(1)} %get-tuple-element.131.refs_2_, ...), custom_call_target="tpu_custom_call" | custom-call | flops 1000 | bytes 1000 | tf_op jit(solution)/shard_map/expand_product/pallas_call | solution.py:33
  102.9 0.7 collective-permute-done.15.refs_2_.refs_8_
  103.6 5.4 %block_weights.1 = (bf16[64,256]{1,0:T(8,128)(2,1)S(1)}, bf16[64,256]{1,0:T(8,128)(2,1)S(1)}) custom-call(bf16[8,32,512]{2,1,0:T(8,128)(2,1)S(1)} %get-tuple-element.89.refs_0_, bf16[3,32,512]{2,1,0:T(8,128)(2,1)S(1)} %collective-permute-done.refs_5_.refs_1_, bf16[3,32,512]{2,1,0:T(8,128)(2,1)S(1)} %collective-permute-done.1.refs_2_, ...), custom_call_target="tpu_custom_call" | custom-call | flops 1000 | bytes 1000 | tf_op jit(solution)/shard_map/block_weights/pallas_call | solution.py:33
  109.0 3.9 %collective-permute-done.32.refs_1_ = bf16[2048,256]{1,0:T(8,128)(2,1)S(1)} collective-permute-done((bf16[2048,256]{1,0:T(8,128)(2,1)S(1)}, bf16[2048,256]{1,0:T(8,128)(2,1)S(1)}, u32[]{:S(2)}, u32[]{:S(2)}) %collective-permute-start.32) | collective-permute-done | bytes 1048608 | tf_op jit(solution)/shard_map/ppermute | solution.py:47
  113.2 1.1 collective-permute-start.33
  114.3 1.6 collective-permute-start.27
  115.9 1.0 collective-permute-start.20
  116.8 1.3 collective-permute-start.18
  118.2 1.1 collective-permute-start.21
  119.2 8.8 %collective-permute-done.33.refs_1_ = bf16[1024,256]{1,0:T(8,128)(2,1)S(1)} collective-permute-done((bf16[1024,256]{1,0:T(8,128)(2,1)S(1)}, bf16[1024,256]{1,0:T(8,128)(2,1)S(1)}, u32[]{:S(2)}, u32[]{:S(2)}) %collective-permute-start.33) | collective-permute-done | bytes 524320 | tf_op jit(solution)/shard_map/ppermute | solution.py:47
  128.1 1.3 collective-permute-start.19
  129.5 1.6 collective-permute-start.34
  131.2 1.1 collective-permute-start.22
  132.5 1.0 collective-permute-start.28
  133.5 6.6 %input_grad.1.refs_4_ = bf16[8,32,512]{2,1,0:T(8,128)(2,1)} custom-call(bf16[8,32,512]{2,1,0:T(8,128)(2,1)S(1)} %get-tuple-element.128.refs_0_.refs_5_, bf16[3,32,512]{2,1,0:T(8,128)(2,1)S(1)} %collective-permute-done.14.refs_1_.refs_7_, bf16[3,32,512]{2,1,0:T(8,128)(2,1)S(1)} %collective-permute-done.15.refs_2_.refs_8_, ...), custom_call_target="tpu_custom_call" | custom-call | flops 1000 | bytes 1000 | tf_op jit(solution)/shard_map/input_grad/pallas_call | solution.py:33
  140.1 0.9 copy-done
  141.2 1.6 collective-permute-start.23
  142.8 1.6 collective-permute-start.35
  144.4 1.0 collective-permute-done.28.refs_1_
  145.5 2.7 %collective-permute-start.29 = (bf16[368,256]{1,0:T(8,128)(2,1)S(1)}, bf16[368,256]{1,0:T(8,128)(2,1)S(1)}, u32[]{:S(2)}, u32[]{:S(2)}) collective-permute-start(bf16[368,256]{1,0:T(8,128)(2,1)S(1)} %get-tuple-element.155), channel_id=1, source_target_pairs={{0,16},{4,20},{8,24},{12,28},{16,0},{20,4},{24,8},{28,12},{1,17},{... | collective-permute-start | bytes 565256 | tf_op jit(solution)/shard_map/ppermute | solution.py:47
  148.1 8.2 %collective-permute-done.23.refs_1_ = bf16[576,256]{1,0:T(8,128)(2,1)S(1)} collective-permute-done((bf16[576,256]{1,0:T(8,128)(2,1)S(1)}, bf16[576,256]{1,0:T(8,128)(2,1)S(1)}, u32[]{:S(2)}, u32[]{:S(2)}) %collective-permute-start.23) | collective-permute-done | bytes 294944 | tf_op jit(solution)/shard_map/ppermute | solution.py:47
  156.7 7.3 %collective-permute-done.29 = bf16[368,256]{1,0:T(8,128)(2,1)S(1)} collective-permute-done((bf16[368,256]{1,0:T(8,128)(2,1)S(1)}, bf16[368,256]{1,0:T(8,128)(2,1)S(1)}, u32[]{:S(2)}, u32[]{:S(2)}) %collective-permute-start.29) | collective-permute-done | bytes 188448 | tf_op jit(solution)/shard_map/ppermute | solution.py:47
  164.0 0.7 collective-permute-start.30
  164.7 1.9 %collective-permute-done.24 = bf16[320,256]{1,0:T(8,128)(2,1)S(1)} collective-permute-done((bf16[320,256]{1,0:T(8,128)(2,1)S(1)}, bf16[320,256]{1,0:T(8,128)(2,1)S(1)}, u32[]{:S(2)}, u32[]{:S(2)}) %collective-permute-start.24) | collective-permute-done | bytes 163872 | tf_op jit(solution)/shard_map/ppermute | solution.py:47
  167.2 3.5 %collective-permute-done.30 = bf16[368,256]{1,0:T(8,128)(2,1)S(1)} collective-permute-done((bf16[368,256]{1,0:T(8,128)(2,1)S(1)}, bf16[368,256]{1,0:T(8,128)(2,1)S(1)}, u32[]{:S(2)}, u32[]{:S(2)}) %collective-permute-start.30) | collective-permute-done | bytes 188448 | tf_op jit(solution)/shard_map/ppermute | solution.py:47
  170.9 2.3 %collective-permute-done.25 = bf16[320,256]{1,0:T(8,128)(2,1)S(1)} collective-permute-done((bf16[320,256]{1,0:T(8,128)(2,1)S(1)}, bf16[320,256]{1,0:T(8,128)(2,1)S(1)}, u32[]{:S(2)}, u32[]{:S(2)}) %collective-permute-start.25) | collective-permute-done | bytes 163872 | tf_op jit(solution)/shard_map/ppermute | solution.py:47
  173.3 1.0 finish_project.1
  174.7 0.9 finish_expand.1
  175.6 1.0 finish_patch.1
  (73 shorter events, 5.7 us)
Async XLA Ops:
  0.6 19.0 %copy-start.6 = (bf16[1,4,16,1024]{3,2,1,0:T(8,128)(2,1)S(1)}, bf16[1,4,16,1024]{3,2,1,0:T(8,128)(2,1)}, u32[]{:S(2)}) copy-start(bf16[1,4,16,1024]{3,2,1,0:T(8,128)(2,1)} %param.22) | copy-start | bytes 393220
  0.7 19.0 %copy-start.7 = (bf16[1,4,16,1024]{3,2,1,0:T(8,128)(2,1)S(1)}, bf16[1,4,16,1024]{3,2,1,0:T(8,128)(2,1)}, u32[]{:S(2)}) copy-start(bf16[1,4,16,1024]{3,2,1,0:T(8,128)(2,1)} %param.23) | copy-start | bytes 393220
  0.7 18.9 %copy-start.9 = (f32[1024]{0:T(1024)S(1)}, f32[1024]{0:T(1024)}, u32[]{:S(2)}) copy-start(f32[1024]{0:T(1024)} %param.21) | copy-start | bytes 12292
  1.7 7.0 %collective-permute-start = (bf16[3,32,512]{2,1,0:T(8,128)(2,1)S(1)}, bf16[3,32,512]{2,1,0:T(8,128)(2,1)S(1)}, u32[]{:S(2)}, u32[]{:S(2)}) collective-permute-start(bf16[3,32,512]{2,1,0:T(8,128)(2,1)S(1)} %get-tuple-element.171), channel_id=1, source_target_pairs={{0,4},{4,8},{8,12},{12,16},{16,20},{20,24},{24,28},{1,5},{5,9},{9,... | collective-permute-start | bytes 294920 | tf_op jit(solution)/shard_map/ppermute | solution.py:119
  6.5 6.5 %collective-permute-start.1 = (bf16[3,32,512]{2,1,0:T(8,128)(2,1)S(1)}, bf16[3,32,512]{2,1,0:T(8,128)(2,1)S(1)}, u32[]{:S(2)}, u32[]{:S(2)}) collective-permute-start(bf16[3,32,512]{2,1,0:T(8,128)(2,1)S(1)} %get-tuple-element.170), channel_id=1, source_target_pairs={{4,0},{8,4},{12,8},{16,12},{20,16},{24,20},{28,24},{5,1},{9,5},{13... | collective-permute-start | bytes 294920 | tf_op jit(solution)/shard_map/ppermute | solution.py:119
  8.7 0.9 copy-start.1
  9.7 0.9 copy-start.8
  10.6 0.7 copy-start.10
  11.3 0.7 copy-start.11
  11.9 0.7 copy-start.12
  12.6 7.0 %copy-start.2 = (bf16[2048,1024]{1,0:T(8,128)(2,1)S(1)}, bf16[2048,1024]{1,0:T(8,128)(2,1)}, u32[]{:S(2)}) copy-start(bf16[2048,1024]{1,0:T(8,128)(2,1)} %refs_11_.1) | copy-start | bytes 12582916
  12.6 7.0 %copy-start.3 = (bf16[512,2048]{1,0:T(8,128)(2,1)S(1)}, bf16[512,2048]{1,0:T(8,128)(2,1)}, u32[]{:S(2)}) copy-start(bf16[512,2048]{1,0:T(8,128)(2,1)} %refs_9_.1) | copy-start | bytes 6291460
  12.6 7.0 %copy-start.4 = (bf16[2048,512]{1,0:T(8,128)(2,1)S(1)}, bf16[2048,512]{1,0:T(8,128)(2,1)}, u32[]{:S(2)}) copy-start(bf16[2048,512]{1,0:T(8,128)(2,1)} %refs_10_.1) | copy-start | bytes 6291460
  12.6 7.0 %copy-start.5 = (f32[7,7,1024]{2,1,0:T(8,128)S(1)}, f32[7,7,1024]{2,1,0:T(8,128)}, u32[]{:S(2)}) copy-start(f32[7,7,1024]{2,1,0:T(8,128)} %refs_12_.1) | copy-start | bytes 602116
  13.1 3.0 %collective-permute-start.2 = (bf16[14,8,512]{2,1,0:T(8,128)(2,1)S(1)}, bf16[14,8,512]{2,1,0:T(8,128)(2,1)S(1)}, u32[]{:S(2)}, u32[]{:S(2)}) collective-permute-start(bf16[14,8,512]{2,1,0:T(8,128)(2,1)S(1)} %get-tuple-element.90), channel_id=1, source_target_pairs={{0,1},{1,2},{2,3},{4,5},{5,6},{6,7},{8,9},{9,10},{10,11},{12,13},{... | collective-permute-start | bytes 344072 | tf_op jit(solution)/shard_map/ppermute | solution.py:119
  14.6 5.0 %collective-permute-start.3 = (bf16[14,8,512]{2,1,0:T(8,128)(2,1)S(1)}, bf16[14,8,512]{2,1,0:T(8,128)(2,1)S(1)}, u32[]{:S(2)}, u32[]{:S(2)}) collective-permute-start(bf16[14,8,512]{2,1,0:T(8,128)(2,1)S(1)} %get-tuple-element.91), channel_id=1, source_target_pairs={{1,0},{2,1},{3,2},{5,4},{6,5},{7,6},{9,8},{10,9},{11,10},{13,12},{... | collective-permute-start | bytes 344072 | tf_op jit(solution)/shard_map/ppermute | solution.py:119
  32.5 6.6 %collective-permute-start.4 = (bf16[3,16,1024]{2,1,0:T(8,128)(2,1)S(1)}, bf16[3,16,1024]{2,1,0:T(8,128)(2,1)S(1)}, u32[]{:S(2)}, u32[]{:S(2)}) collective-permute-start(bf16[3,16,1024]{2,1,0:T(8,128)(2,1)S(1)} %get-tuple-element.97), channel_id=1, source_target_pairs={{0,4},{4,8},{8,12},{12,16},{16,20},{20,24},{24,28},{1,5},{5,9},{9,... | collective-permute-start | bytes 294920 | tf_op jit(solution)/shard_map/ppermute | solution.py:119
  36.8 6.7 %collective-permute-start.5 = (bf16[3,16,1024]{2,1,0:T(8,128)(2,1)S(1)}, bf16[3,16,1024]{2,1,0:T(8,128)(2,1)S(1)}, u32[]{:S(2)}, u32[]{:S(2)}) collective-permute-start(bf16[3,16,1024]{2,1,0:T(8,128)(2,1)S(1)} %get-tuple-element.98), channel_id=1, source_target_pairs={{4,0},{8,4},{12,8},{16,12},{20,16},{24,20},{28,24},{5,1},{9,5},{13... | collective-permute-start | bytes 294920 | tf_op jit(solution)/shard_map/ppermute | solution.py:119
  43.6 5.5 %collective-permute-start.6 = (bf16[10,8,1024]{2,1,0:T(8,128)(2,1)S(1)}, bf16[10,8,1024]{2,1,0:T(8,128)(2,1)S(1)}, u32[]{:S(2)}, u32[]{:S(2)}) collective-permute-start(bf16[10,8,1024]{2,1,0:T(8,128)(2,1)S(1)} %get-tuple-element.99), channel_id=1, source_target_pairs={{0,1},{1,2},{2,3},{4,5},{5,6},{6,7},{8,9},{9,10},{10,11},{12,13},{... | collective-permute-start | bytes 491528 | tf_op jit(solution)/shard_map/ppermute | solution.py:119
  47.8 3.8 %collective-permute-start.7 = (bf16[10,8,1024]{2,1,0:T(8,128)(2,1)S(1)}, bf16[10,8,1024]{2,1,0:T(8,128)(2,1)S(1)}, u32[]{:S(2)}, u32[]{:S(2)}) collective-permute-start(bf16[10,8,1024]{2,1,0:T(8,128)(2,1)S(1)} %get-tuple-element.100), channel_id=1, source_target_pairs={{1,0},{2,1},{3,2},{5,4},{6,5},{7,6},{9,8},{10,9},{11,10},{13,12},{... | collective-permute-start | bytes 491528 | tf_op jit(solution)/shard_map/ppermute | solution.py:119
  54.9 7.0 %collective-permute-start.8 = (bf16[3,16,1024]{2,1,0:T(8,128)(2,1)S(1)}, bf16[3,16,1024]{2,1,0:T(8,128)(2,1)S(1)}, u32[]{:S(2)}, u32[]{:S(2)}) collective-permute-start(bf16[3,16,1024]{2,1,0:T(8,128)(2,1)S(1)} %get-tuple-element.105), channel_id=1, source_target_pairs={{0,4},{4,8},{8,12},{12,16},{16,20},{20,24},{24,28},{1,5},{5,9},{9,... | collective-permute-start | bytes 294920 | tf_op jit(solution)/shard_map/ppermute | solution.py:119
  59.7 6.5 %collective-permute-start.9 = (bf16[3,16,1024]{2,1,0:T(8,128)(2,1)S(1)}, bf16[3,16,1024]{2,1,0:T(8,128)(2,1)S(1)}, u32[]{:S(2)}, u32[]{:S(2)}) collective-permute-start(bf16[3,16,1024]{2,1,0:T(8,128)(2,1)S(1)} %get-tuple-element.106), channel_id=1, source_target_pairs={{4,0},{8,4},{12,8},{16,12},{20,16},{24,20},{28,24},{5,1},{9,5},{13... | collective-permute-start | bytes 294920 | tf_op jit(solution)/shard_map/ppermute | solution.py:119
  66.3 5.8 %collective-permute-start.10 = (bf16[10,8,1024]{2,1,0:T(8,128)(2,1)S(1)}, bf16[10,8,1024]{2,1,0:T(8,128)(2,1)S(1)}, u32[]{:S(2)}, u32[]{:S(2)}) collective-permute-start(bf16[10,8,1024]{2,1,0:T(8,128)(2,1)S(1)} %get-tuple-element.108), channel_id=1, source_target_pairs={{0,1},{1,2},{2,3},{4,5},{5,6},{6,7},{8,9},{9,10},{10,11},{12,13},{... | collective-permute-start | bytes 491528 | tf_op jit(solution)/shard_map/ppermute | solution.py:119
  70.8 3.9 %collective-permute-start.11 = (bf16[10,8,1024]{2,1,0:T(8,128)(2,1)S(1)}, bf16[10,8,1024]{2,1,0:T(8,128)(2,1)S(1)}, u32[]{:S(2)}, u32[]{:S(2)}) collective-permute-start(bf16[10,8,1024]{2,1,0:T(8,128)(2,1)S(1)} %get-tuple-element.109), channel_id=1, source_target_pairs={{1,0},{2,1},{3,2},{5,4},{6,5},{7,6},{9,8},{10,9},{11,10},{13,12},{... | collective-permute-start | bytes 491528 | tf_op jit(solution)/shard_map/ppermute | solution.py:119
  77.8 7.0 %collective-permute-start.12 = (bf16[256,3072]{1,0:T(8,128)(2,1)S(1)}, bf16[256,3072]{1,0:T(8,128)(2,1)S(1)}, u32[]{:S(2)}, u32[]{:S(2)}) collective-permute-start(bf16[256,3072]{1,0:T(8,128)(2,1)S(1)} %get-tuple-element.124.refs_0_), channel_id=1, source_target_pairs={{0,1},{1,0},{2,3},{3,2},{4,5},{5,4},{6,7},{7,6},{8,9},{9,8},{10,11... | collective-permute-start | bytes 4718600 | tf_op jit(solution)/shard_map/ppermute | solution.py:47
  81.7 3.1 %collective-permute-start.13 = (bf16[2,64,256]{2,1,0:T(8,128)(2,1)S(1)}, bf16[2,64,256]{2,1,0:T(8,128)(2,1)S(1)}, u32[]{:S(2)}, u32[]{:S(2)}) collective-permute-start(bf16[2,64,256]{2,1,0:T(8,128)(2,1)S(1)} %get-tuple-element.126), channel_id=1, source_target_pairs={{0,1},{1,0},{2,3},{3,2},{4,5},{5,4},{6,7},{7,6},{8,9},{9,8},{10,11... | collective-permute-start | bytes 196616 | tf_op jit(solution)/shard_map/ppermute | solution.py:47
  87.4 25.5 %collective-permute-start.32 = (bf16[2048,256]{1,0:T(8,128)(2,1)S(1)}, bf16[2048,256]{1,0:T(8,128)(2,1)S(1)}, u32[]{:S(2)}, u32[]{:S(2)}) collective-permute-start(bf16[2048,256]{1,0:T(8,128)(2,1)S(1)} %get-tuple-element.127.refs_7_), channel_id=1, source_target_pairs={{0,2},{1,3},{2,0},{3,1},{4,6},{5,7},{6,4},{7,5},{8,10},{9,11},{10,... | collective-permute-start | bytes 3145736 | tf_op jit(solution)/shard_map/ppermute | solution.py:47
  93.3 7.7 %collective-permute-start.16 = (bf16[256,1024]{1,0:T(8,128)(2,1)S(1)}, bf16[256,1024]{1,0:T(8,128)(2,1)S(1)}, u32[]{:S(2)}, u32[]{:S(2)}) collective-permute-start(bf16[256,1024]{1,0:T(8,128)(2,1)S(1)} %get-tuple-element.132.refs_4_), channel_id=1, source_target_pairs={{0,1},{1,0},{2,3},{3,2},{4,5},{5,4},{6,7},{7,6},{8,9},{9,8},{10,11... | collective-permute-start | bytes 1572872 | tf_op jit(solution)/shard_map/ppermute | solution.py:47
  93.6 4.6 %collective-permute-start.17 = (bf16[368,256]{1,0:T(8,128)(2,1)S(1)}, bf16[368,256]{1,0:T(8,128)(2,1)S(1)}, u32[]{:S(2)}, u32[]{:S(2)}) collective-permute-start(bf16[368,256]{1,0:T(8,128)(2,1)S(1)} %get-tuple-element.134), channel_id=1, source_target_pairs={{0,1},{1,0},{2,3},{3,2},{4,5},{5,4},{6,7},{7,6},{8,9},{9,8},{10,11... | collective-permute-start | bytes 565256 | tf_op jit(solution)/shard_map/ppermute | solution.py:47
  93.8 9.0 %collective-permute-start.14 = (bf16[3,32,512]{2,1,0:T(8,128)(2,1)S(1)}, bf16[3,32,512]{2,1,0:T(8,128)(2,1)S(1)}, u32[]{:S(2)}, u32[]{:S(2)}) collective-permute-start(bf16[3,32,512]{2,1,0:T(8,128)(2,1)S(1)} %get-tuple-element.129), channel_id=1, source_target_pairs={{0,4},{4,8},{8,12},{12,16},{16,20},{20,24},{24,28},{1,5},{5,9},{9,... | collective-permute-start | bytes 294920 | tf_op jit(solution)/shard_map/ppermute | solution.py:119
  96.9 6.8 %collective-permute-start.15 = (bf16[3,32,512]{2,1,0:T(8,128)(2,1)S(1)}, bf16[3,32,512]{2,1,0:T(8,128)(2,1)S(1)}, u32[]{:S(2)}, u32[]{:S(2)}) collective-permute-start(bf16[3,32,512]{2,1,0:T(8,128)(2,1)S(1)} %get-tuple-element.130), channel_id=1, source_target_pairs={{4,0},{8,4},{12,8},{16,12},{20,16},{24,20},{28,24},{5,1},{9,5},{13... | collective-permute-start | bytes 294920 | tf_op jit(solution)/shard_map/ppermute | solution.py:119
  113.2 14.9 %collective-permute-start.33 = (bf16[1024,256]{1,0:T(8,128)(2,1)S(1)}, bf16[1024,256]{1,0:T(8,128)(2,1)S(1)}, u32[]{:S(2)}, u32[]{:S(2)}) collective-permute-start(bf16[1024,256]{1,0:T(8,128)(2,1)S(1)} %get-tuple-element.161), channel_id=1, source_target_pairs={{0,4},{4,0},{8,12},{12,8},{16,20},{20,16},{24,28},{28,24},{1,5},{5... | collective-permute-start | bytes 1572872 | tf_op jit(solution)/shard_map/ppermute | solution.py:47
  114.3 16.9 %collective-permute-start.27 = (bf16[1136,256]{1,0:T(8,128)(2,1)S(1)}, bf16[1136,256]{1,0:T(8,128)(2,1)S(1)}, u32[]{:S(2)}, u32[]{:S(2)}) collective-permute-start(bf16[1136,256]{1,0:T(8,128)(2,1)S(1)} %get-tuple-element.135.refs_4_), channel_id=1, source_target_pairs={{0,8},{4,12},{8,0},{12,4},{16,24},{20,28},{24,16},{28,20},{1,9},{5... | collective-permute-start | bytes 1744904 | tf_op jit(solution)/shard_map/ppermute | solution.py:47
  115.9 24.2 %collective-permute-start.20 = (bf16[1024,256]{1,0:T(8,128)(2,1)S(1)}, bf16[1024,256]{1,0:T(8,128)(2,1)S(1)}, u32[]{:S(2)}, u32[]{:S(2)}) collective-permute-start(bf16[1024,256]{1,0:T(8,128)(2,1)S(1)} %get-tuple-element.136.refs_3_.refs_9_), channel_id=1, source_target_pairs={{0,4},{4,0},{8,12},{12,8},{16,20},{20,16},{24,28},{28,24},{1,5},{5... | collective-permute-start | bytes 1572872 | tf_op jit(solution)/shard_map/ppermute | solution.py:47
  116.8 15.6 %collective-permute-start.18 = (bf16[14,8,512]{2,1,0:T(8,128)(2,1)S(1)}, bf16[14,8,512]{2,1,0:T(8,128)(2,1)S(1)}, u32[]{:S(2)}, u32[]{:S(2)}) collective-permute-start(bf16[14,8,512]{2,1,0:T(8,128)(2,1)S(1)} %get-tuple-element.137), channel_id=1, source_target_pairs={{0,1},{1,2},{2,3},{4,5},{5,6},{6,7},{8,9},{9,10},{10,11},{12,13},{... | collective-permute-start | bytes 344072 | tf_op jit(solution)/shard_map/ppermute | solution.py:119
  118.2 11.4 %collective-permute-start.21 = (bf16[64,256]{1,0:T(8,128)(2,1)S(1)}, bf16[64,256]{1,0:T(8,128)(2,1)S(1)}, u32[]{:S(2)}, u32[]{:S(2)}) collective-permute-start(bf16[64,256]{1,0:T(8,128)(2,1)S(1)} %get-tuple-element.143), channel_id=1, source_target_pairs={{0,1},{1,0},{2,3},{3,2},{4,5},{5,4},{6,7},{7,6},{8,9},{9,8},{10,11... | collective-permute-start | bytes 98312 | tf_op jit(solution)/shard_map/ppermute | solution.py:47
  128.1 5.4 %collective-permute-start.19 = (bf16[14,8,512]{2,1,0:T(8,128)(2,1)S(1)}, bf16[14,8,512]{2,1,0:T(8,128)(2,1)S(1)}, u32[]{:S(2)}, u32[]{:S(2)}) collective-permute-start(bf16[14,8,512]{2,1,0:T(8,128)(2,1)S(1)} %get-tuple-element.138), channel_id=1, source_target_pairs={{1,0},{2,1},{3,2},{5,4},{6,5},{7,6},{9,8},{10,9},{11,10},{13,12},{... | collective-permute-start | bytes 344072 | tf_op jit(solution)/shard_map/ppermute | solution.py:119
  129.5 13.2 %collective-permute-start.34 = (bf16[512,256]{1,0:T(8,128)(2,1)S(1)}, bf16[512,256]{1,0:T(8,128)(2,1)S(1)}, u32[]{:S(2)}, u32[]{:S(2)}) collective-permute-start(bf16[512,256]{1,0:T(8,128)(2,1)S(1)} %get-tuple-element.163), channel_id=1, source_target_pairs={{0,8},{4,12},{8,0},{12,4},{16,24},{20,28},{24,16},{28,20},{1,9},{5... | collective-permute-start | bytes 786440 | tf_op jit(solution)/shard_map/ppermute | solution.py:47
  131.2 8.9 %collective-permute-start.22 = (bf16[64,256]{1,0:T(8,128)(2,1)S(1)}, bf16[64,256]{1,0:T(8,128)(2,1)S(1)}, u32[]{:S(2)}, u32[]{:S(2)}) collective-permute-start(bf16[64,256]{1,0:T(8,128)(2,1)S(1)} %add.23.refs_2_), channel_id=1, source_target_pairs={{0,4},{4,0},{8,12},{12,8},{16,20},{20,16},{24,28},{28,24},{1,5},{5... | collective-permute-start | bytes 98312 | tf_op jit(solution)/shard_map/ppermute | solution.py:47
  132.5 12.9 %collective-permute-start.28 = (bf16[624,256]{1,0:T(8,128)(2,1)S(1)}, bf16[624,256]{1,0:T(8,128)(2,1)S(1)}, u32[]{:S(2)}, u32[]{:S(2)}) collective-permute-start(bf16[624,256]{1,0:T(8,128)(2,1)S(1)} %get-tuple-element.153), channel_id=1, source_target_pairs={{0,4},{4,0},{8,12},{12,8},{16,20},{20,16},{24,28},{28,24},{1,5},{5... | collective-permute-start | bytes 958472 | tf_op jit(solution)/shard_map/ppermute | solution.py:47
  140.1 1.0 copy-start
  141.2 15.2 %collective-permute-start.23 = (bf16[576,256]{1,0:T(8,128)(2,1)S(1)}, bf16[576,256]{1,0:T(8,128)(2,1)S(1)}, u32[]{:S(2)}, u32[]{:S(2)}) collective-permute-start(bf16[576,256]{1,0:T(8,128)(2,1)S(1)} %get-tuple-element.145), channel_id=1, source_target_pairs={{0,8},{4,12},{8,0},{12,4},{16,24},{20,28},{24,16},{28,20},{1,9},{5... | collective-permute-start | bytes 884744 | tf_op jit(solution)/shard_map/ppermute | solution.py:47
  142.8 13.7 %collective-permute-start.35 = (bf16[256,256]{1,0:T(8,128)(2,1)S(1)}, bf16[256,256]{1,0:T(8,128)(2,1)S(1)}, u32[]{:S(2)}, u32[]{:S(2)}) collective-permute-start(bf16[256,256]{1,0:T(8,128)(2,1)S(1)} %get-tuple-element.165), channel_id=1, source_target_pairs={{0,16},{4,20},{8,24},{12,28},{16,0},{20,4},{24,8},{28,12},{1,17},{... | collective-permute-start | bytes 393224 | tf_op jit(solution)/shard_map/ppermute | solution.py:47
  145.5 18.5 %collective-permute-start.29 = (bf16[368,256]{1,0:T(8,128)(2,1)S(1)}, bf16[368,256]{1,0:T(8,128)(2,1)S(1)}, u32[]{:S(2)}, u32[]{:S(2)}) collective-permute-start(bf16[368,256]{1,0:T(8,128)(2,1)S(1)} %get-tuple-element.155), channel_id=1, source_target_pairs={{0,16},{4,20},{8,24},{12,28},{16,0},{20,4},{24,8},{28,12},{1,17},{... | collective-permute-start | bytes 565256 | tf_op jit(solution)/shard_map/ppermute | solution.py:47
  156.4 10.2 %collective-permute-start.24 = (bf16[320,256]{1,0:T(8,128)(2,1)S(1)}, bf16[320,256]{1,0:T(8,128)(2,1)S(1)}, u32[]{:S(2)}, u32[]{:S(2)}) collective-permute-start(bf16[320,256]{1,0:T(8,128)(2,1)S(1)} %get-tuple-element.147), channel_id=1, source_target_pairs={{0,16},{4,20},{8,24},{12,28},{16,0},{20,4},{24,8},{28,12},{1,17},{... | collective-permute-start | bytes 491528 | tf_op jit(solution)/shard_map/ppermute | solution.py:47
  156.6 10.5 %collective-permute-start.36 = (bf16[1,256,256]{2,1,0:T(8,128)(2,1)S(1)}, bf16[1,256,256]{2,1,0:T(8,128)(2,1)S(1)}, u32[]{:S(2)}, u32[]{:S(2)}) collective-permute-start(bf16[1,256,256]{2,1,0:T(8,128)(2,1)S(1)} %add_bitcast_fusion), channel_id=1, source_target_pairs={{0,2},{1,3},{2,0},{3,1},{4,6},{5,7},{6,4},{7,5},{8,10},{9,11},{10,... | collective-permute-start | bytes 393224 | tf_op jit(solution)/shard_map/ppermute | solution.py:47
  164.0 6.7 %collective-permute-start.30 = (bf16[368,256]{1,0:T(8,128)(2,1)S(1)}, bf16[368,256]{1,0:T(8,128)(2,1)S(1)}, u32[]{:S(2)}, u32[]{:S(2)}) collective-permute-start(bf16[368,256]{1,0:T(8,128)(2,1)S(1)} %add.26), channel_id=1, source_target_pairs={{0,2},{1,3},{2,0},{3,1},{4,6},{5,7},{6,4},{7,5},{8,10},{9,11},{10,... | collective-permute-start | bytes 565256 | tf_op jit(solution)/shard_map/ppermute | solution.py:47
  166.7 6.5 %collective-permute-start.25 = (bf16[320,256]{1,0:T(8,128)(2,1)S(1)}, bf16[320,256]{1,0:T(8,128)(2,1)S(1)}, u32[]{:S(2)}, u32[]{:S(2)}) collective-permute-start(bf16[320,256]{1,0:T(8,128)(2,1)S(1)} %add.24), channel_id=1, source_target_pairs={{0,2},{1,3},{2,0},{3,1},{4,6},{5,7},{6,4},{7,5},{8,10},{9,11},{10,... | collective-permute-start | bytes 491528 | tf_op jit(solution)/shard_map/ppermute | solution.py:47
  167.1 8.5 %collective-permute-start.37 = (bf16[2,256,256]{2,1,0:T(8,128)(2,1)S(1)}, bf16[2,256,256]{2,1,0:T(8,128)(2,1)S(1)}, u32[]{:S(2)}, u32[]{:S(2)}) collective-permute-start(bf16[2,256,256]{2,1,0:T(8,128)(2,1)S(1)} %maximum_bitcast_fusion.refs_0_), channel_id=1, source_target_pairs={{0,1},{1,0},{2,3},{3,2},{4,5},{5,4},{6,7},{7,6},{8,9},{9,8},{10,11... | collective-permute-start | bytes 786440 | tf_op jit(solution)/shard_map/ppermute | solution.py:47
  170.8 2.5 %collective-permute-start.31 = (bf16[368,256]{1,0:T(8,128)(2,1)S(1)}, bf16[368,256]{1,0:T(8,128)(2,1)S(1)}, u32[]{:S(2)}, u32[]{:S(2)}) collective-permute-start(bf16[368,256]{1,0:T(8,128)(2,1)S(1)} %add.27.refs_0_), channel_id=1, source_target_pairs={{0,1},{1,0},{2,3},{3,2},{4,5},{5,4},{6,7},{7,6},{8,9},{9,8},{10,11... | collective-permute-start | bytes 565256 | tf_op jit(solution)/shard_map/ppermute | solution.py:47
  173.2 1.5 collective-permute-start.26

commit v4 on v3

--- a/solution.py
+++ b/solution.py
@@ -55,7 +55,7 @@
     return (lax.axis_index(axis) // bit) % 2
 
 
-def chain(keep, send, order, count, rows, extra=(), after=()):
+def chain(keep, send, order, count, rows, extra=(), between=None):
     for place, (axis, bit, _) in enumerate(order):
         received = swap(send, axis, bit)
         if place + 1 == len(order):
@@ -70,8 +70,9 @@
             "sum_step",
             (keep, received, *grown),
             (out, out),
-            after=after if place == 0 else (),
+            after=between(send) if between and place == 1 else (),
             limit=8,
+            us=0.2,
         )
 
 
@@ -495,25 +496,36 @@
     gain_part[...] = part
 
 
-def patch_product_kernel(factor, early, early_other, own, other, keep, send):
+def patch_product_kernel(factor, slices, channels, early, early_other, own, other, *outs):
+    upper_keep, upper_send, lower_keep, lower_send = outs
     blocks, quarter, _ = own.shape
-    rows = keep.shape[0] // max(blocks // 2, 1)
-    channels = rows // 4
+    part = 4 * channels // slices // 2
     at_patches = early.shape[1] - channels
-    bit = (lax.axis_index("col") // 2) % 2
+    lateral = (lax.axis_index("col") // 2) % 2
+    vertical = lax.axis_index("row") % 2
+    per = channels // (2 * part)
     for j in range(4):
         span = slice(j * quarter, (j + 1) * quarter)
         left = jnp.concatenate([early[span, at_patches:], early_other[span, at_patches:]], axis=0)
         for m in range(blocks):
             right = jnp.concatenate([own[m], other[m]], axis=0)
             value = (factor * dot_first(left, right)).astype(BF)
-            at = m // 2 * rows + j * channels
             for i in range(2):
 
-                @pl.when(bit == i)
+                @pl.when(lateral == i)
                 def _():
-                    target = keep if m % 2 == i else send
-                    target[at : at + channels] = value
+                    target = upper_keep if m % 2 == i else upper_send
+                    for k in range(per):
+                        at = (m // 2 * slices + j * per + k) * part
+                        target[at : at + part] = value[2 * k * part : (2 * k + 1) * part]
+
+                @pl.when(vertical == i)
+                def _():
+                    for k in range(per):
+                        r = j * per + k
+                        target = lower_keep if r % 2 == i else lower_send
+                        at = (m * (slices // 2) + r // 2) * part
+                        target[at : at + part] = value[(2 * k + 1) * part : (2 * k + 2) * part]
 
 
 def store_slices(position, value, begin, offset, rows, pitch, keep, send):
@@ -777,15 +789,17 @@
             pltpu.VMEM((8, channels), F32),
         ),
         limit=16,
+        us=0.8,
     )
     branch_other = swap(branch_send, "col", 1)
-    patch_half = shape_of(block_count // 2 * 4 * channels, block, dtype=BF)
-    patch_keep, patch_send = run(
-        functools.partial(patch_product_kernel, scale_four),
+    patch_part = shape_of(block_count // 2 * 2 * channels, block, dtype=BF)
+    upper_keep, upper_send, lower_keep, lower_send = run(
+        functools.partial(patch_product_kernel, scale_four, row_count, channels),
         "patch_product",
         (early, early_other, flat_keep, flat_other),
-        (patch_half, patch_half),
+        (patch_part,) * 4,
         limit=16,
+        us=1,
     )
     deep, shallow = hidden_width // row_count, channels // row_count
     groups = hidden_width // channels
@@ -808,8 +822,9 @@
             pltpu.VMEM((pixels, hidden_width), BF),
             pltpu.VMEM((pixels, channels), F32),
         ),
-        after=(patch_send,),
+        after=(upper_send,),
         limit=16,
+        us=1.2,
     )
     rows_back = neighbours(first, last, "row")
     upward_other = swap(upward_send, "col", 1)
@@ -820,6 +835,7 @@
         (project_half, project_half),
         after=(upward_send,),
         limit=16,
+        us=0.9,
     )
     expand_half = shape_of(row_count // 2 * groups * shallow, half, dtype=BF)
     expand_keep, expand_send = run(
@@ -829,6 +845,7 @@
         (expand_half, expand_half),
         after=(project_send,),
         limit=16,
+        us=0.6,
     )
     framed_back = halo(grad_mixed, rows_back, "strips_back", after=(expand_send,))
     small_half = shape_of(64, half, dtype=BF)
@@ -844,24 +861,32 @@
         ),
         after=(*framed_back[1:3], expand_send),
         limit=12,
-    )
-    (input_grad,) = run(
-        input_kernel,
-        "input_grad",
-        (*framed_back, taps_three, grad_summed),
-        (shape_of(height, breadth, channels, dtype=BF),),
-        scratch=(frame_scratch(center), pltpu.VMEM((height, breadth, channels), F32)),
-        after=(small_keep,),
-        limit=12,
-    )
+        us=1.8,
+    )
+    def finish_input(sent):
+        return run(
+            input_kernel,
+            "input_grad",
+            (*framed_back, taps_three, grad_summed),
+            (shape_of(height, breadth, channels, dtype=BF),),
+            scratch=(frame_scratch(center), pltpu.VMEM((height, breadth, channels), F32)),
+            after=(small_keep, sent),
+            limit=12,
+            us=2,
+        )
 
     row_bits, col_bits = axis_bits("row"), axis_bits("col")
     outer = len(row_bits)
     low_first = [("row", bit, 0) for bit in row_bits]
-    patch_order = [("col", bit, outer) for bit in col_bits[1:]] + low_first
-    patch_sum = chain(
-        patch_keep, patch_send, patch_order, block_count * row_count, 4 * channels // row_count,
-        after=(small_keep,),
+    lateral = [("col", bit, outer) for bit in col_bits[1:]]
+    upper_order = lateral + low_first
+    lower_order = low_first[:1] + [("col", bit, outer - 1) for bit in col_bits[1:]] + low_first[1:]
+    part_rows = 2 * channels // row_count
+    patch_sum = jnp.concatenate(
+        [
+            chain(upper_keep, upper_send, upper_order, block_count * row_count, part_rows),
+            chain(lower_keep, lower_send, lower_order, block_count * row_count, part_rows),
+        ]
     )
     patch_sum = gather(patch_sum, "col", col_bits[1:])
     (patch_grad,) = run(
@@ -872,32 +897,40 @@
         limit=8,
     )
 
-    def share(keep, send, order, rows, extra=(), after=()):
-        total = chain(keep, send, order, row_count, rows, extra, after)
+    def share(total):
         for bit in col_bits[1:]:
             total = total + swap(total, "col", bit)
         return total, swap(total, "col", 1)
 
+    project_order = [("row", row_bits[1], 1), low_first[0], *low_first[2:]]
     vector, wide_vector = shape_of(1, channels), shape_of(1, wide)
     project_grad, wide_taps, wide_gain, merge_sum, layer_sum = run(
         finish_project_kernel,
         "finish_project",
-        share(project_keep, project_send, [("row", row_bits[1], 1), low_first[0], *low_first[2:]], deep),
+        share(chain(project_keep, project_send, project_order, row_count, deep)),
         (shape_of(deep, channels), shape_of(7, 7, wide), wide_vector, vector, vector),
         scratch=(pltpu.VMEM((112, channels), F32),),
         limit=8,
     )
     small = small_keep + swap(small_send, "col", 1)
+    pair = (small, swap(small, "row", 1))
+    input_grad = []
+
+    def between(sent):
+        input_grad.extend(finish_input(sent))
+        return input_grad
+
+    expand_sum = chain(expand_keep, expand_send, low_first, row_count, groups * shallow, pair, between)
     expand_grad, taps_sum, gain_sum = run(
         finish_expand_kernel,
         "finish_expand",
-        share(expand_keep, expand_send, low_first, groups * shallow, (small, swap(small, "row", 1)), (input_grad,)),
+        share(expand_sum),
         (shape_of(shallow, hidden_width), shape_of(7, 7, channels), vector),
         scratch=(pltpu.VMEM((64, channels), F32),),
         limit=8,
     )
     return (
-        input_grad[None],
+        input_grad[0][None],
         taps_sum,
         gain_sum[0],
         expand_grad,

time: 177 us -> 181 us (1.023)
  starting transfers between devices: 59.5 us -> 69.3 us
  waiting for transfers between devices: 58.8 us -> 50.1 us
    ppermute x22 -> x26, waiting for transfers between devices: 40.5 us -> 23.5 us  [swap(): lax.ppermute(values, axis, [(i, i ^ bit) for i in range(lax.axis_size(axi...]
    ppermute x22 -> x26, starting transfers between devices: 20.5 us -> 29.8 us  [swap(): lax.ppermute(values, axis, [(i, i ^ bit) for i in range(lax.axis_size(axi...]
    ppermute x8, waiting for transfers between devices: 2.68 us -> 11.7 us  [neighbours(): lax.ppermute(last, axis, forward)]
    pallas_call x26 -> x29, Pallas kernels: 51 us -> 51.7 us  [run(): pl.pallas_call(inner, name=name, out_shape=outs, in_specs=[spec(i) for i...]
    unnamed x26 -> x30, local copies, waits for them, and re-layouts: 4.87 us -> 4.88 us
  transfers between devices with their start and end apart: 38 -> 42, of which waited for: 20 -> 17; matrix products, arithmetic and copies ran while one was open for 0% -> 1% of each run, Pallas kernels for 16% -> 18%
where the time goes in v4:
time: 181 us; the launch traced here: 180 us
  starting transfers between devices  69.3 us (38%)
  Pallas kernels  51.7 us (29%)
  waiting for transfers between devices  50.1 us (28%)
  local copies, waits for them, and re-layouts  5.88 us (3%)
  other arithmetic  2 us (1%)
    pallas_call x29, Pallas kernels, run(): pl.pallas_call(inner, name=name, out_shape=outs, in_specs=[spec(i) for i...  51.7 us
    ppermute x26, starting transfers between devices, swap(): lax.ppermute(values, axis, [(i, i ^ bit) for i in range(lax.axis_size(axi...  29.8 us
    ppermute x8, starting transfers between devices, neighbours(): lax.ppermute(last, axis, forward)  29 us
    ppermute x26, waiting for transfers between devices, swap(): lax.ppermute(values, axis, [(i, i ^ bit) for i in range(lax.axis_size(axi...  23.5 us
    ppermute x8, waiting for transfers between devices, neighbours(): lax.ppermute(first, axis, backward)  14.8 us
    ppermute x8, waiting for transfers between devices, neighbours(): lax.ppermute(last, axis, forward)  11.7 us
    ppermute x8, starting transfers between devices, neighbours(): lax.ppermute(first, axis, backward)  10.5 us
    unnamed x30, local copies, waits for them, and re-layouts  4.88 us
  transfers between devices with their start and end apart: 42, of which 17 were waited for; matrix products, arithmetic and copies ran while one was open for 1% of the time, Pallas kernels for 18%

profile of v4, /device:TPU:0, one launch (start us, length us, event | category | flops | bytes accessed | tf_op | source)
XLA Modules:
  0.0 180.2 jit_solution(16973277896951563873)
XLA Ops:
  0.7 1.0 slice_bitcast_fusion
  1.7 4.8 %collective-permute-start = (bf16[3,32,512]{2,1,0:T(8,128)(2,1)S(1)}, bf16[3,32,512]{2,1,0:T(8,128)(2,1)S(1)}, u32[]{:S(2)}, u32[]{:S(2)}) collective-permute-start(bf16[3,32,512]{2,1,0:T(8,128)(2,1)S(1)} %get-tuple-element.187), channel_id=1, source_target_pairs={{0,4},{4,8},{8,12},{12,16},{16,20},{20,24},{24,28},{1,5},{5,9},{9,... | collective-permute-start | bytes 294920 | tf_op jit(solution)/shard_map/ppermute | solution.py:120
  6.5 1.3 collective-permute-start.1
  7.8 0.9 collective-permute-done.refs_5_.refs_1_
  8.7 0.9 copy-done.1
  9.7 0.9 copy-done.8
  10.6 0.7 copy-done.10
  13.1 1.6 collective-permute-start.2
  14.6 1.4 collective-permute-start.3
  16.1 3.5 %collective-permute-done.3.refs_4_ = bf16[14,8,512]{2,1,0:T(8,128)(2,1)S(1)} collective-permute-done((bf16[14,8,512]{2,1,0:T(8,128)(2,1)S(1)}, bf16[14,8,512]{2,1,0:T(8,128)(2,1)S(1)}, u32[]{:S(2)}, u32[]{:S(2)}) %collective-permute-start.3) | collective-permute-done | bytes 114720 | tf_op jit(solution)/shard_map/ppermute | solution.py:120
  19.6 12.8 %front.1 = (bf16[256,3072]{1,0:T(8,128)(2,1)S(1)}, f32[256,512]{1,0:T(8,128)S(1)}, f32[256,1]{1,0:T(8,128)S(1)}, bf16[256,2048]{1,0:T(8,128)(2,1)S(1)}, f32[256,...) custom-call(bf16[8,32,512]{2,1,0:T(8,128)(2,1)S(1)} %get-tuple-eleme, ...), custom_call_target="tpu_custom_call" | custom-call | flops 13200001024 | bytes 1000 | tf_op jit(solution)/shard_map/front/pallas_call | solution.py:33
  32.5 4.4 %collective-permute-start.4 = (bf16[3,16,1024]{2,1,0:T(8,128)(2,1)S(1)}, bf16[3,16,1024]{2,1,0:T(8,128)(2,1)S(1)}, u32[]{:S(2)}, u32[]{:S(2)}) collective-permute-start(bf16[3,16,1024]{2,1,0:T(8,128)(2,1)S(1)} %get-tuple-element.105), channel_id=1, source_target_pairs={{0,4},{4,8},{8,12},{12,16},{16,20},{20,24},{24,28},{1,5},{5,9},{9,... | collective-permute-start | bytes 294920 | tf_op jit(solution)/shard_map/ppermute | solution.py:120
  36.8 1.3 collective-permute-start.5
  38.1 0.9 collective-permute-done.4.refs_1_
  39.0 4.6 %collective-permute-done.5.refs_2_ = bf16[3,16,1024]{2,1,0:T(8,128)(2,1)S(1)} collective-permute-done((bf16[3,16,1024]{2,1,0:T(8,128)(2,1)S(1)}, bf16[3,16,1024]{2,1,0:T(8,128)(2,1)S(1)}, u32[]{:S(2)}, u32[]{:S(2)}) %collective-permute-start.5) | collective-permute-done | bytes 98336 | tf_op jit(solution)/shard_map/ppermute | solution.py:120
  43.6 4.2 %collective-permute-start.6 = (bf16[10,8,1024]{2,1,0:T(8,128)(2,1)S(1)}, bf16[10,8,1024]{2,1,0:T(8,128)(2,1)S(1)}, u32[]{:S(2)}, u32[]{:S(2)}) collective-permute-start(bf16[10,8,1024]{2,1,0:T(8,128)(2,1)S(1)} %get-tuple-element.107), channel_id=1, source_target_pairs={{0,1},{1,2},{2,3},{4,5},{5,6},{6,7},{8,9},{9,10},{10,11},{12,13},{... | collective-permute-start | bytes 491528 | tf_op jit(solution)/shard_map/ppermute | solution.py:120
  47.8 1.3 collective-permute-start.7
  49.1 2.5 %collective-permute-done.7.refs_4_ = bf16[10,8,1024]{2,1,0:T(8,128)(2,1)S(1)} collective-permute-done((bf16[10,8,1024]{2,1,0:T(8,128)(2,1)S(1)}, bf16[10,8,1024]{2,1,0:T(8,128)(2,1)S(1)}, u32[]{:S(2)}, u32[]{:S(2)}) %collective-permute-start.7) | collective-permute-done | bytes 163872 | tf_op jit(solution)/shard_map/ppermute | solution.py:120
  51.6 3.3 %mixer.1 = (f32[4,16,1024]{2,1,0:T(8,128)S(1)}, bf16[4,16,1024]{2,1,0:T(8,128)(2,1)S(1)}, bf16[3,16,1024]{2,1,0:T(8,128)(2,1)S(1)}, bf16[3,16,1024]{2,1,0:T(8,128)(2,1)S(1)}, f32[1,1024]{1,0:T(1,128)S(1)}) custom-call(bf16[4,16,1024]{2,1,0:T(8,128)(2,1)S(1)} %get-tuple-element.104.refs_0_, bf16[3,16,1024]{2,1,0:T(8,128)(2,1)S(1)} %collective-permute-done.4.refs_1_, ...), custom_call_target="tpu_custom_call" | custom-call | flops 3300001024 | bytes 1000 | tf_op jit(solution)/shard_map/mixer/pallas_call | solution.py:33
  54.9 4.8 %collective-permute-start.8 = (bf16[3,16,1024]{2,1,0:T(8,128)(2,1)S(1)}, bf16[3,16,1024]{2,1,0:T(8,128)(2,1)S(1)}, u32[]{:S(2)}, u32[]{:S(2)}) collective-permute-start(bf16[3,16,1024]{2,1,0:T(8,128)(2,1)S(1)} %get-tuple-element.113), channel_id=1, source_target_pairs={{0,4},{4,8},{8,12},{12,16},{16,20},{20,24},{24,28},{1,5},{5,9},{9,... | collective-permute-start | bytes 294920 | tf_op jit(solution)/shard_map/ppermute | solution.py:120
  59.8 1.3 collective-permute-start.9
  61.1 0.9 collective-permute-done.8.refs_6_.refs_1_
  62.0 2.9 %mixer_weights.1.refs_3_.refs_7_ = f32[49,1024]{1,0:T(8,128)S(1)} custom-call(bf16[4,16,1024]{2,1,0:T(8,128)(2,1)S(1)} %get-tuple-element.104.refs_0_, bf16[3,16,1024]{2,1,0:T(8,128)(2,1)S(1)} %collective-permute-done.4.refs_1_, bf16[3,16,1024]{2,1,0:T(8,128)(2,1)S(1)} %collective-permute-done.5.refs_2_, ...), custom_call_target="tpu_custom_call" | custom-call | flops 3300001024 | bytes 1000 | tf_op jit(solution)/shard_map/mixer_weights/pallas_call | solution.py:33
  64.8 1.4 collective-permute-done.9.refs_2_
  66.3 4.5 %collective-permute-start.10 = (bf16[10,8,1024]{2,1,0:T(8,128)(2,1)S(1)}, bf16[10,8,1024]{2,1,0:T(8,128)(2,1)S(1)}, u32[]{:S(2)}, u32[]{:S(2)}) collective-permute-start(bf16[10,8,1024]{2,1,0:T(8,128)(2,1)S(1)} %get-tuple-element.116), channel_id=1, source_target_pairs={{0,1},{1,2},{2,3},{4,5},{5,6},{6,7},{8,9},{9,10},{10,11},{12,13},{... | collective-permute-start | bytes 491528 | tf_op jit(solution)/shard_map/ppermute | solution.py:120
  70.8 1.3 collective-permute-start.11
  72.1 2.6 %collective-permute-done.11.refs_4_ = bf16[10,8,1024]{2,1,0:T(8,128)(2,1)S(1)} collective-permute-done((bf16[10,8,1024]{2,1,0:T(8,128)(2,1)S(1)}, bf16[10,8,1024]{2,1,0:T(8,128)(2,1)S(1)}, u32[]{:S(2)}, u32[]{:S(2)}) %collective-permute-start.11) | collective-permute-done | bytes 163872 | tf_op jit(solution)/shard_map/ppermute | solution.py:120
  74.7 3.1 %section_grad.1 = (bf16[64,1024]{1,0:T(8,128)(2,1)S(1)}, bf16[2,64,256]{2,1,0:T(8,128)(2,1)S(1)}, bf16[2,64,256]{2,1,0:T(8,128)(2,1)S(1)}, bf16[256,3072]{1,0:T(8,128)(2,1)S(1)}) custom-call(bf16[4,16,1024]{2,1,0:T(8,128)(2,1)S(1)} %get-tuple-element.112.refs_0_, ...), custom_call_target="tpu_custom_call", output_to_operand_aliasing={{3}: (7, {})} | custom-call | flops 3300001024 | bytes 1000 | tf_op jit(solution)/shard_map/section_grad/pallas_call | solution.py:33
  77.8 3.9 %collective-permute-start.12 = (bf16[256,3072]{1,0:T(8,128)(2,1)S(1)}, bf16[256,3072]{1,0:T(8,128)(2,1)S(1)}, u32[]{:S(2)}, u32[]{:S(2)}) collective-permute-start(bf16[256,3072]{1,0:T(8,128)(2,1)S(1)} %get-tuple-element.132.refs_0_), channel_id=1, source_target_pairs={{0,1},{1,0},{2,3},{3,2},{4,5},{5,4},{6,7},{7,6},{8,9},{9,8},{10,11... | collective-permute-start | bytes 4718600 | tf_op jit(solution)/shard_map/ppermute | solution.py:47
  81.8 2.5 %merge_back.1 = (f32[256,512]{1,0:T(8,128)S(1)}, bf16[256,512]{1,0:T(8,128)(2,1)S(1)}, bf16[368,256]{1,0:T(8,128)(2,1)S(1)}, bf16[368,256]{1,0:T(8,128)(2,1)S(1)}) custom-call(bf16[64,1024]{1,0:T(8,128)(2,1)S(1)} %get-tuple-element.120.refs_0_, bf16[2048,1024]{1,0:T(8,128)(2,1)S(1)} %get-tuple-element.121.refs_1_, ...), custom_call_target="tpu_custom_call" | custom-call | flops 880001024 | bytes 1000 | tf_op jit(solution)/shard_map/merge_back/pallas_call | solution.py:33
  84.8 2.6 %patch_product.1 = (bf16[1024,256]{1,0:T(8,128)(2,1)S(1)}, bf16[1024,256]{1,0:T(8,128)(2,1)S(1)}, bf16[1024,256]{1,0:T(8,128)(2,1)S(1)}, bf16[1024,256]{1,0:T(8,128)(2,1)S(1)}) custom-call(bf16[256,3072]{1,0:T(8,128)(2,1)S(1)} %get-tuple-element.132.refs_0_, bf16[256,3072]{1,0:T(8,128)(2,1)S(1)} %collective-permute-done.12.refs_1_, ...), custom_call_target="tpu_custom_call" | custom-call | flops 1100001024 | bytes 1000 | tf_op jit(solution)/shard_map/patch_product/pallas_call | solution.py:33
  87.5 1.1 collective-permute-start.36
  88.7 3.2 %mlp_back.1 = (bf16[256,1024]{1,0:T(8,128)(2,1)S(1)}, bf16[256,1024]{1,0:T(8,128)(2,1)S(1)}, bf16[8,32,512]{2,1,0:T(8,128)(2,1)S(1)}, bf16[3,32,512]{2,1,0:T(8,1...) custom-call(bf16[256,512]{1,0:T(8,128)(2,1)S(1)} %get-tuple-element.126.refs_0_, ...), custom_call_target="tpu_custom_call" | custom-call | flops 1320001024 | bytes 1000 | tf_op jit(solution)/shard_map/mlp_back/pallas_call | solution.py:33
  92.0 2.6 %project_product.1 = (bf16[1136,256]{1,0:T(8,128)(2,1)S(1)}, bf16[1136,256]{1,0:T(8,128)(2,1)S(1)}) custom-call(bf16[256,3072]{1,0:T(8,128)(2,1)S(1)} %get-tuple-element.132.refs_0_, bf16[256,3072]{1,0:T(8,128)(2,1)S(1)} %collective-permute-done.12.refs_1_, bf16[368,256]{1,0:T(8,128)(2,1)S(1)} %get-tuple-element.141.refs_2_, ...), custom_call_target="tpu_custom_call" | custom-call | flops 990001024 | bytes 1000 | tf_op jit(solution)/shard_map/project_product/pallas_call | solution.py:33
  94.6 1.7 collective-permute-start.27
  96.3 5.4 %collective-permute-done.36.refs_1_ = bf16[1024,256]{1,0:T(8,128)(2,1)S(1)} collective-permute-done((bf16[1024,256]{1,0:T(8,128)(2,1)S(1)}, bf16[1024,256]{1,0:T(8,128)(2,1)S(1)}, u32[]{:S(2)}, u32[]{:S(2)}) %collective-permute-start.36) | collective-permute-done | bytes 524320 | tf_op jit(solution)/shard_map/ppermute | solution.py:47
  102.7 1.0 collective-permute-start.33
  103.7 1.9 %expand_product.1 = (bf16[1024,256]{1,0:T(8,128)(2,1)S(1)}, bf16[1024,256]{1,0:T(8,128)(2,1)S(1)}) custom-call(bf16[256,3072]{1,0:T(8,128)(2,1)S(1)} %get-tuple-element.132.refs_0_, bf16[256,3072]{1,0:T(8,128)(2,1)S(1)} %collective-permute-done.12.refs_1_, bf16[256,1024]{1,0:T(8,128)(2,1)S(1)} %get-tuple-element.139.refs_2_, ...), custom_call_target="tpu_custom_call" | custom-call | flops 660001024 | bytes 1000 | tf_op jit(solution)/shard_map/expand_product/pallas_call | solution.py:33
  105.6 1.1 collective-permute-start.20
  106.7 2.8 %collective-permute-start.14 = (bf16[3,32,512]{2,1,0:T(8,128)(2,1)S(1)}, bf16[3,32,512]{2,1,0:T(8,128)(2,1)S(1)}, u32[]{:S(2)}, u32[]{:S(2)}) collective-permute-start(bf16[3,32,512]{2,1,0:T(8,128)(2,1)S(1)} %get-tuple-element.137), channel_id=1, source_target_pairs={{0,4},{4,8},{8,12},{12,16},{16,20},{20,24},{24,28},{1,5},{5,9},{9,... | collective-permute-start | bytes 294920 | tf_op jit(solution)/shard_map/ppermute | solution.py:120
  110.2 1.3 collective-permute-start.15
  111.5 0.9 sum_step.12
  112.4 2.6 %collective-permute-start.28 = (bf16[624,256]{1,0:T(8,128)(2,1)}, bf16[624,256]{1,0:T(8,128)(2,1)S(1)}, u32[]{:S(2)}, u32[]{:S(2)}) collective-permute-start(bf16[624,256]{1,0:T(8,128)(2,1)} %get-tuple-element.161), channel_id=1, source_target_pairs={{0,4},{4,0},{8,12},{12,8},{16,20},{20,16},{24,28},{28,24},{1,5},{5... | collective-permute-start | bytes 958472 | tf_op jit(solution)/shard_map/ppermute | solution.py:47
  115.1 1.7 collective-permute-start.38
  116.9 9.0 %collective-permute-done.14.refs_1_.refs_7_ = bf16[3,32,512]{2,1,0:T(8,128)(2,1)S(1)} collective-permute-done((bf16[3,32,512]{2,1,0:T(8,128)(2,1)S(1)}, bf16[3,32,512]{2,1,0:T(8,128)(2,1)S(1)}, u32[]{:S(2)}, u32[]{:S(2)}) %collective-permute-start.14) | collective-permute-done | bytes 98336 | tf_op jit(solution)/shard_map/ppermute | solution.py:120
  125.9 1.6 collective-permute-start.34
  127.5 5.4 %block_weights.1 = (bf16[64,256]{1,0:T(8,128)(2,1)S(1)}, bf16[64,256]{1,0:T(8,128)(2,1)S(1)}) custom-call(bf16[8,32,512]{2,1,0:T(8,128)(2,1)S(1)} %get-tuple-element.97.refs_0_, bf16[3,32,512]{2,1,0:T(8,128)(2,1)S(1)} %collective-permute-done.refs_5_.refs_1_, bf16[3,32,512]{2,1,0:T(8,128)(2,1)S(1)} %collective-permute-done.1.refs_2_, ...), custom_call_target="tpu_custom_call" | custom-call | flops 1980001024 | bytes 1000 | tf_op jit(solution)/shard_map/block_weights/pallas_call | solution.py:33
  132.9 2.5 %collective-permute-start.39 = (bf16[128,256]{1,0:T(8,128)(2,1)S(1)}, bf16[128,256]{1,0:T(8,128)(2,1)}, u32[]{:S(2)}, u32[]{:S(2)}) collective-permute-start(bf16[128,256]{1,0:T(8,128)(2,1)S(1)} %get-tuple-element.181), channel_id=1, source_target_pairs={{0,16},{4,20},{8,24},{12,28},{16,0},{20,4},{24,8},{28,12},{1,17},{... | collective-permute-start | bytes 196616 | tf_op jit(solution)/shard_map/ppermute | solution.py:47
  136.0 1.2 collective-permute-done.21
  137.2 2.5 %collective-permute-start.22 = (bf16[64,256]{1,0:T(8,128)(2,1)S(1)}, bf16[64,256]{1,0:T(8,128)(2,1)S(1)}, u32[]{:S(2)}, u32[]{:S(2)}) collective-permute-start(bf16[64,256]{1,0:T(8,128)(2,1)S(1)} %add.26.refs_2_), channel_id=1, source_target_pairs={{0,4},{4,0},{8,12},{12,8},{16,20},{20,16},{24,28},{28,24},{1,5},{5... | collective-permute-start | bytes 98312 | tf_op jit(solution)/shard_map/ppermute | solution.py:47
  139.8 1.9 %collective-permute-start.18 = (bf16[14,8,512]{2,1,0:T(8,128)(2,1)S(1)}, bf16[14,8,512]{2,1,0:T(8,128)(2,1)S(1)}, u32[]{:S(2)}, u32[]{:S(2)}) collective-permute-start(bf16[14,8,512]{2,1,0:T(8,128)(2,1)S(1)} %get-tuple-element.145), channel_id=1, source_target_pairs={{0,1},{1,2},{2,3},{4,5},{5,6},{6,7},{8,9},{9,10},{10,11},{12,13},{... | collective-permute-start | bytes 344072 | tf_op jit(solution)/shard_map/ppermute | solution.py:120
  141.9 1.3 collective-permute-start.19
  143.2 0.9 add.33
  144.0 1.1 collective-permute-start.29
  145.1 0.9 add.32
  146.2 2.1 %collective-permute-start.23 = (bf16[576,256]{1,0:T(8,128)(2,1)S(1)}, bf16[576,256]{1,0:T(8,128)(2,1)S(1)}, u32[]{:S(2)}, u32[]{:S(2)}) collective-permute-start(bf16[576,256]{1,0:T(8,128)(2,1)S(1)} %get-tuple-element.152.refs_8_), channel_id=1, source_target_pairs={{0,8},{4,12},{8,0},{12,4},{16,24},{20,28},{24,16},{28,20},{1,9},{5... | collective-permute-start | bytes 884744 | tf_op jit(solution)/shard_map/ppermute | solution.py:47
  148.3 4.0 %collective-permute-start.40 = (bf16[1,256,256]{2,1,0:T(8,128)(2,1)S(1)}, bf16[1,256,256]{2,1,0:T(8,128)(2,1)S(1)}, u32[]{:S(2)}, u32[]{:S(2)}) collective-permute-start(bf16[1,256,256]{2,1,0:T(8,128)(2,1)S(1)} %maximum_bitcast_fusion.1), channel_id=1, source_target_pairs={{0,2},{1,3},{2,0},{3,1},{4,6},{5,7},{6,4},{7,5},{8,10},{9,11},{10,... | collective-permute-start | bytes 393224 | tf_op jit(solution)/shard_map/ppermute | solution.py:47
  152.3 6.6 %input_grad.1.refs_2_ = bf16[8,32,512]{2,1,0:T(8,128)(2,1)} custom-call(bf16[8,32,512]{2,1,0:T(8,128)(2,1)S(1)} %get-tuple-element.136.refs_0_.refs_5_, bf16[3,32,512]{2,1,0:T(8,128)(2,1)S(1)} %collective-permute-done.14.refs_1_.refs_7_, bf16[3,32,512]{2,1,0:T(8,128)(2,1)S(1)} %collective-permute-done.15.refs_2_.refs_8_, ...), custom_call_target="tpu_custom_call" | custom-call | flops 2200001024 | bytes 1000 | tf_op jit(solution)/shard_map/input_grad/pallas_call | solution.py:33
  159.1 0.9 copy-done
  160.6 10.2 %collective-permute-done.24 = bf16[320,256]{1,0:T(8,128)(2,1)S(1)} collective-permute-done((bf16[320,256]{1,0:T(8,128)(2,1)S(1)}, bf16[320,256]{1,0:T(8,128)(2,1)S(1)}, u32[]{:S(2)}, u32[]{:S(2)}) %collective-permute-start.24) | collective-permute-done | bytes 163872 | tf_op jit(solution)/shard_map/ppermute | solution.py:47
  171.8 5.3 %collective-permute-done.25 = bf16[320,256]{1,0:T(8,128)(2,1)S(1)} collective-permute-done((bf16[320,256]{1,0:T(8,128)(2,1)S(1)}, bf16[320,256]{1,0:T(8,128)(2,1)S(1)}, u32[]{:S(2)}, u32[]{:S(2)}) %collective-permute-start.25) | collective-permute-done | bytes 163872 | tf_op jit(solution)/shard_map/ppermute | solution.py:47
  177.2 1.1 finish_patch.1
  178.3 1.0 finish_project.1
  179.3 0.9 finish_expand.1
  (90 shorter events, 7.1 us)
Async XLA Ops:
  0.6 19.0 %copy-start.6 = (bf16[1,4,16,1024]{3,2,1,0:T(8,128)(2,1)S(1)}, bf16[1,4,16,1024]{3,2,1,0:T(8,128)(2,1)}, u32[]{:S(2)}) copy-start(bf16[1,4,16,1024]{3,2,1,0:T(8,128)(2,1)} %param.22) | copy-start | bytes 393220
  0.7 19.0 %copy-start.7 = (bf16[1,4,16,1024]{3,2,1,0:T(8,128)(2,1)S(1)}, bf16[1,4,16,1024]{3,2,1,0:T(8,128)(2,1)}, u32[]{:S(2)}) copy-start(bf16[1,4,16,1024]{3,2,1,0:T(8,128)(2,1)} %param.23) | copy-start | bytes 393220
  0.7 18.9 %copy-start.9 = (f32[1024]{0:T(1024)S(1)}, f32[1024]{0:T(1024)}, u32[]{:S(2)}) copy-start(f32[1024]{0:T(1024)} %param.21) | copy-start | bytes 12292
  1.7 7.0 %collective-permute-start = (bf16[3,32,512]{2,1,0:T(8,128)(2,1)S(1)}, bf16[3,32,512]{2,1,0:T(8,128)(2,1)S(1)}, u32[]{:S(2)}, u32[]{:S(2)}) collective-permute-start(bf16[3,32,512]{2,1,0:T(8,128)(2,1)S(1)} %get-tuple-element.187), channel_id=1, source_target_pairs={{0,4},{4,8},{8,12},{12,16},{16,20},{20,24},{24,28},{1,5},{5,9},{9,... | collective-permute-start | bytes 294920 | tf_op jit(solution)/shard_map/ppermute | solution.py:120
  6.5 6.5 %collective-permute-start.1 = (bf16[3,32,512]{2,1,0:T(8,128)(2,1)S(1)}, bf16[3,32,512]{2,1,0:T(8,128)(2,1)S(1)}, u32[]{:S(2)}, u32[]{:S(2)}) collective-permute-start(bf16[3,32,512]{2,1,0:T(8,128)(2,1)S(1)} %get-tuple-element.186), channel_id=1, source_target_pairs={{4,0},{8,4},{12,8},{16,12},{20,16},{24,20},{28,24},{5,1},{9,5},{13... | collective-permute-start | bytes 294920 | tf_op jit(solution)/shard_map/ppermute | solution.py:120
  8.7 0.9 copy-start.1
  9.7 0.9 copy-start.8
  10.6 0.7 copy-start.10
  11.3 0.7 copy-start.11
  11.9 0.7 copy-start.12
  12.6 7.0 %copy-start.2 = (bf16[2048,1024]{1,0:T(8,128)(2,1)S(1)}, bf16[2048,1024]{1,0:T(8,128)(2,1)}, u32[]{:S(2)}) copy-start(bf16[2048,1024]{1,0:T(8,128)(2,1)} %refs_11_.1) | copy-start | bytes 12582916
  12.6 7.0 %copy-start.3 = (bf16[512,2048]{1,0:T(8,128)(2,1)S(1)}, bf16[512,2048]{1,0:T(8,128)(2,1)}, u32[]{:S(2)}) copy-start(bf16[512,2048]{1,0:T(8,128)(2,1)} %refs_9_.1) | copy-start | bytes 6291460
  12.6 7.0 %copy-start.4 = (bf16[2048,512]{1,0:T(8,128)(2,1)S(1)}, bf16[2048,512]{1,0:T(8,128)(2,1)}, u32[]{:S(2)}) copy-start(bf16[2048,512]{1,0:T(8,128)(2,1)} %refs_10_.1) | copy-start | bytes 6291460
  12.6 7.0 %copy-start.5 = (f32[7,7,1024]{2,1,0:T(8,128)S(1)}, f32[7,7,1024]{2,1,0:T(8,128)}, u32[]{:S(2)}) copy-start(f32[7,7,1024]{2,1,0:T(8,128)} %refs_12_.1) | copy-start | bytes 602116
  12.9 19.6 %copy-start.13 = (f32[7,7,512]{2,1,0:T(8,128)}, f32[7,7,512]{2,1,0:T(8,128)S(1)}, u32[]{:S(2)}) copy-start(f32[7,7,512]{2,1,0:T(8,128)S(1)} %get-tuple-element.100.refs_5_) | copy-start | bytes 301060
  13.1 3.0 %collective-permute-start.2 = (bf16[14,8,512]{2,1,0:T(8,128)(2,1)S(1)}, bf16[14,8,512]{2,1,0:T(8,128)(2,1)S(1)}, u32[]{:S(2)}, u32[]{:S(2)}) collective-permute-start(bf16[14,8,512]{2,1,0:T(8,128)(2,1)S(1)} %get-tuple-element.98), channel_id=1, source_target_pairs={{0,1},{1,2},{2,3},{4,5},{5,6},{6,7},{8,9},{9,10},{10,11},{12,13},{... | collective-permute-start | bytes 344072 | tf_op jit(solution)/shard_map/ppermute | solution.py:120
  14.6 5.0 %collective-permute-start.3 = (bf16[14,8,512]{2,1,0:T(8,128)(2,1)S(1)}, bf16[14,8,512]{2,1,0:T(8,128)(2,1)S(1)}, u32[]{:S(2)}, u32[]{:S(2)}) collective-permute-start(bf16[14,8,512]{2,1,0:T(8,128)(2,1)S(1)} %get-tuple-element.99), channel_id=1, source_target_pairs={{1,0},{2,1},{3,2},{5,4},{6,5},{7,6},{9,8},{10,9},{11,10},{13,12},{... | collective-permute-start | bytes 344072 | tf_op jit(solution)/shard_map/ppermute | solution.py:120
  32.5 6.6 %collective-permute-start.4 = (bf16[3,16,1024]{2,1,0:T(8,128)(2,1)S(1)}, bf16[3,16,1024]{2,1,0:T(8,128)(2,1)S(1)}, u32[]{:S(2)}, u32[]{:S(2)}) collective-permute-start(bf16[3,16,1024]{2,1,0:T(8,128)(2,1)S(1)} %get-tuple-element.105), channel_id=1, source_target_pairs={{0,4},{4,8},{8,12},{12,16},{16,20},{20,24},{24,28},{1,5},{5,9},{9,... | collective-permute-start | bytes 294920 | tf_op jit(solution)/shard_map/ppermute | solution.py:120
  36.8 6.7 %collective-permute-start.5 = (bf16[3,16,1024]{2,1,0:T(8,128)(2,1)S(1)}, bf16[3,16,1024]{2,1,0:T(8,128)(2,1)S(1)}, u32[]{:S(2)}, u32[]{:S(2)}) collective-permute-start(bf16[3,16,1024]{2,1,0:T(8,128)(2,1)S(1)} %get-tuple-element.106), channel_id=1, source_target_pairs={{4,0},{8,4},{12,8},{16,12},{20,16},{24,20},{28,24},{5,1},{9,5},{13... | collective-permute-start | bytes 294920 | tf_op jit(solution)/shard_map/ppermute | solution.py:120
  43.6 5.5 %collective-permute-start.6 = (bf16[10,8,1024]{2,1,0:T(8,128)(2,1)S(1)}, bf16[10,8,1024]{2,1,0:T(8,128)(2,1)S(1)}, u32[]{:S(2)}, u32[]{:S(2)}) collective-permute-start(bf16[10,8,1024]{2,1,0:T(8,128)(2,1)S(1)} %get-tuple-element.107), channel_id=1, source_target_pairs={{0,1},{1,2},{2,3},{4,5},{5,6},{6,7},{8,9},{9,10},{10,11},{12,13},{... | collective-permute-start | bytes 491528 | tf_op jit(solution)/shard_map/ppermute | solution.py:120
  47.8 3.8 %collective-permute-start.7 = (bf16[10,8,1024]{2,1,0:T(8,128)(2,1)S(1)}, bf16[10,8,1024]{2,1,0:T(8,128)(2,1)S(1)}, u32[]{:S(2)}, u32[]{:S(2)}) collective-permute-start(bf16[10,8,1024]{2,1,0:T(8,128)(2,1)S(1)} %get-tuple-element.108), channel_id=1, source_target_pairs={{1,0},{2,1},{3,2},{5,4},{6,5},{7,6},{9,8},{10,9},{11,10},{13,12},{... | collective-permute-start | bytes 491528 | tf_op jit(solution)/shard_map/ppermute | solution.py:120
  54.9 7.0 %collective-permute-start.8 = (bf16[3,16,1024]{2,1,0:T(8,128)(2,1)S(1)}, bf16[3,16,1024]{2,1,0:T(8,128)(2,1)S(1)}, u32[]{:S(2)}, u32[]{:S(2)}) collective-permute-start(bf16[3,16,1024]{2,1,0:T(8,128)(2,1)S(1)} %get-tuple-element.113), channel_id=1, source_target_pairs={{0,4},{4,8},{8,12},{12,16},{16,20},{20,24},{24,28},{1,5},{5,9},{9,... | collective-permute-start | bytes 294920 | tf_op jit(solution)/shard_map/ppermute | solution.py:120
  59.8 6.5 %collective-permute-start.9 = (bf16[3,16,1024]{2,1,0:T(8,128)(2,1)S(1)}, bf16[3,16,1024]{2,1,0:T(8,128)(2,1)S(1)}, u32[]{:S(2)}, u32[]{:S(2)}) collective-permute-start(bf16[3,16,1024]{2,1,0:T(8,128)(2,1)S(1)} %get-tuple-element.114), channel_id=1, source_target_pairs={{4,0},{8,4},{12,8},{16,12},{20,16},{24,20},{28,24},{5,1},{9,5},{13... | collective-permute-start | bytes 294920 | tf_op jit(solution)/shard_map/ppermute | solution.py:120
  66.3 5.8 %collective-permute-start.10 = (bf16[10,8,1024]{2,1,0:T(8,128)(2,1)S(1)}, bf16[10,8,1024]{2,1,0:T(8,128)(2,1)S(1)}, u32[]{:S(2)}, u32[]{:S(2)}) collective-permute-start(bf16[10,8,1024]{2,1,0:T(8,128)(2,1)S(1)} %get-tuple-element.116), channel_id=1, source_target_pairs={{0,1},{1,2},{2,3},{4,5},{5,6},{6,7},{8,9},{9,10},{10,11},{12,13},{... | collective-permute-start | bytes 491528 | tf_op jit(solution)/shard_map/ppermute | solution.py:120
  70.8 3.9 %collective-permute-start.11 = (bf16[10,8,1024]{2,1,0:T(8,128)(2,1)S(1)}, bf16[10,8,1024]{2,1,0:T(8,128)(2,1)S(1)}, u32[]{:S(2)}, u32[]{:S(2)}) collective-permute-start(bf16[10,8,1024]{2,1,0:T(8,128)(2,1)S(1)} %get-tuple-element.117), channel_id=1, source_target_pairs={{1,0},{2,1},{3,2},{5,4},{6,5},{7,6},{9,8},{10,9},{11,10},{13,12},{... | collective-permute-start | bytes 491528 | tf_op jit(solution)/shard_map/ppermute | solution.py:120
  77.8 7.0 %collective-permute-start.12 = (bf16[256,3072]{1,0:T(8,128)(2,1)S(1)}, bf16[256,3072]{1,0:T(8,128)(2,1)S(1)}, u32[]{:S(2)}, u32[]{:S(2)}) collective-permute-start(bf16[256,3072]{1,0:T(8,128)(2,1)S(1)} %get-tuple-element.132.refs_0_), channel_id=1, source_target_pairs={{0,1},{1,0},{2,3},{3,2},{4,5},{5,4},{6,7},{7,6},{8,9},{9,8},{10,11... | collective-permute-start | bytes 4718600 | tf_op jit(solution)/shard_map/ppermute | solution.py:47
  81.7 3.1 %collective-permute-start.13 = (bf16[2,64,256]{2,1,0:T(8,128)(2,1)S(1)}, bf16[2,64,256]{2,1,0:T(8,128)(2,1)S(1)}, u32[]{:S(2)}, u32[]{:S(2)}) collective-permute-start(bf16[2,64,256]{2,1,0:T(8,128)(2,1)S(1)} %get-tuple-element.134), channel_id=1, source_target_pairs={{0,1},{1,0},{2,3},{3,2},{4,5},{5,4},{6,7},{7,6},{8,9},{9,8},{10,11... | collective-permute-start | bytes 196616 | tf_op jit(solution)/shard_map/ppermute | solution.py:47
  84.3 7.7 %collective-permute-start.17 = (bf16[368,256]{1,0:T(8,128)(2,1)S(1)}, bf16[368,256]{1,0:T(8,128)(2,1)S(1)}, u32[]{:S(2)}, u32[]{:S(2)}) collective-permute-start(bf16[368,256]{1,0:T(8,128)(2,1)S(1)} %get-tuple-element.142), channel_id=1, source_target_pairs={{0,1},{1,0},{2,3},{3,2},{4,5},{5,4},{6,7},{7,6},{8,9},{9,8},{10,11... | collective-permute-start | bytes 565256 | tf_op jit(solution)/shard_map/ppermute | solution.py:47
  87.5 14.3 %collective-permute-start.36 = (bf16[1024,256]{1,0:T(8,128)(2,1)S(1)}, bf16[1024,256]{1,0:T(8,128)(2,1)S(1)}, u32[]{:S(2)}, u32[]{:S(2)}) collective-permute-start(bf16[1024,256]{1,0:T(8,128)(2,1)S(1)} %get-tuple-element.175), channel_id=1, source_target_pairs={{0,4},{4,0},{8,12},{12,8},{16,20},{20,16},{24,28},{28,24},{1,5},{5... | collective-permute-start | bytes 1572872 | tf_op jit(solution)/shard_map/ppermute | solution.py:47
  88.6 13.9 %collective-permute-start.32 = (bf16[1024,256]{1,0:T(8,128)(2,1)S(1)}, bf16[1024,256]{1,0:T(8,128)(2,1)S(1)}, u32[]{:S(2)}, u32[]{:S(2)}) collective-permute-start(bf16[1024,256]{1,0:T(8,128)(2,1)S(1)} %get-tuple-element.135.refs_7_), channel_id=1, source_target_pairs={{0,2},{1,3},{2,0},{3,1},{4,6},{5,7},{6,4},{7,5},{8,10},{9,11},{10,... | collective-permute-start | bytes 1572872 | tf_op jit(solution)/shard_map/ppermute | solution.py:47
  91.9 11.8 %collective-permute-start.16 = (bf16[256,1024]{1,0:T(8,128)(2,1)S(1)}, bf16[256,1024]{1,0:T(8,128)(2,1)S(1)}, u32[]{:S(2)}, u32[]{:S(2)}) collective-permute-start(bf16[256,1024]{1,0:T(8,128)(2,1)S(1)} %get-tuple-element.140.refs_4_), channel_id=1, source_target_pairs={{0,1},{1,0},{2,3},{3,2},{4,5},{5,4},{6,7},{7,6},{8,9},{9,8},{10,11... | collective-permute-start | bytes 1572872 | tf_op jit(solution)/shard_map/ppermute | solution.py:47
  94.6 15.6 %collective-permute-start.27 = (bf16[1136,256]{1,0:T(8,128)(2,1)S(1)}, bf16[1136,256]{1,0:T(8,128)(2,1)S(1)}, u32[]{:S(2)}, u32[]{:S(2)}) collective-permute-start(bf16[1136,256]{1,0:T(8,128)(2,1)S(1)} %get-tuple-element.143.refs_4_), channel_id=1, source_target_pairs={{0,8},{4,12},{8,0},{12,4},{16,24},{20,28},{24,16},{28,20},{1,9},{5... | collective-permute-start | bytes 1744904 | tf_op jit(solution)/shard_map/ppermute | solution.py:47
  101.9 10.5 %collective-permute-start.37 = (bf16[512,256]{1,0:T(8,128)(2,1)S(1)}, bf16[512,256]{1,0:T(8,128)(2,1)S(1)}, u32[]{:S(2)}, u32[]{:S(2)}) collective-permute-start(bf16[512,256]{1,0:T(8,128)(2,1)S(1)} %get-tuple-element.177), channel_id=1, source_target_pairs={{0,2},{1,3},{2,0},{3,1},{4,6},{5,7},{6,4},{7,5},{8,10},{9,11},{10,... | collective-permute-start | bytes 786440 | tf_op jit(solution)/shard_map/ppermute | solution.py:47
  102.7 12.5 %collective-permute-start.33 = (bf16[512,256]{1,0:T(8,128)(2,1)S(1)}, bf16[512,256]{1,0:T(8,128)(2,1)S(1)}, u32[]{:S(2)}, u32[]{:S(2)}) collective-permute-start(bf16[512,256]{1,0:T(8,128)(2,1)S(1)} %get-tuple-element.169), channel_id=1, source_target_pairs={{0,4},{4,0},{8,12},{12,8},{16,20},{20,16},{24,28},{28,24},{1,5},{5... | collective-permute-start | bytes 786440 | tf_op jit(solution)/shard_map/ppermute | solution.py:47
  105.6 40.4 %collective-permute-start.20 = (bf16[1024,256]{1,0:T(8,128)(2,1)S(1)}, bf16[1024,256]{1,0:T(8,128)(2,1)S(1)}, u32[]{:S(2)}, u32[]{:S(2)}) collective-permute-start(bf16[1024,256]{1,0:T(8,128)(2,1)S(1)} %get-tuple-element.144.refs_3_.refs_9_), channel_id=1, source_target_pairs={{0,4},{4,0},{8,12},{12,8},{16,20},{20,16},{24,28},{28,24},{1,5},{5... | collective-permute-start | bytes 1572872 | tf_op jit(solution)/shard_map/ppermute | solution.py:47
  106.7 19.2 %collective-permute-start.14 = (bf16[3,32,512]{2,1,0:T(8,128)(2,1)S(1)}, bf16[3,32,512]{2,1,0:T(8,128)(2,1)S(1)}, u32[]{:S(2)}, u32[]{:S(2)}) collective-permute-start(bf16[3,32,512]{2,1,0:T(8,128)(2,1)S(1)} %get-tuple-element.137), channel_id=1, source_target_pairs={{0,4},{4,8},{8,12},{12,16},{16,20},{20,24},{24,28},{1,5},{5,9},{9,... | collective-permute-start | bytes 294920 | tf_op jit(solution)/shard_map/ppermute | solution.py:120
  110.2 17.2 %collective-permute-start.15 = (bf16[3,32,512]{2,1,0:T(8,128)(2,1)S(1)}, bf16[3,32,512]{2,1,0:T(8,128)(2,1)S(1)}, u32[]{:S(2)}, u32[]{:S(2)}) collective-permute-start(bf16[3,32,512]{2,1,0:T(8,128)(2,1)S(1)} %get-tuple-element.138), channel_id=1, source_target_pairs={{4,0},{8,4},{12,8},{16,12},{20,16},{24,20},{28,24},{5,1},{9,5},{13... | collective-permute-start | bytes 294920 | tf_op jit(solution)/shard_map/ppermute | solution.py:120
  112.4 27.4 %collective-permute-start.28 = (bf16[624,256]{1,0:T(8,128)(2,1)}, bf16[624,256]{1,0:T(8,128)(2,1)S(1)}, u32[]{:S(2)}, u32[]{:S(2)}) collective-permute-start(bf16[624,256]{1,0:T(8,128)(2,1)} %get-tuple-element.161), channel_id=1, source_target_pairs={{0,4},{4,0},{8,12},{12,8},{16,20},{20,16},{24,28},{28,24},{1,5},{5... | collective-permute-start | bytes 958472 | tf_op jit(solution)/shard_map/ppermute | solution.py:47
  115.1 17.7 %collective-permute-start.38 = (bf16[256,256]{1,0:T(8,128)(2,1)S(1)}, bf16[256,256]{1,0:T(8,128)(2,1)S(1)}, u32[]{:S(2)}, u32[]{:S(2)}) collective-permute-start(bf16[256,256]{1,0:T(8,128)(2,1)S(1)} %get-tuple-element.179), channel_id=1, source_target_pairs={{0,8},{4,12},{8,0},{12,4},{16,24},{20,28},{24,16},{28,20},{1,9},{5... | collective-permute-start | bytes 393224 | tf_op jit(solution)/shard_map/ppermute | solution.py:47
  125.9 9.6 %collective-permute-start.34 = (bf16[256,256]{1,0:T(8,128)(2,1)S(1)}, bf16[256,256]{1,0:T(8,128)(2,1)S(1)}, u32[]{:S(2)}, u32[]{:S(2)}) collective-permute-start(bf16[256,256]{1,0:T(8,128)(2,1)S(1)} %get-tuple-element.171), channel_id=1, source_target_pairs={{0,8},{4,12},{8,0},{12,4},{16,24},{20,28},{24,16},{28,20},{1,9},{5... | collective-permute-start | bytes 393224 | tf_op jit(solution)/shard_map/ppermute | solution.py:47
  132.9 8.9 %collective-permute-start.39 = (bf16[128,256]{1,0:T(8,128)(2,1)S(1)}, bf16[128,256]{1,0:T(8,128)(2,1)}, u32[]{:S(2)}, u32[]{:S(2)}) collective-permute-start(bf16[128,256]{1,0:T(8,128)(2,1)S(1)} %get-tuple-element.181), channel_id=1, source_target_pairs={{0,16},{4,20},{8,24},{12,28},{16,0},{20,4},{24,8},{28,12},{1,17},{... | collective-permute-start | bytes 196616 | tf_op jit(solution)/shard_map/ppermute | solution.py:47
  135.5 8.5 %collective-permute-start.35 = (bf16[128,256]{1,0:T(8,128)(2,1)S(1)}, bf16[128,256]{1,0:T(8,128)(2,1)}, u32[]{:S(2)}, u32[]{:S(2)}) collective-permute-start(bf16[128,256]{1,0:T(8,128)(2,1)S(1)} %get-tuple-element.173), channel_id=1, source_target_pairs={{0,16},{4,20},{8,24},{12,28},{16,0},{20,4},{24,8},{28,12},{1,17},{... | collective-permute-start | bytes 196616 | tf_op jit(solution)/shard_map/ppermute | solution.py:47
  136.0 1.2 collective-permute-start.21
  137.2 8.8 %collective-permute-start.22 = (bf16[64,256]{1,0:T(8,128)(2,1)S(1)}, bf16[64,256]{1,0:T(8,128)(2,1)S(1)}, u32[]{:S(2)}, u32[]{:S(2)}) collective-permute-start(bf16[64,256]{1,0:T(8,128)(2,1)S(1)} %add.26.refs_2_), channel_id=1, source_target_pairs={{0,4},{4,0},{8,12},{12,8},{16,20},{20,16},{24,28},{28,24},{1,5},{5... | collective-permute-start | bytes 98312 | tf_op jit(solution)/shard_map/ppermute | solution.py:47
  139.8 12.5 %copy-start.14 = (f32[7,7,512]{2,1,0:T(8,128)S(1)}, f32[7,7,512]{2,1,0:T(8,128)}, u32[]{:S(2)}) copy-start(f32[7,7,512]{2,1,0:T(8,128)} %copy-done.13) | copy-start | bytes 301060
  139.8 12.5 %collective-permute-start.18 = (bf16[14,8,512]{2,1,0:T(8,128)(2,1)S(1)}, bf16[14,8,512]{2,1,0:T(8,128)(2,1)S(1)}, u32[]{:S(2)}, u32[]{:S(2)}) collective-permute-start(bf16[14,8,512]{2,1,0:T(8,128)(2,1)S(1)} %get-tuple-element.145), channel_id=1, source_target_pairs={{0,1},{1,2},{2,3},{4,5},{5,6},{6,7},{8,9},{9,10},{10,11},{12,13},{... | collective-permute-start | bytes 344072 | tf_op jit(solution)/shard_map/ppermute | solution.py:120
  141.9 10.4 %collective-permute-start.19 = (bf16[14,8,512]{2,1,0:T(8,128)(2,1)S(1)}, bf16[14,8,512]{2,1,0:T(8,128)(2,1)S(1)}, u32[]{:S(2)}, u32[]{:S(2)}) collective-permute-start(bf16[14,8,512]{2,1,0:T(8,128)(2,1)S(1)} %get-tuple-element.146), channel_id=1, source_target_pairs={{1,0},{2,1},{3,2},{5,4},{6,5},{7,6},{9,8},{10,9},{11,10},{13,12},{... | collective-permute-start | bytes 344072 | tf_op jit(solution)/shard_map/ppermute | solution.py:120
  144.0 14.9 %collective-permute-start.29 = (bf16[368,256]{1,0:T(8,128)(2,1)S(1)}, bf16[368,256]{1,0:T(8,128)(2,1)S(1)}, u32[]{:S(2)}, u32[]{:S(2)}) collective-permute-start(bf16[368,256]{1,0:T(8,128)(2,1)S(1)} %get-tuple-element.163), channel_id=1, source_target_pairs={{0,16},{4,20},{8,24},{12,28},{16,0},{20,4},{24,8},{28,12},{1,17},{... | collective-permute-start | bytes 565256 | tf_op jit(solution)/shard_map/ppermute | solution.py:47
  146.2 12.9 %collective-permute-start.23 = (bf16[576,256]{1,0:T(8,128)(2,1)S(1)}, bf16[576,256]{1,0:T(8,128)(2,1)S(1)}, u32[]{:S(2)}, u32[]{:S(2)}) collective-permute-start(bf16[576,256]{1,0:T(8,128)(2,1)S(1)} %get-tuple-element.152.refs_8_), channel_id=1, source_target_pairs={{0,8},{4,12},{8,0},{12,4},{16,24},{20,28},{24,16},{28,20},{1,9},{5... | collective-permute-start | bytes 884744 | tf_op jit(solution)/shard_map/ppermute | solution.py:47
  148.3 12.2 %collective-permute-start.40 = (bf16[1,256,256]{2,1,0:T(8,128)(2,1)S(1)}, bf16[1,256,256]{2,1,0:T(8,128)(2,1)S(1)}, u32[]{:S(2)}, u32[]{:S(2)}) collective-permute-start(bf16[1,256,256]{2,1,0:T(8,128)(2,1)S(1)} %maximum_bitcast_fusion.1), channel_id=1, source_target_pairs={{0,2},{1,3},{2,0},{3,1},{4,6},{5,7},{6,4},{7,5},{8,10},{9,11},{10,... | collective-permute-start | bytes 393224 | tf_op jit(solution)/shard_map/ppermute | solution.py:47
  159.0 12.2 %collective-permute-start.30 = (bf16[368,256]{1,0:T(8,128)(2,1)S(1)}, bf16[368,256]{1,0:T(8,128)(2,1)S(1)}, u32[]{:S(2)}, u32[]{:S(2)}) collective-permute-start(bf16[368,256]{1,0:T(8,128)(2,1)S(1)} %add.29), channel_id=1, source_target_pairs={{0,2},{1,3},{2,0},{3,1},{4,6},{5,7},{6,4},{7,5},{8,10},{9,11},{10,... | collective-permute-start | bytes 565256 | tf_op jit(solution)/shard_map/ppermute | solution.py:47
  159.1 1.0 copy-start
  160.1 10.7 %collective-permute-start.24 = (bf16[320,256]{1,0:T(8,128)(2,1)S(1)}, bf16[320,256]{1,0:T(8,128)(2,1)S(1)}, u32[]{:S(2)}, u32[]{:S(2)}) collective-permute-start(bf16[320,256]{1,0:T(8,128)(2,1)S(1)} %get-tuple-element.155), channel_id=1, source_target_pairs={{0,16},{4,20},{8,24},{12,28},{16,0},{20,4},{24,8},{28,12},{1,17},{... | collective-permute-start | bytes 491528 | tf_op jit(solution)/shard_map/ppermute | solution.py:47
  170.8 6.3 %collective-permute-start.25 = (bf16[320,256]{1,0:T(8,128)(2,1)S(1)}, bf16[320,256]{1,0:T(8,128)(2,1)S(1)}, u32[]{:S(2)}, u32[]{:S(2)}) collective-permute-start(bf16[320,256]{1,0:T(8,128)(2,1)S(1)} %add.27), channel_id=1, source_target_pairs={{0,2},{1,3},{2,0},{3,1},{4,6},{5,7},{6,4},{7,5},{8,10},{9,11},{10,... | collective-permute-start | bytes 491528 | tf_op jit(solution)/shard_map/ppermute | solution.py:47
  171.1 6.2 %collective-permute-start.41 = (bf16[2,256,256]{2,1,0:T(8,128)(2,1)S(1)}, bf16[2,256,256]{2,1,0:T(8,128)(2,1)S(1)}, u32[]{:S(2)}, u32[]{:S(2)}) collective-permute-start(bf16[2,256,256]{2,1,0:T(8,128)(2,1)S(1)} %maximum_bitcast_fusion.refs_0_), channel_id=1, source_target_pairs={{0,1},{1,0},{2,3},{3,2},{4,5},{5,4},{6,7},{7,6},{8,9},{9,8},{10,11... | collective-permute-start | bytes 786440 | tf_op jit(solution)/shard_map/ppermute | solution.py:47
  171.2 7.1 %collective-permute-start.31 = (bf16[368,256]{1,0:T(8,128)(2,1)S(1)}, bf16[368,256]{1,0:T(8,128)(2,1)S(1)}, u32[]{:S(2)}, u32[]{:S(2)}) collective-permute-start(bf16[368,256]{1,0:T(8,128)(2,1)S(1)} %add.30.refs_0_), channel_id=1, source_target_pairs={{0,1},{1,0},{2,3},{3,2},{4,5},{5,4},{6,7},{7,6},{8,9},{9,8},{10,11... | collective-permute-start | bytes 565256 | tf_op jit(solution)/shard_map/ppermute | solution.py:47
  177.1 2.1 %collective-permute-start.26 = (bf16[320,256]{1,0:T(8,128)(2,1)S(1)}, bf16[320,256]{1,0:T(8,128)(2,1)S(1)}, u32[]{:S(2)}, u32[]{:S(2)}) collective-permute-start(bf16[320,256]{1,0:T(8,128)(2,1)S(1)} %add.28.refs_0_), channel_id=1, source_target_pairs={{0,1},{1,0},{2,3},{3,2},{4,5},{5,4},{6,7},{7,6},{8,9},{9,8},{10,11... | collective-permute-start | bytes 491528 | tf_op jit(solution)/shard_map/ppermute | solution.py:47

commit v5 on v4

--- a/solution.py
+++ b/solution.py
@@ -843,7 +843,7 @@
         "expand_product",
         (early, early_other, upward_keep, upward_other),
         (expand_half, expand_half),
-        after=(project_send,),
+        after=(project_send, rows_back[0]),
         limit=16,
         us=0.6,
     )
@@ -859,7 +859,7 @@
             pltpu.VMEM((height, breadth, channels), F32),
             pltpu.VMEM((64, channels), F32),
         ),
-        after=(*framed_back[1:3], expand_send),
+        after=(expand_send,),
         limit=12,
         us=1.8,
     )

time: 181 us -> 177 us (0.978)
  waiting for transfers between devices: 50.1 us -> 37.8 us
  starting transfers between devices: 69.3 us -> 77.7 us
    ppermute x8, waiting for transfers between devices: 11.7 us -> 2.68 us  [neighbours(): lax.ppermute(last, axis, forward)]
    ppermute x26, starting transfers between devices: 29.8 us -> 38.6 us  [swap(): lax.ppermute(values, axis, [(i, i ^ bit) for i in range(lax.axis_size(axi...]
    ppermute x26, waiting for transfers between devices: 23.5 us -> 17 us  [swap(): lax.ppermute(values, axis, [(i, i ^ bit) for i in range(lax.axis_size(axi...]
    ppermute x8, waiting for transfers between devices: 14.8 us -> 18 us  [neighbours(): lax.ppermute(first, axis, backward)]
where the time goes in v5:
time: 177 us; the launch traced here: 176 us
  starting transfers between devices  77.7 us (44%)
  Pallas kernels  51.7 us (29%)
  waiting for transfers between devices  37.8 us (21%)
  local copies, waits for them, and re-layouts  5.88 us (3%)
  other arithmetic  2 us (1%)
    pallas_call x29, Pallas kernels, run(): pl.pallas_call(inner, name=name, out_shape=outs, in_specs=[spec(i) for i...  51.7 us
    ppermute x26, starting transfers between devices, swap(): lax.ppermute(values, axis, [(i, i ^ bit) for i in range(lax.axis_size(axi...  38.6 us
    ppermute x8, starting transfers between devices, neighbours(): lax.ppermute(last, axis, forward)  28.7 us
    ppermute x8, waiting for transfers between devices, neighbours(): lax.ppermute(first, axis, backward)  18 us
    ppermute x26, waiting for transfers between devices, swap(): lax.ppermute(values, axis, [(i, i ^ bit) for i in range(lax.axis_size(axi...  17 us
    ppermute x8, starting transfers between devices, neighbours(): lax.ppermute(first, axis, backward)  10.5 us
    unnamed x30, local copies, waits for them, and re-layouts  4.88 us
  transfers between devices with their start and end apart: 42, of which 17 were waited for; matrix products, arithmetic and copies ran while one was open for 1% of the time, Pallas kernels for 18%

profile of v5, /device:TPU:0, one launch (start us, length us, event | category | flops | bytes accessed | tf_op | source)
XLA Modules:
  0.0 176.3 jit_solution(7266844078334821051)
XLA Ops:
  0.7 1.0 slice_bitcast_fusion
  1.7 4.8 %collective-permute-start = (bf16[3,32,512]{2,1,0:T(8,128)(2,1)S(1)}, bf16[3,32,512]{2,1,0:T(8,128)(2,1)S(1)}, u32[]{:S(2)}, u32[]{:S(2)}) collective-permute-start(bf16[3,32,512]{2,1,0:T(8,128)(2,1)S(1)} %get-tuple-element.187), channel_id=1, source_target_pairs={{0,4},{4,8},{8,12},{12,16},{16,20},{20,24},{24,28},{1,5},{5,9},{9,... | collective-permute-start | bytes 294920 | tf_op jit(solution)/shard_map/ppermute | solution.py:120
  6.5 1.3 collective-permute-start.1
  7.8 0.9 collective-permute-done.refs_5_.refs_1_
  8.7 0.9 copy-done.1
  9.7 0.9 copy-done.8
  10.6 0.7 copy-done.10
  13.1 1.6 collective-permute-start.2
  14.6 1.4 collective-permute-start.3
  16.1 3.5 %collective-permute-done.3.refs_4_ = bf16[14,8,512]{2,1,0:T(8,128)(2,1)S(1)} collective-permute-done((bf16[14,8,512]{2,1,0:T(8,128)(2,1)S(1)}, bf16[14,8,512]{2,1,0:T(8,128)(2,1)S(1)}, u32[]{:S(2)}, u32[]{:S(2)}) %collective-permute-start.3) | collective-permute-done | bytes 114720 | tf_op jit(solution)/shard_map/ppermute | solution.py:120
  19.6 12.8 %front.1 = (bf16[256,3072]{1,0:T(8,128)(2,1)S(1)}, f32[256,512]{1,0:T(8,128)S(1)}, f32[256,1]{1,0:T(8,128)S(1)}, bf16[256,2048]{1,0:T(8,128)(2,1)S(1)}, f32[256,...) custom-call(bf16[8,32,512]{2,1,0:T(8,128)(2,1)S(1)} %get-tuple-eleme, ...), custom_call_target="tpu_custom_call" | custom-call | flops 13200001024 | bytes 1000 | tf_op jit(solution)/shard_map/front/pallas_call | solution.py:33
  32.5 4.4 %collective-permute-start.4 = (bf16[3,16,1024]{2,1,0:T(8,128)(2,1)S(1)}, bf16[3,16,1024]{2,1,0:T(8,128)(2,1)S(1)}, u32[]{:S(2)}, u32[]{:S(2)}) collective-permute-start(bf16[3,16,1024]{2,1,0:T(8,128)(2,1)S(1)} %get-tuple-element.105), channel_id=1, source_target_pairs={{0,4},{4,8},{8,12},{12,16},{16,20},{20,24},{24,28},{1,5},{5,9},{9,... | collective-permute-start | bytes 294920 | tf_op jit(solution)/shard_map/ppermute | solution.py:120
  36.8 1.3 collective-permute-start.5
  38.1 0.9 collective-permute-done.4.refs_1_
  39.0 4.6 %collective-permute-done.5.refs_2_ = bf16[3,16,1024]{2,1,0:T(8,128)(2,1)S(1)} collective-permute-done((bf16[3,16,1024]{2,1,0:T(8,128)(2,1)S(1)}, bf16[3,16,1024]{2,1,0:T(8,128)(2,1)S(1)}, u32[]{:S(2)}, u32[]{:S(2)}) %collective-permute-start.5) | collective-permute-done | bytes 98336 | tf_op jit(solution)/shard_map/ppermute | solution.py:120
  43.6 4.2 %collective-permute-start.6 = (bf16[10,8,1024]{2,1,0:T(8,128)(2,1)S(1)}, bf16[10,8,1024]{2,1,0:T(8,128)(2,1)S(1)}, u32[]{:S(2)}, u32[]{:S(2)}) collective-permute-start(bf16[10,8,1024]{2,1,0:T(8,128)(2,1)S(1)} %get-tuple-element.107), channel_id=1, source_target_pairs={{0,1},{1,2},{2,3},{4,5},{5,6},{6,7},{8,9},{9,10},{10,11},{12,13},{... | collective-permute-start | bytes 491528 | tf_op jit(solution)/shard_map/ppermute | solution.py:120
  47.8 1.3 collective-permute-start.7
  49.1 2.5 %collective-permute-done.7.refs_4_ = bf16[10,8,1024]{2,1,0:T(8,128)(2,1)S(1)} collective-permute-done((bf16[10,8,1024]{2,1,0:T(8,128)(2,1)S(1)}, bf16[10,8,1024]{2,1,0:T(8,128)(2,1)S(1)}, u32[]{:S(2)}, u32[]{:S(2)}) %collective-permute-start.7) | collective-permute-done | bytes 163872 | tf_op jit(solution)/shard_map/ppermute | solution.py:120
  51.6 3.3 %mixer.1 = (f32[4,16,1024]{2,1,0:T(8,128)S(1)}, bf16[4,16,1024]{2,1,0:T(8,128)(2,1)S(1)}, bf16[3,16,1024]{2,1,0:T(8,128)(2,1)S(1)}, bf16[3,16,1024]{2,1,0:T(8,128)(2,1)S(1)}, f32[1,1024]{1,0:T(1,128)S(1)}) custom-call(bf16[4,16,1024]{2,1,0:T(8,128)(2,1)S(1)} %get-tuple-element.104.refs_0_, bf16[3,16,1024]{2,1,0:T(8,128)(2,1)S(1)} %collective-permute-done.4.refs_1_, ...), custom_call_target="tpu_custom_call" | custom-call | flops 3300001024 | bytes 1000 | tf_op jit(solution)/shard_map/mixer/pallas_call | solution.py:33
  54.9 4.8 %collective-permute-start.8 = (bf16[3,16,1024]{2,1,0:T(8,128)(2,1)S(1)}, bf16[3,16,1024]{2,1,0:T(8,128)(2,1)S(1)}, u32[]{:S(2)}, u32[]{:S(2)}) collective-permute-start(bf16[3,16,1024]{2,1,0:T(8,128)(2,1)S(1)} %get-tuple-element.113), channel_id=1, source_target_pairs={{0,4},{4,8},{8,12},{12,16},{16,20},{20,24},{24,28},{1,5},{5,9},{9,... | collective-permute-start | bytes 294920 | tf_op jit(solution)/shard_map/ppermute | solution.py:120
  59.8 1.3 collective-permute-start.9
  61.1 0.9 collective-permute-done.8.refs_6_.refs_1_
  62.0 2.9 %mixer_weights.1.refs_3_.refs_7_ = f32[49,1024]{1,0:T(8,128)S(1)} custom-call(bf16[4,16,1024]{2,1,0:T(8,128)(2,1)S(1)} %get-tuple-element.104.refs_0_, bf16[3,16,1024]{2,1,0:T(8,128)(2,1)S(1)} %collective-permute-done.4.refs_1_, bf16[3,16,1024]{2,1,0:T(8,128)(2,1)S(1)} %collective-permute-done.5.refs_2_, ...), custom_call_target="tpu_custom_call" | custom-call | flops 3300001024 | bytes 1000 | tf_op jit(solution)/shard_map/mixer_weights/pallas_call | solution.py:33
  64.8 1.4 collective-permute-done.9.refs_2_
  66.3 4.5 %collective-permute-start.10 = (bf16[10,8,1024]{2,1,0:T(8,128)(2,1)S(1)}, bf16[10,8,1024]{2,1,0:T(8,128)(2,1)S(1)}, u32[]{:S(2)}, u32[]{:S(2)}) collective-permute-start(bf16[10,8,1024]{2,1,0:T(8,128)(2,1)S(1)} %get-tuple-element.116), channel_id=1, source_target_pairs={{0,1},{1,2},{2,3},{4,5},{5,6},{6,7},{8,9},{9,10},{10,11},{12,13},{... | collective-permute-start | bytes 491528 | tf_op jit(solution)/shard_map/ppermute | solution.py:120
  70.8 1.3 collective-permute-start.11
  72.1 2.6 %collective-permute-done.11.refs_4_ = bf16[10,8,1024]{2,1,0:T(8,128)(2,1)S(1)} collective-permute-done((bf16[10,8,1024]{2,1,0:T(8,128)(2,1)S(1)}, bf16[10,8,1024]{2,1,0:T(8,128)(2,1)S(1)}, u32[]{:S(2)}, u32[]{:S(2)}) %collective-permute-start.11) | collective-permute-done | bytes 163872 | tf_op jit(solution)/shard_map/ppermute | solution.py:120
  74.7 3.1 %section_grad.1 = (bf16[64,1024]{1,0:T(8,128)(2,1)S(1)}, bf16[2,64,256]{2,1,0:T(8,128)(2,1)S(1)}, bf16[2,64,256]{2,1,0:T(8,128)(2,1)S(1)}, bf16[256,3072]{1,0:T(8,128)(2,1)S(1)}) custom-call(bf16[4,16,1024]{2,1,0:T(8,128)(2,1)S(1)} %get-tuple-element.112.refs_0_, ...), custom_call_target="tpu_custom_call", output_to_operand_aliasing={{3}: (7, {})} | custom-call | flops 3300001024 | bytes 1000 | tf_op jit(solution)/shard_map/section_grad/pallas_call | solution.py:33
  77.8 3.9 %collective-permute-start.12 = (bf16[256,3072]{1,0:T(8,128)(2,1)S(1)}, bf16[256,3072]{1,0:T(8,128)(2,1)S(1)}, u32[]{:S(2)}, u32[]{:S(2)}) collective-permute-start(bf16[256,3072]{1,0:T(8,128)(2,1)S(1)} %get-tuple-element.132.refs_0_), channel_id=1, source_target_pairs={{0,1},{1,0},{2,3},{3,2},{4,5},{5,4},{6,7},{7,6},{8,9},{9,8},{10,11... | collective-permute-start | bytes 4718600 | tf_op jit(solution)/shard_map/ppermute | solution.py:47
  81.8 2.5 %merge_back.1 = (f32[256,512]{1,0:T(8,128)S(1)}, bf16[256,512]{1,0:T(8,128)(2,1)S(1)}, bf16[368,256]{1,0:T(8,128)(2,1)S(1)}, bf16[368,256]{1,0:T(8,128)(2,1)S(1)}) custom-call(bf16[64,1024]{1,0:T(8,128)(2,1)S(1)} %get-tuple-element.120.refs_0_, bf16[2048,1024]{1,0:T(8,128)(2,1)S(1)} %get-tuple-element.121.refs_1_, ...), custom_call_target="tpu_custom_call" | custom-call | flops 880001024 | bytes 1000 | tf_op jit(solution)/shard_map/merge_back/pallas_call | solution.py:33
  84.8 2.6 %patch_product.1 = (bf16[1024,256]{1,0:T(8,128)(2,1)S(1)}, bf16[1024,256]{1,0:T(8,128)(2,1)S(1)}, bf16[1024,256]{1,0:T(8,128)(2,1)S(1)}, bf16[1024,256]{1,0:T(8,128)(2,1)S(1)}) custom-call(bf16[256,3072]{1,0:T(8,128)(2,1)S(1)} %get-tuple-element.132.refs_0_, bf16[256,3072]{1,0:T(8,128)(2,1)S(1)} %collective-permute-done.12.refs_1_, ...), custom_call_target="tpu_custom_call" | custom-call | flops 1100001024 | bytes 1000 | tf_op jit(solution)/shard_map/patch_product/pallas_call | solution.py:33
  87.5 1.1 collective-permute-start.36
  88.7 3.2 %mlp_back.1 = (bf16[256,1024]{1,0:T(8,128)(2,1)S(1)}, bf16[256,1024]{1,0:T(8,128)(2,1)S(1)}, bf16[8,32,512]{2,1,0:T(8,128)(2,1)S(1)}, bf16[3,32,512]{2,1,0:T(8,1...) custom-call(bf16[256,512]{1,0:T(8,128)(2,1)S(1)} %get-tuple-element.126.refs_0_, ...), custom_call_target="tpu_custom_call" | custom-call | flops 1320001024 | bytes 1000 | tf_op jit(solution)/shard_map/mlp_back/pallas_call | solution.py:33
  92.0 2.6 %project_product.1 = (bf16[1136,256]{1,0:T(8,128)(2,1)S(1)}, bf16[1136,256]{1,0:T(8,128)(2,1)S(1)}) custom-call(bf16[256,3072]{1,0:T(8,128)(2,1)S(1)} %get-tuple-element.132.refs_0_, bf16[256,3072]{1,0:T(8,128)(2,1)S(1)} %collective-permute-done.12.refs_1_, bf16[368,256]{1,0:T(8,128)(2,1)S(1)} %get-tuple-element.141.refs_2_, ...), custom_call_target="tpu_custom_call" | custom-call | flops 990001024 | bytes 1000 | tf_op jit(solution)/shard_map/project_product/pallas_call | solution.py:33
  94.6 1.7 collective-permute-start.27
  96.3 3.0 %collective-permute-start.14 = (bf16[3,32,512]{2,1,0:T(8,128)(2,1)S(1)}, bf16[3,32,512]{2,1,0:T(8,128)(2,1)S(1)}, u32[]{:S(2)}, u32[]{:S(2)}) collective-permute-start(bf16[3,32,512]{2,1,0:T(8,128)(2,1)S(1)} %get-tuple-element.137), channel_id=1, source_target_pairs={{0,4},{4,8},{8,12},{12,16},{16,20},{20,24},{24,28},{1,5},{5,9},{9,... | collective-permute-start | bytes 294920 | tf_op jit(solution)/shard_map/ppermute | solution.py:120
  99.3 2.4 %collective-permute-done.36.refs_1_ = bf16[1024,256]{1,0:T(8,128)(2,1)S(1)} collective-permute-done((bf16[1024,256]{1,0:T(8,128)(2,1)S(1)}, bf16[1024,256]{1,0:T(8,128)(2,1)S(1)}, u32[]{:S(2)}, u32[]{:S(2)}) %collective-permute-start.36) | collective-permute-done | bytes 524320 | tf_op jit(solution)/shard_map/ppermute | solution.py:47
  102.7 1.1 collective-permute-start.33
  103.8 1.9 %expand_product.1 = (bf16[1024,256]{1,0:T(8,128)(2,1)S(1)}, bf16[1024,256]{1,0:T(8,128)(2,1)S(1)}) custom-call(bf16[256,3072]{1,0:T(8,128)(2,1)S(1)} %get-tuple-element.132.refs_0_, bf16[256,3072]{1,0:T(8,128)(2,1)S(1)} %collective-permute-done.12.refs_1_, bf16[256,1024]{1,0:T(8,128)(2,1)S(1)} %get-tuple-element.139.refs_2_, ...), custom_call_target="tpu_custom_call" | custom-call | flops 660001024 | bytes 1000 | tf_op jit(solution)/shard_map/expand_product/pallas_call | solution.py:33
  105.7 8.7 %collective-permute-start.20 = (bf16[1024,256]{1,0:T(8,128)(2,1)S(1)}, bf16[1024,256]{1,0:T(8,128)(2,1)S(1)}, u32[]{:S(2)}, u32[]{:S(2)}) collective-permute-start(bf16[1024,256]{1,0:T(8,128)(2,1)S(1)} %get-tuple-element.144.refs_3_.refs_7_), channel_id=1, source_target_pairs={{0,4},{4,0},{8,12},{12,8},{16,20},{20,16},{24,28},{28,24},{1,5},{5... | collective-permute-start | bytes 1572872 | tf_op jit(solution)/shard_map/ppermute | solution.py:47
  114.4 0.9 sum_step.12
  115.3 1.3 collective-permute-start.15
  116.7 4.6 %collective-permute-start.38 = (bf16[256,256]{1,0:T(8,128)(2,1)S(1)}, bf16[256,256]{1,0:T(8,128)(2,1)S(1)}, u32[]{:S(2)}, u32[]{:S(2)}) collective-permute-start(bf16[256,256]{1,0:T(8,128)(2,1)S(1)} %get-tuple-element.179), channel_id=1, source_target_pairs={{0,8},{4,12},{8,0},{12,4},{16,24},{20,28},{24,16},{28,20},{1,9},{5... | collective-permute-start | bytes 393224 | tf_op jit(solution)/shard_map/ppermute | solution.py:47
  121.5 5.4 %block_weights.1 = (bf16[64,256]{1,0:T(8,128)(2,1)S(1)}, bf16[64,256]{1,0:T(8,128)(2,1)S(1)}) custom-call(bf16[8,32,512]{2,1,0:T(8,128)(2,1)S(1)} %get-tuple-element.97.refs_0_, bf16[3,32,512]{2,1,0:T(8,128)(2,1)S(1)} %collective-permute-done.refs_5_.refs_1_, bf16[3,32,512]{2,1,0:T(8,128)(2,1)S(1)} %collective-permute-done.1.refs_2_, ...), custom_call_target="tpu_custom_call" | custom-call | flops 1980001024 | bytes 1000 | tf_op jit(solution)/shard_map/block_weights/pallas_call | solution.py:33
  127.5 1.4 collective-permute-done.34.refs_1_
  128.9 1.8 %collective-permute-start.39 = (bf16[128,256]{1,0:T(8,128)(2,1)S(1)}, bf16[128,256]{1,0:T(8,128)(2,1)}, u32[]{:S(2)}, u32[]{:S(2)}) collective-permute-start(bf16[128,256]{1,0:T(8,128)(2,1)S(1)} %get-tuple-element.181), channel_id=1, source_target_pairs={{0,16},{4,20},{8,24},{12,28},{16,0},{20,4},{24,8},{28,12},{1,17},{... | collective-permute-start | bytes 196616 | tf_op jit(solution)/shard_map/ppermute | solution.py:47
  130.7 1.2 collective-permute-start.35
  131.9 3.2 %collective-permute-done.15.refs_2_ = bf16[3,32,512]{2,1,0:T(8,128)(2,1)S(1)} collective-permute-done((bf16[3,32,512]{2,1,0:T(8,128)(2,1)S(1)}, bf16[3,32,512]{2,1,0:T(8,128)(2,1)S(1)}, u32[]{:S(2)}, u32[]{:S(2)}) %collective-permute-start.15) | collective-permute-done | bytes 98336 | tf_op jit(solution)/shard_map/ppermute | solution.py:120
  135.2 1.4 collective-permute-start.18
  136.7 1.3 collective-permute-start.19
  138.0 0.9 add.33
  138.9 1.5 collective-permute-start.29
  140.5 0.9 add.32
  141.5 3.7 %collective-permute-start.23 = (bf16[576,256]{1,0:T(8,128)(2,1)S(1)}, bf16[576,256]{1,0:T(8,128)(2,1)S(1)}, u32[]{:S(2)}, u32[]{:S(2)}) collective-permute-start(bf16[576,256]{1,0:T(8,128)(2,1)S(1)} %get-tuple-element.152.refs_8_), channel_id=1, source_target_pairs={{0,8},{4,12},{8,0},{12,4},{16,24},{20,28},{24,16},{28,20},{1,9},{5... | collective-permute-start | bytes 884744 | tf_op jit(solution)/shard_map/ppermute | solution.py:47
  145.2 5.0 %collective-permute-start.40 = (bf16[1,256,256]{2,1,0:T(8,128)(2,1)S(1)}, bf16[1,256,256]{2,1,0:T(8,128)(2,1)S(1)}, u32[]{:S(2)}, u32[]{:S(2)}) collective-permute-start(bf16[1,256,256]{2,1,0:T(8,128)(2,1)S(1)} %maximum_bitcast_fusion.1), channel_id=1, source_target_pairs={{0,2},{1,3},{2,0},{3,1},{4,6},{5,7},{6,4},{7,5},{8,10},{9,11},{10,... | collective-permute-start | bytes 393224 | tf_op jit(solution)/shard_map/ppermute | solution.py:47
  150.2 6.6 %input_grad.1.refs_2_ = bf16[8,32,512]{2,1,0:T(8,128)(2,1)} custom-call(bf16[8,32,512]{2,1,0:T(8,128)(2,1)S(1)} %get-tuple-element.136.refs_0_.refs_5_, bf16[3,32,512]{2,1,0:T(8,128)(2,1)S(1)} %collective-permute-done.14.refs_5_.refs_1_, bf16[3,32,512]{2,1,0:T(8,128)(2,1)S(1)} %collective-permute-done.15.refs_2_, ...), custom_call_target="tpu_custom_call" | custom-call | flops 2200001024 | bytes 1000 | tf_op jit(solution)/shard_map/input_grad/pallas_call | solution.py:33
  156.9 0.9 copy-done
  158.0 1.5 collective-permute-start.24
  159.5 8.3 %collective-permute-done.24 = bf16[320,256]{1,0:T(8,128)(2,1)S(1)} collective-permute-done((bf16[320,256]{1,0:T(8,128)(2,1)S(1)}, bf16[320,256]{1,0:T(8,128)(2,1)S(1)}, u32[]{:S(2)}, u32[]{:S(2)}) %collective-permute-start.24) | collective-permute-done | bytes 163872 | tf_op jit(solution)/shard_map/ppermute | solution.py:47
  167.9 1.0 collective-permute-start.25
  169.6 3.7 %collective-permute-done.25 = bf16[320,256]{1,0:T(8,128)(2,1)S(1)} collective-permute-done((bf16[320,256]{1,0:T(8,128)(2,1)S(1)}, bf16[320,256]{1,0:T(8,128)(2,1)S(1)}, u32[]{:S(2)}, u32[]{:S(2)}) %collective-permute-start.25) | collective-permute-done | bytes 163872 | tf_op jit(solution)/shard_map/ppermute | solution.py:47
  173.4 1.1 finish_patch.1
  174.4 1.0 finish_project.1
  175.4 0.9 finish_expand.1
  (90 shorter events, 6.0 us)
Async XLA Ops:
  0.6 19.0 %copy-start.6 = (bf16[1,4,16,1024]{3,2,1,0:T(8,128)(2,1)S(1)}, bf16[1,4,16,1024]{3,2,1,0:T(8,128)(2,1)}, u32[]{:S(2)}) copy-start(bf16[1,4,16,1024]{3,2,1,0:T(8,128)(2,1)} %param.22) | copy-start | bytes 393220
  0.7 19.0 %copy-start.7 = (bf16[1,4,16,1024]{3,2,1,0:T(8,128)(2,1)S(1)}, bf16[1,4,16,1024]{3,2,1,0:T(8,128)(2,1)}, u32[]{:S(2)}) copy-start(bf16[1,4,16,1024]{3,2,1,0:T(8,128)(2,1)} %param.23) | copy-start | bytes 393220
  0.7 18.9 %copy-start.9 = (f32[1024]{0:T(1024)S(1)}, f32[1024]{0:T(1024)}, u32[]{:S(2)}) copy-start(f32[1024]{0:T(1024)} %param.21) | copy-start | bytes 12292
  1.7 7.0 %collective-permute-start = (bf16[3,32,512]{2,1,0:T(8,128)(2,1)S(1)}, bf16[3,32,512]{2,1,0:T(8,128)(2,1)S(1)}, u32[]{:S(2)}, u32[]{:S(2)}) collective-permute-start(bf16[3,32,512]{2,1,0:T(8,128)(2,1)S(1)} %get-tuple-element.187), channel_id=1, source_target_pairs={{0,4},{4,8},{8,12},{12,16},{16,20},{20,24},{24,28},{1,5},{5,9},{9,... | collective-permute-start | bytes 294920 | tf_op jit(solution)/shard_map/ppermute | solution.py:120
  6.5 6.5 %collective-permute-start.1 = (bf16[3,32,512]{2,1,0:T(8,128)(2,1)S(1)}, bf16[3,32,512]{2,1,0:T(8,128)(2,1)S(1)}, u32[]{:S(2)}, u32[]{:S(2)}) collective-permute-start(bf16[3,32,512]{2,1,0:T(8,128)(2,1)S(1)} %get-tuple-element.186), channel_id=1, source_target_pairs={{4,0},{8,4},{12,8},{16,12},{20,16},{24,20},{28,24},{5,1},{9,5},{13... | collective-permute-start | bytes 294920 | tf_op jit(solution)/shard_map/ppermute | solution.py:120
  8.7 0.9 copy-start.1
  9.7 0.9 copy-start.8
  10.6 0.7 copy-start.10
  11.3 0.7 copy-start.11
  11.9 0.7 copy-start.12
  12.6 7.0 %copy-start.2 = (bf16[2048,1024]{1,0:T(8,128)(2,1)S(1)}, bf16[2048,1024]{1,0:T(8,128)(2,1)}, u32[]{:S(2)}) copy-start(bf16[2048,1024]{1,0:T(8,128)(2,1)} %refs_11_.1) | copy-start | bytes 12582916
  12.6 7.0 %copy-start.3 = (bf16[512,2048]{1,0:T(8,128)(2,1)S(1)}, bf16[512,2048]{1,0:T(8,128)(2,1)}, u32[]{:S(2)}) copy-start(bf16[512,2048]{1,0:T(8,128)(2,1)} %refs_9_.1) | copy-start | bytes 6291460
  12.6 7.0 %copy-start.4 = (bf16[2048,512]{1,0:T(8,128)(2,1)S(1)}, bf16[2048,512]{1,0:T(8,128)(2,1)}, u32[]{:S(2)}) copy-start(bf16[2048,512]{1,0:T(8,128)(2,1)} %refs_10_.1) | copy-start | bytes 6291460
  12.6 7.0 %copy-start.5 = (f32[7,7,1024]{2,1,0:T(8,128)S(1)}, f32[7,7,1024]{2,1,0:T(8,128)}, u32[]{:S(2)}) copy-start(f32[7,7,1024]{2,1,0:T(8,128)} %refs_12_.1) | copy-start | bytes 602116
  12.9 19.6 %copy-start.13 = (f32[7,7,512]{2,1,0:T(8,128)}, f32[7,7,512]{2,1,0:T(8,128)S(1)}, u32[]{:S(2)}) copy-start(f32[7,7,512]{2,1,0:T(8,128)S(1)} %get-tuple-element.100.refs_5_) | copy-start | bytes 301060
  13.1 3.0 %collective-permute-start.2 = (bf16[14,8,512]{2,1,0:T(8,128)(2,1)S(1)}, bf16[14,8,512]{2,1,0:T(8,128)(2,1)S(1)}, u32[]{:S(2)}, u32[]{:S(2)}) collective-permute-start(bf16[14,8,512]{2,1,0:T(8,128)(2,1)S(1)} %get-tuple-element.98), channel_id=1, source_target_pairs={{0,1},{1,2},{2,3},{4,5},{5,6},{6,7},{8,9},{9,10},{10,11},{12,13},{... | collective-permute-start | bytes 344072 | tf_op jit(solution)/shard_map/ppermute | solution.py:120
  14.6 5.0 %collective-permute-start.3 = (bf16[14,8,512]{2,1,0:T(8,128)(2,1)S(1)}, bf16[14,8,512]{2,1,0:T(8,128)(2,1)S(1)}, u32[]{:S(2)}, u32[]{:S(2)}) collective-permute-start(bf16[14,8,512]{2,1,0:T(8,128)(2,1)S(1)} %get-tuple-element.99), channel_id=1, source_target_pairs={{1,0},{2,1},{3,2},{5,4},{6,5},{7,6},{9,8},{10,9},{11,10},{13,12},{... | collective-permute-start | bytes 344072 | tf_op jit(solution)/shard_map/ppermute | solution.py:120
  32.5 6.6 %collective-permute-start.4 = (bf16[3,16,1024]{2,1,0:T(8,128)(2,1)S(1)}, bf16[3,16,1024]{2,1,0:T(8,128)(2,1)S(1)}, u32[]{:S(2)}, u32[]{:S(2)}) collective-permute-start(bf16[3,16,1024]{2,1,0:T(8,128)(2,1)S(1)} %get-tuple-element.105), channel_id=1, source_target_pairs={{0,4},{4,8},{8,12},{12,16},{16,20},{20,24},{24,28},{1,5},{5,9},{9,... | collective-permute-start | bytes 294920 | tf_op jit(solution)/shard_map/ppermute | solution.py:120
  36.8 6.7 %collective-permute-start.5 = (bf16[3,16,1024]{2,1,0:T(8,128)(2,1)S(1)}, bf16[3,16,1024]{2,1,0:T(8,128)(2,1)S(1)}, u32[]{:S(2)}, u32[]{:S(2)}) collective-permute-start(bf16[3,16,1024]{2,1,0:T(8,128)(2,1)S(1)} %get-tuple-element.106), channel_id=1, source_target_pairs={{4,0},{8,4},{12,8},{16,12},{20,16},{24,20},{28,24},{5,1},{9,5},{13... | collective-permute-start | bytes 294920 | tf_op jit(solution)/shard_map/ppermute | solution.py:120
  43.6 5.5 %collective-permute-start.6 = (bf16[10,8,1024]{2,1,0:T(8,128)(2,1)S(1)}, bf16[10,8,1024]{2,1,0:T(8,128)(2,1)S(1)}, u32[]{:S(2)}, u32[]{:S(2)}) collective-permute-start(bf16[10,8,1024]{2,1,0:T(8,128)(2,1)S(1)} %get-tuple-element.107), channel_id=1, source_target_pairs={{0,1},{1,2},{2,3},{4,5},{5,6},{6,7},{8,9},{9,10},{10,11},{12,13},{... | collective-permute-start | bytes 491528 | tf_op jit(solution)/shard_map/ppermute | solution.py:120
  47.8 3.8 %collective-permute-start.7 = (bf16[10,8,1024]{2,1,0:T(8,128)(2,1)S(1)}, bf16[10,8,1024]{2,1,0:T(8,128)(2,1)S(1)}, u32[]{:S(2)}, u32[]{:S(2)}) collective-permute-start(bf16[10,8,1024]{2,1,0:T(8,128)(2,1)S(1)} %get-tuple-element.108), channel_id=1, source_target_pairs={{1,0},{2,1},{3,2},{5,4},{6,5},{7,6},{9,8},{10,9},{11,10},{13,12},{... | collective-permute-start | bytes 491528 | tf_op jit(solution)/shard_map/ppermute | solution.py:120
  54.9 7.0 %collective-permute-start.8 = (bf16[3,16,1024]{2,1,0:T(8,128)(2,1)S(1)}, bf16[3,16,1024]{2,1,0:T(8,128)(2,1)S(1)}, u32[]{:S(2)}, u32[]{:S(2)}) collective-permute-start(bf16[3,16,1024]{2,1,0:T(8,128)(2,1)S(1)} %get-tuple-element.113), channel_id=1, source_target_pairs={{0,4},{4,8},{8,12},{12,16},{16,20},{20,24},{24,28},{1,5},{5,9},{9,... | collective-permute-start | bytes 294920 | tf_op jit(solution)/shard_map/ppermute | solution.py:120
  59.8 6.5 %collective-permute-start.9 = (bf16[3,16,1024]{2,1,0:T(8,128)(2,1)S(1)}, bf16[3,16,1024]{2,1,0:T(8,128)(2,1)S(1)}, u32[]{:S(2)}, u32[]{:S(2)}) collective-permute-start(bf16[3,16,1024]{2,1,0:T(8,128)(2,1)S(1)} %get-tuple-element.114), channel_id=1, source_target_pairs={{4,0},{8,4},{12,8},{16,12},{20,16},{24,20},{28,24},{5,1},{9,5},{13... | collective-permute-start | bytes 294920 | tf_op jit(solution)/shard_map/ppermute | solution.py:120
  66.3 5.8 %collective-permute-start.10 = (bf16[10,8,1024]{2,1,0:T(8,128)(2,1)S(1)}, bf16[10,8,1024]{2,1,0:T(8,128)(2,1)S(1)}, u32[]{:S(2)}, u32[]{:S(2)}) collective-permute-start(bf16[10,8,1024]{2,1,0:T(8,128)(2,1)S(1)} %get-tuple-element.116), channel_id=1, source_target_pairs={{0,1},{1,2},{2,3},{4,5},{5,6},{6,7},{8,9},{9,10},{10,11},{12,13},{... | collective-permute-start | bytes 491528 | tf_op jit(solution)/shard_map/ppermute | solution.py:120
  70.8 3.9 %collective-permute-start.11 = (bf16[10,8,1024]{2,1,0:T(8,128)(2,1)S(1)}, bf16[10,8,1024]{2,1,0:T(8,128)(2,1)S(1)}, u32[]{:S(2)}, u32[]{:S(2)}) collective-permute-start(bf16[10,8,1024]{2,1,0:T(8,128)(2,1)S(1)} %get-tuple-element.117), channel_id=1, source_target_pairs={{1,0},{2,1},{3,2},{5,4},{6,5},{7,6},{9,8},{10,9},{11,10},{13,12},{... | collective-permute-start | bytes 491528 | tf_op jit(solution)/shard_map/ppermute | solution.py:120
  77.8 7.0 %collective-permute-start.12 = (bf16[256,3072]{1,0:T(8,128)(2,1)S(1)}, bf16[256,3072]{1,0:T(8,128)(2,1)S(1)}, u32[]{:S(2)}, u32[]{:S(2)}) collective-permute-start(bf16[256,3072]{1,0:T(8,128)(2,1)S(1)} %get-tuple-element.132.refs_0_), channel_id=1, source_target_pairs={{0,1},{1,0},{2,3},{3,2},{4,5},{5,4},{6,7},{7,6},{8,9},{9,8},{10,11... | collective-permute-start | bytes 4718600 | tf_op jit(solution)/shard_map/ppermute | solution.py:47
  81.7 3.1 %collective-permute-start.13 = (bf16[2,64,256]{2,1,0:T(8,128)(2,1)S(1)}, bf16[2,64,256]{2,1,0:T(8,128)(2,1)S(1)}, u32[]{:S(2)}, u32[]{:S(2)}) collective-permute-start(bf16[2,64,256]{2,1,0:T(8,128)(2,1)S(1)} %get-tuple-element.134), channel_id=1, source_target_pairs={{0,1},{1,0},{2,3},{3,2},{4,5},{5,4},{6,7},{7,6},{8,9},{9,8},{10,11... | collective-permute-start | bytes 196616 | tf_op jit(solution)/shard_map/ppermute | solution.py:47
  84.3 7.7 %collective-permute-start.17 = (bf16[368,256]{1,0:T(8,128)(2,1)S(1)}, bf16[368,256]{1,0:T(8,128)(2,1)S(1)}, u32[]{:S(2)}, u32[]{:S(2)}) collective-permute-start(bf16[368,256]{1,0:T(8,128)(2,1)S(1)} %get-tuple-element.142), channel_id=1, source_target_pairs={{0,1},{1,0},{2,3},{3,2},{4,5},{5,4},{6,7},{7,6},{8,9},{9,8},{10,11... | collective-permute-start | bytes 565256 | tf_op jit(solution)/shard_map/ppermute | solution.py:47
  87.5 14.3 %collective-permute-start.36 = (bf16[1024,256]{1,0:T(8,128)(2,1)S(1)}, bf16[1024,256]{1,0:T(8,128)(2,1)S(1)}, u32[]{:S(2)}, u32[]{:S(2)}) collective-permute-start(bf16[1024,256]{1,0:T(8,128)(2,1)S(1)} %get-tuple-element.175), channel_id=1, source_target_pairs={{0,4},{4,0},{8,12},{12,8},{16,20},{20,16},{24,28},{28,24},{1,5},{5... | collective-permute-start | bytes 1572872 | tf_op jit(solution)/shard_map/ppermute | solution.py:47
  88.6 13.9 %collective-permute-start.32 = (bf16[1024,256]{1,0:T(8,128)(2,1)S(1)}, bf16[1024,256]{1,0:T(8,128)(2,1)S(1)}, u32[]{:S(2)}, u32[]{:S(2)}) collective-permute-start(bf16[1024,256]{1,0:T(8,128)(2,1)S(1)} %get-tuple-element.135.refs_7_), channel_id=1, source_target_pairs={{0,2},{1,3},{2,0},{3,1},{4,6},{5,7},{6,4},{7,5},{8,10},{9,11},{10,... | collective-permute-start | bytes 1572872 | tf_op jit(solution)/shard_map/ppermute | solution.py:47
  91.9 11.9 %collective-permute-start.16 = (bf16[256,1024]{1,0:T(8,128)(2,1)S(1)}, bf16[256,1024]{1,0:T(8,128)(2,1)S(1)}, u32[]{:S(2)}, u32[]{:S(2)}) collective-permute-start(bf16[256,1024]{1,0:T(8,128)(2,1)S(1)} %get-tuple-element.140.refs_4_), channel_id=1, source_target_pairs={{0,1},{1,0},{2,3},{3,2},{4,5},{5,4},{6,7},{7,6},{8,9},{9,8},{10,11... | collective-permute-start | bytes 1572872 | tf_op jit(solution)/shard_map/ppermute | solution.py:47
  94.6 19.8 %collective-permute-start.27 = (bf16[1136,256]{1,0:T(8,128)(2,1)S(1)}, bf16[1136,256]{1,0:T(8,128)(2,1)S(1)}, u32[]{:S(2)}, u32[]{:S(2)}) collective-permute-start(bf16[1136,256]{1,0:T(8,128)(2,1)S(1)} %get-tuple-element.143.refs_4_), channel_id=1, source_target_pairs={{0,8},{4,12},{8,0},{12,4},{16,24},{20,28},{24,16},{28,20},{1,9},{5... | collective-permute-start | bytes 1744904 | tf_op jit(solution)/shard_map/ppermute | solution.py:47
  96.3 7.5 %collective-permute-start.14 = (bf16[3,32,512]{2,1,0:T(8,128)(2,1)S(1)}, bf16[3,32,512]{2,1,0:T(8,128)(2,1)S(1)}, u32[]{:S(2)}, u32[]{:S(2)}) collective-permute-start(bf16[3,32,512]{2,1,0:T(8,128)(2,1)S(1)} %get-tuple-element.137), channel_id=1, source_target_pairs={{0,4},{4,8},{8,12},{12,16},{16,20},{20,24},{24,28},{1,5},{5,9},{9,... | collective-permute-start | bytes 294920 | tf_op jit(solution)/shard_map/ppermute | solution.py:120
  101.9 14.7 %collective-permute-start.37 = (bf16[512,256]{1,0:T(8,128)(2,1)S(1)}, bf16[512,256]{1,0:T(8,128)(2,1)S(1)}, u32[]{:S(2)}, u32[]{:S(2)}) collective-permute-start(bf16[512,256]{1,0:T(8,128)(2,1)S(1)} %get-tuple-element.177), channel_id=1, source_target_pairs={{0,2},{1,3},{2,0},{3,1},{4,6},{5,7},{6,4},{7,5},{8,10},{9,11},{10,... | collective-permute-start | bytes 786440 | tf_op jit(solution)/shard_map/ppermute | solution.py:47
  102.7 18.6 %collective-permute-start.33 = (bf16[512,256]{1,0:T(8,128)(2,1)S(1)}, bf16[512,256]{1,0:T(8,128)(2,1)S(1)}, u32[]{:S(2)}, u32[]{:S(2)}) collective-permute-start(bf16[512,256]{1,0:T(8,128)(2,1)S(1)} %get-tuple-element.169), channel_id=1, source_target_pairs={{0,4},{4,0},{8,12},{12,8},{16,20},{20,16},{24,28},{28,24},{1,5},{5... | collective-permute-start | bytes 786440 | tf_op jit(solution)/shard_map/ppermute | solution.py:47
  105.7 35.6 %collective-permute-start.20 = (bf16[1024,256]{1,0:T(8,128)(2,1)S(1)}, bf16[1024,256]{1,0:T(8,128)(2,1)S(1)}, u32[]{:S(2)}, u32[]{:S(2)}) collective-permute-start(bf16[1024,256]{1,0:T(8,128)(2,1)S(1)} %get-tuple-element.144.refs_3_.refs_7_), channel_id=1, source_target_pairs={{0,4},{4,0},{8,12},{12,8},{16,20},{20,16},{24,28},{28,24},{1,5},{5... | collective-permute-start | bytes 1572872 | tf_op jit(solution)/shard_map/ppermute | solution.py:47
  115.3 19.9 %collective-permute-start.28 = (bf16[624,256]{1,0:T(8,128)(2,1)}, bf16[624,256]{1,0:T(8,128)(2,1)S(1)}, u32[]{:S(2)}, u32[]{:S(2)}) collective-permute-start(bf16[624,256]{1,0:T(8,128)(2,1)} %get-tuple-element.161), channel_id=1, source_target_pairs={{0,4},{4,0},{8,12},{12,8},{16,20},{20,16},{24,28},{28,24},{1,5},{5... | collective-permute-start | bytes 958472 | tf_op jit(solution)/shard_map/ppermute | solution.py:47
  115.3 19.8 %collective-permute-start.15 = (bf16[3,32,512]{2,1,0:T(8,128)(2,1)S(1)}, bf16[3,32,512]{2,1,0:T(8,128)(2,1)S(1)}, u32[]{:S(2)}, u32[]{:S(2)}) collective-permute-start(bf16[3,32,512]{2,1,0:T(8,128)(2,1)S(1)} %get-tuple-element.138), channel_id=1, source_target_pairs={{4,0},{8,4},{12,8},{16,12},{20,16},{24,20},{28,24},{5,1},{9,5},{13... | collective-permute-start | bytes 294920 | tf_op jit(solution)/shard_map/ppermute | solution.py:120
  116.7 10.8 %collective-permute-start.38 = (bf16[256,256]{1,0:T(8,128)(2,1)S(1)}, bf16[256,256]{1,0:T(8,128)(2,1)S(1)}, u32[]{:S(2)}, u32[]{:S(2)}) collective-permute-start(bf16[256,256]{1,0:T(8,128)(2,1)S(1)} %get-tuple-element.179), channel_id=1, source_target_pairs={{0,8},{4,12},{8,0},{12,4},{16,24},{20,28},{24,16},{28,20},{1,9},{5... | collective-permute-start | bytes 393224 | tf_op jit(solution)/shard_map/ppermute | solution.py:47
  121.4 7.5 %collective-permute-start.34 = (bf16[256,256]{1,0:T(8,128)(2,1)S(1)}, bf16[256,256]{1,0:T(8,128)(2,1)S(1)}, u32[]{:S(2)}, u32[]{:S(2)}) collective-permute-start(bf16[256,256]{1,0:T(8,128)(2,1)S(1)} %get-tuple-element.171), channel_id=1, source_target_pairs={{0,8},{4,12},{8,0},{12,4},{16,24},{20,28},{24,16},{28,20},{1,9},{5... | collective-permute-start | bytes 393224 | tf_op jit(solution)/shard_map/ppermute | solution.py:47
  127.4 3.2 %collective-permute-start.21 = (bf16[64,256]{1,0:T(8,128)(2,1)S(1)}, bf16[64,256]{1,0:T(8,128)(2,1)S(1)}, u32[]{:S(2)}, u32[]{:S(2)}) collective-permute-start(bf16[64,256]{1,0:T(8,128)(2,1)S(1)} %get-tuple-element.151), channel_id=1, source_target_pairs={{0,1},{1,0},{2,3},{3,2},{4,5},{5,4},{6,7},{7,6},{8,9},{9,8},{10,11... | collective-permute-start | bytes 98312 | tf_op jit(solution)/shard_map/ppermute | solution.py:47
  128.9 7.9 %collective-permute-start.39 = (bf16[128,256]{1,0:T(8,128)(2,1)S(1)}, bf16[128,256]{1,0:T(8,128)(2,1)}, u32[]{:S(2)}, u32[]{:S(2)}) collective-permute-start(bf16[128,256]{1,0:T(8,128)(2,1)S(1)} %get-tuple-element.181), channel_id=1, source_target_pairs={{0,16},{4,20},{8,24},{12,28},{16,0},{20,4},{24,8},{28,12},{1,17},{... | collective-permute-start | bytes 196616 | tf_op jit(solution)/shard_map/ppermute | solution.py:47
  130.7 8.2 %collective-permute-start.35 = (bf16[128,256]{1,0:T(8,128)(2,1)S(1)}, bf16[128,256]{1,0:T(8,128)(2,1)}, u32[]{:S(2)}, u32[]{:S(2)}) collective-permute-start(bf16[128,256]{1,0:T(8,128)(2,1)S(1)} %get-tuple-element.173), channel_id=1, source_target_pairs={{0,16},{4,20},{8,24},{12,28},{16,0},{20,4},{24,8},{28,12},{1,17},{... | collective-permute-start | bytes 196616 | tf_op jit(solution)/shard_map/ppermute | solution.py:47
  135.1 6.2 %collective-permute-start.22 = (bf16[64,256]{1,0:T(8,128)(2,1)S(1)}, bf16[64,256]{1,0:T(8,128)(2,1)S(1)}, u32[]{:S(2)}, u32[]{:S(2)}) collective-permute-start(bf16[64,256]{1,0:T(8,128)(2,1)S(1)} %add.26.refs_2_), channel_id=1, source_target_pairs={{0,4},{4,0},{8,12},{12,8},{16,20},{20,16},{24,28},{28,24},{1,5},{5... | collective-permute-start | bytes 98312 | tf_op jit(solution)/shard_map/ppermute | solution.py:47
  135.2 15.1 %copy-start.14 = (f32[7,7,512]{2,1,0:T(8,128)S(1)}, f32[7,7,512]{2,1,0:T(8,128)}, u32[]{:S(2)}) copy-start(f32[7,7,512]{2,1,0:T(8,128)} %copy-done.13) | copy-start | bytes 301060
  135.2 15.0 %collective-permute-start.18 = (bf16[14,8,512]{2,1,0:T(8,128)(2,1)S(1)}, bf16[14,8,512]{2,1,0:T(8,128)(2,1)S(1)}, u32[]{:S(2)}, u32[]{:S(2)}) collective-permute-start(bf16[14,8,512]{2,1,0:T(8,128)(2,1)S(1)} %get-tuple-element.145), channel_id=1, source_target_pairs={{0,1},{1,2},{2,3},{4,5},{5,6},{6,7},{8,9},{9,10},{10,11},{12,13},{... | collective-permute-start | bytes 344072 | tf_op jit(solution)/shard_map/ppermute | solution.py:120
  136.7 13.5 %collective-permute-start.19 = (bf16[14,8,512]{2,1,0:T(8,128)(2,1)S(1)}, bf16[14,8,512]{2,1,0:T(8,128)(2,1)S(1)}, u32[]{:S(2)}, u32[]{:S(2)}) collective-permute-start(bf16[14,8,512]{2,1,0:T(8,128)(2,1)S(1)} %get-tuple-element.146), channel_id=1, source_target_pairs={{1,0},{2,1},{3,2},{5,4},{6,5},{7,6},{9,8},{10,9},{11,10},{13,12},{... | collective-permute-start | bytes 344072 | tf_op jit(solution)/shard_map/ppermute | solution.py:120
  138.9 17.9 %collective-permute-start.29 = (bf16[368,256]{1,0:T(8,128)(2,1)S(1)}, bf16[368,256]{1,0:T(8,128)(2,1)S(1)}, u32[]{:S(2)}, u32[]{:S(2)}) collective-permute-start(bf16[368,256]{1,0:T(8,128)(2,1)S(1)} %get-tuple-element.163), channel_id=1, source_target_pairs={{0,16},{4,20},{8,24},{12,28},{16,0},{20,4},{24,8},{28,12},{1,17},{... | collective-permute-start | bytes 565256 | tf_op jit(solution)/shard_map/ppermute | solution.py:47
  141.5 15.4 %collective-permute-start.23 = (bf16[576,256]{1,0:T(8,128)(2,1)S(1)}, bf16[576,256]{1,0:T(8,128)(2,1)S(1)}, u32[]{:S(2)}, u32[]{:S(2)}) collective-permute-start(bf16[576,256]{1,0:T(8,128)(2,1)S(1)} %get-tuple-element.152.refs_8_), channel_id=1, source_target_pairs={{0,8},{4,12},{8,0},{12,4},{16,24},{20,28},{24,16},{28,20},{1,9},{5... | collective-permute-start | bytes 884744 | tf_op jit(solution)/shard_map/ppermute | solution.py:47
  145.2 14.3 %collective-permute-start.40 = (bf16[1,256,256]{2,1,0:T(8,128)(2,1)S(1)}, bf16[1,256,256]{2,1,0:T(8,128)(2,1)S(1)}, u32[]{:S(2)}, u32[]{:S(2)}) collective-permute-start(bf16[1,256,256]{2,1,0:T(8,128)(2,1)S(1)} %maximum_bitcast_fusion.1), channel_id=1, source_target_pairs={{0,2},{1,3},{2,0},{3,1},{4,6},{5,7},{6,4},{7,5},{8,10},{9,11},{10,... | collective-permute-start | bytes 393224 | tf_op jit(solution)/shard_map/ppermute | solution.py:47
  156.8 12.1 %collective-permute-start.30 = (bf16[368,256]{1,0:T(8,128)(2,1)S(1)}, bf16[368,256]{1,0:T(8,128)(2,1)S(1)}, u32[]{:S(2)}, u32[]{:S(2)}) collective-permute-start(bf16[368,256]{1,0:T(8,128)(2,1)S(1)} %add.29), channel_id=1, source_target_pairs={{0,2},{1,3},{2,0},{3,1},{4,6},{5,7},{6,4},{7,5},{8,10},{9,11},{10,... | collective-permute-start | bytes 565256 | tf_op jit(solution)/shard_map/ppermute | solution.py:47
  156.9 1.0 copy-start
  158.0 9.8 %collective-permute-start.24 = (bf16[320,256]{1,0:T(8,128)(2,1)S(1)}, bf16[320,256]{1,0:T(8,128)(2,1)S(1)}, u32[]{:S(2)}, u32[]{:S(2)}) collective-permute-start(bf16[320,256]{1,0:T(8,128)(2,1)S(1)} %get-tuple-element.155), channel_id=1, source_target_pairs={{0,16},{4,20},{8,24},{12,28},{16,0},{20,4},{24,8},{28,12},{1,17},{... | collective-permute-start | bytes 491528 | tf_op jit(solution)/shard_map/ppermute | solution.py:47
  167.9 5.4 %collective-permute-start.25 = (bf16[320,256]{1,0:T(8,128)(2,1)S(1)}, bf16[320,256]{1,0:T(8,128)(2,1)S(1)}, u32[]{:S(2)}, u32[]{:S(2)}) collective-permute-start(bf16[320,256]{1,0:T(8,128)(2,1)S(1)} %add.27), channel_id=1, source_target_pairs={{0,2},{1,3},{2,0},{3,1},{4,6},{5,7},{6,4},{7,5},{8,10},{9,11},{10,... | collective-permute-start | bytes 491528 | tf_op jit(solution)/shard_map/ppermute | solution.py:47
  168.9 4.5 %collective-permute-start.41 = (bf16[2,256,256]{2,1,0:T(8,128)(2,1)S(1)}, bf16[2,256,256]{2,1,0:T(8,128)(2,1)S(1)}, u32[]{:S(2)}, u32[]{:S(2)}) collective-permute-start(bf16[2,256,256]{2,1,0:T(8,128)(2,1)S(1)} %maximum_bitcast_fusion.refs_0_), channel_id=1, source_target_pairs={{0,1},{1,0},{2,3},{3,2},{4,5},{5,4},{6,7},{7,6},{8,9},{9,8},{10,11... | collective-permute-start | bytes 786440 | tf_op jit(solution)/shard_map/ppermute | solution.py:47
  169.0 5.4 %collective-permute-start.31 = (bf16[368,256]{1,0:T(8,128)(2,1)S(1)}, bf16[368,256]{1,0:T(8,128)(2,1)S(1)}, u32[]{:S(2)}, u32[]{:S(2)}) collective-permute-start(bf16[368,256]{1,0:T(8,128)(2,1)S(1)} %add.30.refs_0_), channel_id=1, source_target_pairs={{0,1},{1,0},{2,3},{3,2},{4,5},{5,4},{6,7},{7,6},{8,9},{9,8},{10,11... | collective-permute-start | bytes 565256 | tf_op jit(solution)/shard_map/ppermute | solution.py:47
  173.3 2.1 %collective-permute-start.26 = (bf16[320,256]{1,0:T(8,128)(2,1)S(1)}, bf16[320,256]{1,0:T(8,128)(2,1)S(1)}, u32[]{:S(2)}, u32[]{:S(2)}) collective-permute-start(bf16[320,256]{1,0:T(8,128)(2,1)S(1)} %add.28.refs_0_), channel_id=1, source_target_pairs={{0,1},{1,0},{2,3},{3,2},{4,5},{5,4},{6,7},{7,6},{8,9},{9,8},{10,11... | collective-permute-start | bytes 491528 | tf_op jit(solution)/shard_map/ppermute | solution.py:47

commit v6 on v5

--- a/solution.py
+++ b/solution.py
@@ -496,36 +496,25 @@
     gain_part[...] = part
 
 
-def patch_product_kernel(factor, slices, channels, early, early_other, own, other, *outs):
-    upper_keep, upper_send, lower_keep, lower_send = outs
+def patch_product_kernel(factor, early, early_other, own, other, keep, send):
     blocks, quarter, _ = own.shape
-    part = 4 * channels // slices // 2
+    rows = keep.shape[0] // max(blocks // 2, 1)
+    channels = rows // 4
     at_patches = early.shape[1] - channels
-    lateral = (lax.axis_index("col") // 2) % 2
-    vertical = lax.axis_index("row") % 2
-    per = channels // (2 * part)
+    bit = (lax.axis_index("col") // 2) % 2
     for j in range(4):
         span = slice(j * quarter, (j + 1) * quarter)
         left = jnp.concatenate([early[span, at_patches:], early_other[span, at_patches:]], axis=0)
         for m in range(blocks):
             right = jnp.concatenate([own[m], other[m]], axis=0)
             value = (factor * dot_first(left, right)).astype(BF)
+            at = m // 2 * rows + j * channels
             for i in range(2):
 
-                @pl.when(lateral == i)
+                @pl.when(bit == i)
                 def _():
-                    target = upper_keep if m % 2 == i else upper_send
-                    for k in range(per):
-                        at = (m // 2 * slices + j * per + k) * part
-                        target[at : at + part] = value[2 * k * part : (2 * k + 1) * part]
-
-                @pl.when(vertical == i)
-                def _():
-                    for k in range(per):
-                        r = j * per + k
-                        target = lower_keep if r % 2 == i else lower_send
-                        at = (m * (slices // 2) + r // 2) * part
-                        target[at : at + part] = value[(2 * k + 1) * part : (2 * k + 2) * part]
+                    target = keep if m % 2 == i else send
+                    target[at : at + channels] = value
 
 
 def store_slices(position, value, begin, offset, rows, pitch, keep, send):
@@ -792,18 +781,8 @@
         us=0.8,
     )
     branch_other = swap(branch_send, "col", 1)
-    patch_part = shape_of(block_count // 2 * 2 * channels, block, dtype=BF)
-    upper_keep, upper_send, lower_keep, lower_send = run(
-        functools.partial(patch_product_kernel, scale_four, row_count, channels),
-        "patch_product",
-        (early, early_other, flat_keep, flat_other),
-        (patch_part,) * 4,
-        limit=16,
-        us=1,
-    )
     deep, shallow = hidden_width // row_count, channels // row_count
     groups = hidden_width // channels
-    project_half = shape_of(row_count // 2 * deep + 112, half, dtype=BF)
     upward_half = shape_of(pixels, hidden_width // 2, dtype=BF)
     upward_keep, upward_send, grad_mixed, first, last, gain_part = run(
         back_kernel,
@@ -822,17 +801,17 @@
             pltpu.VMEM((pixels, hidden_width), BF),
             pltpu.VMEM((pixels, channels), F32),
         ),
-        after=(upper_send,),
         limit=16,
         us=1.2,
     )
     rows_back = neighbours(first, last, "row")
     upward_other = swap(upward_send, "col", 1)
-    project_keep, project_send = run(
-        functools.partial(project_product_kernel, scale_three, row_count),
-        "project_product",
-        (early, early_other, branch_keep, branch_other),
-        (project_half, project_half),
+    patch_half = shape_of(block_count // 2 * 4 * channels, block, dtype=BF)
+    patch_keep, patch_send = run(
+        functools.partial(patch_product_kernel, scale_four),
+        "patch_product",
+        (early, early_other, flat_keep, flat_other),
+        (patch_half, patch_half),
         after=(upward_send,),
         limit=16,
         us=0.9,
@@ -843,11 +822,21 @@
         "expand_product",
         (early, early_other, upward_keep, upward_other),
         (expand_half, expand_half),
-        after=(project_send, rows_back[0]),
+        after=(patch_send,),
         limit=16,
         us=0.6,
     )
-    framed_back = halo(grad_mixed, rows_back, "strips_back", after=(expand_send,))
+    project_half = shape_of(row_count // 2 * deep + 112, half, dtype=BF)
+    project_keep, project_send = run(
+        functools.partial(project_product_kernel, scale_three, row_count),
+        "project_product",
+        (early, early_other, branch_keep, branch_other),
+        (project_half, project_half),
+        after=(expand_send,),
+        limit=16,
+        us=0.9,
+    )
+    framed_back = halo(grad_mixed, rows_back, "strips_back", after=(project_send,))
     small_half = shape_of(64, half, dtype=BF)
     small_keep, small_send = run(
         functools.partial(weight_pack_kernel, scale_three),
@@ -859,7 +848,7 @@
             pltpu.VMEM((height, breadth, channels), F32),
             pltpu.VMEM((64, channels), F32),
         ),
-        after=(expand_send,),
+        after=(project_send,),
         limit=12,
         us=1.8,
     )
@@ -878,15 +867,9 @@
     row_bits, col_bits = axis_bits("row"), axis_bits("col")
     outer = len(row_bits)
     low_first = [("row", bit, 0) for bit in row_bits]
-    lateral = [("col", bit, outer) for bit in col_bits[1:]]
-    upper_order = lateral + low_first
-    lower_order = low_first[:1] + [("col", bit, outer - 1) for bit in col_bits[1:]] + low_first[1:]
-    part_rows = 2 * channels // row_count
-    patch_sum = jnp.concatenate(
-        [
-            chain(upper_keep, upper_send, upper_order, block_count * row_count, part_rows),
-            chain(lower_keep, lower_send, lower_order, block_count * row_count, part_rows),
-        ]
+    patch_order = [("col", bit, outer) for bit in col_bits[1:]] + low_first
+    patch_sum = chain(
+        patch_keep, patch_send, patch_order, block_count * row_count, 4 * channels // row_count
     )
     patch_sum = gather(patch_sum, "col", col_bits[1:])
     (patch_grad,) = run(

time: 177 us -> 196 us (1.11)
  waiting for transfers between devices: 37.8 us -> 76.3 us
  starting transfers between devices: 77.7 us -> 61.1 us
    ppermute x26 -> x22, waiting for transfers between devices: 17 us -> 55.5 us  [swap(): lax.ppermute(values, axis, [(i, i ^ bit) for i in range(lax.axis_size(axi...]
    ppermute x26 -> x22, starting transfers between devices: 38.6 us -> 22.2 us  [swap(): lax.ppermute(values, axis, [(i, i ^ bit) for i in range(lax.axis_size(axi...]
    pallas_call x29 -> x26, Pallas kernels: 51.7 us -> 51 us  [run(): pl.pallas_call(inner, name=name, out_shape=outs, in_specs=[spec(i) for i...]
    unnamed x30 -> x26, local copies, waits for them, and re-layouts: 4.88 us -> 4.87 us
  transfers between devices with their start and end apart: 42 -> 38, of which waited for: 17 -> 18; matrix products, arithmetic and copies ran while one was open for 1% -> 0% of each run, Pallas kernels for 18% -> 14%
where the time goes in v6:
time: 196 us
  waiting for transfers between devices  76.3 us (39%)
  starting transfers between devices  61.1 us (31%)
  Pallas kernels  51 us (26%)
  local copies, waits for them, and re-layouts  5.87 us (3%)
    ppermute x22, waiting for transfers between devices, swap(): lax.ppermute(values, axis, [(i, i ^ bit) for i in range(lax.axis_size(axi...  55.5 us
    pallas_call x26, Pallas kernels, run(): pl.pallas_call(inner, name=name, out_shape=outs, in_specs=[spec(i) for i...  51 us
    ppermute x8, starting transfers between devices, neighbours(): lax.ppermute(last, axis, forward)  28.5 us
    ppermute x22, starting transfers between devices, swap(): lax.ppermute(values, axis, [(i, i ^ bit) for i in range(lax.axis_size(axi...  22.2 us
    ppermute x8, waiting for transfers between devices, neighbours(): lax.ppermute(first, axis, backward)  16.8 us
    ppermute x8, starting transfers between devices, neighbours(): lax.ppermute(first, axis, backward)  10.5 us
    unnamed x26, local copies, waits for them, and re-layouts  4.87 us
    ppermute x8, waiting for transfers between devices, neighbours(): lax.ppermute(last, axis, forward)  4.03 us
  transfers between devices with their start and end apart: 38, of which 18 were waited for; matrix products, arithmetic and copies ran while one was open for 0% of the time, Pallas kernels for 14%

profile of v6, /device:TPU:0, one launch (start us, length us, event | category | flops | bytes accessed | tf_op | source)
XLA Modules:
  0.0 195.8 jit_solution(18120286719493767700)
XLA Ops:
  0.7 1.0 slice_bitcast_fusion
  1.7 4.8 %collective-permute-start = (bf16[3,32,512]{2,1,0:T(8,128)(2,1)S(1)}, bf16[3,32,512]{2,1,0:T(8,128)(2,1)S(1)}, u32[]{:S(2)}, u32[]{:S(2)}) collective-permute-start(bf16[3,32,512]{2,1,0:T(8,128)(2,1)S(1)} %get-tuple-element.171), channel_id=1, source_target_pairs={{0,4},{4,8},{8,12},{12,16},{16,20},{20,24},{24,28},{1,5},{5,9},{9,... | collective-permute-start | bytes 294920 | tf_op jit(solution)/shard_map/ppermute | solution.py:120
  6.5 1.3 collective-permute-start.1
  7.8 0.9 collective-permute-done.refs_5_.refs_1_
  8.7 0.9 copy-done.1
  9.7 0.9 copy-done.8
  10.6 0.7 copy-done.10
  11.3 0.7 copy-done.11
  13.1 1.6 collective-permute-start.2
  14.6 1.4 collective-permute-start.3
  16.1 3.5 %collective-permute-done.3.refs_4_ = bf16[14,8,512]{2,1,0:T(8,128)(2,1)S(1)} collective-permute-done((bf16[14,8,512]{2,1,0:T(8,128)(2,1)S(1)}, bf16[14,8,512]{2,1,0:T(8,128)(2,1)S(1)}, u32[]{:S(2)}, u32[]{:S(2)}) %collective-permute-start.3) | collective-permute-done | bytes 114720 | tf_op jit(solution)/shard_map/ppermute | solution.py:120
  19.6 12.8 %front.1 = (bf16[256,3072]{1,0:T(8,128)(2,1)S(1)}, f32[256,512]{1,0:T(8,128)S(1)}, f32[256,1]{1,0:T(8,128)S(1)}, bf16[256,2048]{1,0:T(8,128)(2,1)S(1)}, f32[256,...) custom-call(bf16[8,32,512]{2,1,0:T(8,128)(2,1)S(1)} %get-tuple-eleme, ...), custom_call_target="tpu_custom_call" | custom-call | flops 13200001024 | bytes 1000 | tf_op jit(solution)/shard_map/front/pallas_call | solution.py:33
  32.5 4.4 %collective-permute-start.4 = (bf16[3,16,1024]{2,1,0:T(8,128)(2,1)S(1)}, bf16[3,16,1024]{2,1,0:T(8,128)(2,1)S(1)}, u32[]{:S(2)}, u32[]{:S(2)}) collective-permute-start(bf16[3,16,1024]{2,1,0:T(8,128)(2,1)S(1)} %get-tuple-element.97), channel_id=1, source_target_pairs={{0,4},{4,8},{8,12},{12,16},{16,20},{20,24},{24,28},{1,5},{5,9},{9,... | collective-permute-start | bytes 294920 | tf_op jit(solution)/shard_map/ppermute | solution.py:120
  36.8 1.3 collective-permute-start.5
  38.1 0.9 collective-permute-done.4.refs_1_
  39.0 4.5 %collective-permute-done.5.refs_2_ = bf16[3,16,1024]{2,1,0:T(8,128)(2,1)S(1)} collective-permute-done((bf16[3,16,1024]{2,1,0:T(8,128)(2,1)S(1)}, bf16[3,16,1024]{2,1,0:T(8,128)(2,1)S(1)}, u32[]{:S(2)}, u32[]{:S(2)}) %collective-permute-start.5) | collective-permute-done | bytes 98336 | tf_op jit(solution)/shard_map/ppermute | solution.py:120
  43.6 4.2 %collective-permute-start.6 = (bf16[10,8,1024]{2,1,0:T(8,128)(2,1)S(1)}, bf16[10,8,1024]{2,1,0:T(8,128)(2,1)S(1)}, u32[]{:S(2)}, u32[]{:S(2)}) collective-permute-start(bf16[10,8,1024]{2,1,0:T(8,128)(2,1)S(1)} %get-tuple-element.99), channel_id=1, source_target_pairs={{0,1},{1,2},{2,3},{4,5},{5,6},{6,7},{8,9},{9,10},{10,11},{12,13},{... | collective-permute-start | bytes 491528 | tf_op jit(solution)/shard_map/ppermute | solution.py:120
  47.8 1.3 collective-permute-start.7
  49.1 2.5 %collective-permute-done.7.refs_4_ = bf16[10,8,1024]{2,1,0:T(8,128)(2,1)S(1)} collective-permute-done((bf16[10,8,1024]{2,1,0:T(8,128)(2,1)S(1)}, bf16[10,8,1024]{2,1,0:T(8,128)(2,1)S(1)}, u32[]{:S(2)}, u32[]{:S(2)}) %collective-permute-start.7) | collective-permute-done | bytes 163872 | tf_op jit(solution)/shard_map/ppermute | solution.py:120
  51.6 3.3 %mixer.1 = (f32[4,16,1024]{2,1,0:T(8,128)S(1)}, bf16[4,16,1024]{2,1,0:T(8,128)(2,1)S(1)}, bf16[3,16,1024]{2,1,0:T(8,128)(2,1)S(1)}, bf16[3,16,1024]{2,1,0:T(8,128)(2,1)S(1)}, f32[1,1024]{1,0:T(1,128)S(1)}) custom-call(bf16[4,16,1024]{2,1,0:T(8,128)(2,1)S(1)} %get-tuple-element.96.refs_0_, bf16[3,16,1024]{2,1,0:T(8,128)(2,1)S(1)} %collective-permute-done.4.refs_1_, ...), custom_call_target="tpu_custom_call" | custom-call | flops 3300001024 | bytes 1000 | tf_op jit(solution)/shard_map/mixer/pallas_call | solution.py:33
  54.9 4.8 %collective-permute-start.8 = (bf16[3,16,1024]{2,1,0:T(8,128)(2,1)S(1)}, bf16[3,16,1024]{2,1,0:T(8,128)(2,1)S(1)}, u32[]{:S(2)}, u32[]{:S(2)}) collective-permute-start(bf16[3,16,1024]{2,1,0:T(8,128)(2,1)S(1)} %get-tuple-element.105), channel_id=1, source_target_pairs={{0,4},{4,8},{8,12},{12,16},{16,20},{20,24},{24,28},{1,5},{5,9},{9,... | collective-permute-start | bytes 294920 | tf_op jit(solution)/shard_map/ppermute | solution.py:120
  59.7 1.3 collective-permute-start.9
  61.0 0.9 collective-permute-done.8.refs_6_.refs_1_
  61.9 2.9 %mixer_weights.1.refs_3_.refs_7_ = f32[49,1024]{1,0:T(8,128)S(1)} custom-call(bf16[4,16,1024]{2,1,0:T(8,128)(2,1)S(1)} %get-tuple-element.96.refs_0_, bf16[3,16,1024]{2,1,0:T(8,128)(2,1)S(1)} %collective-permute-done.4.refs_1_, bf16[3,16,1024]{2,1,0:T(8,128)(2,1)S(1)} %collective-permute-done.5.refs_2_, ...), custom_call_target="tpu_custom_call" | custom-call | flops 3300001024 | bytes 1000 | tf_op jit(solution)/shard_map/mixer_weights/pallas_call | solution.py:33
  64.8 1.4 collective-permute-done.9.refs_2_
  66.3 4.5 %collective-permute-start.10 = (bf16[10,8,1024]{2,1,0:T(8,128)(2,1)S(1)}, bf16[10,8,1024]{2,1,0:T(8,128)(2,1)S(1)}, u32[]{:S(2)}, u32[]{:S(2)}) collective-permute-start(bf16[10,8,1024]{2,1,0:T(8,128)(2,1)S(1)} %get-tuple-element.108), channel_id=1, source_target_pairs={{0,1},{1,2},{2,3},{4,5},{5,6},{6,7},{8,9},{9,10},{10,11},{12,13},{... | collective-permute-start | bytes 491528 | tf_op jit(solution)/shard_map/ppermute | solution.py:120
  70.8 1.3 collective-permute-start.11
  72.1 2.6 %collective-permute-done.11.refs_4_ = bf16[10,8,1024]{2,1,0:T(8,128)(2,1)S(1)} collective-permute-done((bf16[10,8,1024]{2,1,0:T(8,128)(2,1)S(1)}, bf16[10,8,1024]{2,1,0:T(8,128)(2,1)S(1)}, u32[]{:S(2)}, u32[]{:S(2)}) %collective-permute-start.11) | collective-permute-done | bytes 163872 | tf_op jit(solution)/shard_map/ppermute | solution.py:120
  74.7 3.1 %section_grad.1 = (bf16[64,1024]{1,0:T(8,128)(2,1)S(1)}, bf16[2,64,256]{2,1,0:T(8,128)(2,1)S(1)}, bf16[2,64,256]{2,1,0:T(8,128)(2,1)S(1)}, bf16[256,3072]{1,0:T(8,128)(2,1)S(1)}) custom-call(bf16[4,16,1024]{2,1,0:T(8,128)(2,1)S(1)} %get-tuple-element.104.refs_0_, ...), custom_call_target="tpu_custom_call", output_to_operand_aliasing={{3}: (7, {})} | custom-call | flops 3300001024 | bytes 1000 | tf_op jit(solution)/shard_map/section_grad/pallas_call | solution.py:33
  77.8 3.9 %collective-permute-start.14 = (bf16[256,3072]{1,0:T(8,128)(2,1)S(1)}, bf16[256,3072]{1,0:T(8,128)(2,1)S(1)}, u32[]{:S(2)}, u32[]{:S(2)}) collective-permute-start(bf16[256,3072]{1,0:T(8,128)(2,1)S(1)} %get-tuple-element.127.refs_0_), channel_id=1, source_target_pairs={{0,1},{1,0},{2,3},{3,2},{4,5},{5,4},{6,7},{7,6},{8,9},{9,8},{10,11... | collective-permute-start | bytes 4718600 | tf_op jit(solution)/shard_map/ppermute | solution.py:47
  81.8 2.5 %merge_back.1 = (f32[256,512]{1,0:T(8,128)S(1)}, bf16[256,512]{1,0:T(8,128)(2,1)S(1)}, bf16[368,256]{1,0:T(8,128)(2,1)S(1)}, bf16[368,256]{1,0:T(8,128)(2,1)S(1)}) custom-call(bf16[64,1024]{1,0:T(8,128)(2,1)S(1)} %get-tuple-element.112.refs_0_, bf16[2048,1024]{1,0:T(8,128)(2,1)S(1)} %get-tuple-element.113.refs_1_, ...), custom_call_target="tpu_custom_call" | custom-call | flops 880001024 | bytes 1000 | tf_op jit(solution)/shard_map/merge_back/pallas_call | solution.py:33
  84.2 3.2 %mlp_back.1 = (bf16[256,1024]{1,0:T(8,128)(2,1)S(1)}, bf16[256,1024]{1,0:T(8,128)(2,1)S(1)}, bf16[8,32,512]{2,1,0:T(8,128)(2,1)S(1)}, bf16[3,32,512]{2,1,0:T(8,1...) custom-call(bf16[256,512]{1,0:T(8,128)(2,1)S(1)} %get-tuple-element.118.refs_0_, ...), custom_call_target="tpu_custom_call" | custom-call | flops 1320001024 | bytes 1000 | tf_op jit(solution)/shard_map/mlp_back/pallas_call | solution.py:33
  87.5 2.6 %patch_product.1 = (bf16[2048,256]{1,0:T(8,128)(2,1)S(1)}, bf16[2048,256]{1,0:T(8,128)(2,1)S(1)}) custom-call(bf16[256,3072]{1,0:T(8,128)(2,1)S(1)} %get-tuple-element.127.refs_0_, bf16[256,3072]{1,0:T(8,128)(2,1)S(1)} %collective-permute-done.14.refs_1_, bf16[2,64,256]{2,1,0:T(8,128)(2,1)S(1)} %get-tuple-element.132.refs_2_, ...), custom_call_target="tpu_custom_call" | custom-call | flops 990001024 | bytes 1000 | tf_op jit(solution)/shard_map/patch_product/pallas_call | solution.py:33
  90.8 24.8 %collective-permute-done.32.refs_1_ = bf16[2048,256]{1,0:T(8,128)(2,1)S(1)} collective-permute-done((bf16[2048,256]{1,0:T(8,128)(2,1)S(1)}, bf16[2048,256]{1,0:T(8,128)(2,1)S(1)}, u32[]{:S(2)}, u32[]{:S(2)}) %collective-permute-start.32) | collective-permute-done | bytes 1048608 | tf_op jit(solution)/shard_map/ppermute | solution.py:47
  115.9 1.1 collective-permute-start.33
  117.0 2.0 %expand_product.1 = (bf16[1024,256]{1,0:T(8,128)(2,1)S(1)}, bf16[1024,256]{1,0:T(8,128)(2,1)S(1)}) custom-call(bf16[256,3072]{1,0:T(8,128)(2,1)S(1)} %get-tuple-element.127.refs_0_, bf16[256,3072]{1,0:T(8,128)(2,1)S(1)} %collective-permute-done.14.refs_1_, bf16[256,1024]{1,0:T(8,128)(2,1)S(1)} %get-tuple-element.130.refs_2_, ...), custom_call_target="tpu_custom_call" | custom-call | flops 660001024 | bytes 1000 | tf_op jit(solution)/shard_map/expand_product/pallas_call | solution.py:33
  119.1 2.6 %project_product.1 = (bf16[1136,256]{1,0:T(8,128)(2,1)S(1)}, bf16[1136,256]{1,0:T(8,128)(2,1)S(1)}) custom-call(bf16[256,3072]{1,0:T(8,128)(2,1)S(1)} %get-tuple-element.127.refs_0_, bf16[256,3072]{1,0:T(8,128)(2,1)S(1)} %collective-permute-done.14.refs_1_, bf16[368,256]{1,0:T(8,128)(2,1)S(1)} %get-tuple-element.128.refs_2_, ...), custom_call_target="tpu_custom_call" | custom-call | flops 990001024 | bytes 1000 | tf_op jit(solution)/shard_map/project_product/pallas_call | solution.py:33
  121.7 1.7 collective-permute-start.27
  123.4 1.0 collective-permute-start.20
  124.3 6.4 %collective-permute-done.33.refs_1_ = bf16[1024,256]{1,0:T(8,128)(2,1)S(1)} collective-permute-done((bf16[1024,256]{1,0:T(8,128)(2,1)S(1)}, bf16[1024,256]{1,0:T(8,128)(2,1)S(1)}, u32[]{:S(2)}, u32[]{:S(2)}) %collective-permute-start.33) | collective-permute-done | bytes 524320 | tf_op jit(solution)/shard_map/ppermute | solution.py:47
  130.9 1.6 collective-permute-start.34
  132.5 5.4 %block_weights.1 = (bf16[64,256]{1,0:T(8,128)(2,1)S(1)}, bf16[64,256]{1,0:T(8,128)(2,1)S(1)}) custom-call(bf16[8,32,512]{2,1,0:T(8,128)(2,1)S(1)} %get-tuple-element.89.refs_0_, bf16[3,32,512]{2,1,0:T(8,128)(2,1)S(1)} %collective-permute-done.refs_5_.refs_1_, bf16[3,32,512]{2,1,0:T(8,128)(2,1)S(1)} %collective-permute-done.1.refs_2_, ...), custom_call_target="tpu_custom_call" | custom-call | flops 1980001024 | bytes 1000 | tf_op jit(solution)/shard_map/block_weights/pallas_call | solution.py:33
  138.0 3.0 %collective-permute-start.12 = (bf16[3,32,512]{2,1,0:T(8,128)(2,1)S(1)}, bf16[3,32,512]{2,1,0:T(8,128)(2,1)S(1)}, u32[]{:S(2)}, u32[]{:S(2)}) collective-permute-start(bf16[3,32,512]{2,1,0:T(8,128)(2,1)S(1)} %get-tuple-element.125), channel_id=1, source_target_pairs={{0,4},{4,8},{8,12},{12,16},{16,20},{20,24},{24,28},{1,5},{5,9},{9,... | collective-permute-start | bytes 294920 | tf_op jit(solution)/shard_map/ppermute | solution.py:120
  141.0 1.3 collective-permute-start.13
  142.3 1.3 collective-permute-done.12.refs_1_
  143.7 2.5 %collective-permute-start.22 = (bf16[64,256]{1,0:T(8,128)(2,1)S(1)}, bf16[64,256]{1,0:T(8,128)(2,1)S(1)}, u32[]{:S(2)}, u32[]{:S(2)}) collective-permute-start(bf16[64,256]{1,0:T(8,128)(2,1)S(1)} %add.23.refs_2_), channel_id=1, source_target_pairs={{0,4},{4,0},{8,12},{12,8},{16,20},{20,16},{24,28},{28,24},{1,5},{5... | collective-permute-start | bytes 98312 | tf_op jit(solution)/shard_map/ppermute | solution.py:47
  146.1 2.0 %collective-permute-done.13.refs_2_ = bf16[3,32,512]{2,1,0:T(8,128)(2,1)S(1)} collective-permute-done((bf16[3,32,512]{2,1,0:T(8,128)(2,1)S(1)}, bf16[3,32,512]{2,1,0:T(8,128)(2,1)S(1)}, u32[]{:S(2)}, u32[]{:S(2)}) %collective-permute-start.13) | collective-permute-done | bytes 98336 | tf_op jit(solution)/shard_map/ppermute | solution.py:120
  148.1 1.3 collective-permute-start.18
  149.5 1.3 collective-permute-start.19
  150.9 1.6 collective-permute-start.28
  152.7 1.7 collective-permute-start.23
  154.4 1.1 collective-permute-start.35
  155.5 6.6 %input_grad.1.refs_2_ = bf16[8,32,512]{2,1,0:T(8,128)(2,1)} custom-call(bf16[8,32,512]{2,1,0:T(8,128)(2,1)S(1)} %get-tuple-element.124.refs_0_.refs_5_, bf16[3,32,512]{2,1,0:T(8,128)(2,1)S(1)} %collective-permute-done.12.refs_1_, bf16[3,32,512]{2,1,0:T(8,128)(2,1)S(1)} %collective-permute-done.13.refs_2_, ...), custom_call_target="tpu_custom_call" | custom-call | flops 2200001024 | bytes 1000 | tf_op jit(solution)/shard_map/input_grad/pallas_call | solution.py:33
  162.1 3.0 %collective-permute-done.23.refs_1_ = bf16[576,256]{1,0:T(8,128)(2,1)S(1)} collective-permute-done((bf16[576,256]{1,0:T(8,128)(2,1)S(1)}, bf16[576,256]{1,0:T(8,128)(2,1)S(1)}, u32[]{:S(2)}, u32[]{:S(2)}) %collective-permute-start.23) | collective-permute-done | bytes 294944 | tf_op jit(solution)/shard_map/ppermute | solution.py:47
  165.1 0.9 copy-done
  166.3 3.0 %collective-permute-start.29 = (bf16[368,256]{1,0:T(8,128)(2,1)S(1)}, bf16[368,256]{1,0:T(8,128)(2,1)S(1)}, u32[]{:S(2)}, u32[]{:S(2)}) collective-permute-start(bf16[368,256]{1,0:T(8,128)(2,1)S(1)} %get-tuple-element.155), channel_id=1, source_target_pairs={{0,16},{4,20},{8,24},{12,28},{16,0},{20,4},{24,8},{28,12},{1,17},{... | collective-permute-start | bytes 565256 | tf_op jit(solution)/shard_map/ppermute | solution.py:47
  169.3 1.1 collective-permute-start.36
  170.4 9.9 %collective-permute-done.24 = bf16[320,256]{1,0:T(8,128)(2,1)S(1)} collective-permute-done((bf16[320,256]{1,0:T(8,128)(2,1)S(1)}, bf16[320,256]{1,0:T(8,128)(2,1)S(1)}, u32[]{:S(2)}, u32[]{:S(2)}) %collective-permute-start.24) | collective-permute-done | bytes 163872 | tf_op jit(solution)/shard_map/ppermute | solution.py:47
  180.6 3.7 %collective-permute-done.29 = bf16[368,256]{1,0:T(8,128)(2,1)S(1)} collective-permute-done((bf16[368,256]{1,0:T(8,128)(2,1)S(1)}, bf16[368,256]{1,0:T(8,128)(2,1)S(1)}, u32[]{:S(2)}, u32[]{:S(2)}) %collective-permute-start.29) | collective-permute-done | bytes 188448 | tf_op jit(solution)/shard_map/ppermute | solution.py:47
  184.6 6.5 %collective-permute-done.30 = bf16[368,256]{1,0:T(8,128)(2,1)S(1)} collective-permute-done((bf16[368,256]{1,0:T(8,128)(2,1)S(1)}, bf16[368,256]{1,0:T(8,128)(2,1)S(1)}, u32[]{:S(2)}, u32[]{:S(2)}) %collective-permute-start.30) | collective-permute-done | bytes 188448 | tf_op jit(solution)/shard_map/ppermute | solution.py:47
  191.8 1.0 collective-permute-done.26.refs_1_
  192.9 0.9 finish_expand.1
  193.8 1.0 finish_project.1
  194.7 1.0 finish_patch.1
  (73 shorter events, 4.4 us)
Async XLA Ops:
  0.6 19.0 %copy-start.6 = (bf16[1,4,16,1024]{3,2,1,0:T(8,128)(2,1)S(1)}, bf16[1,4,16,1024]{3,2,1,0:T(8,128)(2,1)}, u32[]{:S(2)}) copy-start(bf16[1,4,16,1024]{3,2,1,0:T(8,128)(2,1)} %param.22) | copy-start | bytes 393220
  0.7 19.0 %copy-start.7 = (bf16[1,4,16,1024]{3,2,1,0:T(8,128)(2,1)S(1)}, bf16[1,4,16,1024]{3,2,1,0:T(8,128)(2,1)}, u32[]{:S(2)}) copy-start(bf16[1,4,16,1024]{3,2,1,0:T(8,128)(2,1)} %param.23) | copy-start | bytes 393220
  0.7 18.9 %copy-start.9 = (f32[1024]{0:T(1024)S(1)}, f32[1024]{0:T(1024)}, u32[]{:S(2)}) copy-start(f32[1024]{0:T(1024)} %param.21) | copy-start | bytes 12292
  1.7 7.0 %collective-permute-start = (bf16[3,32,512]{2,1,0:T(8,128)(2,1)S(1)}, bf16[3,32,512]{2,1,0:T(8,128)(2,1)S(1)}, u32[]{:S(2)}, u32[]{:S(2)}) collective-permute-start(bf16[3,32,512]{2,1,0:T(8,128)(2,1)S(1)} %get-tuple-element.171), channel_id=1, source_target_pairs={{0,4},{4,8},{8,12},{12,16},{16,20},{20,24},{24,28},{1,5},{5,9},{9,... | collective-permute-start | bytes 294920 | tf_op jit(solution)/shard_map/ppermute | solution.py:120
  6.5 6.5 %collective-permute-start.1 = (bf16[3,32,512]{2,1,0:T(8,128)(2,1)S(1)}, bf16[3,32,512]{2,1,0:T(8,128)(2,1)S(1)}, u32[]{:S(2)}, u32[]{:S(2)}) collective-permute-start(bf16[3,32,512]{2,1,0:T(8,128)(2,1)S(1)} %get-tuple-element.170), channel_id=1, source_target_pairs={{4,0},{8,4},{12,8},{16,12},{20,16},{24,20},{28,24},{5,1},{9,5},{13... | collective-permute-start | bytes 294920 | tf_op jit(solution)/shard_map/ppermute | solution.py:120
  8.7 0.9 copy-start.1
  9.7 0.9 copy-start.8
  10.6 0.7 copy-start.10
  11.3 0.7 copy-start.11
  11.9 0.7 copy-start.12
  12.6 7.0 %copy-start.2 = (bf16[2048,1024]{1,0:T(8,128)(2,1)S(1)}, bf16[2048,1024]{1,0:T(8,128)(2,1)}, u32[]{:S(2)}) copy-start(bf16[2048,1024]{1,0:T(8,128)(2,1)} %refs_11_.1) | copy-start | bytes 12582916
  12.6 7.0 %copy-start.3 = (bf16[512,2048]{1,0:T(8,128)(2,1)S(1)}, bf16[512,2048]{1,0:T(8,128)(2,1)}, u32[]{:S(2)}) copy-start(bf16[512,2048]{1,0:T(8,128)(2,1)} %refs_9_.1) | copy-start | bytes 6291460
  12.6 7.0 %copy-start.4 = (bf16[2048,512]{1,0:T(8,128)(2,1)S(1)}, bf16[2048,512]{1,0:T(8,128)(2,1)}, u32[]{:S(2)}) copy-start(bf16[2048,512]{1,0:T(8,128)(2,1)} %refs_10_.1) | copy-start | bytes 6291460
  12.6 7.0 %copy-start.5 = (f32[7,7,1024]{2,1,0:T(8,128)S(1)}, f32[7,7,1024]{2,1,0:T(8,128)}, u32[]{:S(2)}) copy-start(f32[7,7,1024]{2,1,0:T(8,128)} %refs_12_.1) | copy-start | bytes 602116
  13.1 3.0 %collective-permute-start.2 = (bf16[14,8,512]{2,1,0:T(8,128)(2,1)S(1)}, bf16[14,8,512]{2,1,0:T(8,128)(2,1)S(1)}, u32[]{:S(2)}, u32[]{:S(2)}) collective-permute-start(bf16[14,8,512]{2,1,0:T(8,128)(2,1)S(1)} %get-tuple-element.90), channel_id=1, source_target_pairs={{0,1},{1,2},{2,3},{4,5},{5,6},{6,7},{8,9},{9,10},{10,11},{12,13},{... | collective-permute-start | bytes 344072 | tf_op jit(solution)/shard_map/ppermute | solution.py:120
  14.6 5.0 %collective-permute-start.3 = (bf16[14,8,512]{2,1,0:T(8,128)(2,1)S(1)}, bf16[14,8,512]{2,1,0:T(8,128)(2,1)S(1)}, u32[]{:S(2)}, u32[]{:S(2)}) collective-permute-start(bf16[14,8,512]{2,1,0:T(8,128)(2,1)S(1)} %get-tuple-element.91), channel_id=1, source_target_pairs={{1,0},{2,1},{3,2},{5,4},{6,5},{7,6},{9,8},{10,9},{11,10},{13,12},{... | collective-permute-start | bytes 344072 | tf_op jit(solution)/shard_map/ppermute | solution.py:120
  32.5 6.6 %collective-permute-start.4 = (bf16[3,16,1024]{2,1,0:T(8,128)(2,1)S(1)}, bf16[3,16,1024]{2,1,0:T(8,128)(2,1)S(1)}, u32[]{:S(2)}, u32[]{:S(2)}) collective-permute-start(bf16[3,16,1024]{2,1,0:T(8,128)(2,1)S(1)} %get-tuple-element.97), channel_id=1, source_target_pairs={{0,4},{4,8},{8,12},{12,16},{16,20},{20,24},{24,28},{1,5},{5,9},{9,... | collective-permute-start | bytes 294920 | tf_op jit(solution)/shard_map/ppermute | solution.py:120
  36.8 6.7 %collective-permute-start.5 = (bf16[3,16,1024]{2,1,0:T(8,128)(2,1)S(1)}, bf16[3,16,1024]{2,1,0:T(8,128)(2,1)S(1)}, u32[]{:S(2)}, u32[]{:S(2)}) collective-permute-start(bf16[3,16,1024]{2,1,0:T(8,128)(2,1)S(1)} %get-tuple-element.98), channel_id=1, source_target_pairs={{4,0},{8,4},{12,8},{16,12},{20,16},{24,20},{28,24},{5,1},{9,5},{13... | collective-permute-start | bytes 294920 | tf_op jit(solution)/shard_map/ppermute | solution.py:120
  43.6 5.5 %collective-permute-start.6 = (bf16[10,8,1024]{2,1,0:T(8,128)(2,1)S(1)}, bf16[10,8,1024]{2,1,0:T(8,128)(2,1)S(1)}, u32[]{:S(2)}, u32[]{:S(2)}) collective-permute-start(bf16[10,8,1024]{2,1,0:T(8,128)(2,1)S(1)} %get-tuple-element.99), channel_id=1, source_target_pairs={{0,1},{1,2},{2,3},{4,5},{5,6},{6,7},{8,9},{9,10},{10,11},{12,13},{... | collective-permute-start | bytes 491528 | tf_op jit(solution)/shard_map/ppermute | solution.py:120
  47.8 3.8 %collective-permute-start.7 = (bf16[10,8,1024]{2,1,0:T(8,128)(2,1)S(1)}, bf16[10,8,1024]{2,1,0:T(8,128)(2,1)S(1)}, u32[]{:S(2)}, u32[]{:S(2)}) collective-permute-start(bf16[10,8,1024]{2,1,0:T(8,128)(2,1)S(1)} %get-tuple-element.100), channel_id=1, source_target_pairs={{1,0},{2,1},{3,2},{5,4},{6,5},{7,6},{9,8},{10,9},{11,10},{13,12},{... | collective-permute-start | bytes 491528 | tf_op jit(solution)/shard_map/ppermute | solution.py:120
  54.9 7.0 %collective-permute-start.8 = (bf16[3,16,1024]{2,1,0:T(8,128)(2,1)S(1)}, bf16[3,16,1024]{2,1,0:T(8,128)(2,1)S(1)}, u32[]{:S(2)}, u32[]{:S(2)}) collective-permute-start(bf16[3,16,1024]{2,1,0:T(8,128)(2,1)S(1)} %get-tuple-element.105), channel_id=1, source_target_pairs={{0,4},{4,8},{8,12},{12,16},{16,20},{20,24},{24,28},{1,5},{5,9},{9,... | collective-permute-start | bytes 294920 | tf_op jit(solution)/shard_map/ppermute | solution.py:120
  59.7 6.5 %collective-permute-start.9 = (bf16[3,16,1024]{2,1,0:T(8,128)(2,1)S(1)}, bf16[3,16,1024]{2,1,0:T(8,128)(2,1)S(1)}, u32[]{:S(2)}, u32[]{:S(2)}) collective-permute-start(bf16[3,16,1024]{2,1,0:T(8,128)(2,1)S(1)} %get-tuple-element.106), channel_id=1, source_target_pairs={{4,0},{8,4},{12,8},{16,12},{20,16},{24,20},{28,24},{5,1},{9,5},{13... | collective-permute-start | bytes 294920 | tf_op jit(solution)/shard_map/ppermute | solution.py:120
  66.3 5.8 %collective-permute-start.10 = (bf16[10,8,1024]{2,1,0:T(8,128)(2,1)S(1)}, bf16[10,8,1024]{2,1,0:T(8,128)(2,1)S(1)}, u32[]{:S(2)}, u32[]{:S(2)}) collective-permute-start(bf16[10,8,1024]{2,1,0:T(8,128)(2,1)S(1)} %get-tuple-element.108), channel_id=1, source_target_pairs={{0,1},{1,2},{2,3},{4,5},{5,6},{6,7},{8,9},{9,10},{10,11},{12,13},{... | collective-permute-start | bytes 491528 | tf_op jit(solution)/shard_map/ppermute | solution.py:120
  70.8 3.9 %collective-permute-start.11 = (bf16[10,8,1024]{2,1,0:T(8,128)(2,1)S(1)}, bf16[10,8,1024]{2,1,0:T(8,128)(2,1)S(1)}, u32[]{:S(2)}, u32[]{:S(2)}) collective-permute-start(bf16[10,8,1024]{2,1,0:T(8,128)(2,1)S(1)} %get-tuple-element.109), channel_id=1, source_target_pairs={{1,0},{2,1},{3,2},{5,4},{6,5},{7,6},{9,8},{10,9},{11,10},{13,12},{... | collective-permute-start | bytes 491528 | tf_op jit(solution)/shard_map/ppermute | solution.py:120
  77.8 9.7 %collective-permute-start.14 = (bf16[256,3072]{1,0:T(8,128)(2,1)S(1)}, bf16[256,3072]{1,0:T(8,128)(2,1)S(1)}, u32[]{:S(2)}, u32[]{:S(2)}) collective-permute-start(bf16[256,3072]{1,0:T(8,128)(2,1)S(1)} %get-tuple-element.127.refs_0_), channel_id=1, source_target_pairs={{0,1},{1,0},{2,3},{3,2},{4,5},{5,4},{6,7},{7,6},{8,9},{9,8},{10,11... | collective-permute-start | bytes 4718600 | tf_op jit(solution)/shard_map/ppermute | solution.py:47
  81.7 5.8 %collective-permute-start.17 = (bf16[2,64,256]{2,1,0:T(8,128)(2,1)S(1)}, bf16[2,64,256]{2,1,0:T(8,128)(2,1)S(1)}, u32[]{:S(2)}, u32[]{:S(2)}) collective-permute-start(bf16[2,64,256]{2,1,0:T(8,128)(2,1)S(1)} %get-tuple-element.133), channel_id=1, source_target_pairs={{0,1},{1,0},{2,3},{3,2},{4,5},{5,4},{6,7},{7,6},{8,9},{9,8},{10,11... | collective-permute-start | bytes 196616 | tf_op jit(solution)/shard_map/ppermute | solution.py:47
  90.1 25.6 %collective-permute-start.32 = (bf16[2048,256]{1,0:T(8,128)(2,1)S(1)}, bf16[2048,256]{1,0:T(8,128)(2,1)S(1)}, u32[]{:S(2)}, u32[]{:S(2)}) collective-permute-start(bf16[2048,256]{1,0:T(8,128)(2,1)S(1)} %get-tuple-element.134.refs_4_), channel_id=1, source_target_pairs={{0,2},{1,3},{2,0},{3,1},{4,6},{5,7},{6,4},{7,5},{8,10},{9,11},{10,... | collective-permute-start | bytes 3145736 | tf_op jit(solution)/shard_map/ppermute | solution.py:47
  90.3 26.7 %collective-permute-start.16 = (bf16[256,1024]{1,0:T(8,128)(2,1)S(1)}, bf16[256,1024]{1,0:T(8,128)(2,1)S(1)}, u32[]{:S(2)}, u32[]{:S(2)}) collective-permute-start(bf16[256,1024]{1,0:T(8,128)(2,1)S(1)} %get-tuple-element.131.refs_4_), channel_id=1, source_target_pairs={{0,1},{1,0},{2,3},{3,2},{4,5},{5,4},{6,7},{7,6},{8,9},{9,8},{10,11... | collective-permute-start | bytes 1572872 | tf_op jit(solution)/shard_map/ppermute | solution.py:47
  90.6 28.4 %collective-permute-start.15 = (bf16[368,256]{1,0:T(8,128)(2,1)S(1)}, bf16[368,256]{1,0:T(8,128)(2,1)S(1)}, u32[]{:S(2)}, u32[]{:S(2)}) collective-permute-start(bf16[368,256]{1,0:T(8,128)(2,1)S(1)} %get-tuple-element.129), channel_id=1, source_target_pairs={{0,1},{1,0},{2,3},{3,2},{4,5},{5,4},{6,7},{7,6},{8,9},{9,8},{10,11... | collective-permute-start | bytes 565256 | tf_op jit(solution)/shard_map/ppermute | solution.py:47
  115.9 14.9 %collective-permute-start.33 = (bf16[1024,256]{1,0:T(8,128)(2,1)S(1)}, bf16[1024,256]{1,0:T(8,128)(2,1)S(1)}, u32[]{:S(2)}, u32[]{:S(2)}) collective-permute-start(bf16[1024,256]{1,0:T(8,128)(2,1)S(1)} %get-tuple-element.161), channel_id=1, source_target_pairs={{0,4},{4,0},{8,12},{12,8},{16,20},{20,16},{24,28},{28,24},{1,5},{5... | collective-permute-start | bytes 1572872 | tf_op jit(solution)/shard_map/ppermute | solution.py:47
  121.7 27.8 %collective-permute-start.27 = (bf16[1136,256]{1,0:T(8,128)(2,1)S(1)}, bf16[1136,256]{1,0:T(8,128)(2,1)S(1)}, u32[]{:S(2)}, u32[]{:S(2)}) collective-permute-start(bf16[1136,256]{1,0:T(8,128)(2,1)S(1)} %get-tuple-element.136.refs_3_.refs_7_), channel_id=1, source_target_pairs={{0,8},{4,12},{8,0},{12,4},{16,24},{20,28},{24,16},{28,20},{1,9},{5... | collective-permute-start | bytes 1744904 | tf_op jit(solution)/shard_map/ppermute | solution.py:47
  123.4 29.2 %collective-permute-start.20 = (bf16[1024,256]{1,0:T(8,128)(2,1)S(1)}, bf16[1024,256]{1,0:T(8,128)(2,1)S(1)}, u32[]{:S(2)}, u32[]{:S(2)}) collective-permute-start(bf16[1024,256]{1,0:T(8,128)(2,1)S(1)} %get-tuple-element.135.refs_4_), channel_id=1, source_target_pairs={{0,4},{4,0},{8,12},{12,8},{16,20},{20,16},{24,28},{28,24},{1,5},{5... | collective-permute-start | bytes 1572872 | tf_op jit(solution)/shard_map/ppermute | solution.py:47
  130.9 23.4 %collective-permute-start.34 = (bf16[512,256]{1,0:T(8,128)(2,1)S(1)}, bf16[512,256]{1,0:T(8,128)(2,1)S(1)}, u32[]{:S(2)}, u32[]{:S(2)}) collective-permute-start(bf16[512,256]{1,0:T(8,128)(2,1)S(1)} %get-tuple-element.163), channel_id=1, source_target_pairs={{0,8},{4,12},{8,0},{12,4},{16,24},{20,28},{24,16},{28,20},{1,9},{5... | collective-permute-start | bytes 786440 | tf_op jit(solution)/shard_map/ppermute | solution.py:47
  137.9 3.1 %collective-permute-start.21 = (bf16[64,256]{1,0:T(8,128)(2,1)S(1)}, bf16[64,256]{1,0:T(8,128)(2,1)S(1)}, u32[]{:S(2)}, u32[]{:S(2)}) collective-permute-start(bf16[64,256]{1,0:T(8,128)(2,1)S(1)} %get-tuple-element.143), channel_id=1, source_target_pairs={{0,1},{1,0},{2,3},{3,2},{4,5},{5,4},{6,7},{7,6},{8,9},{9,8},{10,11... | collective-permute-start | bytes 98312 | tf_op jit(solution)/shard_map/ppermute | solution.py:47
  138.0 5.7 %collective-permute-start.12 = (bf16[3,32,512]{2,1,0:T(8,128)(2,1)S(1)}, bf16[3,32,512]{2,1,0:T(8,128)(2,1)S(1)}, u32[]{:S(2)}, u32[]{:S(2)}) collective-permute-start(bf16[3,32,512]{2,1,0:T(8,128)(2,1)S(1)} %get-tuple-element.125), channel_id=1, source_target_pairs={{0,4},{4,8},{8,12},{12,16},{16,20},{20,24},{24,28},{1,5},{5,9},{9,... | collective-permute-start | bytes 294920 | tf_op jit(solution)/shard_map/ppermute | solution.py:120
  141.0 7.1 %collective-permute-start.13 = (bf16[3,32,512]{2,1,0:T(8,128)(2,1)S(1)}, bf16[3,32,512]{2,1,0:T(8,128)(2,1)S(1)}, u32[]{:S(2)}, u32[]{:S(2)}) collective-permute-start(bf16[3,32,512]{2,1,0:T(8,128)(2,1)S(1)} %get-tuple-element.126), channel_id=1, source_target_pairs={{4,0},{8,4},{12,8},{16,12},{20,16},{24,20},{28,24},{5,1},{9,5},{13... | collective-permute-start | bytes 294920 | tf_op jit(solution)/shard_map/ppermute | solution.py:120
  143.7 7.3 %collective-permute-start.22 = (bf16[64,256]{1,0:T(8,128)(2,1)S(1)}, bf16[64,256]{1,0:T(8,128)(2,1)S(1)}, u32[]{:S(2)}, u32[]{:S(2)}) collective-permute-start(bf16[64,256]{1,0:T(8,128)(2,1)S(1)} %add.23.refs_2_), channel_id=1, source_target_pairs={{0,4},{4,0},{8,12},{12,8},{16,20},{20,16},{24,28},{28,24},{1,5},{5... | collective-permute-start | bytes 98312 | tf_op jit(solution)/shard_map/ppermute | solution.py:47
  148.1 7.3 %collective-permute-start.18 = (bf16[14,8,512]{2,1,0:T(8,128)(2,1)S(1)}, bf16[14,8,512]{2,1,0:T(8,128)(2,1)S(1)}, u32[]{:S(2)}, u32[]{:S(2)}) collective-permute-start(bf16[14,8,512]{2,1,0:T(8,128)(2,1)S(1)} %get-tuple-element.137), channel_id=1, source_target_pairs={{0,1},{1,2},{2,3},{4,5},{5,6},{6,7},{8,9},{9,10},{10,11},{12,13},{... | collective-permute-start | bytes 344072 | tf_op jit(solution)/shard_map/ppermute | solution.py:120
  149.5 6.0 %collective-permute-start.19 = (bf16[14,8,512]{2,1,0:T(8,128)(2,1)S(1)}, bf16[14,8,512]{2,1,0:T(8,128)(2,1)S(1)}, u32[]{:S(2)}, u32[]{:S(2)}) collective-permute-start(bf16[14,8,512]{2,1,0:T(8,128)(2,1)S(1)} %get-tuple-element.138), channel_id=1, source_target_pairs={{1,0},{2,1},{3,2},{5,4},{6,5},{7,6},{9,8},{10,9},{11,10},{13,12},{... | collective-permute-start | bytes 344072 | tf_op jit(solution)/shard_map/ppermute | solution.py:120
  150.9 15.3 %collective-permute-start.28 = (bf16[624,256]{1,0:T(8,128)(2,1)S(1)}, bf16[624,256]{1,0:T(8,128)(2,1)S(1)}, u32[]{:S(2)}, u32[]{:S(2)}) collective-permute-start(bf16[624,256]{1,0:T(8,128)(2,1)S(1)} %get-tuple-element.153), channel_id=1, source_target_pairs={{0,4},{4,0},{8,12},{12,8},{16,20},{20,16},{24,28},{28,24},{1,5},{5... | collective-permute-start | bytes 958472 | tf_op jit(solution)/shard_map/ppermute | solution.py:47
  152.7 12.5 %collective-permute-start.23 = (bf16[576,256]{1,0:T(8,128)(2,1)S(1)}, bf16[576,256]{1,0:T(8,128)(2,1)S(1)}, u32[]{:S(2)}, u32[]{:S(2)}) collective-permute-start(bf16[576,256]{1,0:T(8,128)(2,1)S(1)} %get-tuple-element.144.refs_8_), channel_id=1, source_target_pairs={{0,8},{4,12},{8,0},{12,4},{16,24},{20,28},{24,16},{28,20},{1,9},{5... | collective-permute-start | bytes 884744 | tf_op jit(solution)/shard_map/ppermute | solution.py:47
  154.4 14.9 %collective-permute-start.35 = (bf16[256,256]{1,0:T(8,128)(2,1)S(1)}, bf16[256,256]{1,0:T(8,128)(2,1)S(1)}, u32[]{:S(2)}, u32[]{:S(2)}) collective-permute-start(bf16[256,256]{1,0:T(8,128)(2,1)S(1)} %get-tuple-element.165), channel_id=1, source_target_pairs={{0,16},{4,20},{8,24},{12,28},{16,0},{20,4},{24,8},{28,12},{1,17},{... | collective-permute-start | bytes 393224 | tf_op jit(solution)/shard_map/ppermute | solution.py:47
  165.1 1.0 copy-start
  166.1 14.2 %collective-permute-start.24 = (bf16[320,256]{1,0:T(8,128)(2,1)S(1)}, bf16[320,256]{1,0:T(8,128)(2,1)S(1)}, u32[]{:S(2)}, u32[]{:S(2)}) collective-permute-start(bf16[320,256]{1,0:T(8,128)(2,1)S(1)} %get-tuple-element.147), channel_id=1, source_target_pairs={{0,16},{4,20},{8,24},{12,28},{16,0},{20,4},{24,8},{28,12},{1,17},{... | collective-permute-start | bytes 491528 | tf_op jit(solution)/shard_map/ppermute | solution.py:47
  166.3 18.0 %collective-permute-start.29 = (bf16[368,256]{1,0:T(8,128)(2,1)S(1)}, bf16[368,256]{1,0:T(8,128)(2,1)S(1)}, u32[]{:S(2)}, u32[]{:S(2)}) collective-permute-start(bf16[368,256]{1,0:T(8,128)(2,1)S(1)} %get-tuple-element.155), channel_id=1, source_target_pairs={{0,16},{4,20},{8,24},{12,28},{16,0},{20,4},{24,8},{28,12},{1,17},{... | collective-permute-start | bytes 565256 | tf_op jit(solution)/shard_map/ppermute | solution.py:47
  169.3 15.1 %collective-permute-start.36 = (bf16[1,256,256]{2,1,0:T(8,128)(2,1)S(1)}, bf16[1,256,256]{2,1,0:T(8,128)(2,1)S(1)}, u32[]{:S(2)}, u32[]{:S(2)}) collective-permute-start(bf16[1,256,256]{2,1,0:T(8,128)(2,1)S(1)} %add_bitcast_fusion), channel_id=1, source_target_pairs={{0,2},{1,3},{2,0},{3,1},{4,6},{5,7},{6,4},{7,5},{8,10},{9,11},{10,... | collective-permute-start | bytes 393224 | tf_op jit(solution)/shard_map/ppermute | solution.py:47
  180.4 10.8 %collective-permute-start.25 = (bf16[320,256]{1,0:T(8,128)(2,1)S(1)}, bf16[320,256]{1,0:T(8,128)(2,1)S(1)}, u32[]{:S(2)}, u32[]{:S(2)}) collective-permute-start(bf16[320,256]{1,0:T(8,128)(2,1)S(1)} %add.24), channel_id=1, source_target_pairs={{0,2},{1,3},{2,0},{3,1},{4,6},{5,7},{6,4},{7,5},{8,10},{9,11},{10,... | collective-permute-start | bytes 491528 | tf_op jit(solution)/shard_map/ppermute | solution.py:47
  184.4 6.7 %collective-permute-start.30 = (bf16[368,256]{1,0:T(8,128)(2,1)S(1)}, bf16[368,256]{1,0:T(8,128)(2,1)S(1)}, u32[]{:S(2)}, u32[]{:S(2)}) collective-permute-start(bf16[368,256]{1,0:T(8,128)(2,1)S(1)} %add.26), channel_id=1, source_target_pairs={{0,2},{1,3},{2,0},{3,1},{4,6},{5,7},{6,4},{7,5},{8,10},{9,11},{10,... | collective-permute-start | bytes 565256 | tf_op jit(solution)/shard_map/ppermute | solution.py:47
  184.5 10.2 %collective-permute-start.37 = (bf16[2,256,256]{2,1,0:T(8,128)(2,1)S(1)}, bf16[2,256,256]{2,1,0:T(8,128)(2,1)S(1)}, u32[]{:S(2)}, u32[]{:S(2)}) collective-permute-start(bf16[2,256,256]{2,1,0:T(8,128)(2,1)S(1)} %maximum_bitcast_fusion.refs_0_), channel_id=1, source_target_pairs={{0,1},{1,0},{2,3},{3,2},{4,5},{5,4},{6,7},{7,6},{8,9},{9,8},{10,11... | collective-permute-start | bytes 786440 | tf_op jit(solution)/shard_map/ppermute | solution.py:47
  191.1 2.6 %collective-permute-start.31 = (bf16[368,256]{1,0:T(8,128)(2,1)S(1)}, bf16[368,256]{1,0:T(8,128)(2,1)S(1)}, u32[]{:S(2)}, u32[]{:S(2)}) collective-permute-start(bf16[368,256]{1,0:T(8,128)(2,1)S(1)} %add.27.refs_0_), channel_id=1, source_target_pairs={{0,1},{1,0},{2,3},{3,2},{4,5},{5,4},{6,7},{7,6},{8,9},{9,8},{10,11... | collective-permute-start | bytes 565256 | tf_op jit(solution)/shard_map/ppermute | solution.py:47
  191.3 1.6 collective-permute-start.26

commit v7 on v6

--- a/solution.py
+++ b/solution.py
@@ -55,25 +55,36 @@
     return (lax.axis_index(axis) // bit) % 2
 
 
-def chain(keep, send, order, count, rows, extra=(), between=None):
-    for place, (axis, bit, _) in enumerate(order):
-        received = swap(send, axis, bit)
-        if place + 1 == len(order):
-            return keep + received
-        axis, bit, position = order[place + 1]
-        grown = extra if place == 0 else ()
-        count //= 2
-        tail = keep.shape[0] - count * rows + (grown[0].shape[0] if grown else 0)
-        out = shape_of(count // 2 * rows + tail, keep.shape[1], dtype=BF)
-        keep, send = run(
-            functools.partial(step_kernel, axis, bit, position, count, rows),
+class Chain:
+    def __init__(self, keep, send, order, count, rows):
+        self.keep, self.send, self.order = keep, send, list(order)
+        self.count, self.rows = count, rows
+
+    def advance(self, after=(), extra=()):
+        axis, bit, _ = self.order.pop(0)
+        keep, received = self.keep, swap(self.send, axis, bit)
+        if not self.order:
+            self.keep = keep + received
+            return ()
+        axis, bit, position = self.order[0]
+        self.count //= 2
+        tail = keep.shape[0] - self.count * self.rows + (extra[0].shape[0] if extra else 0)
+        out = shape_of(self.count // 2 * self.rows + tail, keep.shape[1], dtype=BF)
+        self.keep, self.send = run(
+            functools.partial(step_kernel, axis, bit, position, self.count, self.rows),
             "sum_step",
-            (keep, received, *grown),
+            (keep, received, *extra),
             (out, out),
-            after=between(send) if between and place == 1 else (),
+            after=after,
             limit=8,
             us=0.2,
         )
+        return (self.send,)
+
+    def finish(self):
+        while self.order:
+            self.advance()
+        return self.keep
 
 
 def step_kernel(axis, bit, position, count, rows, keep, received, *refs):
@@ -822,7 +833,7 @@
         "expand_product",
         (early, early_other, upward_keep, upward_other),
         (expand_half, expand_half),
-        after=(patch_send,),
+        after=(patch_send, rows_back[0]),
         limit=16,
         us=0.6,
     )
@@ -852,25 +863,32 @@
         limit=12,
         us=1.8,
     )
-    def finish_input(sent):
-        return run(
-            input_kernel,
-            "input_grad",
-            (*framed_back, taps_three, grad_summed),
-            (shape_of(height, breadth, channels, dtype=BF),),
-            scratch=(frame_scratch(center), pltpu.VMEM((height, breadth, channels), F32)),
-            after=(small_keep, sent),
-            limit=12,
-            us=2,
-        )
-
     row_bits, col_bits = axis_bits("row"), axis_bits("col")
     outer = len(row_bits)
     low_first = [("row", bit, 0) for bit in row_bits]
     patch_order = [("col", bit, outer) for bit in col_bits[1:]] + low_first
-    patch_sum = chain(
-        patch_keep, patch_send, patch_order, block_count * row_count, 4 * channels // row_count
-    )
+    project_order = [("row", row_bits[1], 1), low_first[0], *low_first[2:]]
+    patch_chain = Chain(patch_keep, patch_send, patch_order, block_count * row_count, 4 * channels // row_count)
+    project_chain = Chain(project_keep, project_send, project_order, row_count, deep)
+    expand_chain = Chain(expand_keep, expand_send, low_first, row_count, groups * shallow)
+    small = small_keep + swap(small_send, "col", 1)
+    sent = expand_chain.advance(extra=(small, swap(small, "row", 1)))
+    sent = project_chain.advance(sent)
+    sent = patch_chain.advance(sent)
+    (input_grad,) = run(
+        input_kernel,
+        "input_grad",
+        (*framed_back, taps_three, grad_summed),
+        (shape_of(height, breadth, channels, dtype=BF),),
+        scratch=(frame_scratch(center), pltpu.VMEM((height, breadth, channels), F32)),
+        after=sent,
+        limit=12,
+        us=2,
+    )
+    sent = expand_chain.advance((input_grad,))
+    sent = project_chain.advance(sent)
+    patch_chain.advance(sent)
+    patch_sum = patch_chain.finish()
     patch_sum = gather(patch_sum, "col", col_bits[1:])
     (patch_grad,) = run(
         finish_patch_kernel,
@@ -885,35 +903,25 @@
             total = total + swap(total, "col", bit)
         return total, swap(total, "col", 1)
 
-    project_order = [("row", row_bits[1], 1), low_first[0], *low_first[2:]]
     vector, wide_vector = shape_of(1, channels), shape_of(1, wide)
     project_grad, wide_taps, wide_gain, merge_sum, layer_sum = run(
         finish_project_kernel,
         "finish_project",
-        share(chain(project_keep, project_send, project_order, row_count, deep)),
+        share(project_chain.finish()),
         (shape_of(deep, channels), shape_of(7, 7, wide), wide_vector, vector, vector),
         scratch=(pltpu.VMEM((112, channels), F32),),
         limit=8,
     )
-    small = small_keep + swap(small_send, "col", 1)
-    pair = (small, swap(small, "row", 1))
-    input_grad = []
-
-    def between(sent):
-        input_grad.extend(finish_input(sent))
-        return input_grad
-
-    expand_sum = chain(expand_keep, expand_send, low_first, row_count, groups * shallow, pair, between)
     expand_grad, taps_sum, gain_sum = run(
         finish_expand_kernel,
         "finish_expand",
-        share(expand_sum),
+        share(expand_chain.finish()),
         (shape_of(shallow, hidden_width), shape_of(7, 7, channels), vector),
         scratch=(pltpu.VMEM((64, channels), F32),),
         limit=8,
     )
     return (
-        input_grad[0][None],
+        input_grad[None],
         taps_sum,
         gain_sum[0],
         expand_grad,

time: 196 us -> 198 us (1.010)
    ppermute x8, waiting for transfers between devices: 16.8 us -> 30.9 us  [neighbours(): lax.ppermute(first, axis, backward)]
    ppermute x22, waiting for transfers between devices: 55.5 us -> 42 us  [swap(): lax.ppermute(values, axis, [(i, i ^ bit) for i in range(lax.axis_size(axi...]
  transfers between devices with their start and end apart: 38 -> 38, of which waited for: 18 -> 20; matrix products, arithmetic and copies ran while one was open for 0% -> 0% of each run, Pallas kernels for 14% -> 15%
where the time goes in v7:
time: 198 us; the launch traced here: 197 us
  waiting for transfers between devices  78.1 us (39%)
  starting transfers between devices  60.6 us (31%)
  Pallas kernels  51.1 us (26%)
  local copies, waits for them, and re-layouts  5.87 us (3%)
    pallas_call x26, Pallas kernels, run(): pl.pallas_call(inner, name=name, out_shape=outs, in_specs=[spec(i) for i...  51.1 us
    ppermute x22, waiting for transfers between devices, swap(): lax.ppermute(values, axis, [(i, i ^ bit) for i in range(lax.axis_size(axi...  42 us
    ppermute x8, waiting for transfers between devices, neighbours(): lax.ppermute(first, axis, backward)  30.9 us
    ppermute x8, starting transfers between devices, neighbours(): lax.ppermute(last, axis, forward)  28.5 us
    ppermute x22, starting transfers between devices, swap(): lax.ppermute(values, axis, [(i, i ^ bit) for i in range(lax.axis_size(axi...  21.6 us
    ppermute x8, starting transfers between devices, neighbours(): lax.ppermute(first, axis, backward)  10.5 us
    ppermute x8, waiting for transfers between devices, neighbours(): lax.ppermute(last, axis, forward)  5.24 us
    unnamed x26, local copies, waits for them, and re-layouts  4.87 us
  transfers between devices with their start and end apart: 38, of which 20 were waited for; matrix products, arithmetic and copies ran while one was open for 0% of the time, Pallas kernels for 15%

profile of v7, /device:TPU:0, one launch (start us, length us, event | category | flops | bytes accessed | tf_op | source)
XLA Modules:
  0.0 197.1 jit_solution(1498897296764350930)
XLA Ops:
  0.7 1.0 slice_bitcast_fusion
  1.7 4.8 %collective-permute-start = (bf16[3,32,512]{2,1,0:T(8,128)(2,1)S(1)}, bf16[3,32,512]{2,1,0:T(8,128)(2,1)S(1)}, u32[]{:S(2)}, u32[]{:S(2)}) collective-permute-start(bf16[3,32,512]{2,1,0:T(8,128)(2,1)S(1)} %get-tuple-element.171), channel_id=1, source_target_pairs={{0,4},{4,8},{8,12},{12,16},{16,20},{20,24},{24,28},{1,5},{5,9},{9,... | collective-permute-start | bytes 294920 | tf_op jit(solution)/shard_map/ppermute | solution.py:131
  6.5 1.3 collective-permute-start.1
  7.8 0.9 collective-permute-done.refs_5_.refs_1_
  8.7 0.9 copy-done.1
  9.7 0.9 copy-done.8
  11.3 0.7 copy-done.11
  11.9 0.7 copy-done.12
  13.1 1.6 collective-permute-start.2
  14.6 1.4 collective-permute-start.3
  16.1 3.5 %collective-permute-done.3.refs_4_ = bf16[14,8,512]{2,1,0:T(8,128)(2,1)S(1)} collective-permute-done((bf16[14,8,512]{2,1,0:T(8,128)(2,1)S(1)}, bf16[14,8,512]{2,1,0:T(8,128)(2,1)S(1)}, u32[]{:S(2)}, u32[]{:S(2)}) %collective-permute-start.3) | collective-permute-done | bytes 114720 | tf_op jit(solution)/shard_map/ppermute | solution.py:131
  19.6 12.8 %front.1 = (bf16[256,3072]{1,0:T(8,128)(2,1)S(1)}, f32[256,512]{1,0:T(8,128)S(1)}, f32[256,1]{1,0:T(8,128)S(1)}, bf16[256,2048]{1,0:T(8,128)(2,1)S(1)}, f32[256,...) custom-call(bf16[8,32,512]{2,1,0:T(8,128)(2,1)S(1)} %get-tuple-eleme, ...), custom_call_target="tpu_custom_call" | custom-call | flops 13200001024 | bytes 1000 | tf_op jit(solution)/shard_map/front/pallas_call | solution.py:33
  32.5 4.4 %collective-permute-start.4 = (bf16[3,16,1024]{2,1,0:T(8,128)(2,1)S(1)}, bf16[3,16,1024]{2,1,0:T(8,128)(2,1)S(1)}, u32[]{:S(2)}, u32[]{:S(2)}) collective-permute-start(bf16[3,16,1024]{2,1,0:T(8,128)(2,1)S(1)} %get-tuple-element.97), channel_id=1, source_target_pairs={{0,4},{4,8},{8,12},{12,16},{16,20},{20,24},{24,28},{1,5},{5,9},{9,... | collective-permute-start | bytes 294920 | tf_op jit(solution)/shard_map/ppermute | solution.py:131
  36.8 1.3 collective-permute-start.5
  38.1 0.9 collective-permute-done.4.refs_1_
  39.0 4.5 %collective-permute-done.5.refs_2_ = bf16[3,16,1024]{2,1,0:T(8,128)(2,1)S(1)} collective-permute-done((bf16[3,16,1024]{2,1,0:T(8,128)(2,1)S(1)}, bf16[3,16,1024]{2,1,0:T(8,128)(2,1)S(1)}, u32[]{:S(2)}, u32[]{:S(2)}) %collective-permute-start.5) | collective-permute-done | bytes 98336 | tf_op jit(solution)/shard_map/ppermute | solution.py:131
  43.6 4.2 %collective-permute-start.6 = (bf16[10,8,1024]{2,1,0:T(8,128)(2,1)S(1)}, bf16[10,8,1024]{2,1,0:T(8,128)(2,1)S(1)}, u32[]{:S(2)}, u32[]{:S(2)}) collective-permute-start(bf16[10,8,1024]{2,1,0:T(8,128)(2,1)S(1)} %get-tuple-element.99), channel_id=1, source_target_pairs={{0,1},{1,2},{2,3},{4,5},{5,6},{6,7},{8,9},{9,10},{10,11},{12,13},{... | collective-permute-start | bytes 491528 | tf_op jit(solution)/shard_map/ppermute | solution.py:131
  47.8 1.3 collective-permute-start.7
  49.1 2.5 %collective-permute-done.7.refs_4_ = bf16[10,8,1024]{2,1,0:T(8,128)(2,1)S(1)} collective-permute-done((bf16[10,8,1024]{2,1,0:T(8,128)(2,1)S(1)}, bf16[10,8,1024]{2,1,0:T(8,128)(2,1)S(1)}, u32[]{:S(2)}, u32[]{:S(2)}) %collective-permute-start.7) | collective-permute-done | bytes 163872 | tf_op jit(solution)/shard_map/ppermute | solution.py:131
  51.6 3.3 %mixer.1 = (f32[4,16,1024]{2,1,0:T(8,128)S(1)}, bf16[4,16,1024]{2,1,0:T(8,128)(2,1)S(1)}, bf16[3,16,1024]{2,1,0:T(8,128)(2,1)S(1)}, bf16[3,16,1024]{2,1,0:T(8,128)(2,1)S(1)}, f32[1,1024]{1,0:T(1,128)S(1)}) custom-call(bf16[4,16,1024]{2,1,0:T(8,128)(2,1)S(1)} %get-tuple-element.96.refs_0_, bf16[3,16,1024]{2,1,0:T(8,128)(2,1)S(1)} %collective-permute-done.4.refs_1_, ...), custom_call_target="tpu_custom_call" | custom-call | flops 3300001024 | bytes 1000 | tf_op jit(solution)/shard_map/mixer/pallas_call | solution.py:33
  54.9 4.8 %collective-permute-start.8 = (bf16[3,16,1024]{2,1,0:T(8,128)(2,1)S(1)}, bf16[3,16,1024]{2,1,0:T(8,128)(2,1)S(1)}, u32[]{:S(2)}, u32[]{:S(2)}) collective-permute-start(bf16[3,16,1024]{2,1,0:T(8,128)(2,1)S(1)} %get-tuple-element.105), channel_id=1, source_target_pairs={{0,4},{4,8},{8,12},{12,16},{16,20},{20,24},{24,28},{1,5},{5,9},{9,... | collective-permute-start | bytes 294920 | tf_op jit(solution)/shard_map/ppermute | solution.py:131
  59.7 1.3 collective-permute-start.9
  61.0 0.9 collective-permute-done.8.refs_6_.refs_1_
  61.9 2.9 %mixer_weights.1.refs_3_.refs_7_ = f32[49,1024]{1,0:T(8,128)S(1)} custom-call(bf16[4,16,1024]{2,1,0:T(8,128)(2,1)S(1)} %get-tuple-element.96.refs_0_, bf16[3,16,1024]{2,1,0:T(8,128)(2,1)S(1)} %collective-permute-done.4.refs_1_, bf16[3,16,1024]{2,1,0:T(8,128)(2,1)S(1)} %collective-permute-done.5.refs_2_, ...), custom_call_target="tpu_custom_call" | custom-call | flops 3300001024 | bytes 1000 | tf_op jit(solution)/shard_map/mixer_weights/pallas_call | solution.py:33
  64.8 1.4 collective-permute-done.9.refs_2_
  66.3 4.5 %collective-permute-start.10 = (bf16[10,8,1024]{2,1,0:T(8,128)(2,1)S(1)}, bf16[10,8,1024]{2,1,0:T(8,128)(2,1)S(1)}, u32[]{:S(2)}, u32[]{:S(2)}) collective-permute-start(bf16[10,8,1024]{2,1,0:T(8,128)(2,1)S(1)} %get-tuple-element.108), channel_id=1, source_target_pairs={{0,1},{1,2},{2,3},{4,5},{5,6},{6,7},{8,9},{9,10},{10,11},{12,13},{... | collective-permute-start | bytes 491528 | tf_op jit(solution)/shard_map/ppermute | solution.py:131
  70.8 1.3 collective-permute-start.11
  72.1 2.6 %collective-permute-done.11.refs_4_ = bf16[10,8,1024]{2,1,0:T(8,128)(2,1)S(1)} collective-permute-done((bf16[10,8,1024]{2,1,0:T(8,128)(2,1)S(1)}, bf16[10,8,1024]{2,1,0:T(8,128)(2,1)S(1)}, u32[]{:S(2)}, u32[]{:S(2)}) %collective-permute-start.11) | collective-permute-done | bytes 163872 | tf_op jit(solution)/shard_map/ppermute | solution.py:131
  74.7 3.1 %section_grad.1 = (bf16[64,1024]{1,0:T(8,128)(2,1)S(1)}, bf16[2,64,256]{2,1,0:T(8,128)(2,1)S(1)}, bf16[2,64,256]{2,1,0:T(8,128)(2,1)S(1)}, bf16[256,3072]{1,0:T(8,128)(2,1)S(1)}) custom-call(bf16[4,16,1024]{2,1,0:T(8,128)(2,1)S(1)} %get-tuple-element.104.refs_0_, ...), custom_call_target="tpu_custom_call", output_to_operand_aliasing={{3}: (7, {})} | custom-call | flops 3300001024 | bytes 1000 | tf_op jit(solution)/shard_map/section_grad/pallas_call | solution.py:33
  77.8 3.9 %collective-permute-start.14 = (bf16[256,3072]{1,0:T(8,128)(2,1)S(1)}, bf16[256,3072]{1,0:T(8,128)(2,1)S(1)}, u32[]{:S(2)}, u32[]{:S(2)}) collective-permute-start(bf16[256,3072]{1,0:T(8,128)(2,1)S(1)} %get-tuple-element.127.refs_0_), channel_id=1, source_target_pairs={{0,1},{1,0},{2,3},{3,2},{4,5},{5,4},{6,7},{7,6},{8,9},{9,8},{10,11... | collective-permute-start | bytes 4718600 | tf_op jit(solution)/shard_map/ppermute | solution.py:47
  81.7 2.5 %merge_back.1 = (f32[256,512]{1,0:T(8,128)S(1)}, bf16[256,512]{1,0:T(8,128)(2,1)S(1)}, bf16[368,256]{1,0:T(8,128)(2,1)S(1)}, bf16[368,256]{1,0:T(8,128)(2,1)S(1)}) custom-call(bf16[64,1024]{1,0:T(8,128)(2,1)S(1)} %get-tuple-element.112.refs_0_, bf16[2048,1024]{1,0:T(8,128)(2,1)S(1)} %get-tuple-element.113.refs_1_, ...), custom_call_target="tpu_custom_call" | custom-call | flops 880001024 | bytes 1000 | tf_op jit(solution)/shard_map/merge_back/pallas_call | solution.py:33
  84.2 3.2 %mlp_back.1 = (bf16[256,1024]{1,0:T(8,128)(2,1)S(1)}, bf16[256,1024]{1,0:T(8,128)(2,1)S(1)}, bf16[8,32,512]{2,1,0:T(8,128)(2,1)S(1)}, bf16[3,32,512]{2,1,0:T(8,1...) custom-call(bf16[256,512]{1,0:T(8,128)(2,1)S(1)} %get-tuple-element.118.refs_0_, ...), custom_call_target="tpu_custom_call" | custom-call | flops 1320001024 | bytes 1000 | tf_op jit(solution)/shard_map/mlp_back/pallas_call | solution.py:33
  88.0 1.5 collective-permute-done.17.refs_3_
  89.5 2.6 %patch_product.1 = (bf16[2048,256]{1,0:T(8,128)(2,1)S(1)}, bf16[2048,256]{1,0:T(8,128)(2,1)S(1)}) custom-call(bf16[256,3072]{1,0:T(8,128)(2,1)S(1)} %get-tuple-element.127.refs_0_, bf16[256,3072]{1,0:T(8,128)(2,1)S(1)} %collective-permute-done.14.refs_1_, bf16[2,64,256]{2,1,0:T(8,128)(2,1)S(1)} %get-tuple-element.132.refs_2_, ...), custom_call_target="tpu_custom_call" | custom-call | flops 990001024 | bytes 1000 | tf_op jit(solution)/shard_map/patch_product/pallas_call | solution.py:33
  92.3 3.0 %collective-permute-start.12 = (bf16[3,32,512]{2,1,0:T(8,128)(2,1)S(1)}, bf16[3,32,512]{2,1,0:T(8,128)(2,1)S(1)}, u32[]{:S(2)}, u32[]{:S(2)}) collective-permute-start(bf16[3,32,512]{2,1,0:T(8,128)(2,1)S(1)} %get-tuple-element.125), channel_id=1, source_target_pairs={{0,4},{4,8},{8,12},{12,16},{16,20},{20,24},{24,28},{1,5},{5,9},{9,... | collective-permute-start | bytes 294920 | tf_op jit(solution)/shard_map/ppermute | solution.py:131
  95.3 2.6 %collective-permute-done.12.refs_5_.refs_1_ = bf16[3,32,512]{2,1,0:T(8,128)(2,1)S(1)} collective-permute-done((bf16[3,32,512]{2,1,0:T(8,128)(2,1)S(1)}, bf16[3,32,512]{2,1,0:T(8,128)(2,1)S(1)}, u32[]{:S(2)}, u32[]{:S(2)}) %collective-permute-start.12) | collective-permute-done | bytes 98336 | tf_op jit(solution)/shard_map/ppermute | solution.py:131
  97.9 1.9 expand_product.1
  99.7 2.8 %project_product.1 = (bf16[1136,256]{1,0:T(8,128)(2,1)S(1)}, bf16[1136,256]{1,0:T(8,128)(2,1)S(1)}) custom-call(bf16[256,3072]{1,0:T(8,128)(2,1)S(1)} %get-tuple-element.127.refs_0_, bf16[256,3072]{1,0:T(8,128)(2,1)S(1)} %collective-permute-done.14.refs_1_, bf16[368,256]{1,0:T(8,128)(2,1)S(1)} %get-tuple-element.128.refs_2_, ...), custom_call_target="tpu_custom_call" | custom-call | flops 990001024 | bytes 1000 | tf_op jit(solution)/shard_map/project_product/pallas_call | solution.py:33
  102.5 4.0 %collective-permute-start.21 = (bf16[1136,256]{1,0:T(8,128)(2,1)S(1)}, bf16[1136,256]{1,0:T(8,128)(2,1)S(1)}, u32[]{:S(2)}, u32[]{:S(2)}) collective-permute-start(bf16[1136,256]{1,0:T(8,128)(2,1)S(1)} %get-tuple-element.136.refs_3_.refs_7_), channel_id=1, source_target_pairs={{0,8},{4,12},{8,0},{12,4},{16,24},{20,28},{24,16},{28,20},{1,9},{5... | collective-permute-start | bytes 1744904 | tf_op jit(solution)/shard_map/ppermute | solution.py:47
  106.7 5.4 %block_weights.1 = (bf16[64,256]{1,0:T(8,128)(2,1)S(1)}, bf16[64,256]{1,0:T(8,128)(2,1)S(1)}) custom-call(bf16[8,32,512]{2,1,0:T(8,128)(2,1)S(1)} %get-tuple-element.89.refs_0_, bf16[3,32,512]{2,1,0:T(8,128)(2,1)S(1)} %collective-permute-done.refs_5_.refs_1_, bf16[3,32,512]{2,1,0:T(8,128)(2,1)S(1)} %collective-permute-done.1.refs_2_, ...), custom_call_target="tpu_custom_call" | custom-call | flops 1980001024 | bytes 1000 | tf_op jit(solution)/shard_map/block_weights/pallas_call | solution.py:33
  112.2 1.2 collective-permute-done.23
  113.4 1.9 collective-permute-start.24
  115.3 5.1 %collective-permute-done.24.refs_3_ = bf16[64,256]{1,0:T(8,128)(2,1)S(1)} collective-permute-done((bf16[64,256]{1,0:T(8,128)(2,1)S(1)}, bf16[64,256]{1,0:T(8,128)(2,1)S(1)}, u32[]{:S(2)}, u32[]{:S(2)}) %collective-permute-start.24) | collective-permute-done | bytes 32800 | tf_op jit(solution)/shard_map/ppermute | solution.py:47
  121.3 1.3 collective-permute-start.13
  122.6 12.7 %collective-permute-done.13.refs_2_ = bf16[3,32,512]{2,1,0:T(8,128)(2,1)S(1)} collective-permute-done((bf16[3,32,512]{2,1,0:T(8,128)(2,1)S(1)}, bf16[3,32,512]{2,1,0:T(8,128)(2,1)S(1)}, u32[]{:S(2)}, u32[]{:S(2)}) %collective-permute-start.13) | collective-permute-done | bytes 98336 | tf_op jit(solution)/shard_map/ppermute | solution.py:131
  135.3 1.3 collective-permute-start.18
  136.6 1.3 collective-permute-start.19
  138.0 1.0 collective-permute-start.25
  139.0 3.3 %collective-permute-done.19.refs_4_ = bf16[14,8,512]{2,1,0:T(8,128)(2,1)S(1)} collective-permute-done((bf16[14,8,512]{2,1,0:T(8,128)(2,1)S(1)}, bf16[14,8,512]{2,1,0:T(8,128)(2,1)S(1)}, u32[]{:S(2)}, u32[]{:S(2)}) %collective-permute-start.19) | collective-permute-done | bytes 114720 | tf_op jit(solution)/shard_map/ppermute | solution.py:131
  142.4 6.6 %input_grad.1.refs_2_ = bf16[8,32,512]{2,1,0:T(8,128)(2,1)} custom-call(bf16[8,32,512]{2,1,0:T(8,128)(2,1)S(1)} %get-tuple-element.124.refs_0_.refs_5_, bf16[3,32,512]{2,1,0:T(8,128)(2,1)S(1)} %collective-permute-done.12.refs_5_.refs_1_, bf16[3,32,512]{2,1,0:T(8,128)(2,1)S(1)} %collective-permute-done.13.refs_2_, ...), custom_call_target="tpu_custom_call" | custom-call | flops 2200001024 | bytes 1000 | tf_op jit(solution)/shard_map/input_grad/pallas_call | solution.py:33
  149.0 0.9 copy-done
  150.3 1.0 collective-permute-start.34
  151.3 5.7 %collective-permute-done.34.refs_1_ = bf16[512,256]{1,0:T(8,128)(2,1)S(1)} collective-permute-done((bf16[512,256]{1,0:T(8,128)(2,1)S(1)}, bf16[512,256]{1,0:T(8,128)(2,1)S(1)}, u32[]{:S(2)}, u32[]{:S(2)}) %collective-permute-start.34) | collective-permute-done | bytes 262176 | tf_op jit(solution)/shard_map/ppermute | solution.py:47
  157.1 2.0 %collective-permute-start.35 = (bf16[256,256]{1,0:T(8,128)(2,1)S(1)}, bf16[256,256]{1,0:T(8,128)(2,1)S(1)}, u32[]{:S(2)}, u32[]{:S(2)}) collective-permute-start(bf16[256,256]{1,0:T(8,128)(2,1)S(1)} %get-tuple-element.165), channel_id=1, source_target_pairs={{0,16},{4,20},{8,24},{12,28},{16,0},{20,4},{24,8},{28,12},{1,17},{... | collective-permute-start | bytes 393224 | tf_op jit(solution)/shard_map/ppermute | solution.py:47
  159.1 1.0 collective-permute-start.30
  160.1 2.0 %collective-permute-start.26 = (bf16[320,256]{1,0:T(8,128)(2,1)S(1)}, bf16[320,256]{1,0:T(8,128)(2,1)S(1)}, u32[]{:S(2)}, u32[]{:S(2)}) collective-permute-start(bf16[320,256]{1,0:T(8,128)(2,1)S(1)} %get-tuple-element.151.refs_2_), channel_id=1, source_target_pairs={{0,16},{4,20},{8,24},{12,28},{16,0},{20,4},{24,8},{28,12},{1,17},{... | collective-permute-start | bytes 491528 | tf_op jit(solution)/shard_map/ppermute | solution.py:47
  162.1 12.1 %collective-permute-done.35 = bf16[256,256]{1,0:T(8,128)(2,1)S(1)} collective-permute-done((bf16[256,256]{1,0:T(8,128)(2,1)S(1)}, bf16[256,256]{1,0:T(8,128)(2,1)S(1)}, u32[]{:S(2)}, u32[]{:S(2)}) %collective-permute-start.35) | collective-permute-done | bytes 131104 | tf_op jit(solution)/shard_map/ppermute | solution.py:47
  174.7 7.1 %collective-permute-done.26 = bf16[320,256]{1,0:T(8,128)(2,1)S(1)} collective-permute-done((bf16[320,256]{1,0:T(8,128)(2,1)S(1)}, bf16[320,256]{1,0:T(8,128)(2,1)S(1)}, u32[]{:S(2)}, u32[]{:S(2)}) %collective-permute-start.26) | collective-permute-done | bytes 163872 | tf_op jit(solution)/shard_map/ppermute | solution.py:47
  181.9 2.1 %collective-permute-start.31 = (bf16[368,256]{1,0:T(8,128)(2,1)S(1)}, bf16[368,256]{1,0:T(8,128)(2,1)S(1)}, u32[]{:S(2)}, u32[]{:S(2)}) collective-permute-start(bf16[368,256]{1,0:T(8,128)(2,1)S(1)} %add.26), channel_id=1, source_target_pairs={{0,2},{1,3},{2,0},{3,1},{4,6},{5,7},{6,4},{7,5},{8,10},{9,11},{10,... | collective-permute-start | bytes 565256 | tf_op jit(solution)/shard_map/ppermute | solution.py:47
  184.1 8.3 %collective-permute-done.31 = bf16[368,256]{1,0:T(8,128)(2,1)S(1)} collective-permute-done((bf16[368,256]{1,0:T(8,128)(2,1)S(1)}, bf16[368,256]{1,0:T(8,128)(2,1)S(1)}, u32[]{:S(2)}, u32[]{:S(2)}) %collective-permute-start.31) | collective-permute-done | bytes 188448 | tf_op jit(solution)/shard_map/ppermute | solution.py:47
  193.2 1.0 collective-permute-done.28.refs_1_
  194.2 0.9 finish_expand.1
  195.1 1.0 finish_project.1
  196.1 1.0 finish_patch.1
  (73 shorter events, 5.2 us)
Async XLA Ops:
  0.6 19.0 %copy-start.6 = (bf16[1,4,16,1024]{3,2,1,0:T(8,128)(2,1)S(1)}, bf16[1,4,16,1024]{3,2,1,0:T(8,128)(2,1)}, u32[]{:S(2)}) copy-start(bf16[1,4,16,1024]{3,2,1,0:T(8,128)(2,1)} %param.22) | copy-start | bytes 393220
  0.7 19.0 %copy-start.7 = (bf16[1,4,16,1024]{3,2,1,0:T(8,128)(2,1)S(1)}, bf16[1,4,16,1024]{3,2,1,0:T(8,128)(2,1)}, u32[]{:S(2)}) copy-start(bf16[1,4,16,1024]{3,2,1,0:T(8,128)(2,1)} %param.23) | copy-start | bytes 393220
  0.7 18.9 %copy-start.9 = (f32[1024]{0:T(1024)S(1)}, f32[1024]{0:T(1024)}, u32[]{:S(2)}) copy-start(f32[1024]{0:T(1024)} %param.21) | copy-start | bytes 12292
  1.7 7.0 %collective-permute-start = (bf16[3,32,512]{2,1,0:T(8,128)(2,1)S(1)}, bf16[3,32,512]{2,1,0:T(8,128)(2,1)S(1)}, u32[]{:S(2)}, u32[]{:S(2)}) collective-permute-start(bf16[3,32,512]{2,1,0:T(8,128)(2,1)S(1)} %get-tuple-element.171), channel_id=1, source_target_pairs={{0,4},{4,8},{8,12},{12,16},{16,20},{20,24},{24,28},{1,5},{5,9},{9,... | collective-permute-start | bytes 294920 | tf_op jit(solution)/shard_map/ppermute | solution.py:131
  6.5 6.5 %collective-permute-start.1 = (bf16[3,32,512]{2,1,0:T(8,128)(2,1)S(1)}, bf16[3,32,512]{2,1,0:T(8,128)(2,1)S(1)}, u32[]{:S(2)}, u32[]{:S(2)}) collective-permute-start(bf16[3,32,512]{2,1,0:T(8,128)(2,1)S(1)} %get-tuple-element.170), channel_id=1, source_target_pairs={{4,0},{8,4},{12,8},{16,12},{20,16},{24,20},{28,24},{5,1},{9,5},{13... | collective-permute-start | bytes 294920 | tf_op jit(solution)/shard_map/ppermute | solution.py:131
  8.7 0.9 copy-start.1
  9.7 0.9 copy-start.8
  10.6 0.7 copy-start.10
  11.3 0.7 copy-start.11
  11.9 0.7 copy-start.12
  12.6 7.0 %copy-start.2 = (bf16[2048,1024]{1,0:T(8,128)(2,1)S(1)}, bf16[2048,1024]{1,0:T(8,128)(2,1)}, u32[]{:S(2)}) copy-start(bf16[2048,1024]{1,0:T(8,128)(2,1)} %refs_11_.1) | copy-start | bytes 12582916
  12.6 7.0 %copy-start.3 = (bf16[512,2048]{1,0:T(8,128)(2,1)S(1)}, bf16[512,2048]{1,0:T(8,128)(2,1)}, u32[]{:S(2)}) copy-start(bf16[512,2048]{1,0:T(8,128)(2,1)} %refs_9_.1) | copy-start | bytes 6291460
  12.6 7.0 %copy-start.4 = (bf16[2048,512]{1,0:T(8,128)(2,1)S(1)}, bf16[2048,512]{1,0:T(8,128)(2,1)}, u32[]{:S(2)}) copy-start(bf16[2048,512]{1,0:T(8,128)(2,1)} %refs_10_.1) | copy-start | bytes 6291460
  12.6 7.0 %copy-start.5 = (f32[7,7,1024]{2,1,0:T(8,128)S(1)}, f32[7,7,1024]{2,1,0:T(8,128)}, u32[]{:S(2)}) copy-start(f32[7,7,1024]{2,1,0:T(8,128)} %refs_12_.1) | copy-start | bytes 602116
  13.1 3.0 %collective-permute-start.2 = (bf16[14,8,512]{2,1,0:T(8,128)(2,1)S(1)}, bf16[14,8,512]{2,1,0:T(8,128)(2,1)S(1)}, u32[]{:S(2)}, u32[]{:S(2)}) collective-permute-start(bf16[14,8,512]{2,1,0:T(8,128)(2,1)S(1)} %get-tuple-element.90), channel_id=1, source_target_pairs={{0,1},{1,2},{2,3},{4,5},{5,6},{6,7},{8,9},{9,10},{10,11},{12,13},{... | collective-permute-start | bytes 344072 | tf_op jit(solution)/shard_map/ppermute | solution.py:131
  14.6 5.0 %collective-permute-start.3 = (bf16[14,8,512]{2,1,0:T(8,128)(2,1)S(1)}, bf16[14,8,512]{2,1,0:T(8,128)(2,1)S(1)}, u32[]{:S(2)}, u32[]{:S(2)}) collective-permute-start(bf16[14,8,512]{2,1,0:T(8,128)(2,1)S(1)} %get-tuple-element.91), channel_id=1, source_target_pairs={{1,0},{2,1},{3,2},{5,4},{6,5},{7,6},{9,8},{10,9},{11,10},{13,12},{... | collective-permute-start | bytes 344072 | tf_op jit(solution)/shard_map/ppermute | solution.py:131
  32.5 6.6 %collective-permute-start.4 = (bf16[3,16,1024]{2,1,0:T(8,128)(2,1)S(1)}, bf16[3,16,1024]{2,1,0:T(8,128)(2,1)S(1)}, u32[]{:S(2)}, u32[]{:S(2)}) collective-permute-start(bf16[3,16,1024]{2,1,0:T(8,128)(2,1)S(1)} %get-tuple-element.97), channel_id=1, source_target_pairs={{0,4},{4,8},{8,12},{12,16},{16,20},{20,24},{24,28},{1,5},{5,9},{9,... | collective-permute-start | bytes 294920 | tf_op jit(solution)/shard_map/ppermute | solution.py:131
  36.8 6.7 %collective-permute-start.5 = (bf16[3,16,1024]{2,1,0:T(8,128)(2,1)S(1)}, bf16[3,16,1024]{2,1,0:T(8,128)(2,1)S(1)}, u32[]{:S(2)}, u32[]{:S(2)}) collective-permute-start(bf16[3,16,1024]{2,1,0:T(8,128)(2,1)S(1)} %get-tuple-element.98), channel_id=1, source_target_pairs={{4,0},{8,4},{12,8},{16,12},{20,16},{24,20},{28,24},{5,1},{9,5},{13... | collective-permute-start | bytes 294920 | tf_op jit(solution)/shard_map/ppermute | solution.py:131
  43.6 5.5 %collective-permute-start.6 = (bf16[10,8,1024]{2,1,0:T(8,128)(2,1)S(1)}, bf16[10,8,1024]{2,1,0:T(8,128)(2,1)S(1)}, u32[]{:S(2)}, u32[]{:S(2)}) collective-permute-start(bf16[10,8,1024]{2,1,0:T(8,128)(2,1)S(1)} %get-tuple-element.99), channel_id=1, source_target_pairs={{0,1},{1,2},{2,3},{4,5},{5,6},{6,7},{8,9},{9,10},{10,11},{12,13},{... | collective-permute-start | bytes 491528 | tf_op jit(solution)/shard_map/ppermute | solution.py:131
  47.8 3.8 %collective-permute-start.7 = (bf16[10,8,1024]{2,1,0:T(8,128)(2,1)S(1)}, bf16[10,8,1024]{2,1,0:T(8,128)(2,1)S(1)}, u32[]{:S(2)}, u32[]{:S(2)}) collective-permute-start(bf16[10,8,1024]{2,1,0:T(8,128)(2,1)S(1)} %get-tuple-element.100), channel_id=1, source_target_pairs={{1,0},{2,1},{3,2},{5,4},{6,5},{7,6},{9,8},{10,9},{11,10},{13,12},{... | collective-permute-start | bytes 491528 | tf_op jit(solution)/shard_map/ppermute | solution.py:131
  54.9 7.0 %collective-permute-start.8 = (bf16[3,16,1024]{2,1,0:T(8,128)(2,1)S(1)}, bf16[3,16,1024]{2,1,0:T(8,128)(2,1)S(1)}, u32[]{:S(2)}, u32[]{:S(2)}) collective-permute-start(bf16[3,16,1024]{2,1,0:T(8,128)(2,1)S(1)} %get-tuple-element.105), channel_id=1, source_target_pairs={{0,4},{4,8},{8,12},{12,16},{16,20},{20,24},{24,28},{1,5},{5,9},{9,... | collective-permute-start | bytes 294920 | tf_op jit(solution)/shard_map/ppermute | solution.py:131
  59.7 6.5 %collective-permute-start.9 = (bf16[3,16,1024]{2,1,0:T(8,128)(2,1)S(1)}, bf16[3,16,1024]{2,1,0:T(8,128)(2,1)S(1)}, u32[]{:S(2)}, u32[]{:S(2)}) collective-permute-start(bf16[3,16,1024]{2,1,0:T(8,128)(2,1)S(1)} %get-tuple-element.106), channel_id=1, source_target_pairs={{4,0},{8,4},{12,8},{16,12},{20,16},{24,20},{28,24},{5,1},{9,5},{13... | collective-permute-start | bytes 294920 | tf_op jit(solution)/shard_map/ppermute | solution.py:131
  66.3 5.8 %collective-permute-start.10 = (bf16[10,8,1024]{2,1,0:T(8,128)(2,1)S(1)}, bf16[10,8,1024]{2,1,0:T(8,128)(2,1)S(1)}, u32[]{:S(2)}, u32[]{:S(2)}) collective-permute-start(bf16[10,8,1024]{2,1,0:T(8,128)(2,1)S(1)} %get-tuple-element.108), channel_id=1, source_target_pairs={{0,1},{1,2},{2,3},{4,5},{5,6},{6,7},{8,9},{9,10},{10,11},{12,13},{... | collective-permute-start | bytes 491528 | tf_op jit(solution)/shard_map/ppermute | solution.py:131
  70.8 3.9 %collective-permute-start.11 = (bf16[10,8,1024]{2,1,0:T(8,128)(2,1)S(1)}, bf16[10,8,1024]{2,1,0:T(8,128)(2,1)S(1)}, u32[]{:S(2)}, u32[]{:S(2)}) collective-permute-start(bf16[10,8,1024]{2,1,0:T(8,128)(2,1)S(1)} %get-tuple-element.109), channel_id=1, source_target_pairs={{1,0},{2,1},{3,2},{5,4},{6,5},{7,6},{9,8},{10,9},{11,10},{13,12},{... | collective-permute-start | bytes 491528 | tf_op jit(solution)/shard_map/ppermute | solution.py:131
  77.8 11.7 %collective-permute-start.14 = (bf16[256,3072]{1,0:T(8,128)(2,1)S(1)}, bf16[256,3072]{1,0:T(8,128)(2,1)S(1)}, u32[]{:S(2)}, u32[]{:S(2)}) collective-permute-start(bf16[256,3072]{1,0:T(8,128)(2,1)S(1)} %get-tuple-element.127.refs_0_), channel_id=1, source_target_pairs={{0,1},{1,0},{2,3},{3,2},{4,5},{5,4},{6,7},{7,6},{8,9},{9,8},{10,11... | collective-permute-start | bytes 4718600 | tf_op jit(solution)/shard_map/ppermute | solution.py:47
  87.4 10.5 %collective-permute-start.16 = (bf16[256,1024]{1,0:T(8,128)(2,1)S(1)}, bf16[256,1024]{1,0:T(8,128)(2,1)S(1)}, u32[]{:S(2)}, u32[]{:S(2)}) collective-permute-start(bf16[256,1024]{1,0:T(8,128)(2,1)S(1)} %get-tuple-element.131.refs_4_), channel_id=1, source_target_pairs={{0,1},{1,0},{2,3},{3,2},{4,5},{5,4},{6,7},{7,6},{8,9},{9,8},{10,11... | collective-permute-start | bytes 1572872 | tf_op jit(solution)/shard_map/ppermute | solution.py:47
  87.5 2.0 %collective-permute-start.17 = (bf16[2,64,256]{2,1,0:T(8,128)(2,1)S(1)}, bf16[2,64,256]{2,1,0:T(8,128)(2,1)S(1)}, u32[]{:S(2)}, u32[]{:S(2)}) collective-permute-start(bf16[2,64,256]{2,1,0:T(8,128)(2,1)S(1)} %get-tuple-element.133), channel_id=1, source_target_pairs={{0,1},{1,0},{2,3},{3,2},{4,5},{5,4},{6,7},{7,6},{8,9},{9,8},{10,11... | collective-permute-start | bytes 196616 | tf_op jit(solution)/shard_map/ppermute | solution.py:47
  92.0 28.6 %collective-permute-start.20 = (bf16[2048,256]{1,0:T(8,128)(2,1)S(1)}, bf16[2048,256]{1,0:T(8,128)(2,1)S(1)}, u32[]{:S(2)}, u32[]{:S(2)}) collective-permute-start(bf16[2048,256]{1,0:T(8,128)(2,1)S(1)} %get-tuple-element.134.refs_4_), channel_id=1, source_target_pairs={{0,2},{1,3},{2,0},{3,1},{4,6},{5,7},{6,4},{7,5},{8,10},{9,11},{10,... | collective-permute-start | bytes 3145736 | tf_op jit(solution)/shard_map/ppermute | solution.py:47
  92.1 7.6 %collective-permute-start.15 = (bf16[368,256]{1,0:T(8,128)(2,1)S(1)}, bf16[368,256]{1,0:T(8,128)(2,1)S(1)}, u32[]{:S(2)}, u32[]{:S(2)}) collective-permute-start(bf16[368,256]{1,0:T(8,128)(2,1)S(1)} %get-tuple-element.129), channel_id=1, source_target_pairs={{0,1},{1,0},{2,3},{3,2},{4,5},{5,4},{6,7},{7,6},{8,9},{9,8},{10,11... | collective-permute-start | bytes 565256 | tf_op jit(solution)/shard_map/ppermute | solution.py:47
  92.3 5.5 %collective-permute-start.12 = (bf16[3,32,512]{2,1,0:T(8,128)(2,1)S(1)}, bf16[3,32,512]{2,1,0:T(8,128)(2,1)S(1)}, u32[]{:S(2)}, u32[]{:S(2)}) collective-permute-start(bf16[3,32,512]{2,1,0:T(8,128)(2,1)S(1)} %get-tuple-element.125), channel_id=1, source_target_pairs={{0,4},{4,8},{8,12},{12,16},{16,20},{20,24},{24,28},{1,5},{5,9},{9,... | collective-permute-start | bytes 294920 | tf_op jit(solution)/shard_map/ppermute | solution.py:131
  102.5 17.9 %collective-permute-start.21 = (bf16[1136,256]{1,0:T(8,128)(2,1)S(1)}, bf16[1136,256]{1,0:T(8,128)(2,1)S(1)}, u32[]{:S(2)}, u32[]{:S(2)}) collective-permute-start(bf16[1136,256]{1,0:T(8,128)(2,1)S(1)} %get-tuple-element.136.refs_3_.refs_7_), channel_id=1, source_target_pairs={{0,8},{4,12},{8,0},{12,4},{16,24},{20,28},{24,16},{28,20},{1,9},{5... | collective-permute-start | bytes 1744904 | tf_op jit(solution)/shard_map/ppermute | solution.py:47
  106.5 13.8 %collective-permute-start.22 = (bf16[1024,256]{1,0:T(8,128)(2,1)S(1)}, bf16[1024,256]{1,0:T(8,128)(2,1)S(1)}, u32[]{:S(2)}, u32[]{:S(2)}) collective-permute-start(bf16[1024,256]{1,0:T(8,128)(2,1)S(1)} %get-tuple-element.135.refs_4_), channel_id=1, source_target_pairs={{0,4},{4,0},{8,12},{12,8},{16,20},{20,16},{24,28},{28,24},{1,5},{5... | collective-permute-start | bytes 1572872 | tf_op jit(solution)/shard_map/ppermute | solution.py:47
  112.1 1.3 collective-permute-start.23
  113.4 7.0 %collective-permute-start.24 = (bf16[64,256]{1,0:T(8,128)(2,1)S(1)}, bf16[64,256]{1,0:T(8,128)(2,1)S(1)}, u32[]{:S(2)}, u32[]{:S(2)}) collective-permute-start(bf16[64,256]{1,0:T(8,128)(2,1)S(1)} %add.23.refs_2_), channel_id=1, source_target_pairs={{0,4},{4,0},{8,12},{12,8},{16,20},{20,16},{24,28},{28,24},{1,5},{5... | collective-permute-start | bytes 98312 | tf_op jit(solution)/shard_map/ppermute | solution.py:47
  120.9 29.2 %collective-permute-start.33 = (bf16[1024,256]{1,0:T(8,128)(2,1)S(1)}, bf16[1024,256]{1,0:T(8,128)(2,1)S(1)}, u32[]{:S(2)}, u32[]{:S(2)}) collective-permute-start(bf16[1024,256]{1,0:T(8,128)(2,1)S(1)} %get-tuple-element.148.refs_7_), channel_id=1, source_target_pairs={{0,4},{4,0},{8,12},{12,8},{16,20},{20,16},{24,28},{28,24},{1,5},{5... | collective-permute-start | bytes 1572872 | tf_op jit(solution)/shard_map/ppermute | solution.py:47
  121.3 14.0 %collective-permute-start.13 = (bf16[3,32,512]{2,1,0:T(8,128)(2,1)S(1)}, bf16[3,32,512]{2,1,0:T(8,128)(2,1)S(1)}, u32[]{:S(2)}, u32[]{:S(2)}) collective-permute-start(bf16[3,32,512]{2,1,0:T(8,128)(2,1)S(1)} %get-tuple-element.126), channel_id=1, source_target_pairs={{4,0},{8,4},{12,8},{16,12},{20,16},{24,20},{28,24},{5,1},{9,5},{13... | collective-permute-start | bytes 294920 | tf_op jit(solution)/shard_map/ppermute | solution.py:131
  135.3 3.7 %collective-permute-start.18 = (bf16[14,8,512]{2,1,0:T(8,128)(2,1)S(1)}, bf16[14,8,512]{2,1,0:T(8,128)(2,1)S(1)}, u32[]{:S(2)}, u32[]{:S(2)}) collective-permute-start(bf16[14,8,512]{2,1,0:T(8,128)(2,1)S(1)} %get-tuple-element.137), channel_id=1, source_target_pairs={{0,1},{1,2},{2,3},{4,5},{5,6},{6,7},{8,9},{9,10},{10,11},{12,13},{... | collective-permute-start | bytes 344072 | tf_op jit(solution)/shard_map/ppermute | solution.py:131
  136.6 5.7 %collective-permute-start.19 = (bf16[14,8,512]{2,1,0:T(8,128)(2,1)S(1)}, bf16[14,8,512]{2,1,0:T(8,128)(2,1)S(1)}, u32[]{:S(2)}, u32[]{:S(2)}) collective-permute-start(bf16[14,8,512]{2,1,0:T(8,128)(2,1)S(1)} %get-tuple-element.138), channel_id=1, source_target_pairs={{1,0},{2,1},{3,2},{5,4},{6,5},{7,6},{9,8},{10,9},{11,10},{13,12},{... | collective-permute-start | bytes 344072 | tf_op jit(solution)/shard_map/ppermute | solution.py:131
  137.9 12.1 %collective-permute-start.29 = (bf16[624,256]{1,0:T(8,128)(2,1)S(1)}, bf16[624,256]{1,0:T(8,128)(2,1)S(1)}, u32[]{:S(2)}, u32[]{:S(2)}) collective-permute-start(bf16[624,256]{1,0:T(8,128)(2,1)S(1)} %get-tuple-element.147.refs_2_), channel_id=1, source_target_pairs={{0,4},{4,0},{8,12},{12,8},{16,20},{20,16},{24,28},{28,24},{1,5},{5... | collective-permute-start | bytes 958472 | tf_op jit(solution)/shard_map/ppermute | solution.py:47
  138.0 11.0 %collective-permute-start.25 = (bf16[576,256]{1,0:T(8,128)(2,1)S(1)}, bf16[576,256]{1,0:T(8,128)(2,1)S(1)}, u32[]{:S(2)}, u32[]{:S(2)}) collective-permute-start(bf16[576,256]{1,0:T(8,128)(2,1)S(1)} %get-tuple-element.146.refs_2_), channel_id=1, source_target_pairs={{0,8},{4,12},{8,0},{12,4},{16,24},{20,28},{24,16},{28,20},{1,9},{5... | collective-permute-start | bytes 884744 | tf_op jit(solution)/shard_map/ppermute | solution.py:47
  149.0 1.0 copy-start
  150.3 6.7 %collective-permute-start.34 = (bf16[512,256]{1,0:T(8,128)(2,1)S(1)}, bf16[512,256]{1,0:T(8,128)(2,1)S(1)}, u32[]{:S(2)}, u32[]{:S(2)}) collective-permute-start(bf16[512,256]{1,0:T(8,128)(2,1)S(1)} %get-tuple-element.163), channel_id=1, source_target_pairs={{0,8},{4,12},{8,0},{12,4},{16,24},{20,28},{24,16},{28,20},{1,9},{5... | collective-permute-start | bytes 786440 | tf_op jit(solution)/shard_map/ppermute | solution.py:47
  157.1 17.1 %collective-permute-start.35 = (bf16[256,256]{1,0:T(8,128)(2,1)S(1)}, bf16[256,256]{1,0:T(8,128)(2,1)S(1)}, u32[]{:S(2)}, u32[]{:S(2)}) collective-permute-start(bf16[256,256]{1,0:T(8,128)(2,1)S(1)} %get-tuple-element.165), channel_id=1, source_target_pairs={{0,16},{4,20},{8,24},{12,28},{16,0},{20,4},{24,8},{28,12},{1,17},{... | collective-permute-start | bytes 393224 | tf_op jit(solution)/shard_map/ppermute | solution.py:47
  159.1 22.8 %collective-permute-start.30 = (bf16[368,256]{1,0:T(8,128)(2,1)S(1)}, bf16[368,256]{1,0:T(8,128)(2,1)S(1)}, u32[]{:S(2)}, u32[]{:S(2)}) collective-permute-start(bf16[368,256]{1,0:T(8,128)(2,1)S(1)} %get-tuple-element.157.refs_2_), channel_id=1, source_target_pairs={{0,16},{4,20},{8,24},{12,28},{16,0},{20,4},{24,8},{28,12},{1,17},{... | collective-permute-start | bytes 565256 | tf_op jit(solution)/shard_map/ppermute | solution.py:47
  160.1 21.7 %collective-permute-start.26 = (bf16[320,256]{1,0:T(8,128)(2,1)S(1)}, bf16[320,256]{1,0:T(8,128)(2,1)S(1)}, u32[]{:S(2)}, u32[]{:S(2)}) collective-permute-start(bf16[320,256]{1,0:T(8,128)(2,1)S(1)} %get-tuple-element.151.refs_2_), channel_id=1, source_target_pairs={{0,16},{4,20},{8,24},{12,28},{16,0},{20,4},{24,8},{28,12},{1,17},{... | collective-permute-start | bytes 491528 | tf_op jit(solution)/shard_map/ppermute | solution.py:47
  174.2 9.8 %collective-permute-start.36 = (bf16[1,256,256]{2,1,0:T(8,128)(2,1)S(1)}, bf16[1,256,256]{2,1,0:T(8,128)(2,1)S(1)}, u32[]{:S(2)}, u32[]{:S(2)}) collective-permute-start(bf16[1,256,256]{2,1,0:T(8,128)(2,1)S(1)} %add_bitcast_fusion), channel_id=1, source_target_pairs={{0,2},{1,3},{2,0},{3,1},{4,6},{5,7},{6,4},{7,5},{8,10},{9,11},{10,... | collective-permute-start | bytes 393224 | tf_op jit(solution)/shard_map/ppermute | solution.py:47
  181.8 10.8 %collective-permute-start.27 = (bf16[320,256]{1,0:T(8,128)(2,1)S(1)}, bf16[320,256]{1,0:T(8,128)(2,1)S(1)}, u32[]{:S(2)}, u32[]{:S(2)}) collective-permute-start(bf16[320,256]{1,0:T(8,128)(2,1)S(1)} %add.24), channel_id=1, source_target_pairs={{0,2},{1,3},{2,0},{3,1},{4,6},{5,7},{6,4},{7,5},{8,10},{9,11},{10,... | collective-permute-start | bytes 491528 | tf_op jit(solution)/shard_map/ppermute | solution.py:47
  181.9 10.5 %collective-permute-start.31 = (bf16[368,256]{1,0:T(8,128)(2,1)S(1)}, bf16[368,256]{1,0:T(8,128)(2,1)S(1)}, u32[]{:S(2)}, u32[]{:S(2)}) collective-permute-start(bf16[368,256]{1,0:T(8,128)(2,1)S(1)} %add.26), channel_id=1, source_target_pairs={{0,2},{1,3},{2,0},{3,1},{4,6},{5,7},{6,4},{7,5},{8,10},{9,11},{10,... | collective-permute-start | bytes 565256 | tf_op jit(solution)/shard_map/ppermute | solution.py:47
  184.1 12.0 %collective-permute-start.37 = (bf16[2,256,256]{2,1,0:T(8,128)(2,1)S(1)}, bf16[2,256,256]{2,1,0:T(8,128)(2,1)S(1)}, u32[]{:S(2)}, u32[]{:S(2)}) collective-permute-start(bf16[2,256,256]{2,1,0:T(8,128)(2,1)S(1)} %maximum_bitcast_fusion.refs_0_), channel_id=1, source_target_pairs={{0,1},{1,0},{2,3},{3,2},{4,5},{5,4},{6,7},{7,6},{8,9},{9,8},{10,11... | collective-permute-start | bytes 786440 | tf_op jit(solution)/shard_map/ppermute | solution.py:47
  192.5 2.6 %collective-permute-start.32 = (bf16[368,256]{1,0:T(8,128)(2,1)S(1)}, bf16[368,256]{1,0:T(8,128)(2,1)S(1)}, u32[]{:S(2)}, u32[]{:S(2)}) collective-permute-start(bf16[368,256]{1,0:T(8,128)(2,1)S(1)} %add.27.refs_0_), channel_id=1, source_target_pairs={{0,1},{1,0},{2,3},{3,2},{4,5},{5,4},{6,7},{7,6},{8,9},{9,8},{10,11... | collective-permute-start | bytes 565256 | tf_op jit(solution)/shard_map/ppermute | solution.py:47
  192.6 1.6 collective-permute-start.28

commit v8 on v7

--- a/solution.py
+++ b/solution.py
@@ -833,7 +833,7 @@
         "expand_product",
         (early, early_other, upward_keep, upward_other),
         (expand_half, expand_half),
-        after=(patch_send, rows_back[0]),
+        after=(patch_send, *rows_back),
         limit=16,
         us=0.6,
     )
@@ -874,7 +874,7 @@
     small = small_keep + swap(small_send, "col", 1)
     sent = expand_chain.advance(extra=(small, swap(small, "row", 1)))
     sent = project_chain.advance(sent)
-    sent = patch_chain.advance(sent)
+    sent = patch_chain.advance((*sent, *framed_back[3:]))
     (input_grad,) = run(
         input_kernel,
         "input_grad",

time: 198 us -> 195 us (0.985)
  waiting for transfers between devices: 78.1 us -> 75.9 us
    ppermute x8, waiting for transfers between devices: 30.9 us -> 20.7 us  [neighbours(): lax.ppermute(first, axis, backward)]
    ppermute x22, waiting for transfers between devices: 42 us -> 51.3 us  [swap(): lax.ppermute(values, axis, [(i, i ^ bit) for i in range(lax.axis_size(axi...]
  transfers between devices with their start and end apart: 38 -> 38, of which waited for: 20 -> 22; matrix products, arithmetic and copies ran while one was open for 0% -> 0% of each run, Pallas kernels for 15% -> 16%
where the time goes in v8:
time: 195 us; the launch traced here: 194 us
  waiting for transfers between devices  75.9 us (39%)
  starting transfers between devices  59.6 us (31%)
  Pallas kernels  51.1 us (26%)
  local copies, waits for them, and re-layouts  5.87 us (3%)
    ppermute x22, waiting for transfers between devices, swap(): lax.ppermute(values, axis, [(i, i ^ bit) for i in range(lax.axis_size(axi...  51.3 us
    pallas_call x26, Pallas kernels, run(): pl.pallas_call(inner, name=name, out_shape=outs, in_specs=[spec(i) for i...  51.1 us
    ppermute x8, starting transfers between devices, neighbours(): lax.ppermute(last, axis, forward)  29.3 us
    ppermute x8, waiting for transfers between devices, neighbours(): lax.ppermute(first, axis, backward)  20.7 us
    ppermute x22, starting transfers between devices, swap(): lax.ppermute(values, axis, [(i, i ^ bit) for i in range(lax.axis_size(axi...  19.9 us
    ppermute x8, starting transfers between devices, neighbours(): lax.ppermute(first, axis, backward)  10.5 us
    unnamed x26, local copies, waits for them, and re-layouts  4.87 us
    ppermute x8, waiting for transfers between devices, neighbours(): lax.ppermute(last, axis, forward)  3.94 us
  transfers between devices with their start and end apart: 38, of which 22 were waited for; matrix products, arithmetic and copies ran while one was open for 0% of the time, Pallas kernels for 16%

profile of v8, /device:TPU:0, one launch (start us, length us, event | category | flops | bytes accessed | tf_op | source)
XLA Modules:
  0.0 194.0 jit_solution(17348172198562054834)
XLA Ops:
  0.7 1.0 slice_bitcast_fusion
  1.7 4.8 %collective-permute-start = (bf16[3,32,512]{2,1,0:T(8,128)(2,1)S(1)}, bf16[3,32,512]{2,1,0:T(8,128)(2,1)S(1)}, u32[]{:S(2)}, u32[]{:S(2)}) collective-permute-start(bf16[3,32,512]{2,1,0:T(8,128)(2,1)S(1)} %get-tuple-element.171), channel_id=1, source_target_pairs={{0,4},{4,8},{8,12},{12,16},{16,20},{20,24},{24,28},{1,5},{5,9},{9,... | collective-permute-start | bytes 294920 | tf_op jit(solution)/shard_map/ppermute | solution.py:131
  6.5 1.3 collective-permute-start.1
  7.8 0.9 collective-permute-done.refs_5_.refs_1_
  8.7 0.9 copy-done.1
  9.7 0.9 copy-done.8
  10.6 0.7 copy-done.10
  13.1 1.6 collective-permute-start.2
  14.6 1.4 collective-permute-start.3
  16.1 3.5 %collective-permute-done.3.refs_4_ = bf16[14,8,512]{2,1,0:T(8,128)(2,1)S(1)} collective-permute-done((bf16[14,8,512]{2,1,0:T(8,128)(2,1)S(1)}, bf16[14,8,512]{2,1,0:T(8,128)(2,1)S(1)}, u32[]{:S(2)}, u32[]{:S(2)}) %collective-permute-start.3) | collective-permute-done | bytes 114720 | tf_op jit(solution)/shard_map/ppermute | solution.py:131
  19.6 12.8 %front.1 = (bf16[256,3072]{1,0:T(8,128)(2,1)S(1)}, f32[256,512]{1,0:T(8,128)S(1)}, f32[256,1]{1,0:T(8,128)S(1)}, bf16[256,2048]{1,0:T(8,128)(2,1)S(1)}, f32[256,...) custom-call(bf16[8,32,512]{2,1,0:T(8,128)(2,1)S(1)} %get-tuple-eleme, ...), custom_call_target="tpu_custom_call" | custom-call | flops 13200001024 | bytes 1000 | tf_op jit(solution)/shard_map/front/pallas_call | solution.py:33
  32.5 4.4 %collective-permute-start.4 = (bf16[3,16,1024]{2,1,0:T(8,128)(2,1)S(1)}, bf16[3,16,1024]{2,1,0:T(8,128)(2,1)S(1)}, u32[]{:S(2)}, u32[]{:S(2)}) collective-permute-start(bf16[3,16,1024]{2,1,0:T(8,128)(2,1)S(1)} %get-tuple-element.97), channel_id=1, source_target_pairs={{0,4},{4,8},{8,12},{12,16},{16,20},{20,24},{24,28},{1,5},{5,9},{9,... | collective-permute-start | bytes 294920 | tf_op jit(solution)/shard_map/ppermute | solution.py:131
  36.8 1.3 collective-permute-start.5
  38.1 0.9 collective-permute-done.4.refs_1_
  39.0 4.5 %collective-permute-done.5.refs_2_ = bf16[3,16,1024]{2,1,0:T(8,128)(2,1)S(1)} collective-permute-done((bf16[3,16,1024]{2,1,0:T(8,128)(2,1)S(1)}, bf16[3,16,1024]{2,1,0:T(8,128)(2,1)S(1)}, u32[]{:S(2)}, u32[]{:S(2)}) %collective-permute-start.5) | collective-permute-done | bytes 98336 | tf_op jit(solution)/shard_map/ppermute | solution.py:131
  43.6 4.2 %collective-permute-start.6 = (bf16[10,8,1024]{2,1,0:T(8,128)(2,1)S(1)}, bf16[10,8,1024]{2,1,0:T(8,128)(2,1)S(1)}, u32[]{:S(2)}, u32[]{:S(2)}) collective-permute-start(bf16[10,8,1024]{2,1,0:T(8,128)(2,1)S(1)} %get-tuple-element.99), channel_id=1, source_target_pairs={{0,1},{1,2},{2,3},{4,5},{5,6},{6,7},{8,9},{9,10},{10,11},{12,13},{... | collective-permute-start | bytes 491528 | tf_op jit(solution)/shard_map/ppermute | solution.py:131
  47.8 1.3 collective-permute-start.7
  49.1 2.5 %collective-permute-done.7.refs_4_ = bf16[10,8,1024]{2,1,0:T(8,128)(2,1)S(1)} collective-permute-done((bf16[10,8,1024]{2,1,0:T(8,128)(2,1)S(1)}, bf16[10,8,1024]{2,1,0:T(8,128)(2,1)S(1)}, u32[]{:S(2)}, u32[]{:S(2)}) %collective-permute-start.7) | collective-permute-done | bytes 163872 | tf_op jit(solution)/shard_map/ppermute | solution.py:131
  51.6 3.3 %mixer.1 = (f32[4,16,1024]{2,1,0:T(8,128)S(1)}, bf16[4,16,1024]{2,1,0:T(8,128)(2,1)S(1)}, bf16[3,16,1024]{2,1,0:T(8,128)(2,1)S(1)}, bf16[3,16,1024]{2,1,0:T(8,128)(2,1)S(1)}, f32[1,1024]{1,0:T(1,128)S(1)}) custom-call(bf16[4,16,1024]{2,1,0:T(8,128)(2,1)S(1)} %get-tuple-element.96.refs_0_, bf16[3,16,1024]{2,1,0:T(8,128)(2,1)S(1)} %collective-permute-done.4.refs_1_, ...), custom_call_target="tpu_custom_call" | custom-call | flops 3300001024 | bytes 1000 | tf_op jit(solution)/shard_map/mixer/pallas_call | solution.py:33
  54.9 4.8 %collective-permute-start.8 = (bf16[3,16,1024]{2,1,0:T(8,128)(2,1)S(1)}, bf16[3,16,1024]{2,1,0:T(8,128)(2,1)S(1)}, u32[]{:S(2)}, u32[]{:S(2)}) collective-permute-start(bf16[3,16,1024]{2,1,0:T(8,128)(2,1)S(1)} %get-tuple-element.105), channel_id=1, source_target_pairs={{0,4},{4,8},{8,12},{12,16},{16,20},{20,24},{24,28},{1,5},{5,9},{9,... | collective-permute-start | bytes 294920 | tf_op jit(solution)/shard_map/ppermute | solution.py:131
  59.7 1.3 collective-permute-start.9
  61.0 0.9 collective-permute-done.8.refs_6_.refs_1_
  61.9 2.9 %mixer_weights.1.refs_3_.refs_7_ = f32[49,1024]{1,0:T(8,128)S(1)} custom-call(bf16[4,16,1024]{2,1,0:T(8,128)(2,1)S(1)} %get-tuple-element.96.refs_0_, bf16[3,16,1024]{2,1,0:T(8,128)(2,1)S(1)} %collective-permute-done.4.refs_1_, bf16[3,16,1024]{2,1,0:T(8,128)(2,1)S(1)} %collective-permute-done.5.refs_2_, ...), custom_call_target="tpu_custom_call" | custom-call | flops 3300001024 | bytes 1000 | tf_op jit(solution)/shard_map/mixer_weights/pallas_call | solution.py:33
  64.8 1.4 collective-permute-done.9.refs_2_
  66.3 4.5 %collective-permute-start.10 = (bf16[10,8,1024]{2,1,0:T(8,128)(2,1)S(1)}, bf16[10,8,1024]{2,1,0:T(8,128)(2,1)S(1)}, u32[]{:S(2)}, u32[]{:S(2)}) collective-permute-start(bf16[10,8,1024]{2,1,0:T(8,128)(2,1)S(1)} %get-tuple-element.108), channel_id=1, source_target_pairs={{0,1},{1,2},{2,3},{4,5},{5,6},{6,7},{8,9},{9,10},{10,11},{12,13},{... | collective-permute-start | bytes 491528 | tf_op jit(solution)/shard_map/ppermute | solution.py:131
  70.8 1.3 collective-permute-start.11
  72.1 2.6 %collective-permute-done.11.refs_4_ = bf16[10,8,1024]{2,1,0:T(8,128)(2,1)S(1)} collective-permute-done((bf16[10,8,1024]{2,1,0:T(8,128)(2,1)S(1)}, bf16[10,8,1024]{2,1,0:T(8,128)(2,1)S(1)}, u32[]{:S(2)}, u32[]{:S(2)}) %collective-permute-start.11) | collective-permute-done | bytes 163872 | tf_op jit(solution)/shard_map/ppermute | solution.py:131
  74.7 3.1 %section_grad.1 = (bf16[64,1024]{1,0:T(8,128)(2,1)S(1)}, bf16[2,64,256]{2,1,0:T(8,128)(2,1)S(1)}, bf16[2,64,256]{2,1,0:T(8,128)(2,1)S(1)}, bf16[256,3072]{1,0:T(8,128)(2,1)S(1)}) custom-call(bf16[4,16,1024]{2,1,0:T(8,128)(2,1)S(1)} %get-tuple-element.104.refs_0_, ...), custom_call_target="tpu_custom_call", output_to_operand_aliasing={{3}: (7, {})} | custom-call | flops 3300001024 | bytes 1000 | tf_op jit(solution)/shard_map/section_grad/pallas_call | solution.py:33
  77.8 3.9 %collective-permute-start.14 = (bf16[256,3072]{1,0:T(8,128)(2,1)S(1)}, bf16[256,3072]{1,0:T(8,128)(2,1)S(1)}, u32[]{:S(2)}, u32[]{:S(2)}) collective-permute-start(bf16[256,3072]{1,0:T(8,128)(2,1)S(1)} %get-tuple-element.127.refs_0_), channel_id=1, source_target_pairs={{0,1},{1,0},{2,3},{3,2},{4,5},{5,4},{6,7},{7,6},{8,9},{9,8},{10,11... | collective-permute-start | bytes 4718600 | tf_op jit(solution)/shard_map/ppermute | solution.py:47
  81.7 2.5 %merge_back.1 = (f32[256,512]{1,0:T(8,128)S(1)}, bf16[256,512]{1,0:T(8,128)(2,1)S(1)}, bf16[368,256]{1,0:T(8,128)(2,1)S(1)}, bf16[368,256]{1,0:T(8,128)(2,1)S(1)}) custom-call(bf16[64,1024]{1,0:T(8,128)(2,1)S(1)} %get-tuple-element.112.refs_0_, bf16[2048,1024]{1,0:T(8,128)(2,1)S(1)} %get-tuple-element.113.refs_1_, ...), custom_call_target="tpu_custom_call" | custom-call | flops 880001024 | bytes 1000 | tf_op jit(solution)/shard_map/merge_back/pallas_call | solution.py:33
  84.2 3.2 %mlp_back.1 = (bf16[256,1024]{1,0:T(8,128)(2,1)S(1)}, bf16[256,1024]{1,0:T(8,128)(2,1)S(1)}, bf16[8,32,512]{2,1,0:T(8,128)(2,1)S(1)}, bf16[3,32,512]{2,1,0:T(8,1...) custom-call(bf16[256,512]{1,0:T(8,128)(2,1)S(1)} %get-tuple-element.118.refs_0_, ...), custom_call_target="tpu_custom_call" | custom-call | flops 1320001024 | bytes 1000 | tf_op jit(solution)/shard_map/mlp_back/pallas_call | solution.py:33
  88.0 1.5 collective-permute-done.17.refs_3_
  89.5 2.6 %patch_product.1 = (bf16[2048,256]{1,0:T(8,128)(2,1)S(1)}, bf16[2048,256]{1,0:T(8,128)(2,1)S(1)}) custom-call(bf16[256,3072]{1,0:T(8,128)(2,1)S(1)} %get-tuple-element.127.refs_0_, bf16[256,3072]{1,0:T(8,128)(2,1)S(1)} %collective-permute-done.14.refs_1_, bf16[2,64,256]{2,1,0:T(8,128)(2,1)S(1)} %get-tuple-element.132.refs_2_, ...), custom_call_target="tpu_custom_call" | custom-call | flops 990001024 | bytes 1000 | tf_op jit(solution)/shard_map/patch_product/pallas_call | solution.py:33
  92.3 3.0 %collective-permute-start.12 = (bf16[3,32,512]{2,1,0:T(8,128)(2,1)S(1)}, bf16[3,32,512]{2,1,0:T(8,128)(2,1)S(1)}, u32[]{:S(2)}, u32[]{:S(2)}) collective-permute-start(bf16[3,32,512]{2,1,0:T(8,128)(2,1)S(1)} %get-tuple-element.125), channel_id=1, source_target_pairs={{0,4},{4,8},{8,12},{12,16},{16,20},{20,24},{24,28},{1,5},{5,9},{9,... | collective-permute-start | bytes 294920 | tf_op jit(solution)/shard_map/ppermute | solution.py:131
  95.3 1.3 collective-permute-start.13
  96.6 1.3 collective-permute-done.12.refs_5_.refs_1_
  97.9 4.4 %collective-permute-done.13.refs_6_.refs_2_ = bf16[3,32,512]{2,1,0:T(8,128)(2,1)S(1)} collective-permute-done((bf16[3,32,512]{2,1,0:T(8,128)(2,1)S(1)}, bf16[3,32,512]{2,1,0:T(8,128)(2,1)S(1)}, u32[]{:S(2)}, u32[]{:S(2)}) %collective-permute-start.13) | collective-permute-done | bytes 98336 | tf_op jit(solution)/shard_map/ppermute | solution.py:131
  102.2 1.9 expand_product.1
  104.1 2.8 %project_product.1 = (bf16[1136,256]{1,0:T(8,128)(2,1)S(1)}, bf16[1136,256]{1,0:T(8,128)(2,1)S(1)}) custom-call(bf16[256,3072]{1,0:T(8,128)(2,1)S(1)} %get-tuple-element.127.refs_0_, bf16[256,3072]{1,0:T(8,128)(2,1)S(1)} %collective-permute-done.14.refs_1_, bf16[368,256]{1,0:T(8,128)(2,1)S(1)} %get-tuple-element.128.refs_2_, ...), custom_call_target="tpu_custom_call" | custom-call | flops 990001024 | bytes 1000 | tf_op jit(solution)/shard_map/project_product/pallas_call | solution.py:33
  106.9 1.7 collective-permute-start.21
  108.6 2.6 %collective-permute-start.22 = (bf16[1024,256]{1,0:T(8,128)(2,1)S(1)}, bf16[1024,256]{1,0:T(8,128)(2,1)S(1)}, u32[]{:S(2)}, u32[]{:S(2)}) collective-permute-start(bf16[1024,256]{1,0:T(8,128)(2,1)S(1)} %get-tuple-element.135.refs_4_), channel_id=1, source_target_pairs={{0,4},{4,0},{8,12},{12,8},{16,20},{20,16},{24,28},{28,24},{1,5},{5... | collective-permute-start | bytes 1572872 | tf_op jit(solution)/shard_map/ppermute | solution.py:47
  111.2 5.4 %block_weights.1 = (bf16[64,256]{1,0:T(8,128)(2,1)S(1)}, bf16[64,256]{1,0:T(8,128)(2,1)S(1)}) custom-call(bf16[8,32,512]{2,1,0:T(8,128)(2,1)S(1)} %get-tuple-element.89.refs_0_, bf16[3,32,512]{2,1,0:T(8,128)(2,1)S(1)} %collective-permute-done.refs_5_.refs_1_, bf16[3,32,512]{2,1,0:T(8,128)(2,1)S(1)} %collective-permute-done.1.refs_2_, ...), custom_call_target="tpu_custom_call" | custom-call | flops 1980001024 | bytes 1000 | tf_op jit(solution)/shard_map/block_weights/pallas_call | solution.py:33
  116.7 1.2 collective-permute-done.23
  118.0 2.1 %collective-permute-start.18 = (bf16[14,8,512]{2,1,0:T(8,128)(2,1)S(1)}, bf16[14,8,512]{2,1,0:T(8,128)(2,1)S(1)}, u32[]{:S(2)}, u32[]{:S(2)}) collective-permute-start(bf16[14,8,512]{2,1,0:T(8,128)(2,1)S(1)} %get-tuple-element.137), channel_id=1, source_target_pairs={{0,1},{1,2},{2,3},{4,5},{5,6},{6,7},{8,9},{9,10},{10,11},{12,13},{... | collective-permute-start | bytes 344072 | tf_op jit(solution)/shard_map/ppermute | solution.py:131
  120.1 2.9 %collective-permute-done.24.refs_3_ = bf16[64,256]{1,0:T(8,128)(2,1)S(1)} collective-permute-done((bf16[64,256]{1,0:T(8,128)(2,1)S(1)}, bf16[64,256]{1,0:T(8,128)(2,1)S(1)}, u32[]{:S(2)}, u32[]{:S(2)}) %collective-permute-start.24) | collective-permute-done | bytes 32800 | tf_op jit(solution)/shard_map/ppermute | solution.py:47
  123.0 1.3 collective-permute-start.19
  124.6 1.5 collective-permute-done.19.refs_4_
  126.4 1.8 collective-permute-start.33
  128.9 6.6 %input_grad.1.refs_2_ = bf16[8,32,512]{2,1,0:T(8,128)(2,1)} custom-call(bf16[8,32,512]{2,1,0:T(8,128)(2,1)S(1)} %get-tuple-element.124.refs_0_.refs_5_, bf16[3,32,512]{2,1,0:T(8,128)(2,1)S(1)} %collective-permute-done.12.refs_5_.refs_1_, bf16[3,32,512]{2,1,0:T(8,128)(2,1)S(1)} %collective-permute-done.13.refs_6_.refs_2_, ...), custom_call_target="tpu_custom_call" | custom-call | flops 2200001024 | bytes 1000 | tf_op jit(solution)/shard_map/input_grad/pallas_call | solution.py:33
  135.6 0.9 collective-permute-done.25.refs_1_
  136.4 0.9 copy-done
  137.4 8.2 %collective-permute-done.29.refs_1_ = bf16[624,256]{1,0:T(8,128)(2,1)S(1)} collective-permute-done((bf16[624,256]{1,0:T(8,128)(2,1)S(1)}, bf16[624,256]{1,0:T(8,128)(2,1)S(1)}, u32[]{:S(2)}, u32[]{:S(2)}) %collective-permute-start.29) | collective-permute-done | bytes 319520 | tf_op jit(solution)/shard_map/ppermute | solution.py:47
  146.4 7.4 %collective-permute-done.34.refs_1_ = bf16[512,256]{1,0:T(8,128)(2,1)S(1)} collective-permute-done((bf16[512,256]{1,0:T(8,128)(2,1)S(1)}, bf16[512,256]{1,0:T(8,128)(2,1)S(1)}, u32[]{:S(2)}, u32[]{:S(2)}) %collective-permute-start.34) | collective-permute-done | bytes 262176 | tf_op jit(solution)/shard_map/ppermute | solution.py:47
  153.8 1.8 collective-permute-start.35
  155.7 1.2 collective-permute-start.30
  156.8 1.8 collective-permute-start.26
  158.6 12.8 %collective-permute-done.35 = bf16[256,256]{1,0:T(8,128)(2,1)S(1)} collective-permute-done((bf16[256,256]{1,0:T(8,128)(2,1)S(1)}, bf16[256,256]{1,0:T(8,128)(2,1)S(1)}, u32[]{:S(2)}, u32[]{:S(2)}) %collective-permute-start.35) | collective-permute-done | bytes 131104 | tf_op jit(solution)/shard_map/ppermute | solution.py:47
  171.5 7.4 %collective-permute-done.26 = bf16[320,256]{1,0:T(8,128)(2,1)S(1)} collective-permute-done((bf16[320,256]{1,0:T(8,128)(2,1)S(1)}, bf16[320,256]{1,0:T(8,128)(2,1)S(1)}, u32[]{:S(2)}, u32[]{:S(2)}) %collective-permute-start.26) | collective-permute-done | bytes 163872 | tf_op jit(solution)/shard_map/ppermute | solution.py:47
  179.1 2.1 %collective-permute-start.31 = (bf16[368,256]{1,0:T(8,128)(2,1)S(1)}, bf16[368,256]{1,0:T(8,128)(2,1)S(1)}, u32[]{:S(2)}, u32[]{:S(2)}) collective-permute-start(bf16[368,256]{1,0:T(8,128)(2,1)S(1)} %add.26), channel_id=1, source_target_pairs={{0,2},{1,3},{2,0},{3,1},{4,6},{5,7},{6,4},{7,5},{8,10},{9,11},{10,... | collective-permute-start | bytes 565256 | tf_op jit(solution)/shard_map/ppermute | solution.py:47
  181.3 8.0 %collective-permute-done.31 = bf16[368,256]{1,0:T(8,128)(2,1)S(1)} collective-permute-done((bf16[368,256]{1,0:T(8,128)(2,1)S(1)}, bf16[368,256]{1,0:T(8,128)(2,1)S(1)}, u32[]{:S(2)}, u32[]{:S(2)}) %collective-permute-start.31) | collective-permute-done | bytes 188448 | tf_op jit(solution)/shard_map/ppermute | solution.py:47
  190.0 1.0 collective-permute-done.28.refs_1_
  191.1 0.9 finish_expand.1
  192.0 1.0 finish_project.1
  192.9 1.0 finish_patch.1
  (73 shorter events, 6.1 us)
Async XLA Ops:
  0.6 19.0 %copy-start.6 = (bf16[1,4,16,1024]{3,2,1,0:T(8,128)(2,1)S(1)}, bf16[1,4,16,1024]{3,2,1,0:T(8,128)(2,1)}, u32[]{:S(2)}) copy-start(bf16[1,4,16,1024]{3,2,1,0:T(8,128)(2,1)} %param.22) | copy-start | bytes 393220
  0.7 19.0 %copy-start.7 = (bf16[1,4,16,1024]{3,2,1,0:T(8,128)(2,1)S(1)}, bf16[1,4,16,1024]{3,2,1,0:T(8,128)(2,1)}, u32[]{:S(2)}) copy-start(bf16[1,4,16,1024]{3,2,1,0:T(8,128)(2,1)} %param.23) | copy-start | bytes 393220
  0.7 18.9 %copy-start.9 = (f32[1024]{0:T(1024)S(1)}, f32[1024]{0:T(1024)}, u32[]{:S(2)}) copy-start(f32[1024]{0:T(1024)} %param.21) | copy-start | bytes 12292
  1.7 7.0 %collective-permute-start = (bf16[3,32,512]{2,1,0:T(8,128)(2,1)S(1)}, bf16[3,32,512]{2,1,0:T(8,128)(2,1)S(1)}, u32[]{:S(2)}, u32[]{:S(2)}) collective-permute-start(bf16[3,32,512]{2,1,0:T(8,128)(2,1)S(1)} %get-tuple-element.171), channel_id=1, source_target_pairs={{0,4},{4,8},{8,12},{12,16},{16,20},{20,24},{24,28},{1,5},{5,9},{9,... | collective-permute-start | bytes 294920 | tf_op jit(solution)/shard_map/ppermute | solution.py:131
  6.5 6.5 %collective-permute-start.1 = (bf16[3,32,512]{2,1,0:T(8,128)(2,1)S(1)}, bf16[3,32,512]{2,1,0:T(8,128)(2,1)S(1)}, u32[]{:S(2)}, u32[]{:S(2)}) collective-permute-start(bf16[3,32,512]{2,1,0:T(8,128)(2,1)S(1)} %get-tuple-element.170), channel_id=1, source_target_pairs={{4,0},{8,4},{12,8},{16,12},{20,16},{24,20},{28,24},{5,1},{9,5},{13... | collective-permute-start | bytes 294920 | tf_op jit(solution)/shard_map/ppermute | solution.py:131
  8.7 0.9 copy-start.1
  9.7 0.9 copy-start.8
  10.6 0.7 copy-start.10
  11.3 0.7 copy-start.11
  11.9 0.7 copy-start.12
  12.6 7.0 %copy-start.2 = (bf16[2048,1024]{1,0:T(8,128)(2,1)S(1)}, bf16[2048,1024]{1,0:T(8,128)(2,1)}, u32[]{:S(2)}) copy-start(bf16[2048,1024]{1,0:T(8,128)(2,1)} %refs_11_.1) | copy-start | bytes 12582916
  12.6 7.0 %copy-start.3 = (bf16[512,2048]{1,0:T(8,128)(2,1)S(1)}, bf16[512,2048]{1,0:T(8,128)(2,1)}, u32[]{:S(2)}) copy-start(bf16[512,2048]{1,0:T(8,128)(2,1)} %refs_9_.1) | copy-start | bytes 6291460
  12.6 7.0 %copy-start.4 = (bf16[2048,512]{1,0:T(8,128)(2,1)S(1)}, bf16[2048,512]{1,0:T(8,128)(2,1)}, u32[]{:S(2)}) copy-start(bf16[2048,512]{1,0:T(8,128)(2,1)} %refs_10_.1) | copy-start | bytes 6291460
  12.6 7.0 %copy-start.5 = (f32[7,7,1024]{2,1,0:T(8,128)S(1)}, f32[7,7,1024]{2,1,0:T(8,128)}, u32[]{:S(2)}) copy-start(f32[7,7,1024]{2,1,0:T(8,128)} %refs_12_.1) | copy-start | bytes 602116
  13.1 3.0 %collective-permute-start.2 = (bf16[14,8,512]{2,1,0:T(8,128)(2,1)S(1)}, bf16[14,8,512]{2,1,0:T(8,128)(2,1)S(1)}, u32[]{:S(2)}, u32[]{:S(2)}) collective-permute-start(bf16[14,8,512]{2,1,0:T(8,128)(2,1)S(1)} %get-tuple-element.90), channel_id=1, source_target_pairs={{0,1},{1,2},{2,3},{4,5},{5,6},{6,7},{8,9},{9,10},{10,11},{12,13},{... | collective-permute-start | bytes 344072 | tf_op jit(solution)/shard_map/ppermute | solution.py:131
  14.6 5.0 %collective-permute-start.3 = (bf16[14,8,512]{2,1,0:T(8,128)(2,1)S(1)}, bf16[14,8,512]{2,1,0:T(8,128)(2,1)S(1)}, u32[]{:S(2)}, u32[]{:S(2)}) collective-permute-start(bf16[14,8,512]{2,1,0:T(8,128)(2,1)S(1)} %get-tuple-element.91), channel_id=1, source_target_pairs={{1,0},{2,1},{3,2},{5,4},{6,5},{7,6},{9,8},{10,9},{11,10},{13,12},{... | collective-permute-start | bytes 344072 | tf_op jit(solution)/shard_map/ppermute | solution.py:131
  32.5 6.6 %collective-permute-start.4 = (bf16[3,16,1024]{2,1,0:T(8,128)(2,1)S(1)}, bf16[3,16,1024]{2,1,0:T(8,128)(2,1)S(1)}, u32[]{:S(2)}, u32[]{:S(2)}) collective-permute-start(bf16[3,16,1024]{2,1,0:T(8,128)(2,1)S(1)} %get-tuple-element.97), channel_id=1, source_target_pairs={{0,4},{4,8},{8,12},{12,16},{16,20},{20,24},{24,28},{1,5},{5,9},{9,... | collective-permute-start | bytes 294920 | tf_op jit(solution)/shard_map/ppermute | solution.py:131
  36.8 6.7 %collective-permute-start.5 = (bf16[3,16,1024]{2,1,0:T(8,128)(2,1)S(1)}, bf16[3,16,1024]{2,1,0:T(8,128)(2,1)S(1)}, u32[]{:S(2)}, u32[]{:S(2)}) collective-permute-start(bf16[3,16,1024]{2,1,0:T(8,128)(2,1)S(1)} %get-tuple-element.98), channel_id=1, source_target_pairs={{4,0},{8,4},{12,8},{16,12},{20,16},{24,20},{28,24},{5,1},{9,5},{13... | collective-permute-start | bytes 294920 | tf_op jit(solution)/shard_map/ppermute | solution.py:131
  43.6 5.5 %collective-permute-start.6 = (bf16[10,8,1024]{2,1,0:T(8,128)(2,1)S(1)}, bf16[10,8,1024]{2,1,0:T(8,128)(2,1)S(1)}, u32[]{:S(2)}, u32[]{:S(2)}) collective-permute-start(bf16[10,8,1024]{2,1,0:T(8,128)(2,1)S(1)} %get-tuple-element.99), channel_id=1, source_target_pairs={{0,1},{1,2},{2,3},{4,5},{5,6},{6,7},{8,9},{9,10},{10,11},{12,13},{... | collective-permute-start | bytes 491528 | tf_op jit(solution)/shard_map/ppermute | solution.py:131
  47.8 3.8 %collective-permute-start.7 = (bf16[10,8,1024]{2,1,0:T(8,128)(2,1)S(1)}, bf16[10,8,1024]{2,1,0:T(8,128)(2,1)S(1)}, u32[]{:S(2)}, u32[]{:S(2)}) collective-permute-start(bf16[10,8,1024]{2,1,0:T(8,128)(2,1)S(1)} %get-tuple-element.100), channel_id=1, source_target_pairs={{1,0},{2,1},{3,2},{5,4},{6,5},{7,6},{9,8},{10,9},{11,10},{13,12},{... | collective-permute-start | bytes 491528 | tf_op jit(solution)/shard_map/ppermute | solution.py:131
  54.9 7.0 %collective-permute-start.8 = (bf16[3,16,1024]{2,1,0:T(8,128)(2,1)S(1)}, bf16[3,16,1024]{2,1,0:T(8,128)(2,1)S(1)}, u32[]{:S(2)}, u32[]{:S(2)}) collective-permute-start(bf16[3,16,1024]{2,1,0:T(8,128)(2,1)S(1)} %get-tuple-element.105), channel_id=1, source_target_pairs={{0,4},{4,8},{8,12},{12,16},{16,20},{20,24},{24,28},{1,5},{5,9},{9,... | collective-permute-start | bytes 294920 | tf_op jit(solution)/shard_map/ppermute | solution.py:131
  59.7 6.5 %collective-permute-start.9 = (bf16[3,16,1024]{2,1,0:T(8,128)(2,1)S(1)}, bf16[3,16,1024]{2,1,0:T(8,128)(2,1)S(1)}, u32[]{:S(2)}, u32[]{:S(2)}) collective-permute-start(bf16[3,16,1024]{2,1,0:T(8,128)(2,1)S(1)} %get-tuple-element.106), channel_id=1, source_target_pairs={{4,0},{8,4},{12,8},{16,12},{20,16},{24,20},{28,24},{5,1},{9,5},{13... | collective-permute-start | bytes 294920 | tf_op jit(solution)/shard_map/ppermute | solution.py:131
  66.3 5.8 %collective-permute-start.10 = (bf16[10,8,1024]{2,1,0:T(8,128)(2,1)S(1)}, bf16[10,8,1024]{2,1,0:T(8,128)(2,1)S(1)}, u32[]{:S(2)}, u32[]{:S(2)}) collective-permute-start(bf16[10,8,1024]{2,1,0:T(8,128)(2,1)S(1)} %get-tuple-element.108), channel_id=1, source_target_pairs={{0,1},{1,2},{2,3},{4,5},{5,6},{6,7},{8,9},{9,10},{10,11},{12,13},{... | collective-permute-start | bytes 491528 | tf_op jit(solution)/shard_map/ppermute | solution.py:131
  70.8 3.9 %collective-permute-start.11 = (bf16[10,8,1024]{2,1,0:T(8,128)(2,1)S(1)}, bf16[10,8,1024]{2,1,0:T(8,128)(2,1)S(1)}, u32[]{:S(2)}, u32[]{:S(2)}) collective-permute-start(bf16[10,8,1024]{2,1,0:T(8,128)(2,1)S(1)} %get-tuple-element.109), channel_id=1, source_target_pairs={{1,0},{2,1},{3,2},{5,4},{6,5},{7,6},{9,8},{10,9},{11,10},{13,12},{... | collective-permute-start | bytes 491528 | tf_op jit(solution)/shard_map/ppermute | solution.py:131
  77.8 11.7 %collective-permute-start.14 = (bf16[256,3072]{1,0:T(8,128)(2,1)S(1)}, bf16[256,3072]{1,0:T(8,128)(2,1)S(1)}, u32[]{:S(2)}, u32[]{:S(2)}) collective-permute-start(bf16[256,3072]{1,0:T(8,128)(2,1)S(1)} %get-tuple-element.127.refs_0_), channel_id=1, source_target_pairs={{0,1},{1,0},{2,3},{3,2},{4,5},{5,4},{6,7},{7,6},{8,9},{9,8},{10,11... | collective-permute-start | bytes 4718600 | tf_op jit(solution)/shard_map/ppermute | solution.py:47
  87.4 14.8 %collective-permute-start.16 = (bf16[256,1024]{1,0:T(8,128)(2,1)S(1)}, bf16[256,1024]{1,0:T(8,128)(2,1)S(1)}, u32[]{:S(2)}, u32[]{:S(2)}) collective-permute-start(bf16[256,1024]{1,0:T(8,128)(2,1)S(1)} %get-tuple-element.131.refs_4_), channel_id=1, source_target_pairs={{0,1},{1,0},{2,3},{3,2},{4,5},{5,4},{6,7},{7,6},{8,9},{9,8},{10,11... | collective-permute-start | bytes 1572872 | tf_op jit(solution)/shard_map/ppermute | solution.py:47
  87.5 2.0 %collective-permute-start.17 = (bf16[2,64,256]{2,1,0:T(8,128)(2,1)S(1)}, bf16[2,64,256]{2,1,0:T(8,128)(2,1)S(1)}, u32[]{:S(2)}, u32[]{:S(2)}) collective-permute-start(bf16[2,64,256]{2,1,0:T(8,128)(2,1)S(1)} %get-tuple-element.133), channel_id=1, source_target_pairs={{0,1},{1,0},{2,3},{3,2},{4,5},{5,4},{6,7},{7,6},{8,9},{9,8},{10,11... | collective-permute-start | bytes 196616 | tf_op jit(solution)/shard_map/ppermute | solution.py:47
  92.0 34.1 %collective-permute-start.20 = (bf16[2048,256]{1,0:T(8,128)(2,1)S(1)}, bf16[2048,256]{1,0:T(8,128)(2,1)S(1)}, u32[]{:S(2)}, u32[]{:S(2)}) collective-permute-start(bf16[2048,256]{1,0:T(8,128)(2,1)S(1)} %get-tuple-element.134.refs_4_), channel_id=1, source_target_pairs={{0,2},{1,3},{2,0},{3,1},{4,6},{5,7},{6,4},{7,5},{8,10},{9,11},{10,... | collective-permute-start | bytes 3145736 | tf_op jit(solution)/shard_map/ppermute | solution.py:47
  92.1 12.0 %collective-permute-start.15 = (bf16[368,256]{1,0:T(8,128)(2,1)S(1)}, bf16[368,256]{1,0:T(8,128)(2,1)S(1)}, u32[]{:S(2)}, u32[]{:S(2)}) collective-permute-start(bf16[368,256]{1,0:T(8,128)(2,1)S(1)} %get-tuple-element.129), channel_id=1, source_target_pairs={{0,1},{1,0},{2,3},{3,2},{4,5},{5,4},{6,7},{7,6},{8,9},{9,8},{10,11... | collective-permute-start | bytes 565256 | tf_op jit(solution)/shard_map/ppermute | solution.py:47
  92.3 5.5 %collective-permute-start.12 = (bf16[3,32,512]{2,1,0:T(8,128)(2,1)S(1)}, bf16[3,32,512]{2,1,0:T(8,128)(2,1)S(1)}, u32[]{:S(2)}, u32[]{:S(2)}) collective-permute-start(bf16[3,32,512]{2,1,0:T(8,128)(2,1)S(1)} %get-tuple-element.125), channel_id=1, source_target_pairs={{0,4},{4,8},{8,12},{12,16},{16,20},{20,24},{24,28},{1,5},{5,9},{9,... | collective-permute-start | bytes 294920 | tf_op jit(solution)/shard_map/ppermute | solution.py:131
  95.3 6.9 %collective-permute-start.13 = (bf16[3,32,512]{2,1,0:T(8,128)(2,1)S(1)}, bf16[3,32,512]{2,1,0:T(8,128)(2,1)S(1)}, u32[]{:S(2)}, u32[]{:S(2)}) collective-permute-start(bf16[3,32,512]{2,1,0:T(8,128)(2,1)S(1)} %get-tuple-element.126), channel_id=1, source_target_pairs={{4,0},{8,4},{12,8},{16,12},{20,16},{24,20},{28,24},{5,1},{9,5},{13... | collective-permute-start | bytes 294920 | tf_op jit(solution)/shard_map/ppermute | solution.py:131
  106.9 17.5 %collective-permute-start.21 = (bf16[1136,256]{1,0:T(8,128)(2,1)S(1)}, bf16[1136,256]{1,0:T(8,128)(2,1)S(1)}, u32[]{:S(2)}, u32[]{:S(2)}) collective-permute-start(bf16[1136,256]{1,0:T(8,128)(2,1)S(1)} %get-tuple-element.136.refs_3_.refs_7_), channel_id=1, source_target_pairs={{0,8},{4,12},{8,0},{12,4},{16,24},{20,28},{24,16},{28,20},{1,9},{5... | collective-permute-start | bytes 1744904 | tf_op jit(solution)/shard_map/ppermute | solution.py:47
  108.6 15.6 %collective-permute-start.22 = (bf16[1024,256]{1,0:T(8,128)(2,1)S(1)}, bf16[1024,256]{1,0:T(8,128)(2,1)S(1)}, u32[]{:S(2)}, u32[]{:S(2)}) collective-permute-start(bf16[1024,256]{1,0:T(8,128)(2,1)S(1)} %get-tuple-element.135.refs_4_), channel_id=1, source_target_pairs={{0,4},{4,0},{8,12},{12,8},{16,20},{20,16},{24,28},{28,24},{1,5},{5... | collective-permute-start | bytes 1572872 | tf_op jit(solution)/shard_map/ppermute | solution.py:47
  116.6 1.3 collective-permute-start.23
  117.9 5.1 %collective-permute-start.24 = (bf16[64,256]{1,0:T(8,128)(2,1)S(1)}, bf16[64,256]{1,0:T(8,128)(2,1)S(1)}, u32[]{:S(2)}, u32[]{:S(2)}) collective-permute-start(bf16[64,256]{1,0:T(8,128)(2,1)S(1)} %add.23.refs_2_), channel_id=1, source_target_pairs={{0,4},{4,0},{8,12},{12,8},{16,20},{20,16},{24,28},{28,24},{1,5},{5... | collective-permute-start | bytes 98312 | tf_op jit(solution)/shard_map/ppermute | solution.py:47
  118.0 6.6 %collective-permute-start.18 = (bf16[14,8,512]{2,1,0:T(8,128)(2,1)S(1)}, bf16[14,8,512]{2,1,0:T(8,128)(2,1)S(1)}, u32[]{:S(2)}, u32[]{:S(2)}) collective-permute-start(bf16[14,8,512]{2,1,0:T(8,128)(2,1)S(1)} %get-tuple-element.137), channel_id=1, source_target_pairs={{0,1},{1,2},{2,3},{4,5},{5,6},{6,7},{8,9},{9,10},{10,11},{12,13},{... | collective-permute-start | bytes 344072 | tf_op jit(solution)/shard_map/ppermute | solution.py:131
  123.0 3.2 %collective-permute-start.19 = (bf16[14,8,512]{2,1,0:T(8,128)(2,1)S(1)}, bf16[14,8,512]{2,1,0:T(8,128)(2,1)S(1)}, u32[]{:S(2)}, u32[]{:S(2)}) collective-permute-start(bf16[14,8,512]{2,1,0:T(8,128)(2,1)S(1)} %get-tuple-element.138), channel_id=1, source_target_pairs={{1,0},{2,1},{3,2},{5,4},{6,5},{7,6},{9,8},{10,9},{11,10},{13,12},{... | collective-permute-start | bytes 344072 | tf_op jit(solution)/shard_map/ppermute | solution.py:131
  126.4 19.3 %collective-permute-start.33 = (bf16[1024,256]{1,0:T(8,128)(2,1)S(1)}, bf16[1024,256]{1,0:T(8,128)(2,1)S(1)}, u32[]{:S(2)}, u32[]{:S(2)}) collective-permute-start(bf16[1024,256]{1,0:T(8,128)(2,1)S(1)} %get-tuple-element.148.refs_7_), channel_id=1, source_target_pairs={{0,4},{4,0},{8,12},{12,8},{16,20},{20,16},{24,28},{28,24},{1,5},{5... | collective-permute-start | bytes 1572872 | tf_op jit(solution)/shard_map/ppermute | solution.py:47
  128.2 17.4 %collective-permute-start.29 = (bf16[624,256]{1,0:T(8,128)(2,1)S(1)}, bf16[624,256]{1,0:T(8,128)(2,1)S(1)}, u32[]{:S(2)}, u32[]{:S(2)}) collective-permute-start(bf16[624,256]{1,0:T(8,128)(2,1)S(1)} %get-tuple-element.147.refs_2_), channel_id=1, source_target_pairs={{0,4},{4,0},{8,12},{12,8},{16,20},{20,16},{24,28},{28,24},{1,5},{5... | collective-permute-start | bytes 958472 | tf_op jit(solution)/shard_map/ppermute | solution.py:47
  128.5 7.9 %collective-permute-start.25 = (bf16[576,256]{1,0:T(8,128)(2,1)S(1)}, bf16[576,256]{1,0:T(8,128)(2,1)S(1)}, u32[]{:S(2)}, u32[]{:S(2)}) collective-permute-start(bf16[576,256]{1,0:T(8,128)(2,1)S(1)} %get-tuple-element.146.refs_2_), channel_id=1, source_target_pairs={{0,8},{4,12},{8,0},{12,4},{16,24},{20,28},{24,16},{28,20},{1,9},{5... | collective-permute-start | bytes 884744 | tf_op jit(solution)/shard_map/ppermute | solution.py:47
  136.4 1.0 copy-start
  145.9 7.9 %collective-permute-start.34 = (bf16[512,256]{1,0:T(8,128)(2,1)S(1)}, bf16[512,256]{1,0:T(8,128)(2,1)S(1)}, u32[]{:S(2)}, u32[]{:S(2)}) collective-permute-start(bf16[512,256]{1,0:T(8,128)(2,1)S(1)} %get-tuple-element.163), channel_id=1, source_target_pairs={{0,8},{4,12},{8,0},{12,4},{16,24},{20,28},{24,16},{28,20},{1,9},{5... | collective-permute-start | bytes 786440 | tf_op jit(solution)/shard_map/ppermute | solution.py:47
  153.8 17.5 %collective-permute-start.35 = (bf16[256,256]{1,0:T(8,128)(2,1)S(1)}, bf16[256,256]{1,0:T(8,128)(2,1)S(1)}, u32[]{:S(2)}, u32[]{:S(2)}) collective-permute-start(bf16[256,256]{1,0:T(8,128)(2,1)S(1)} %get-tuple-element.165), channel_id=1, source_target_pairs={{0,16},{4,20},{8,24},{12,28},{16,0},{20,4},{24,8},{28,12},{1,17},{... | collective-permute-start | bytes 393224 | tf_op jit(solution)/shard_map/ppermute | solution.py:47
  155.7 23.4 %collective-permute-start.30 = (bf16[368,256]{1,0:T(8,128)(2,1)S(1)}, bf16[368,256]{1,0:T(8,128)(2,1)S(1)}, u32[]{:S(2)}, u32[]{:S(2)}) collective-permute-start(bf16[368,256]{1,0:T(8,128)(2,1)S(1)} %get-tuple-element.157.refs_2_), channel_id=1, source_target_pairs={{0,16},{4,20},{8,24},{12,28},{16,0},{20,4},{24,8},{28,12},{1,17},{... | collective-permute-start | bytes 565256 | tf_op jit(solution)/shard_map/ppermute | solution.py:47
  156.8 22.1 %collective-permute-start.26 = (bf16[320,256]{1,0:T(8,128)(2,1)S(1)}, bf16[320,256]{1,0:T(8,128)(2,1)S(1)}, u32[]{:S(2)}, u32[]{:S(2)}) collective-permute-start(bf16[320,256]{1,0:T(8,128)(2,1)S(1)} %get-tuple-element.151.refs_2_), channel_id=1, source_target_pairs={{0,16},{4,20},{8,24},{12,28},{16,0},{20,4},{24,8},{28,12},{1,17},{... | collective-permute-start | bytes 491528 | tf_op jit(solution)/shard_map/ppermute | solution.py:47
  171.4 9.8 %collective-permute-start.36 = (bf16[1,256,256]{2,1,0:T(8,128)(2,1)S(1)}, bf16[1,256,256]{2,1,0:T(8,128)(2,1)S(1)}, u32[]{:S(2)}, u32[]{:S(2)}) collective-permute-start(bf16[1,256,256]{2,1,0:T(8,128)(2,1)S(1)} %add_bitcast_fusion), channel_id=1, source_target_pairs={{0,2},{1,3},{2,0},{3,1},{4,6},{5,7},{6,4},{7,5},{8,10},{9,11},{10,... | collective-permute-start | bytes 393224 | tf_op jit(solution)/shard_map/ppermute | solution.py:47
  179.0 10.5 %collective-permute-start.27 = (bf16[320,256]{1,0:T(8,128)(2,1)S(1)}, bf16[320,256]{1,0:T(8,128)(2,1)S(1)}, u32[]{:S(2)}, u32[]{:S(2)}) collective-permute-start(bf16[320,256]{1,0:T(8,128)(2,1)S(1)} %add.24), channel_id=1, source_target_pairs={{0,2},{1,3},{2,0},{3,1},{4,6},{5,7},{6,4},{7,5},{8,10},{9,11},{10,... | collective-permute-start | bytes 491528 | tf_op jit(solution)/shard_map/ppermute | solution.py:47
  179.1 10.2 %collective-permute-start.31 = (bf16[368,256]{1,0:T(8,128)(2,1)S(1)}, bf16[368,256]{1,0:T(8,128)(2,1)S(1)}, u32[]{:S(2)}, u32[]{:S(2)}) collective-permute-start(bf16[368,256]{1,0:T(8,128)(2,1)S(1)} %add.26), channel_id=1, source_target_pairs={{0,2},{1,3},{2,0},{3,1},{4,6},{5,7},{6,4},{7,5},{8,10},{9,11},{10,... | collective-permute-start | bytes 565256 | tf_op jit(solution)/shard_map/ppermute | solution.py:47
  181.2 11.7 %collective-permute-start.37 = (bf16[2,256,256]{2,1,0:T(8,128)(2,1)S(1)}, bf16[2,256,256]{2,1,0:T(8,128)(2,1)S(1)}, u32[]{:S(2)}, u32[]{:S(2)}) collective-permute-start(bf16[2,256,256]{2,1,0:T(8,128)(2,1)S(1)} %maximum_bitcast_fusion.refs_0_), channel_id=1, source_target_pairs={{0,1},{1,0},{2,3},{3,2},{4,5},{5,4},{6,7},{7,6},{8,9},{9,8},{10,11... | collective-permute-start | bytes 786440 | tf_op jit(solution)/shard_map/ppermute | solution.py:47
  189.4 2.6 %collective-permute-start.32 = (bf16[368,256]{1,0:T(8,128)(2,1)S(1)}, bf16[368,256]{1,0:T(8,128)(2,1)S(1)}, u32[]{:S(2)}, u32[]{:S(2)}) collective-permute-start(bf16[368,256]{1,0:T(8,128)(2,1)S(1)} %add.27.refs_0_), channel_id=1, source_target_pairs={{0,1},{1,0},{2,3},{3,2},{4,5},{5,4},{6,7},{7,6},{8,9},{9,8},{10,11... | collective-permute-start | bytes 565256 | tf_op jit(solution)/shard_map/ppermute | solution.py:47
  189.5 1.6 collective-permute-start.28

commit v9 on v3

--- a/solution.py
+++ b/solution.py
@@ -72,6 +72,7 @@
             (out, out),
             after=after if place == 0 else (),
             limit=8,
+            us=0.2,
         )
 
 
@@ -777,6 +778,7 @@
             pltpu.VMEM((8, channels), F32),
         ),
         limit=16,
+        us=0.8,
     )
     branch_other = swap(branch_send, "col", 1)
     patch_half = shape_of(block_count // 2 * 4 * channels, block, dtype=BF)
@@ -786,6 +788,7 @@
         (early, early_other, flat_keep, flat_other),
         (patch_half, patch_half),
         limit=16,
+        us=0.9,
     )
     deep, shallow = hidden_width // row_count, channels // row_count
     groups = hidden_width // channels
@@ -810,6 +813,7 @@
         ),
         after=(patch_send,),
         limit=16,
+        us=1.2,
     )
     rows_back = neighbours(first, last, "row")
     upward_other = swap(upward_send, "col", 1)
@@ -820,6 +824,7 @@
         (project_half, project_half),
         after=(upward_send,),
         limit=16,
+        us=0.9,
     )
     expand_half = shape_of(row_count // 2 * groups * shallow, half, dtype=BF)
     expand_keep, expand_send = run(
@@ -827,8 +832,9 @@
         "expand_product",
         (early, early_other, upward_keep, upward_other),
         (expand_half, expand_half),
-        after=(project_send,),
+        after=(project_send, *rows_back),
         limit=16,
+        us=0.6,
     )
     framed_back = halo(grad_mixed, rows_back, "strips_back", after=(expand_send,))
     small_half = shape_of(64, half, dtype=BF)
@@ -844,6 +850,7 @@
         ),
         after=(*framed_back[1:3], expand_send),
         limit=12,
+        us=1.8,
     )
     (input_grad,) = run(
         input_kernel,
@@ -853,6 +860,7 @@
         scratch=(frame_scratch(center), pltpu.VMEM((height, breadth, channels), F32)),
         after=(small_keep,),
         limit=12,
+        us=2,
     )
 
     row_bits, col_bits = axis_bits("row"), axis_bits("col")
@@ -878,11 +886,12 @@
             total = total + swap(total, "col", bit)
         return total, swap(total, "col", 1)
 
+    project_order = [("row", bit, 1) for bit in row_bits[1:]] + low_first[:1]
     vector, wide_vector = shape_of(1, channels), shape_of(1, wide)
     project_grad, wide_taps, wide_gain, merge_sum, layer_sum = run(
         finish_project_kernel,
         "finish_project",
-        share(project_keep, project_send, [("row", row_bits[1], 1), low_first[0], *low_first[2:]], deep),
+        share(project_keep, project_send, project_order, deep, after=(small_keep,)),
         (shape_of(deep, channels), shape_of(7, 7, wide), wide_vector, vector, vector),
         scratch=(pltpu.VMEM((112, channels), F32),),
         limit=8,

time: 177 us -> 172 us (0.972)
  waiting for transfers between devices: 58.8 us -> 48.8 us
  starting transfers between devices: 59.5 us -> 63.9 us
    ppermute x22, waiting for transfers between devices: 40.5 us -> 31.3 us  [swap(): lax.ppermute(values, axis, [(i, i ^ bit) for i in range(lax.axis_size(axi...]
    ppermute x22, starting transfers between devices: 20.5 us -> 23.8 us  [swap(): lax.ppermute(values, axis, [(i, i ^ bit) for i in range(lax.axis_size(axi...]
  transfers between devices with their start and end apart: 38 -> 38, of which waited for: 20 -> 17; matrix products, arithmetic and copies ran while one was open for 0% -> 0% of each run, Pallas kernels for 16% -> 16%
where the time goes in v9:
time: 172 us; the launch traced here: 171 us
  starting transfers between devices  63.9 us (37%)
  Pallas kernels  51 us (30%)
  waiting for transfers between devices  48.8 us (28%)
  local copies, waits for them, and re-layouts  5.87 us (3%)
    pallas_call x26, Pallas kernels, run(): pl.pallas_call(inner, name=name, out_shape=outs, in_specs=[spec(i) for i...  51 us
    ppermute x22, waiting for transfers between devices, swap(): lax.ppermute(values, axis, [(i, i ^ bit) for i in range(lax.axis_size(axi...  31.3 us
    ppermute x8, starting transfers between devices, neighbours(): lax.ppermute(last, axis, forward)  29.6 us
    ppermute x22, starting transfers between devices, swap(): lax.ppermute(values, axis, [(i, i ^ bit) for i in range(lax.axis_size(axi...  23.8 us
    ppermute x8, waiting for transfers between devices, neighbours(): lax.ppermute(first, axis, backward)  14.8 us
    ppermute x8, starting transfers between devices, neighbours(): lax.ppermute(first, axis, backward)  10.5 us
    unnamed x26, local copies, waits for them, and re-layouts  4.87 us
  transfers between devices with their start and end apart: 38, of which 17 were waited for; matrix products, arithmetic and copies ran while one was open for 0% of the time, Pallas kernels for 16%

profile of v9, /device:TPU:0, one launch (start us, length us, event | category | flops | bytes accessed | tf_op | source)
XLA Modules:
  0.0 170.9 jit_solution(18420353411980291563)
XLA Ops:
  0.7 1.0 slice_bitcast_fusion
  1.7 4.8 %collective-permute-start = (bf16[3,32,512]{2,1,0:T(8,128)(2,1)S(1)}, bf16[3,32,512]{2,1,0:T(8,128)(2,1)S(1)}, u32[]{:S(2)}, u32[]{:S(2)}) collective-permute-start(bf16[3,32,512]{2,1,0:T(8,128)(2,1)S(1)} %get-tuple-element.171), channel_id=1, source_target_pairs={{0,4},{4,8},{8,12},{12,16},{16,20},{20,24},{24,28},{1,5},{5,9},{9,... | collective-permute-start | bytes 294920 | tf_op jit(solution)/shard_map/ppermute | solution.py:120
  6.5 1.3 collective-permute-start.1
  7.8 0.9 collective-permute-done.refs_5_.refs_1_
  8.7 0.9 copy-done.1
  9.7 0.9 copy-done.8
  10.6 0.7 copy-done.10
  11.3 0.7 copy-done.11
  11.9 0.7 copy-done.12
  13.1 1.6 collective-permute-start.2
  14.6 1.4 collective-permute-start.3
  16.1 3.5 %collective-permute-done.3.refs_4_ = bf16[14,8,512]{2,1,0:T(8,128)(2,1)S(1)} collective-permute-done((bf16[14,8,512]{2,1,0:T(8,128)(2,1)S(1)}, bf16[14,8,512]{2,1,0:T(8,128)(2,1)S(1)}, u32[]{:S(2)}, u32[]{:S(2)}) %collective-permute-start.3) | collective-permute-done | bytes 114720 | tf_op jit(solution)/shard_map/ppermute | solution.py:120
  19.6 12.8 %front.1 = (bf16[256,3072]{1,0:T(8,128)(2,1)S(1)}, f32[256,512]{1,0:T(8,128)S(1)}, f32[256,1]{1,0:T(8,128)S(1)}, bf16[256,2048]{1,0:T(8,128)(2,1)S(1)}, f32[256,...) custom-call(bf16[8,32,512]{2,1,0:T(8,128)(2,1)S(1)} %get-tuple-eleme, ...), custom_call_target="tpu_custom_call" | custom-call | flops 13200001024 | bytes 1000 | tf_op jit(solution)/shard_map/front/pallas_call | solution.py:33
  32.5 4.4 %collective-permute-start.4 = (bf16[3,16,1024]{2,1,0:T(8,128)(2,1)S(1)}, bf16[3,16,1024]{2,1,0:T(8,128)(2,1)S(1)}, u32[]{:S(2)}, u32[]{:S(2)}) collective-permute-start(bf16[3,16,1024]{2,1,0:T(8,128)(2,1)S(1)} %get-tuple-element.97), channel_id=1, source_target_pairs={{0,4},{4,8},{8,12},{12,16},{16,20},{20,24},{24,28},{1,5},{5,9},{9,... | collective-permute-start | bytes 294920 | tf_op jit(solution)/shard_map/ppermute | solution.py:120
  36.8 1.3 collective-permute-start.5
  38.1 0.9 collective-permute-done.4.refs_1_
  39.0 4.5 %collective-permute-done.5.refs_2_ = bf16[3,16,1024]{2,1,0:T(8,128)(2,1)S(1)} collective-permute-done((bf16[3,16,1024]{2,1,0:T(8,128)(2,1)S(1)}, bf16[3,16,1024]{2,1,0:T(8,128)(2,1)S(1)}, u32[]{:S(2)}, u32[]{:S(2)}) %collective-permute-start.5) | collective-permute-done | bytes 98336 | tf_op jit(solution)/shard_map/ppermute | solution.py:120
  43.6 4.2 %collective-permute-start.6 = (bf16[10,8,1024]{2,1,0:T(8,128)(2,1)S(1)}, bf16[10,8,1024]{2,1,0:T(8,128)(2,1)S(1)}, u32[]{:S(2)}, u32[]{:S(2)}) collective-permute-start(bf16[10,8,1024]{2,1,0:T(8,128)(2,1)S(1)} %get-tuple-element.99), channel_id=1, source_target_pairs={{0,1},{1,2},{2,3},{4,5},{5,6},{6,7},{8,9},{9,10},{10,11},{12,13},{... | collective-permute-start | bytes 491528 | tf_op jit(solution)/shard_map/ppermute | solution.py:120
  47.8 1.3 collective-permute-start.7
  49.1 2.5 %collective-permute-done.7.refs_4_ = bf16[10,8,1024]{2,1,0:T(8,128)(2,1)S(1)} collective-permute-done((bf16[10,8,1024]{2,1,0:T(8,128)(2,1)S(1)}, bf16[10,8,1024]{2,1,0:T(8,128)(2,1)S(1)}, u32[]{:S(2)}, u32[]{:S(2)}) %collective-permute-start.7) | collective-permute-done | bytes 163872 | tf_op jit(solution)/shard_map/ppermute | solution.py:120
  51.6 3.3 %mixer.1 = (f32[4,16,1024]{2,1,0:T(8,128)S(1)}, bf16[4,16,1024]{2,1,0:T(8,128)(2,1)S(1)}, bf16[3,16,1024]{2,1,0:T(8,128)(2,1)S(1)}, bf16[3,16,1024]{2,1,0:T(8,128)(2,1)S(1)}, f32[1,1024]{1,0:T(1,128)S(1)}) custom-call(bf16[4,16,1024]{2,1,0:T(8,128)(2,1)S(1)} %get-tuple-element.96.refs_0_, bf16[3,16,1024]{2,1,0:T(8,128)(2,1)S(1)} %collective-permute-done.4.refs_1_, ...), custom_call_target="tpu_custom_call" | custom-call | flops 3300001024 | bytes 1000 | tf_op jit(solution)/shard_map/mixer/pallas_call | solution.py:33
  54.9 4.8 %collective-permute-start.8 = (bf16[3,16,1024]{2,1,0:T(8,128)(2,1)S(1)}, bf16[3,16,1024]{2,1,0:T(8,128)(2,1)S(1)}, u32[]{:S(2)}, u32[]{:S(2)}) collective-permute-start(bf16[3,16,1024]{2,1,0:T(8,128)(2,1)S(1)} %get-tuple-element.105), channel_id=1, source_target_pairs={{0,4},{4,8},{8,12},{12,16},{16,20},{20,24},{24,28},{1,5},{5,9},{9,... | collective-permute-start | bytes 294920 | tf_op jit(solution)/shard_map/ppermute | solution.py:120
  59.7 1.3 collective-permute-start.9
  61.0 0.9 collective-permute-done.8.refs_6_.refs_1_
  61.9 2.9 %mixer_weights.1.refs_3_.refs_7_ = f32[49,1024]{1,0:T(8,128)S(1)} custom-call(bf16[4,16,1024]{2,1,0:T(8,128)(2,1)S(1)} %get-tuple-element.96.refs_0_, bf16[3,16,1024]{2,1,0:T(8,128)(2,1)S(1)} %collective-permute-done.4.refs_1_, bf16[3,16,1024]{2,1,0:T(8,128)(2,1)S(1)} %collective-permute-done.5.refs_2_, ...), custom_call_target="tpu_custom_call" | custom-call | flops 3300001024 | bytes 1000 | tf_op jit(solution)/shard_map/mixer_weights/pallas_call | solution.py:33
  64.8 1.4 collective-permute-done.9.refs_2_
  66.3 4.5 %collective-permute-start.10 = (bf16[10,8,1024]{2,1,0:T(8,128)(2,1)S(1)}, bf16[10,8,1024]{2,1,0:T(8,128)(2,1)S(1)}, u32[]{:S(2)}, u32[]{:S(2)}) collective-permute-start(bf16[10,8,1024]{2,1,0:T(8,128)(2,1)S(1)} %get-tuple-element.108), channel_id=1, source_target_pairs={{0,1},{1,2},{2,3},{4,5},{5,6},{6,7},{8,9},{9,10},{10,11},{12,13},{... | collective-permute-start | bytes 491528 | tf_op jit(solution)/shard_map/ppermute | solution.py:120
  70.8 1.3 collective-permute-start.11
  72.1 2.6 %collective-permute-done.11.refs_4_ = bf16[10,8,1024]{2,1,0:T(8,128)(2,1)S(1)} collective-permute-done((bf16[10,8,1024]{2,1,0:T(8,128)(2,1)S(1)}, bf16[10,8,1024]{2,1,0:T(8,128)(2,1)S(1)}, u32[]{:S(2)}, u32[]{:S(2)}) %collective-permute-start.11) | collective-permute-done | bytes 163872 | tf_op jit(solution)/shard_map/ppermute | solution.py:120
  74.7 3.1 %section_grad.1 = (bf16[64,1024]{1,0:T(8,128)(2,1)S(1)}, bf16[2,64,256]{2,1,0:T(8,128)(2,1)S(1)}, bf16[2,64,256]{2,1,0:T(8,128)(2,1)S(1)}, bf16[256,3072]{1,0:T(8,128)(2,1)S(1)}) custom-call(bf16[4,16,1024]{2,1,0:T(8,128)(2,1)S(1)} %get-tuple-element.104.refs_0_, ...), custom_call_target="tpu_custom_call", output_to_operand_aliasing={{3}: (7, {})} | custom-call | flops 3300001024 | bytes 1000 | tf_op jit(solution)/shard_map/section_grad/pallas_call | solution.py:33
  77.8 3.9 %collective-permute-start.12 = (bf16[256,3072]{1,0:T(8,128)(2,1)S(1)}, bf16[256,3072]{1,0:T(8,128)(2,1)S(1)}, u32[]{:S(2)}, u32[]{:S(2)}) collective-permute-start(bf16[256,3072]{1,0:T(8,128)(2,1)S(1)} %get-tuple-element.124.refs_0_), channel_id=1, source_target_pairs={{0,1},{1,0},{2,3},{3,2},{4,5},{5,4},{6,7},{7,6},{8,9},{9,8},{10,11... | collective-permute-start | bytes 4718600 | tf_op jit(solution)/shard_map/ppermute | solution.py:47
  81.8 3.1 %collective-permute-done.13.refs_3_ = bf16[2,64,256]{2,1,0:T(8,128)(2,1)S(1)} collective-permute-done((bf16[2,64,256]{2,1,0:T(8,128)(2,1)S(1)}, bf16[2,64,256]{2,1,0:T(8,128)(2,1)S(1)}, u32[]{:S(2)}, u32[]{:S(2)}) %collective-permute-start.13) | collective-permute-done | bytes 65568 | tf_op jit(solution)/shard_map/ppermute | solution.py:47
  84.8 2.6 %patch_product.1 = (bf16[2048,256]{1,0:T(8,128)(2,1)S(1)}, bf16[2048,256]{1,0:T(8,128)(2,1)S(1)}) custom-call(bf16[256,3072]{1,0:T(8,128)(2,1)S(1)} %get-tuple-element.124.refs_0_, bf16[256,3072]{1,0:T(8,128)(2,1)S(1)} %collective-permute-done.12.refs_1_, bf16[2,64,256]{2,1,0:T(8,128)(2,1)S(1)} %get-tuple-element.125.refs_2_, ...), custom_call_target="tpu_custom_call" | custom-call | flops 990001024 | bytes 1000 | tf_op jit(solution)/shard_map/patch_product/pallas_call | solution.py:33
  87.6 2.5 %merge_back.1 = (f32[256,512]{1,0:T(8,128)S(1)}, bf16[256,512]{1,0:T(8,128)(2,1)S(1)}, bf16[368,256]{1,0:T(8,128)(2,1)S(1)}, bf16[368,256]{1,0:T(8,128)(2,1)S(1)}) custom-call(bf16[64,1024]{1,0:T(8,128)(2,1)S(1)} %get-tuple-element.112.refs_0_, bf16[2048,1024]{1,0:T(8,128)(2,1)S(1)} %get-tuple-element.113.refs_1_, ...), custom_call_target="tpu_custom_call" | custom-call | flops 880001024 | bytes 1000 | tf_op jit(solution)/shard_map/merge_back/pallas_call | solution.py:33
  90.1 3.2 %mlp_back.1 = (bf16[256,1024]{1,0:T(8,128)(2,1)S(1)}, bf16[256,1024]{1,0:T(8,128)(2,1)S(1)}, bf16[8,32,512]{2,1,0:T(8,128)(2,1)S(1)}, bf16[3,32,512]{2,1,0:T(8,1...) custom-call(bf16[256,512]{1,0:T(8,128)(2,1)S(1)} %get-tuple-element.118.refs_0_, ...), custom_call_target="tpu_custom_call" | custom-call | flops 1320001024 | bytes 1000 | tf_op jit(solution)/shard_map/mlp_back/pallas_call | solution.py:33
  93.8 3.0 %collective-permute-start.14 = (bf16[3,32,512]{2,1,0:T(8,128)(2,1)S(1)}, bf16[3,32,512]{2,1,0:T(8,128)(2,1)S(1)}, u32[]{:S(2)}, u32[]{:S(2)}) collective-permute-start(bf16[3,32,512]{2,1,0:T(8,128)(2,1)S(1)} %get-tuple-element.129), channel_id=1, source_target_pairs={{0,4},{4,8},{8,12},{12,16},{16,20},{20,24},{24,28},{1,5},{5,9},{9,... | collective-permute-start | bytes 294920 | tf_op jit(solution)/shard_map/ppermute | solution.py:120
  96.8 1.3 collective-permute-start.15
  98.1 2.8 %project_product.1 = (bf16[1136,256]{1,0:T(8,128)(2,1)S(1)}, bf16[1136,256]{1,0:T(8,128)(2,1)S(1)}) custom-call(bf16[256,3072]{1,0:T(8,128)(2,1)S(1)} %get-tuple-element.124.refs_0_, bf16[256,3072]{1,0:T(8,128)(2,1)S(1)} %collective-permute-done.12.refs_1_, bf16[368,256]{1,0:T(8,128)(2,1)S(1)} %get-tuple-element.133.refs_2_, ...), custom_call_target="tpu_custom_call" | custom-call | flops 990001024 | bytes 1000 | tf_op jit(solution)/shard_map/project_product/pallas_call | solution.py:33
  100.9 4.1 %collective-permute-start.27 = (bf16[1136,256]{1,0:T(8,128)(2,1)S(1)}, bf16[1136,256]{1,0:T(8,128)(2,1)S(1)}, u32[]{:S(2)}, u32[]{:S(2)}) collective-permute-start(bf16[1136,256]{1,0:T(8,128)(2,1)S(1)} %get-tuple-element.135.refs_4_), channel_id=1, source_target_pairs={{0,8},{4,12},{8,0},{12,4},{16,24},{20,28},{24,16},{28,20},{1,9},{5... | collective-permute-start | bytes 1744904 | tf_op jit(solution)/shard_map/ppermute | solution.py:47
  105.1 1.9 %expand_product.1 = (bf16[1024,256]{1,0:T(8,128)(2,1)S(1)}, bf16[1024,256]{1,0:T(8,128)(2,1)S(1)}) custom-call(bf16[256,3072]{1,0:T(8,128)(2,1)S(1)} %get-tuple-element.124.refs_0_, bf16[256,3072]{1,0:T(8,128)(2,1)S(1)} %collective-permute-done.12.refs_1_, bf16[256,1024]{1,0:T(8,128)(2,1)S(1)} %get-tuple-element.131.refs_2_, ...), custom_call_target="tpu_custom_call" | custom-call | flops 660001024 | bytes 1000 | tf_op jit(solution)/shard_map/expand_product/pallas_call | solution.py:33
  107.0 5.4 %block_weights.1 = (bf16[64,256]{1,0:T(8,128)(2,1)S(1)}, bf16[64,256]{1,0:T(8,128)(2,1)S(1)}) custom-call(bf16[8,32,512]{2,1,0:T(8,128)(2,1)S(1)} %get-tuple-element.89.refs_0_, bf16[3,32,512]{2,1,0:T(8,128)(2,1)S(1)} %collective-permute-done.refs_5_.refs_1_, bf16[3,32,512]{2,1,0:T(8,128)(2,1)S(1)} %collective-permute-done.1.refs_2_, ...), custom_call_target="tpu_custom_call" | custom-call | flops 1980001024 | bytes 1000 | tf_op jit(solution)/shard_map/block_weights/pallas_call | solution.py:33
  113.1 1.1 collective-permute-start.33
  114.3 1.0 collective-permute-start.20
  115.3 2.4 %collective-permute-start.18 = (bf16[14,8,512]{2,1,0:T(8,128)(2,1)S(1)}, bf16[14,8,512]{2,1,0:T(8,128)(2,1)S(1)}, u32[]{:S(2)}, u32[]{:S(2)}) collective-permute-start(bf16[14,8,512]{2,1,0:T(8,128)(2,1)S(1)} %get-tuple-element.137), channel_id=1, source_target_pairs={{0,1},{1,2},{2,3},{4,5},{5,6},{6,7},{8,9},{9,10},{10,11},{12,13},{... | collective-permute-start | bytes 344072 | tf_op jit(solution)/shard_map/ppermute | solution.py:120
  117.7 1.3 collective-permute-start.19
  119.0 1.1 collective-permute-start.22
  120.3 7.8 %collective-permute-done.33.refs_1_ = bf16[1024,256]{1,0:T(8,128)(2,1)S(1)} collective-permute-done((bf16[1024,256]{1,0:T(8,128)(2,1)S(1)}, bf16[1024,256]{1,0:T(8,128)(2,1)S(1)}, u32[]{:S(2)}, u32[]{:S(2)}) %collective-permute-start.33) | collective-permute-done | bytes 524320 | tf_op jit(solution)/shard_map/ppermute | solution.py:47
  128.1 2.6 %collective-permute-start.28 = (bf16[624,256]{1,0:T(8,128)(2,1)S(1)}, bf16[624,256]{1,0:T(8,128)(2,1)S(1)}, u32[]{:S(2)}, u32[]{:S(2)}) collective-permute-start(bf16[624,256]{1,0:T(8,128)(2,1)S(1)} %get-tuple-element.153), channel_id=1, source_target_pairs={{0,16},{4,20},{8,24},{12,28},{16,0},{20,4},{24,8},{28,12},{1,17},{... | collective-permute-start | bytes 958472 | tf_op jit(solution)/shard_map/ppermute | solution.py:47
  131.3 6.6 %input_grad.1.refs_4_ = bf16[8,32,512]{2,1,0:T(8,128)(2,1)} custom-call(bf16[8,32,512]{2,1,0:T(8,128)(2,1)S(1)} %get-tuple-element.128.refs_0_.refs_5_, bf16[3,32,512]{2,1,0:T(8,128)(2,1)S(1)} %collective-permute-done.14.refs_5_.refs_1_.refs_7_, bf16[3,32,512]{2,1,0:T(8,128)(2,1)S(1)} %collective-permute-done.15.refs_6_.refs_2_.refs_8_, ...), custom_call_target="tpu_custom_call" | custom-call | flops 2200001024 | bytes 1000 | tf_op jit(solution)/shard_map/input_grad/pallas_call | solution.py:33
  137.9 0.6 collective-permute-done.22.refs_3_
  138.5 0.9 copy-done
  139.6 1.6 collective-permute-start.23
  141.3 1.6 collective-permute-start.35
  143.1 1.1 collective-permute-start.29
  144.2 7.4 %collective-permute-done.23.refs_1_ = bf16[576,256]{1,0:T(8,128)(2,1)S(1)} collective-permute-done((bf16[576,256]{1,0:T(8,128)(2,1)S(1)}, bf16[576,256]{1,0:T(8,128)(2,1)S(1)}, u32[]{:S(2)}, u32[]{:S(2)}) %collective-permute-start.23) | collective-permute-done | bytes 294944 | tf_op jit(solution)/shard_map/ppermute | solution.py:47
  151.6 0.6 collective-permute-start.24
  152.3 0.8 collective-permute-start.36
  153.1 1.3 collective-permute-start.30
  154.5 6.8 %collective-permute-done.24 = bf16[320,256]{1,0:T(8,128)(2,1)S(1)} collective-permute-done((bf16[320,256]{1,0:T(8,128)(2,1)S(1)}, bf16[320,256]{1,0:T(8,128)(2,1)S(1)}, u32[]{:S(2)}, u32[]{:S(2)}) %collective-permute-start.24) | collective-permute-done | bytes 163872 | tf_op jit(solution)/shard_map/ppermute | solution.py:47
  161.3 0.8 collective-permute-start.25
  162.8 4.7 %collective-permute-done.25 = bf16[320,256]{1,0:T(8,128)(2,1)S(1)} collective-permute-done((bf16[320,256]{1,0:T(8,128)(2,1)S(1)}, bf16[320,256]{1,0:T(8,128)(2,1)S(1)}, u32[]{:S(2)}, u32[]{:S(2)}) %collective-permute-start.25) | collective-permute-done | bytes 163872 | tf_op jit(solution)/shard_map/ppermute | solution.py:47
  167.6 1.0 finish_project.1
  169.0 0.9 finish_expand.1
  169.9 1.0 finish_patch.1
  (73 shorter events, 4.7 us)
Async XLA Ops:
  0.6 19.0 %copy-start.6 = (bf16[1,4,16,1024]{3,2,1,0:T(8,128)(2,1)S(1)}, bf16[1,4,16,1024]{3,2,1,0:T(8,128)(2,1)}, u32[]{:S(2)}) copy-start(bf16[1,4,16,1024]{3,2,1,0:T(8,128)(2,1)} %param.22) | copy-start | bytes 393220
  0.7 19.0 %copy-start.7 = (bf16[1,4,16,1024]{3,2,1,0:T(8,128)(2,1)S(1)}, bf16[1,4,16,1024]{3,2,1,0:T(8,128)(2,1)}, u32[]{:S(2)}) copy-start(bf16[1,4,16,1024]{3,2,1,0:T(8,128)(2,1)} %param.23) | copy-start | bytes 393220
  0.7 18.9 %copy-start.9 = (f32[1024]{0:T(1024)S(1)}, f32[1024]{0:T(1024)}, u32[]{:S(2)}) copy-start(f32[1024]{0:T(1024)} %param.21) | copy-start | bytes 12292
  1.7 7.0 %collective-permute-start = (bf16[3,32,512]{2,1,0:T(8,128)(2,1)S(1)}, bf16[3,32,512]{2,1,0:T(8,128)(2,1)S(1)}, u32[]{:S(2)}, u32[]{:S(2)}) collective-permute-start(bf16[3,32,512]{2,1,0:T(8,128)(2,1)S(1)} %get-tuple-element.171), channel_id=1, source_target_pairs={{0,4},{4,8},{8,12},{12,16},{16,20},{20,24},{24,28},{1,5},{5,9},{9,... | collective-permute-start | bytes 294920 | tf_op jit(solution)/shard_map/ppermute | solution.py:120
  6.5 6.5 %collective-permute-start.1 = (bf16[3,32,512]{2,1,0:T(8,128)(2,1)S(1)}, bf16[3,32,512]{2,1,0:T(8,128)(2,1)S(1)}, u32[]{:S(2)}, u32[]{:S(2)}) collective-permute-start(bf16[3,32,512]{2,1,0:T(8,128)(2,1)S(1)} %get-tuple-element.170), channel_id=1, source_target_pairs={{4,0},{8,4},{12,8},{16,12},{20,16},{24,20},{28,24},{5,1},{9,5},{13... | collective-permute-start | bytes 294920 | tf_op jit(solution)/shard_map/ppermute | solution.py:120
  8.7 0.9 copy-start.1
  9.7 0.9 copy-start.8
  10.6 0.7 copy-start.10
  11.3 0.7 copy-start.11
  11.9 0.7 copy-start.12
  12.6 7.0 %copy-start.2 = (bf16[2048,1024]{1,0:T(8,128)(2,1)S(1)}, bf16[2048,1024]{1,0:T(8,128)(2,1)}, u32[]{:S(2)}) copy-start(bf16[2048,1024]{1,0:T(8,128)(2,1)} %refs_11_.1) | copy-start | bytes 12582916
  12.6 7.0 %copy-start.3 = (bf16[512,2048]{1,0:T(8,128)(2,1)S(1)}, bf16[512,2048]{1,0:T(8,128)(2,1)}, u32[]{:S(2)}) copy-start(bf16[512,2048]{1,0:T(8,128)(2,1)} %refs_9_.1) | copy-start | bytes 6291460
  12.6 7.0 %copy-start.4 = (bf16[2048,512]{1,0:T(8,128)(2,1)S(1)}, bf16[2048,512]{1,0:T(8,128)(2,1)}, u32[]{:S(2)}) copy-start(bf16[2048,512]{1,0:T(8,128)(2,1)} %refs_10_.1) | copy-start | bytes 6291460
  12.6 7.0 %copy-start.5 = (f32[7,7,1024]{2,1,0:T(8,128)S(1)}, f32[7,7,1024]{2,1,0:T(8,128)}, u32[]{:S(2)}) copy-start(f32[7,7,1024]{2,1,0:T(8,128)} %refs_12_.1) | copy-start | bytes 602116
  13.1 3.0 %collective-permute-start.2 = (bf16[14,8,512]{2,1,0:T(8,128)(2,1)S(1)}, bf16[14,8,512]{2,1,0:T(8,128)(2,1)S(1)}, u32[]{:S(2)}, u32[]{:S(2)}) collective-permute-start(bf16[14,8,512]{2,1,0:T(8,128)(2,1)S(1)} %get-tuple-element.90), channel_id=1, source_target_pairs={{0,1},{1,2},{2,3},{4,5},{5,6},{6,7},{8,9},{9,10},{10,11},{12,13},{... | collective-permute-start | bytes 344072 | tf_op jit(solution)/shard_map/ppermute | solution.py:120
  14.6 5.0 %collective-permute-start.3 = (bf16[14,8,512]{2,1,0:T(8,128)(2,1)S(1)}, bf16[14,8,512]{2,1,0:T(8,128)(2,1)S(1)}, u32[]{:S(2)}, u32[]{:S(2)}) collective-permute-start(bf16[14,8,512]{2,1,0:T(8,128)(2,1)S(1)} %get-tuple-element.91), channel_id=1, source_target_pairs={{1,0},{2,1},{3,2},{5,4},{6,5},{7,6},{9,8},{10,9},{11,10},{13,12},{... | collective-permute-start | bytes 344072 | tf_op jit(solution)/shard_map/ppermute | solution.py:120
  32.5 6.6 %collective-permute-start.4 = (bf16[3,16,1024]{2,1,0:T(8,128)(2,1)S(1)}, bf16[3,16,1024]{2,1,0:T(8,128)(2,1)S(1)}, u32[]{:S(2)}, u32[]{:S(2)}) collective-permute-start(bf16[3,16,1024]{2,1,0:T(8,128)(2,1)S(1)} %get-tuple-element.97), channel_id=1, source_target_pairs={{0,4},{4,8},{8,12},{12,16},{16,20},{20,24},{24,28},{1,5},{5,9},{9,... | collective-permute-start | bytes 294920 | tf_op jit(solution)/shard_map/ppermute | solution.py:120
  36.8 6.7 %collective-permute-start.5 = (bf16[3,16,1024]{2,1,0:T(8,128)(2,1)S(1)}, bf16[3,16,1024]{2,1,0:T(8,128)(2,1)S(1)}, u32[]{:S(2)}, u32[]{:S(2)}) collective-permute-start(bf16[3,16,1024]{2,1,0:T(8,128)(2,1)S(1)} %get-tuple-element.98), channel_id=1, source_target_pairs={{4,0},{8,4},{12,8},{16,12},{20,16},{24,20},{28,24},{5,1},{9,5},{13... | collective-permute-start | bytes 294920 | tf_op jit(solution)/shard_map/ppermute | solution.py:120
  43.6 5.5 %collective-permute-start.6 = (bf16[10,8,1024]{2,1,0:T(8,128)(2,1)S(1)}, bf16[10,8,1024]{2,1,0:T(8,128)(2,1)S(1)}, u32[]{:S(2)}, u32[]{:S(2)}) collective-permute-start(bf16[10,8,1024]{2,1,0:T(8,128)(2,1)S(1)} %get-tuple-element.99), channel_id=1, source_target_pairs={{0,1},{1,2},{2,3},{4,5},{5,6},{6,7},{8,9},{9,10},{10,11},{12,13},{... | collective-permute-start | bytes 491528 | tf_op jit(solution)/shard_map/ppermute | solution.py:120
  47.8 3.8 %collective-permute-start.7 = (bf16[10,8,1024]{2,1,0:T(8,128)(2,1)S(1)}, bf16[10,8,1024]{2,1,0:T(8,128)(2,1)S(1)}, u32[]{:S(2)}, u32[]{:S(2)}) collective-permute-start(bf16[10,8,1024]{2,1,0:T(8,128)(2,1)S(1)} %get-tuple-element.100), channel_id=1, source_target_pairs={{1,0},{2,1},{3,2},{5,4},{6,5},{7,6},{9,8},{10,9},{11,10},{13,12},{... | collective-permute-start | bytes 491528 | tf_op jit(solution)/shard_map/ppermute | solution.py:120
  54.9 7.0 %collective-permute-start.8 = (bf16[3,16,1024]{2,1,0:T(8,128)(2,1)S(1)}, bf16[3,16,1024]{2,1,0:T(8,128)(2,1)S(1)}, u32[]{:S(2)}, u32[]{:S(2)}) collective-permute-start(bf16[3,16,1024]{2,1,0:T(8,128)(2,1)S(1)} %get-tuple-element.105), channel_id=1, source_target_pairs={{0,4},{4,8},{8,12},{12,16},{16,20},{20,24},{24,28},{1,5},{5,9},{9,... | collective-permute-start | bytes 294920 | tf_op jit(solution)/shard_map/ppermute | solution.py:120
  59.7 6.5 %collective-permute-start.9 = (bf16[3,16,1024]{2,1,0:T(8,128)(2,1)S(1)}, bf16[3,16,1024]{2,1,0:T(8,128)(2,1)S(1)}, u32[]{:S(2)}, u32[]{:S(2)}) collective-permute-start(bf16[3,16,1024]{2,1,0:T(8,128)(2,1)S(1)} %get-tuple-element.106), channel_id=1, source_target_pairs={{4,0},{8,4},{12,8},{16,12},{20,16},{24,20},{28,24},{5,1},{9,5},{13... | collective-permute-start | bytes 294920 | tf_op jit(solution)/shard_map/ppermute | solution.py:120
  66.3 5.8 %collective-permute-start.10 = (bf16[10,8,1024]{2,1,0:T(8,128)(2,1)S(1)}, bf16[10,8,1024]{2,1,0:T(8,128)(2,1)S(1)}, u32[]{:S(2)}, u32[]{:S(2)}) collective-permute-start(bf16[10,8,1024]{2,1,0:T(8,128)(2,1)S(1)} %get-tuple-element.108), channel_id=1, source_target_pairs={{0,1},{1,2},{2,3},{4,5},{5,6},{6,7},{8,9},{9,10},{10,11},{12,13},{... | collective-permute-start | bytes 491528 | tf_op jit(solution)/shard_map/ppermute | solution.py:120
  70.8 3.9 %collective-permute-start.11 = (bf16[10,8,1024]{2,1,0:T(8,128)(2,1)S(1)}, bf16[10,8,1024]{2,1,0:T(8,128)(2,1)S(1)}, u32[]{:S(2)}, u32[]{:S(2)}) collective-permute-start(bf16[10,8,1024]{2,1,0:T(8,128)(2,1)S(1)} %get-tuple-element.109), channel_id=1, source_target_pairs={{1,0},{2,1},{3,2},{5,4},{6,5},{7,6},{9,8},{10,9},{11,10},{13,12},{... | collective-permute-start | bytes 491528 | tf_op jit(solution)/shard_map/ppermute | solution.py:120
  77.8 7.0 %collective-permute-start.12 = (bf16[256,3072]{1,0:T(8,128)(2,1)S(1)}, bf16[256,3072]{1,0:T(8,128)(2,1)S(1)}, u32[]{:S(2)}, u32[]{:S(2)}) collective-permute-start(bf16[256,3072]{1,0:T(8,128)(2,1)S(1)} %get-tuple-element.124.refs_0_), channel_id=1, source_target_pairs={{0,1},{1,0},{2,3},{3,2},{4,5},{5,4},{6,7},{7,6},{8,9},{9,8},{10,11... | collective-permute-start | bytes 4718600 | tf_op jit(solution)/shard_map/ppermute | solution.py:47
  81.7 3.1 %collective-permute-start.13 = (bf16[2,64,256]{2,1,0:T(8,128)(2,1)S(1)}, bf16[2,64,256]{2,1,0:T(8,128)(2,1)S(1)}, u32[]{:S(2)}, u32[]{:S(2)}) collective-permute-start(bf16[2,64,256]{2,1,0:T(8,128)(2,1)S(1)} %get-tuple-element.126), channel_id=1, source_target_pairs={{0,1},{1,0},{2,3},{3,2},{4,5},{5,4},{6,7},{7,6},{8,9},{9,8},{10,11... | collective-permute-start | bytes 196616 | tf_op jit(solution)/shard_map/ppermute | solution.py:47
  87.4 25.5 %collective-permute-start.32 = (bf16[2048,256]{1,0:T(8,128)(2,1)S(1)}, bf16[2048,256]{1,0:T(8,128)(2,1)S(1)}, u32[]{:S(2)}, u32[]{:S(2)}) collective-permute-start(bf16[2048,256]{1,0:T(8,128)(2,1)S(1)} %get-tuple-element.127.refs_7_), channel_id=1, source_target_pairs={{0,2},{1,3},{2,0},{3,1},{4,6},{5,7},{6,4},{7,5},{8,10},{9,11},{10,... | collective-permute-start | bytes 3145736 | tf_op jit(solution)/shard_map/ppermute | solution.py:47
  93.2 11.8 %collective-permute-start.16 = (bf16[256,1024]{1,0:T(8,128)(2,1)S(1)}, bf16[256,1024]{1,0:T(8,128)(2,1)S(1)}, u32[]{:S(2)}, u32[]{:S(2)}) collective-permute-start(bf16[256,1024]{1,0:T(8,128)(2,1)S(1)} %get-tuple-element.132.refs_4_), channel_id=1, source_target_pairs={{0,1},{1,0},{2,3},{3,2},{4,5},{5,4},{6,7},{7,6},{8,9},{9,8},{10,11... | collective-permute-start | bytes 1572872 | tf_op jit(solution)/shard_map/ppermute | solution.py:47
  93.6 4.5 %collective-permute-start.17 = (bf16[368,256]{1,0:T(8,128)(2,1)S(1)}, bf16[368,256]{1,0:T(8,128)(2,1)S(1)}, u32[]{:S(2)}, u32[]{:S(2)}) collective-permute-start(bf16[368,256]{1,0:T(8,128)(2,1)S(1)} %get-tuple-element.134), channel_id=1, source_target_pairs={{0,1},{1,0},{2,3},{3,2},{4,5},{5,4},{6,7},{7,6},{8,9},{9,8},{10,11... | collective-permute-start | bytes 565256 | tf_op jit(solution)/shard_map/ppermute | solution.py:47
  93.8 11.3 %collective-permute-start.14 = (bf16[3,32,512]{2,1,0:T(8,128)(2,1)S(1)}, bf16[3,32,512]{2,1,0:T(8,128)(2,1)S(1)}, u32[]{:S(2)}, u32[]{:S(2)}) collective-permute-start(bf16[3,32,512]{2,1,0:T(8,128)(2,1)S(1)} %get-tuple-element.129), channel_id=1, source_target_pairs={{0,4},{4,8},{8,12},{12,16},{16,20},{20,24},{24,28},{1,5},{5,9},{9,... | collective-permute-start | bytes 294920 | tf_op jit(solution)/shard_map/ppermute | solution.py:120
  96.8 8.3 %collective-permute-start.15 = (bf16[3,32,512]{2,1,0:T(8,128)(2,1)S(1)}, bf16[3,32,512]{2,1,0:T(8,128)(2,1)S(1)}, u32[]{:S(2)}, u32[]{:S(2)}) collective-permute-start(bf16[3,32,512]{2,1,0:T(8,128)(2,1)S(1)} %get-tuple-element.130), channel_id=1, source_target_pairs={{4,0},{8,4},{12,8},{16,12},{20,16},{24,20},{28,24},{5,1},{9,5},{13... | collective-permute-start | bytes 294920 | tf_op jit(solution)/shard_map/ppermute | solution.py:120
  100.9 18.1 %collective-permute-start.27 = (bf16[1136,256]{1,0:T(8,128)(2,1)S(1)}, bf16[1136,256]{1,0:T(8,128)(2,1)S(1)}, u32[]{:S(2)}, u32[]{:S(2)}) collective-permute-start(bf16[1136,256]{1,0:T(8,128)(2,1)S(1)} %get-tuple-element.135.refs_4_), channel_id=1, source_target_pairs={{0,8},{4,12},{8,0},{12,4},{16,24},{20,28},{24,16},{28,20},{1,9},{5... | collective-permute-start | bytes 1744904 | tf_op jit(solution)/shard_map/ppermute | solution.py:47
  113.1 14.9 %collective-permute-start.33 = (bf16[1024,256]{1,0:T(8,128)(2,1)S(1)}, bf16[1024,256]{1,0:T(8,128)(2,1)S(1)}, u32[]{:S(2)}, u32[]{:S(2)}) collective-permute-start(bf16[1024,256]{1,0:T(8,128)(2,1)S(1)} %get-tuple-element.161), channel_id=1, source_target_pairs={{0,4},{4,0},{8,12},{12,8},{16,20},{20,16},{24,28},{28,24},{1,5},{5... | collective-permute-start | bytes 1572872 | tf_op jit(solution)/shard_map/ppermute | solution.py:47
  114.3 24.3 %collective-permute-start.20 = (bf16[1024,256]{1,0:T(8,128)(2,1)S(1)}, bf16[1024,256]{1,0:T(8,128)(2,1)S(1)}, u32[]{:S(2)}, u32[]{:S(2)}) collective-permute-start(bf16[1024,256]{1,0:T(8,128)(2,1)S(1)} %get-tuple-element.136.refs_3_.refs_9_), channel_id=1, source_target_pairs={{0,4},{4,0},{8,12},{12,8},{16,20},{20,16},{24,28},{28,24},{1,5},{5... | collective-permute-start | bytes 1572872 | tf_op jit(solution)/shard_map/ppermute | solution.py:47
  115.2 2.5 %collective-permute-start.21 = (bf16[64,256]{1,0:T(8,128)(2,1)S(1)}, bf16[64,256]{1,0:T(8,128)(2,1)S(1)}, u32[]{:S(2)}, u32[]{:S(2)}) collective-permute-start(bf16[64,256]{1,0:T(8,128)(2,1)S(1)} %get-tuple-element.143), channel_id=1, source_target_pairs={{0,1},{1,0},{2,3},{3,2},{4,5},{5,4},{6,7},{7,6},{8,9},{9,8},{10,11... | collective-permute-start | bytes 98312 | tf_op jit(solution)/shard_map/ppermute | solution.py:47
  115.3 15.5 %collective-permute-start.18 = (bf16[14,8,512]{2,1,0:T(8,128)(2,1)S(1)}, bf16[14,8,512]{2,1,0:T(8,128)(2,1)S(1)}, u32[]{:S(2)}, u32[]{:S(2)}) collective-permute-start(bf16[14,8,512]{2,1,0:T(8,128)(2,1)S(1)} %get-tuple-element.137), channel_id=1, source_target_pairs={{0,1},{1,2},{2,3},{4,5},{5,6},{6,7},{8,9},{9,10},{10,11},{12,13},{... | collective-permute-start | bytes 344072 | tf_op jit(solution)/shard_map/ppermute | solution.py:120
  117.7 13.6 %collective-permute-start.19 = (bf16[14,8,512]{2,1,0:T(8,128)(2,1)S(1)}, bf16[14,8,512]{2,1,0:T(8,128)(2,1)S(1)}, u32[]{:S(2)}, u32[]{:S(2)}) collective-permute-start(bf16[14,8,512]{2,1,0:T(8,128)(2,1)S(1)} %get-tuple-element.138), channel_id=1, source_target_pairs={{1,0},{2,1},{3,2},{5,4},{6,5},{7,6},{9,8},{10,9},{11,10},{13,12},{... | collective-permute-start | bytes 344072 | tf_op jit(solution)/shard_map/ppermute | solution.py:120
  119.0 19.5 %collective-permute-start.22 = (bf16[64,256]{1,0:T(8,128)(2,1)S(1)}, bf16[64,256]{1,0:T(8,128)(2,1)S(1)}, u32[]{:S(2)}, u32[]{:S(2)}) collective-permute-start(bf16[64,256]{1,0:T(8,128)(2,1)S(1)} %add.23.refs_2_), channel_id=1, source_target_pairs={{0,4},{4,0},{8,12},{12,8},{16,20},{20,16},{24,28},{28,24},{1,5},{5... | collective-permute-start | bytes 98312 | tf_op jit(solution)/shard_map/ppermute | solution.py:47
  128.1 14.9 %collective-permute-start.28 = (bf16[624,256]{1,0:T(8,128)(2,1)S(1)}, bf16[624,256]{1,0:T(8,128)(2,1)S(1)}, u32[]{:S(2)}, u32[]{:S(2)}) collective-permute-start(bf16[624,256]{1,0:T(8,128)(2,1)S(1)} %get-tuple-element.153), channel_id=1, source_target_pairs={{0,16},{4,20},{8,24},{12,28},{16,0},{20,4},{24,8},{28,12},{1,17},{... | collective-permute-start | bytes 958472 | tf_op jit(solution)/shard_map/ppermute | solution.py:47
  130.8 10.5 %collective-permute-start.34 = (bf16[512,256]{1,0:T(8,128)(2,1)S(1)}, bf16[512,256]{1,0:T(8,128)(2,1)S(1)}, u32[]{:S(2)}, u32[]{:S(2)}) collective-permute-start(bf16[512,256]{1,0:T(8,128)(2,1)S(1)} %get-tuple-element.163), channel_id=1, source_target_pairs={{0,8},{4,12},{8,0},{12,4},{16,24},{20,28},{24,16},{28,20},{1,9},{5... | collective-permute-start | bytes 786440 | tf_op jit(solution)/shard_map/ppermute | solution.py:47
  138.5 1.0 copy-start
  139.6 11.9 %collective-permute-start.23 = (bf16[576,256]{1,0:T(8,128)(2,1)S(1)}, bf16[576,256]{1,0:T(8,128)(2,1)S(1)}, u32[]{:S(2)}, u32[]{:S(2)}) collective-permute-start(bf16[576,256]{1,0:T(8,128)(2,1)S(1)} %get-tuple-element.145), channel_id=1, source_target_pairs={{0,8},{4,12},{8,0},{12,4},{16,24},{20,28},{24,16},{28,20},{1,9},{5... | collective-permute-start | bytes 884744 | tf_op jit(solution)/shard_map/ppermute | solution.py:47
  141.3 10.9 %collective-permute-start.35 = (bf16[256,256]{1,0:T(8,128)(2,1)S(1)}, bf16[256,256]{1,0:T(8,128)(2,1)S(1)}, u32[]{:S(2)}, u32[]{:S(2)}) collective-permute-start(bf16[256,256]{1,0:T(8,128)(2,1)S(1)} %get-tuple-element.165), channel_id=1, source_target_pairs={{0,16},{4,20},{8,24},{12,28},{16,0},{20,4},{24,8},{28,12},{1,17},{... | collective-permute-start | bytes 393224 | tf_op jit(solution)/shard_map/ppermute | solution.py:47
  143.1 10.0 %collective-permute-start.29 = (bf16[368,256]{1,0:T(8,128)(2,1)S(1)}, bf16[368,256]{1,0:T(8,128)(2,1)S(1)}, u32[]{:S(2)}, u32[]{:S(2)}) collective-permute-start(bf16[368,256]{1,0:T(8,128)(2,1)S(1)} %get-tuple-element.155), channel_id=1, source_target_pairs={{0,4},{4,0},{8,12},{12,8},{16,20},{20,16},{24,28},{28,24},{1,5},{5... | collective-permute-start | bytes 565256 | tf_op jit(solution)/shard_map/ppermute | solution.py:47
  151.6 9.6 %collective-permute-start.24 = (bf16[320,256]{1,0:T(8,128)(2,1)S(1)}, bf16[320,256]{1,0:T(8,128)(2,1)S(1)}, u32[]{:S(2)}, u32[]{:S(2)}) collective-permute-start(bf16[320,256]{1,0:T(8,128)(2,1)S(1)} %get-tuple-element.147), channel_id=1, source_target_pairs={{0,16},{4,20},{8,24},{12,28},{16,0},{20,4},{24,8},{28,12},{1,17},{... | collective-permute-start | bytes 491528 | tf_op jit(solution)/shard_map/ppermute | solution.py:47
  152.3 9.8 %collective-permute-start.36 = (bf16[1,256,256]{2,1,0:T(8,128)(2,1)S(1)}, bf16[1,256,256]{2,1,0:T(8,128)(2,1)S(1)}, u32[]{:S(2)}, u32[]{:S(2)}) collective-permute-start(bf16[1,256,256]{2,1,0:T(8,128)(2,1)S(1)} %add_bitcast_fusion), channel_id=1, source_target_pairs={{0,2},{1,3},{2,0},{3,1},{4,6},{5,7},{6,4},{7,5},{8,10},{9,11},{10,... | collective-permute-start | bytes 393224 | tf_op jit(solution)/shard_map/ppermute | solution.py:47
  153.1 9.1 %collective-permute-start.30 = (bf16[368,256]{1,0:T(8,128)(2,1)S(1)}, bf16[368,256]{1,0:T(8,128)(2,1)S(1)}, u32[]{:S(2)}, u32[]{:S(2)}) collective-permute-start(bf16[368,256]{1,0:T(8,128)(2,1)S(1)} %add.26), channel_id=1, source_target_pairs={{0,2},{1,3},{2,0},{3,1},{4,6},{5,7},{6,4},{7,5},{8,10},{9,11},{10,... | collective-permute-start | bytes 565256 | tf_op jit(solution)/shard_map/ppermute | solution.py:47
  161.3 6.2 %collective-permute-start.25 = (bf16[320,256]{1,0:T(8,128)(2,1)S(1)}, bf16[320,256]{1,0:T(8,128)(2,1)S(1)}, u32[]{:S(2)}, u32[]{:S(2)}) collective-permute-start(bf16[320,256]{1,0:T(8,128)(2,1)S(1)} %add.24), channel_id=1, source_target_pairs={{0,2},{1,3},{2,0},{3,1},{4,6},{5,7},{6,4},{7,5},{8,10},{9,11},{10,... | collective-permute-start | bytes 491528 | tf_op jit(solution)/shard_map/ppermute | solution.py:47
  162.1 7.8 %collective-permute-start.37 = (bf16[2,256,256]{2,1,0:T(8,128)(2,1)S(1)}, bf16[2,256,256]{2,1,0:T(8,128)(2,1)S(1)}, u32[]{:S(2)}, u32[]{:S(2)}) collective-permute-start(bf16[2,256,256]{2,1,0:T(8,128)(2,1)S(1)} %maximum_bitcast_fusion.refs_0_), channel_id=1, source_target_pairs={{0,1},{1,0},{2,3},{3,2},{4,5},{5,4},{6,7},{7,6},{8,9},{9,8},{10,11... | collective-permute-start | bytes 786440 | tf_op jit(solution)/shard_map/ppermute | solution.py:47
  162.3 5.3 %collective-permute-start.31 = (bf16[368,256]{1,0:T(8,128)(2,1)S(1)}, bf16[368,256]{1,0:T(8,128)(2,1)S(1)}, u32[]{:S(2)}, u32[]{:S(2)}) collective-permute-start(bf16[368,256]{1,0:T(8,128)(2,1)S(1)} %add.27.refs_0_), channel_id=1, source_target_pairs={{0,1},{1,0},{2,3},{3,2},{4,5},{5,4},{6,7},{7,6},{8,9},{9,8},{10,11... | collective-permute-start | bytes 565256 | tf_op jit(solution)/shard_map/ppermute | solution.py:47
  167.6 1.5 collective-permute-start.26

commit v10 on v8

--- a/solution.py
+++ b/solution.py
@@ -77,7 +77,7 @@
             (out, out),
             after=after,
             limit=8,
-            us=0.2,
+            us=0.1,
         )
         return (self.send,)
 
@@ -792,8 +792,18 @@
         us=0.8,
     )
     branch_other = swap(branch_send, "col", 1)
+    patch_half = shape_of(block_count // 2 * 4 * channels, block, dtype=BF)
+    patch_keep, patch_send = run(
+        functools.partial(patch_product_kernel, scale_four),
+        "patch_product",
+        (early, early_other, flat_keep, flat_other),
+        (patch_half, patch_half),
+        limit=16,
+        us=0.9,
+    )
     deep, shallow = hidden_width // row_count, channels // row_count
     groups = hidden_width // channels
+    project_half = shape_of(row_count // 2 * deep + 112, half, dtype=BF)
     upward_half = shape_of(pixels, hidden_width // 2, dtype=BF)
     upward_keep, upward_send, grad_mixed, first, last, gain_part = run(
         back_kernel,
@@ -812,17 +822,17 @@
             pltpu.VMEM((pixels, hidden_width), BF),
             pltpu.VMEM((pixels, channels), F32),
         ),
+        after=(patch_send,),
         limit=16,
         us=1.2,
     )
     rows_back = neighbours(first, last, "row")
     upward_other = swap(upward_send, "col", 1)
-    patch_half = shape_of(block_count // 2 * 4 * channels, block, dtype=BF)
-    patch_keep, patch_send = run(
-        functools.partial(patch_product_kernel, scale_four),
-        "patch_product",
-        (early, early_other, flat_keep, flat_other),
-        (patch_half, patch_half),
+    project_keep, project_send = run(
+        functools.partial(project_product_kernel, scale_three, row_count),
+        "project_product",
+        (early, early_other, branch_keep, branch_other),
+        (project_half, project_half),
         after=(upward_send,),
         limit=16,
         us=0.9,
@@ -833,21 +843,11 @@
         "expand_product",
         (early, early_other, upward_keep, upward_other),
         (expand_half, expand_half),
-        after=(patch_send, *rows_back),
+        after=(project_send, *rows_back),
         limit=16,
         us=0.6,
     )
-    project_half = shape_of(row_count // 2 * deep + 112, half, dtype=BF)
-    project_keep, project_send = run(
-        functools.partial(project_product_kernel, scale_three, row_count),
-        "project_product",
-        (early, early_other, branch_keep, branch_other),
-        (project_half, project_half),
-        after=(expand_send,),
-        limit=16,
-        us=0.9,
-    )
-    framed_back = halo(grad_mixed, rows_back, "strips_back", after=(project_send,))
+    framed_back = halo(grad_mixed, rows_back, "strips_back", after=(expand_send,))
     small_half = shape_of(64, half, dtype=BF)
     small_keep, small_send = run(
         functools.partial(weight_pack_kernel, scale_three),
@@ -859,7 +859,7 @@
             pltpu.VMEM((height, breadth, channels), F32),
             pltpu.VMEM((64, channels), F32),
         ),
-        after=(project_send,),
+        after=(*framed_back[1:3], expand_send),
         limit=12,
         us=1.8,
     )
@@ -867,27 +867,25 @@
     outer = len(row_bits)
     low_first = [("row", bit, 0) for bit in row_bits]
     patch_order = [("col", bit, outer) for bit in col_bits[1:]] + low_first
-    project_order = [("row", row_bits[1], 1), low_first[0], *low_first[2:]]
+    project_order = [("row", bit, 1) for bit in row_bits[1:]] + low_first[:1]
     patch_chain = Chain(patch_keep, patch_send, patch_order, block_count * row_count, 4 * channels // row_count)
     project_chain = Chain(project_keep, project_send, project_order, row_count, deep)
     expand_chain = Chain(expand_keep, expand_send, low_first, row_count, groups * shallow)
-    small = small_keep + swap(small_send, "col", 1)
-    sent = expand_chain.advance(extra=(small, swap(small, "row", 1)))
-    sent = project_chain.advance(sent)
-    sent = patch_chain.advance((*sent, *framed_back[3:]))
+    sent = project_chain.advance((small_keep,))
+    sent = patch_chain.advance((small_keep, *sent))
     (input_grad,) = run(
         input_kernel,
         "input_grad",
         (*framed_back, taps_three, grad_summed),
         (shape_of(height, breadth, channels, dtype=BF),),
         scratch=(frame_scratch(center), pltpu.VMEM((height, breadth, channels), F32)),
-        after=sent,
+        after=(small_keep, *sent),
         limit=12,
-        us=2,
-    )
-    sent = expand_chain.advance((input_grad,))
-    sent = project_chain.advance(sent)
-    patch_chain.advance(sent)
+        us=0.4,
+    )
+    small = small_keep + swap(small_send, "col", 1)
+    expand_chain.advance((input_grad,), (small, swap(small, "row", 1)))
+    patch_chain.advance((input_grad,))
     patch_sum = patch_chain.finish()
     patch_sum = gather(patch_sum, "col", col_bits[1:])
     (patch_grad,) = run(

time: 195 us -> 185 us (0.949)
  waiting for transfers between devices: 75.9 us -> 56.1 us
  starting transfers between devices: 59.6 us -> 68.7 us
    ppermute x22, waiting for transfers between devices: 51.3 us -> 29.7 us  [swap(): lax.ppermute(values, axis, [(i, i ^ bit) for i in range(lax.axis_size(axi...]
    ppermute x22, starting transfers between devices: 19.9 us -> 29.6 us  [swap(): lax.ppermute(values, axis, [(i, i ^ bit) for i in range(lax.axis_size(axi...]
    ppermute x8, waiting for transfers between devices: 20.7 us -> 23 us  [neighbours(): lax.ppermute(first, axis, backward)]
    unnamed x26 -> x28, local copies, waits for them, and re-layouts: 4.87 us -> 5.82 us
  transfers between devices with their start and end apart: 38 -> 38, of which waited for: 22 -> 22; matrix products, arithmetic and copies ran while one was open for 0% -> 0% of each run, Pallas kernels for 16% -> 15%
where the time goes in v10:
time: 185 us; the launch traced here: 184 us
  starting transfers between devices  68.7 us (37%)
  waiting for transfers between devices  56.1 us (30%)
  Pallas kernels  50.9 us (28%)
  local copies, waits for them, and re-layouts  6.82 us (4%)
    pallas_call x26, Pallas kernels, run(): pl.pallas_call(inner, name=name, out_shape=outs, in_specs=[spec(i) for i...  50.9 us
    ppermute x22, waiting for transfers between devices, swap(): lax.ppermute(values, axis, [(i, i ^ bit) for i in range(lax.axis_size(axi...  29.7 us
    ppermute x22, starting transfers between devices, swap(): lax.ppermute(values, axis, [(i, i ^ bit) for i in range(lax.axis_size(axi...  29.6 us
    ppermute x8, starting transfers between devices, neighbours(): lax.ppermute(last, axis, forward)  28.4 us
    ppermute x8, waiting for transfers between devices, neighbours(): lax.ppermute(first, axis, backward)  23 us
    ppermute x8, starting transfers between devices, neighbours(): lax.ppermute(first, axis, backward)  10.6 us
    unnamed x28, local copies, waits for them, and re-layouts  5.82 us
  transfers between devices with their start and end apart: 38, of which 22 were waited for; matrix products, arithmetic and copies ran while one was open for 0% of the time, Pallas kernels for 15%

profile of v10, /device:TPU:0, one launch (start us, length us, event | category | flops | bytes accessed | tf_op | source)
XLA Modules:
  0.0 183.9 jit_solution(2713755316397627843)
XLA Ops:
  0.7 1.0 slice_bitcast_fusion
  1.7 4.8 %collective-permute-start = (bf16[3,32,512]{2,1,0:T(8,128)(2,1)S(1)}, bf16[3,32,512]{2,1,0:T(8,128)(2,1)S(1)}, u32[]{:S(2)}, u32[]{:S(2)}) collective-permute-start(bf16[3,32,512]{2,1,0:T(8,128)(2,1)S(1)} %get-tuple-element.171), channel_id=1, source_target_pairs={{0,4},{4,8},{8,12},{12,16},{16,20},{20,24},{24,28},{1,5},{5,9},{9,... | collective-permute-start | bytes 294920 | tf_op jit(solution)/shard_map/ppermute | solution.py:131
  6.5 1.3 collective-permute-start.1
  7.8 0.9 collective-permute-done.refs_5_.refs_1_
  8.7 0.9 copy-done.2
  9.7 0.9 copy-done.9
  13.1 1.6 collective-permute-start.2
  14.6 1.4 collective-permute-start.3
  16.1 3.5 %collective-permute-done.3.refs_4_ = bf16[14,8,512]{2,1,0:T(8,128)(2,1)S(1)} collective-permute-done((bf16[14,8,512]{2,1,0:T(8,128)(2,1)S(1)}, bf16[14,8,512]{2,1,0:T(8,128)(2,1)S(1)}, u32[]{:S(2)}, u32[]{:S(2)}) %collective-permute-start.3) | collective-permute-done | bytes 114720 | tf_op jit(solution)/shard_map/ppermute | solution.py:131
  19.6 12.8 %front.1 = (bf16[256,3072]{1,0:T(8,128)(2,1)S(1)}, f32[256,512]{1,0:T(8,128)S(1)}, f32[256,1]{1,0:T(8,128)S(1)}, bf16[256,2048]{1,0:T(8,128)(2,1)S(1)}, f32[256,...) custom-call(bf16[8,32,512]{2,1,0:T(8,128)(2,1)S(1)} %get-tuple-eleme, ...), custom_call_target="tpu_custom_call" | custom-call | flops 13200001024 | bytes 1000 | tf_op jit(solution)/shard_map/front/pallas_call | solution.py:33
  32.5 4.4 %collective-permute-start.4 = (bf16[3,16,1024]{2,1,0:T(8,128)(2,1)S(1)}, bf16[3,16,1024]{2,1,0:T(8,128)(2,1)S(1)}, u32[]{:S(2)}, u32[]{:S(2)}) collective-permute-start(bf16[3,16,1024]{2,1,0:T(8,128)(2,1)S(1)} %get-tuple-element.97), channel_id=1, source_target_pairs={{0,4},{4,8},{8,12},{12,16},{16,20},{20,24},{24,28},{1,5},{5,9},{9,... | collective-permute-start | bytes 294920 | tf_op jit(solution)/shard_map/ppermute | solution.py:131
  36.8 1.3 collective-permute-start.5
  38.1 0.9 collective-permute-done.4.refs_1_
  39.0 4.5 %collective-permute-done.5.refs_2_ = bf16[3,16,1024]{2,1,0:T(8,128)(2,1)S(1)} collective-permute-done((bf16[3,16,1024]{2,1,0:T(8,128)(2,1)S(1)}, bf16[3,16,1024]{2,1,0:T(8,128)(2,1)S(1)}, u32[]{:S(2)}, u32[]{:S(2)}) %collective-permute-start.5) | collective-permute-done | bytes 98336 | tf_op jit(solution)/shard_map/ppermute | solution.py:131
  43.6 4.2 %collective-permute-start.6 = (bf16[10,8,1024]{2,1,0:T(8,128)(2,1)S(1)}, bf16[10,8,1024]{2,1,0:T(8,128)(2,1)S(1)}, u32[]{:S(2)}, u32[]{:S(2)}) collective-permute-start(bf16[10,8,1024]{2,1,0:T(8,128)(2,1)S(1)} %get-tuple-element.99), channel_id=1, source_target_pairs={{0,1},{1,2},{2,3},{4,5},{5,6},{6,7},{8,9},{9,10},{10,11},{12,13},{... | collective-permute-start | bytes 491528 | tf_op jit(solution)/shard_map/ppermute | solution.py:131
  47.8 1.3 collective-permute-start.7
  49.1 2.5 %collective-permute-done.7.refs_4_ = bf16[10,8,1024]{2,1,0:T(8,128)(2,1)S(1)} collective-permute-done((bf16[10,8,1024]{2,1,0:T(8,128)(2,1)S(1)}, bf16[10,8,1024]{2,1,0:T(8,128)(2,1)S(1)}, u32[]{:S(2)}, u32[]{:S(2)}) %collective-permute-start.7) | collective-permute-done | bytes 163872 | tf_op jit(solution)/shard_map/ppermute | solution.py:131
  51.6 3.3 %mixer.1 = (f32[4,16,1024]{2,1,0:T(8,128)S(1)}, bf16[4,16,1024]{2,1,0:T(8,128)(2,1)S(1)}, bf16[3,16,1024]{2,1,0:T(8,128)(2,1)S(1)}, bf16[3,16,1024]{2,1,0:T(8,128)(2,1)S(1)}, f32[1,1024]{1,0:T(1,128)S(1)}) custom-call(bf16[4,16,1024]{2,1,0:T(8,128)(2,1)S(1)} %get-tuple-element.96.refs_0_, bf16[3,16,1024]{2,1,0:T(8,128)(2,1)S(1)} %collective-permute-done.4.refs_1_, ...), custom_call_target="tpu_custom_call" | custom-call | flops 3300001024 | bytes 1000 | tf_op jit(solution)/shard_map/mixer/pallas_call | solution.py:33
  54.9 4.8 %collective-permute-start.8 = (bf16[3,16,1024]{2,1,0:T(8,128)(2,1)S(1)}, bf16[3,16,1024]{2,1,0:T(8,128)(2,1)S(1)}, u32[]{:S(2)}, u32[]{:S(2)}) collective-permute-start(bf16[3,16,1024]{2,1,0:T(8,128)(2,1)S(1)} %get-tuple-element.105), channel_id=1, source_target_pairs={{0,4},{4,8},{8,12},{12,16},{16,20},{20,24},{24,28},{1,5},{5,9},{9,... | collective-permute-start | bytes 294920 | tf_op jit(solution)/shard_map/ppermute | solution.py:131
  59.7 1.3 collective-permute-start.9
  61.0 0.9 collective-permute-done.8.refs_6_.refs_1_
  61.9 2.9 %mixer_weights.1.refs_3_.refs_7_ = f32[49,1024]{1,0:T(8,128)S(1)} custom-call(bf16[4,16,1024]{2,1,0:T(8,128)(2,1)S(1)} %get-tuple-element.96.refs_0_, bf16[3,16,1024]{2,1,0:T(8,128)(2,1)S(1)} %collective-permute-done.4.refs_1_, bf16[3,16,1024]{2,1,0:T(8,128)(2,1)S(1)} %collective-permute-done.5.refs_2_, ...), custom_call_target="tpu_custom_call" | custom-call | flops 3300001024 | bytes 1000 | tf_op jit(solution)/shard_map/mixer_weights/pallas_call | solution.py:33
  64.8 1.4 collective-permute-done.9.refs_2_
  66.3 4.5 %collective-permute-start.10 = (bf16[10,8,1024]{2,1,0:T(8,128)(2,1)S(1)}, bf16[10,8,1024]{2,1,0:T(8,128)(2,1)S(1)}, u32[]{:S(2)}, u32[]{:S(2)}) collective-permute-start(bf16[10,8,1024]{2,1,0:T(8,128)(2,1)S(1)} %get-tuple-element.108), channel_id=1, source_target_pairs={{0,1},{1,2},{2,3},{4,5},{5,6},{6,7},{8,9},{9,10},{10,11},{12,13},{... | collective-permute-start | bytes 491528 | tf_op jit(solution)/shard_map/ppermute | solution.py:131
  70.8 1.3 collective-permute-start.11
  72.1 2.6 %collective-permute-done.11.refs_4_ = bf16[10,8,1024]{2,1,0:T(8,128)(2,1)S(1)} collective-permute-done((bf16[10,8,1024]{2,1,0:T(8,128)(2,1)S(1)}, bf16[10,8,1024]{2,1,0:T(8,128)(2,1)S(1)}, u32[]{:S(2)}, u32[]{:S(2)}) %collective-permute-start.11) | collective-permute-done | bytes 163872 | tf_op jit(solution)/shard_map/ppermute | solution.py:131
  74.7 3.1 %section_grad.1 = (bf16[64,1024]{1,0:T(8,128)(2,1)S(1)}, bf16[2,64,256]{2,1,0:T(8,128)(2,1)S(1)}, bf16[2,64,256]{2,1,0:T(8,128)(2,1)S(1)}, bf16[256,3072]{1,0:T(8,128)(2,1)S(1)}) custom-call(bf16[4,16,1024]{2,1,0:T(8,128)(2,1)S(1)} %get-tuple-element.104.refs_0_, ...), custom_call_target="tpu_custom_call", output_to_operand_aliasing={{3}: (7, {})} | custom-call | flops 3300001024 | bytes 1000 | tf_op jit(solution)/shard_map/section_grad/pallas_call | solution.py:33
  77.8 3.9 %collective-permute-start.12 = (bf16[256,3072]{1,0:T(8,128)(2,1)S(1)}, bf16[256,3072]{1,0:T(8,128)(2,1)S(1)}, u32[]{:S(2)}, u32[]{:S(2)}) collective-permute-start(bf16[256,3072]{1,0:T(8,128)(2,1)S(1)} %get-tuple-element.124.refs_0_), channel_id=1, source_target_pairs={{0,1},{1,0},{2,3},{3,2},{4,5},{5,4},{6,7},{7,6},{8,9},{9,8},{10,11... | collective-permute-start | bytes 4718600 | tf_op jit(solution)/shard_map/ppermute | solution.py:47
  81.8 3.1 %collective-permute-done.13.refs_3_ = bf16[2,64,256]{2,1,0:T(8,128)(2,1)S(1)} collective-permute-done((bf16[2,64,256]{2,1,0:T(8,128)(2,1)S(1)}, bf16[2,64,256]{2,1,0:T(8,128)(2,1)S(1)}, u32[]{:S(2)}, u32[]{:S(2)}) %collective-permute-start.13) | collective-permute-done | bytes 65568 | tf_op jit(solution)/shard_map/ppermute | solution.py:47
  84.8 2.6 %patch_product.1 = (bf16[2048,256]{1,0:T(8,128)(2,1)S(1)}, bf16[2048,256]{1,0:T(8,128)(2,1)S(1)}) custom-call(bf16[256,3072]{1,0:T(8,128)(2,1)S(1)} %get-tuple-element.124.refs_0_, bf16[256,3072]{1,0:T(8,128)(2,1)S(1)} %collective-permute-done.12.refs_1_, bf16[2,64,256]{2,1,0:T(8,128)(2,1)S(1)} %get-tuple-element.125.refs_2_, ...), custom_call_target="tpu_custom_call" | custom-call | flops 990001024 | bytes 1000 | tf_op jit(solution)/shard_map/patch_product/pallas_call | solution.py:33
  87.6 2.5 %merge_back.1 = (f32[256,512]{1,0:T(8,128)S(1)}, bf16[256,512]{1,0:T(8,128)(2,1)S(1)}, bf16[368,256]{1,0:T(8,128)(2,1)S(1)}, bf16[368,256]{1,0:T(8,128)(2,1)S(1)}) custom-call(bf16[64,1024]{1,0:T(8,128)(2,1)S(1)} %get-tuple-element.112.refs_0_, bf16[2048,1024]{1,0:T(8,128)(2,1)S(1)} %get-tuple-element.113.refs_1_, ...), custom_call_target="tpu_custom_call" | custom-call | flops 880001024 | bytes 1000 | tf_op jit(solution)/shard_map/merge_back/pallas_call | solution.py:33
  90.4 3.2 %mlp_back.1 = (bf16[256,1024]{1,0:T(8,128)(2,1)S(1)}, bf16[256,1024]{1,0:T(8,128)(2,1)S(1)}, bf16[8,32,512]{2,1,0:T(8,128)(2,1)S(1)}, bf16[3,32,512]{2,1,0:T(8,1...) custom-call(bf16[256,512]{1,0:T(8,128)(2,1)S(1)} %get-tuple-element.118.refs_0_, ...), custom_call_target="tpu_custom_call" | custom-call | flops 1320001024 | bytes 1000 | tf_op jit(solution)/shard_map/mlp_back/pallas_call | solution.py:33
  93.9 2.6 %project_product.1 = (bf16[1136,256]{1,0:T(8,128)(2,1)S(1)}, bf16[1136,256]{1,0:T(8,128)(2,1)S(1)}) custom-call(bf16[256,3072]{1,0:T(8,128)(2,1)S(1)} %get-tuple-element.124.refs_0_, bf16[256,3072]{1,0:T(8,128)(2,1)S(1)} %collective-permute-done.12.refs_1_, bf16[368,256]{1,0:T(8,128)(2,1)S(1)} %get-tuple-element.133.refs_2_, ...), custom_call_target="tpu_custom_call" | custom-call | flops 990001024 | bytes 1000 | tf_op jit(solution)/shard_map/project_product/pallas_call | solution.py:33
  96.5 1.7 collective-permute-start.21
  98.3 2.9 %collective-permute-start.14 = (bf16[3,32,512]{2,1,0:T(8,128)(2,1)S(1)}, bf16[3,32,512]{2,1,0:T(8,128)(2,1)S(1)}, u32[]{:S(2)}, u32[]{:S(2)}) collective-permute-start(bf16[3,32,512]{2,1,0:T(8,128)(2,1)S(1)} %get-tuple-element.129), channel_id=1, source_target_pairs={{0,4},{4,8},{8,12},{12,16},{16,20},{20,24},{24,28},{1,5},{5,9},{9,... | collective-permute-start | bytes 294920 | tf_op jit(solution)/shard_map/ppermute | solution.py:131
  101.2 1.5 collective-permute-start.15
  102.7 0.7 collective-permute-done.14.refs_5_.refs_1_.refs_7_
  103.4 4.3 %collective-permute-done.15.refs_6_.refs_2_.refs_8_ = bf16[3,32,512]{2,1,0:T(8,128)(2,1)S(1)} collective-permute-done((bf16[3,32,512]{2,1,0:T(8,128)(2,1)S(1)}, bf16[3,32,512]{2,1,0:T(8,128)(2,1)S(1)}, u32[]{:S(2)}, u32[]{:S(2)}) %collective-permute-start.15) | collective-permute-done | bytes 98336 | tf_op jit(solution)/shard_map/ppermute | solution.py:131
  107.7 1.9 %expand_product.1 = (bf16[1024,256]{1,0:T(8,128)(2,1)S(1)}, bf16[1024,256]{1,0:T(8,128)(2,1)S(1)}) custom-call(bf16[256,3072]{1,0:T(8,128)(2,1)S(1)} %get-tuple-element.124.refs_0_, bf16[256,3072]{1,0:T(8,128)(2,1)S(1)} %collective-permute-done.12.refs_1_, bf16[256,1024]{1,0:T(8,128)(2,1)S(1)} %get-tuple-element.131.refs_2_, ...), custom_call_target="tpu_custom_call" | custom-call | flops 660001024 | bytes 1000 | tf_op jit(solution)/shard_map/expand_product/pallas_call | solution.py:33
  109.6 5.4 %block_weights.1 = (bf16[64,256]{1,0:T(8,128)(2,1)S(1)}, bf16[64,256]{1,0:T(8,128)(2,1)S(1)}) custom-call(bf16[8,32,512]{2,1,0:T(8,128)(2,1)S(1)} %get-tuple-element.89.refs_0_, bf16[3,32,512]{2,1,0:T(8,128)(2,1)S(1)} %collective-permute-done.refs_5_.refs_1_, bf16[3,32,512]{2,1,0:T(8,128)(2,1)S(1)} %collective-permute-done.1.refs_2_, ...), custom_call_target="tpu_custom_call" | custom-call | flops 1980001024 | bytes 1000 | tf_op jit(solution)/shard_map/block_weights/pallas_call | solution.py:33
  115.4 7.9 %collective-permute-start.33 = (bf16[1024,256]{1,0:T(8,128)(2,1)S(1)}, bf16[1024,256]{1,0:T(8,128)(2,1)S(1)}, u32[]{:S(2)}, u32[]{:S(2)}) collective-permute-start(bf16[1024,256]{1,0:T(8,128)(2,1)S(1)} %get-tuple-element.145.refs_8_), channel_id=1, source_target_pairs={{0,4},{4,0},{8,12},{12,8},{16,20},{20,16},{24,28},{28,24},{1,5},{5... | collective-permute-start | bytes 1572872 | tf_op jit(solution)/shard_map/ppermute | solution.py:47
  123.4 1.3 collective-permute-start.18
  124.7 1.3 collective-permute-start.19
  126.0 3.9 %collective-permute-done.19.refs_4_ = bf16[14,8,512]{2,1,0:T(8,128)(2,1)S(1)} collective-permute-done((bf16[14,8,512]{2,1,0:T(8,128)(2,1)S(1)}, bf16[14,8,512]{2,1,0:T(8,128)(2,1)S(1)}, u32[]{:S(2)}, u32[]{:S(2)}) %collective-permute-start.19) | collective-permute-done | bytes 114720 | tf_op jit(solution)/shard_map/ppermute | solution.py:131
  129.8 6.6 %input_grad.1.refs_4_.refs_2_ = bf16[8,32,512]{2,1,0:T(8,128)(2,1)} custom-call(bf16[8,32,512]{2,1,0:T(8,128)(2,1)S(1)} %get-tuple-element.128.refs_0_.refs_5_, bf16[3,32,512]{2,1,0:T(8,128)(2,1)S(1)} %collective-permute-done.14.refs_5_.refs_1_.refs_7_, bf16[3,32,512]{2,1,0:T(8,128)(2,1)S(1)} %collective-permute-done.15.refs_6_.refs_2_.refs_8_, ...), custom_call_target="tpu_custom_call" | custom-call | flops 440000992 | bytes 1000 | tf_op jit(solution)/shard_map/input_grad/pallas_call | solution.py:33
  136.4 0.9 copy-done
  137.5 2.6 %collective-permute-start.34 = (bf16[512,256]{1,0:T(8,128)(2,1)S(1)}, bf16[512,256]{1,0:T(8,128)(2,1)S(1)}, u32[]{:S(2)}, u32[]{:S(2)}) collective-permute-start(bf16[512,256]{1,0:T(8,128)(2,1)S(1)} %get-tuple-element.163), channel_id=1, source_target_pairs={{0,8},{4,12},{8,0},{12,4},{16,24},{20,28},{24,16},{28,20},{1,9},{5... | collective-permute-start | bytes 786440 | tf_op jit(solution)/shard_map/ppermute | solution.py:47
  140.1 3.4 %collective-permute-start.23 = (bf16[64,256]{1,0:T(8,128)(2,1)S(1)}, bf16[64,256]{1,0:T(8,128)(2,1)S(1)}, u32[]{:S(2)}, u32[]{:S(2)}) collective-permute-start(bf16[64,256]{1,0:T(8,128)(2,1)S(1)} %get-tuple-element.147), channel_id=1, source_target_pairs={{0,1},{1,0},{2,3},{3,2},{4,5},{5,4},{6,7},{7,6},{8,9},{9,8},{10,11... | collective-permute-start | bytes 98312 | tf_op jit(solution)/shard_map/ppermute | solution.py:47
  143.6 0.9 collective-permute-done.23
  144.6 2.2 %collective-permute-start.29 = (bf16[624,256]{1,0:T(8,128)(2,1)S(1)}, bf16[624,256]{1,0:T(8,128)(2,1)S(1)}, u32[]{:S(2)}, u32[]{:S(2)}) collective-permute-start(bf16[624,256]{1,0:T(8,128)(2,1)S(1)} %get-tuple-element.144.refs_3_), channel_id=1, source_target_pairs={{0,16},{4,20},{8,24},{12,28},{16,0},{20,4},{24,8},{28,12},{1,17},{... | collective-permute-start | bytes 958472 | tf_op jit(solution)/shard_map/ppermute | solution.py:47
  146.8 1.6 collective-permute-done.24.refs_3_
  148.4 0.9 copy-done.1
  149.5 0.8 collective-permute-start.25
  150.4 1.6 collective-permute-start.35
  151.9 13.5 %collective-permute-done.29.refs_1_ = bf16[624,256]{1,0:T(8,128)(2,1)S(1)} collective-permute-done((bf16[624,256]{1,0:T(8,128)(2,1)S(1)}, bf16[624,256]{1,0:T(8,128)(2,1)S(1)}, u32[]{:S(2)}, u32[]{:S(2)}) %collective-permute-start.29) | collective-permute-done | bytes 319520 | tf_op jit(solution)/shard_map/ppermute | solution.py:47
  165.6 1.9 %collective-permute-start.30 = (bf16[368,256]{1,0:T(8,128)(2,1)S(1)}, bf16[368,256]{1,0:T(8,128)(2,1)S(1)}, u32[]{:S(2)}, u32[]{:S(2)}) collective-permute-start(bf16[368,256]{1,0:T(8,128)(2,1)S(1)} %get-tuple-element.157), channel_id=1, source_target_pairs={{0,4},{4,0},{8,12},{12,8},{16,20},{20,16},{24,28},{28,24},{1,5},{5... | collective-permute-start | bytes 565256 | tf_op jit(solution)/shard_map/ppermute | solution.py:47
  168.3 1.9 %collective-permute-start.36 = (bf16[1,256,256]{2,1,0:T(8,128)(2,1)S(1)}, bf16[1,256,256]{2,1,0:T(8,128)(2,1)S(1)}, u32[]{:S(2)}, u32[]{:S(2)}) collective-permute-start(bf16[1,256,256]{2,1,0:T(8,128)(2,1)S(1)} %add_bitcast_fusion), channel_id=1, source_target_pairs={{0,2},{1,3},{2,0},{3,1},{4,6},{5,7},{6,4},{7,5},{8,10},{9,11},{10,... | collective-permute-start | bytes 393224 | tf_op jit(solution)/shard_map/ppermute | solution.py:47
  170.2 1.0 collective-permute-done.30
  171.4 3.4 %collective-permute-done.26 = bf16[320,256]{1,0:T(8,128)(2,1)S(1)} collective-permute-done((bf16[320,256]{1,0:T(8,128)(2,1)S(1)}, bf16[320,256]{1,0:T(8,128)(2,1)S(1)}, u32[]{:S(2)}, u32[]{:S(2)}) %collective-permute-start.26) | collective-permute-done | bytes 163872 | tf_op jit(solution)/shard_map/ppermute | solution.py:47
  175.1 2.7 %collective-permute-done.31 = bf16[368,256]{1,0:T(8,128)(2,1)S(1)} collective-permute-done((bf16[368,256]{1,0:T(8,128)(2,1)S(1)}, bf16[368,256]{1,0:T(8,128)(2,1)S(1)}, u32[]{:S(2)}, u32[]{:S(2)}) %collective-permute-start.31) | collective-permute-done | bytes 188448 | tf_op jit(solution)/shard_map/ppermute | solution.py:47
  177.9 2.5 %collective-permute-done.27 = bf16[320,256]{1,0:T(8,128)(2,1)S(1)} collective-permute-done((bf16[320,256]{1,0:T(8,128)(2,1)S(1)}, bf16[320,256]{1,0:T(8,128)(2,1)S(1)}, u32[]{:S(2)}, u32[]{:S(2)}) %collective-permute-start.27) | collective-permute-done | bytes 163872 | tf_op jit(solution)/shard_map/ppermute | solution.py:47
  180.6 1.0 finish_project.1
  181.9 0.9 finish_expand.1
  182.8 1.0 finish_patch.1
  (75 shorter events, 6.4 us)
Async XLA Ops:
  0.6 19.0 %copy-start.7 = (bf16[1,4,16,1024]{3,2,1,0:T(8,128)(2,1)S(1)}, bf16[1,4,16,1024]{3,2,1,0:T(8,128)(2,1)}, u32[]{:S(2)}) copy-start(bf16[1,4,16,1024]{3,2,1,0:T(8,128)(2,1)} %param.22) | copy-start | bytes 393220
  0.7 19.0 %copy-start.8 = (bf16[1,4,16,1024]{3,2,1,0:T(8,128)(2,1)S(1)}, bf16[1,4,16,1024]{3,2,1,0:T(8,128)(2,1)}, u32[]{:S(2)}) copy-start(bf16[1,4,16,1024]{3,2,1,0:T(8,128)(2,1)} %param.23) | copy-start | bytes 393220
  0.7 18.9 %copy-start.10 = (f32[1024]{0:T(1024)S(1)}, f32[1024]{0:T(1024)}, u32[]{:S(2)}) copy-start(f32[1024]{0:T(1024)} %param.21) | copy-start | bytes 12292
  1.7 7.0 %collective-permute-start = (bf16[3,32,512]{2,1,0:T(8,128)(2,1)S(1)}, bf16[3,32,512]{2,1,0:T(8,128)(2,1)S(1)}, u32[]{:S(2)}, u32[]{:S(2)}) collective-permute-start(bf16[3,32,512]{2,1,0:T(8,128)(2,1)S(1)} %get-tuple-element.171), channel_id=1, source_target_pairs={{0,4},{4,8},{8,12},{12,16},{16,20},{20,24},{24,28},{1,5},{5,9},{9,... | collective-permute-start | bytes 294920 | tf_op jit(solution)/shard_map/ppermute | solution.py:131
  6.5 6.5 %collective-permute-start.1 = (bf16[3,32,512]{2,1,0:T(8,128)(2,1)S(1)}, bf16[3,32,512]{2,1,0:T(8,128)(2,1)S(1)}, u32[]{:S(2)}, u32[]{:S(2)}) collective-permute-start(bf16[3,32,512]{2,1,0:T(8,128)(2,1)S(1)} %get-tuple-element.170), channel_id=1, source_target_pairs={{4,0},{8,4},{12,8},{16,12},{20,16},{24,20},{28,24},{5,1},{9,5},{13... | collective-permute-start | bytes 294920 | tf_op jit(solution)/shard_map/ppermute | solution.py:131
  8.7 0.9 copy-start.2
  9.7 0.9 copy-start.9
  10.6 0.7 copy-start.11
  11.3 0.7 copy-start.12
  11.9 0.7 copy-start.13
  12.6 7.0 %copy-start.3 = (bf16[2048,1024]{1,0:T(8,128)(2,1)S(1)}, bf16[2048,1024]{1,0:T(8,128)(2,1)}, u32[]{:S(2)}) copy-start(bf16[2048,1024]{1,0:T(8,128)(2,1)} %refs_11_.1) | copy-start | bytes 12582916
  12.6 7.0 %copy-start.4 = (bf16[512,2048]{1,0:T(8,128)(2,1)S(1)}, bf16[512,2048]{1,0:T(8,128)(2,1)}, u32[]{:S(2)}) copy-start(bf16[512,2048]{1,0:T(8,128)(2,1)} %refs_9_.1) | copy-start | bytes 6291460
  12.6 7.0 %copy-start.5 = (bf16[2048,512]{1,0:T(8,128)(2,1)S(1)}, bf16[2048,512]{1,0:T(8,128)(2,1)}, u32[]{:S(2)}) copy-start(bf16[2048,512]{1,0:T(8,128)(2,1)} %refs_10_.1) | copy-start | bytes 6291460
  12.6 7.0 %copy-start.6 = (f32[7,7,1024]{2,1,0:T(8,128)S(1)}, f32[7,7,1024]{2,1,0:T(8,128)}, u32[]{:S(2)}) copy-start(f32[7,7,1024]{2,1,0:T(8,128)} %refs_12_.1) | copy-start | bytes 602116
  13.1 3.0 %collective-permute-start.2 = (bf16[14,8,512]{2,1,0:T(8,128)(2,1)S(1)}, bf16[14,8,512]{2,1,0:T(8,128)(2,1)S(1)}, u32[]{:S(2)}, u32[]{:S(2)}) collective-permute-start(bf16[14,8,512]{2,1,0:T(8,128)(2,1)S(1)} %get-tuple-element.90), channel_id=1, source_target_pairs={{0,1},{1,2},{2,3},{4,5},{5,6},{6,7},{8,9},{9,10},{10,11},{12,13},{... | collective-permute-start | bytes 344072 | tf_op jit(solution)/shard_map/ppermute | solution.py:131
  14.6 5.0 %collective-permute-start.3 = (bf16[14,8,512]{2,1,0:T(8,128)(2,1)S(1)}, bf16[14,8,512]{2,1,0:T(8,128)(2,1)S(1)}, u32[]{:S(2)}, u32[]{:S(2)}) collective-permute-start(bf16[14,8,512]{2,1,0:T(8,128)(2,1)S(1)} %get-tuple-element.91), channel_id=1, source_target_pairs={{1,0},{2,1},{3,2},{5,4},{6,5},{7,6},{9,8},{10,9},{11,10},{13,12},{... | collective-permute-start | bytes 344072 | tf_op jit(solution)/shard_map/ppermute | solution.py:131
  32.5 6.6 %collective-permute-start.4 = (bf16[3,16,1024]{2,1,0:T(8,128)(2,1)S(1)}, bf16[3,16,1024]{2,1,0:T(8,128)(2,1)S(1)}, u32[]{:S(2)}, u32[]{:S(2)}) collective-permute-start(bf16[3,16,1024]{2,1,0:T(8,128)(2,1)S(1)} %get-tuple-element.97), channel_id=1, source_target_pairs={{0,4},{4,8},{8,12},{12,16},{16,20},{20,24},{24,28},{1,5},{5,9},{9,... | collective-permute-start | bytes 294920 | tf_op jit(solution)/shard_map/ppermute | solution.py:131
  36.8 6.7 %collective-permute-start.5 = (bf16[3,16,1024]{2,1,0:T(8,128)(2,1)S(1)}, bf16[3,16,1024]{2,1,0:T(8,128)(2,1)S(1)}, u32[]{:S(2)}, u32[]{:S(2)}) collective-permute-start(bf16[3,16,1024]{2,1,0:T(8,128)(2,1)S(1)} %get-tuple-element.98), channel_id=1, source_target_pairs={{4,0},{8,4},{12,8},{16,12},{20,16},{24,20},{28,24},{5,1},{9,5},{13... | collective-permute-start | bytes 294920 | tf_op jit(solution)/shard_map/ppermute | solution.py:131
  43.6 5.5 %collective-permute-start.6 = (bf16[10,8,1024]{2,1,0:T(8,128)(2,1)S(1)}, bf16[10,8,1024]{2,1,0:T(8,128)(2,1)S(1)}, u32[]{:S(2)}, u32[]{:S(2)}) collective-permute-start(bf16[10,8,1024]{2,1,0:T(8,128)(2,1)S(1)} %get-tuple-element.99), channel_id=1, source_target_pairs={{0,1},{1,2},{2,3},{4,5},{5,6},{6,7},{8,9},{9,10},{10,11},{12,13},{... | collective-permute-start | bytes 491528 | tf_op jit(solution)/shard_map/ppermute | solution.py:131
  47.8 3.8 %collective-permute-start.7 = (bf16[10,8,1024]{2,1,0:T(8,128)(2,1)S(1)}, bf16[10,8,1024]{2,1,0:T(8,128)(2,1)S(1)}, u32[]{:S(2)}, u32[]{:S(2)}) collective-permute-start(bf16[10,8,1024]{2,1,0:T(8,128)(2,1)S(1)} %get-tuple-element.100), channel_id=1, source_target_pairs={{1,0},{2,1},{3,2},{5,4},{6,5},{7,6},{9,8},{10,9},{11,10},{13,12},{... | collective-permute-start | bytes 491528 | tf_op jit(solution)/shard_map/ppermute | solution.py:131
  54.9 7.0 %collective-permute-start.8 = (bf16[3,16,1024]{2,1,0:T(8,128)(2,1)S(1)}, bf16[3,16,1024]{2,1,0:T(8,128)(2,1)S(1)}, u32[]{:S(2)}, u32[]{:S(2)}) collective-permute-start(bf16[3,16,1024]{2,1,0:T(8,128)(2,1)S(1)} %get-tuple-element.105), channel_id=1, source_target_pairs={{0,4},{4,8},{8,12},{12,16},{16,20},{20,24},{24,28},{1,5},{5,9},{9,... | collective-permute-start | bytes 294920 | tf_op jit(solution)/shard_map/ppermute | solution.py:131
  59.7 6.5 %collective-permute-start.9 = (bf16[3,16,1024]{2,1,0:T(8,128)(2,1)S(1)}, bf16[3,16,1024]{2,1,0:T(8,128)(2,1)S(1)}, u32[]{:S(2)}, u32[]{:S(2)}) collective-permute-start(bf16[3,16,1024]{2,1,0:T(8,128)(2,1)S(1)} %get-tuple-element.106), channel_id=1, source_target_pairs={{4,0},{8,4},{12,8},{16,12},{20,16},{24,20},{28,24},{5,1},{9,5},{13... | collective-permute-start | bytes 294920 | tf_op jit(solution)/shard_map/ppermute | solution.py:131
  66.3 5.8 %collective-permute-start.10 = (bf16[10,8,1024]{2,1,0:T(8,128)(2,1)S(1)}, bf16[10,8,1024]{2,1,0:T(8,128)(2,1)S(1)}, u32[]{:S(2)}, u32[]{:S(2)}) collective-permute-start(bf16[10,8,1024]{2,1,0:T(8,128)(2,1)S(1)} %get-tuple-element.108), channel_id=1, source_target_pairs={{0,1},{1,2},{2,3},{4,5},{5,6},{6,7},{8,9},{9,10},{10,11},{12,13},{... | collective-permute-start | bytes 491528 | tf_op jit(solution)/shard_map/ppermute | solution.py:131
  70.8 3.9 %collective-permute-start.11 = (bf16[10,8,1024]{2,1,0:T(8,128)(2,1)S(1)}, bf16[10,8,1024]{2,1,0:T(8,128)(2,1)S(1)}, u32[]{:S(2)}, u32[]{:S(2)}) collective-permute-start(bf16[10,8,1024]{2,1,0:T(8,128)(2,1)S(1)} %get-tuple-element.109), channel_id=1, source_target_pairs={{1,0},{2,1},{3,2},{5,4},{6,5},{7,6},{9,8},{10,9},{11,10},{13,12},{... | collective-permute-start | bytes 491528 | tf_op jit(solution)/shard_map/ppermute | solution.py:131
  77.8 7.0 %collective-permute-start.12 = (bf16[256,3072]{1,0:T(8,128)(2,1)S(1)}, bf16[256,3072]{1,0:T(8,128)(2,1)S(1)}, u32[]{:S(2)}, u32[]{:S(2)}) collective-permute-start(bf16[256,3072]{1,0:T(8,128)(2,1)S(1)} %get-tuple-element.124.refs_0_), channel_id=1, source_target_pairs={{0,1},{1,0},{2,3},{3,2},{4,5},{5,4},{6,7},{7,6},{8,9},{9,8},{10,11... | collective-permute-start | bytes 4718600 | tf_op jit(solution)/shard_map/ppermute | solution.py:47
  81.7 3.1 %collective-permute-start.13 = (bf16[2,64,256]{2,1,0:T(8,128)(2,1)S(1)}, bf16[2,64,256]{2,1,0:T(8,128)(2,1)S(1)}, u32[]{:S(2)}, u32[]{:S(2)}) collective-permute-start(bf16[2,64,256]{2,1,0:T(8,128)(2,1)S(1)} %get-tuple-element.126), channel_id=1, source_target_pairs={{0,1},{1,0},{2,3},{3,2},{4,5},{5,4},{6,7},{7,6},{8,9},{9,8},{10,11... | collective-permute-start | bytes 196616 | tf_op jit(solution)/shard_map/ppermute | solution.py:47
  87.4 27.7 %collective-permute-start.20 = (bf16[2048,256]{1,0:T(8,128)(2,1)S(1)}, bf16[2048,256]{1,0:T(8,128)(2,1)S(1)}, u32[]{:S(2)}, u32[]{:S(2)}) collective-permute-start(bf16[2048,256]{1,0:T(8,128)(2,1)S(1)} %get-tuple-element.127.refs_7_), channel_id=1, source_target_pairs={{0,2},{1,3},{2,0},{3,1},{4,6},{5,7},{6,4},{7,5},{8,10},{9,11},{10,... | collective-permute-start | bytes 3145736 | tf_op jit(solution)/shard_map/ppermute | solution.py:47
  90.1 3.8 %collective-permute-start.17 = (bf16[368,256]{1,0:T(8,128)(2,1)S(1)}, bf16[368,256]{1,0:T(8,128)(2,1)S(1)}, u32[]{:S(2)}, u32[]{:S(2)}) collective-permute-start(bf16[368,256]{1,0:T(8,128)(2,1)S(1)} %get-tuple-element.134), channel_id=1, source_target_pairs={{0,1},{1,0},{2,3},{3,2},{4,5},{5,4},{6,7},{7,6},{8,9},{9,8},{10,11... | collective-permute-start | bytes 565256 | tf_op jit(solution)/shard_map/ppermute | solution.py:47
  93.6 14.1 %collective-permute-start.16 = (bf16[256,1024]{1,0:T(8,128)(2,1)S(1)}, bf16[256,1024]{1,0:T(8,128)(2,1)S(1)}, u32[]{:S(2)}, u32[]{:S(2)}) collective-permute-start(bf16[256,1024]{1,0:T(8,128)(2,1)S(1)} %get-tuple-element.132.refs_4_), channel_id=1, source_target_pairs={{0,1},{1,0},{2,3},{3,2},{4,5},{5,4},{6,7},{7,6},{8,9},{9,8},{10,11... | collective-permute-start | bytes 1572872 | tf_op jit(solution)/shard_map/ppermute | solution.py:47
  96.5 18.4 %collective-permute-start.21 = (bf16[1136,256]{1,0:T(8,128)(2,1)S(1)}, bf16[1136,256]{1,0:T(8,128)(2,1)S(1)}, u32[]{:S(2)}, u32[]{:S(2)}) collective-permute-start(bf16[1136,256]{1,0:T(8,128)(2,1)S(1)} %get-tuple-element.135.refs_4_), channel_id=1, source_target_pairs={{0,8},{4,12},{8,0},{12,4},{16,24},{20,28},{24,16},{28,20},{1,9},{5... | collective-permute-start | bytes 1744904 | tf_op jit(solution)/shard_map/ppermute | solution.py:47
  98.3 5.1 %collective-permute-start.14 = (bf16[3,32,512]{2,1,0:T(8,128)(2,1)S(1)}, bf16[3,32,512]{2,1,0:T(8,128)(2,1)S(1)}, u32[]{:S(2)}, u32[]{:S(2)}) collective-permute-start(bf16[3,32,512]{2,1,0:T(8,128)(2,1)S(1)} %get-tuple-element.129), channel_id=1, source_target_pairs={{0,4},{4,8},{8,12},{12,16},{16,20},{20,24},{24,28},{1,5},{5,9},{9,... | collective-permute-start | bytes 294920 | tf_op jit(solution)/shard_map/ppermute | solution.py:131
  101.2 6.5 %collective-permute-start.15 = (bf16[3,32,512]{2,1,0:T(8,128)(2,1)S(1)}, bf16[3,32,512]{2,1,0:T(8,128)(2,1)S(1)}, u32[]{:S(2)}, u32[]{:S(2)}) collective-permute-start(bf16[3,32,512]{2,1,0:T(8,128)(2,1)S(1)} %get-tuple-element.130), channel_id=1, source_target_pairs={{4,0},{8,4},{12,8},{16,12},{20,16},{24,20},{28,24},{5,1},{9,5},{13... | collective-permute-start | bytes 294920 | tf_op jit(solution)/shard_map/ppermute | solution.py:131
  115.4 21.0 %collective-permute-start.33 = (bf16[1024,256]{1,0:T(8,128)(2,1)S(1)}, bf16[1024,256]{1,0:T(8,128)(2,1)S(1)}, u32[]{:S(2)}, u32[]{:S(2)}) collective-permute-start(bf16[1024,256]{1,0:T(8,128)(2,1)S(1)} %get-tuple-element.145.refs_8_), channel_id=1, source_target_pairs={{0,4},{4,0},{8,12},{12,8},{16,20},{20,16},{24,28},{28,24},{1,5},{5... | collective-permute-start | bytes 1572872 | tf_op jit(solution)/shard_map/ppermute | solution.py:47
  123.3 25.1 %collective-permute-start.22 = (bf16[1024,256]{1,0:T(8,128)(2,1)S(1)}, bf16[1024,256]{1,0:T(8,128)(2,1)S(1)}, u32[]{:S(2)}, u32[]{:S(2)}) collective-permute-start(bf16[1024,256]{1,0:T(8,128)(2,1)S(1)} %get-tuple-element.136.refs_3_.refs_9_), channel_id=1, source_target_pairs={{0,4},{4,0},{8,12},{12,8},{16,20},{20,16},{24,28},{28,24},{1,5},{5... | collective-permute-start | bytes 1572872 | tf_op jit(solution)/shard_map/ppermute | solution.py:47
  123.4 2.6 %collective-permute-start.18 = (bf16[14,8,512]{2,1,0:T(8,128)(2,1)S(1)}, bf16[14,8,512]{2,1,0:T(8,128)(2,1)S(1)}, u32[]{:S(2)}, u32[]{:S(2)}) collective-permute-start(bf16[14,8,512]{2,1,0:T(8,128)(2,1)S(1)} %get-tuple-element.137), channel_id=1, source_target_pairs={{0,1},{1,2},{2,3},{4,5},{5,6},{6,7},{8,9},{9,10},{10,11},{12,13},{... | collective-permute-start | bytes 344072 | tf_op jit(solution)/shard_map/ppermute | solution.py:131
  124.7 5.2 %collective-permute-start.19 = (bf16[14,8,512]{2,1,0:T(8,128)(2,1)S(1)}, bf16[14,8,512]{2,1,0:T(8,128)(2,1)S(1)}, u32[]{:S(2)}, u32[]{:S(2)}) collective-permute-start(bf16[14,8,512]{2,1,0:T(8,128)(2,1)S(1)} %get-tuple-element.138), channel_id=1, source_target_pairs={{1,0},{2,1},{3,2},{5,4},{6,5},{7,6},{9,8},{10,9},{11,10},{13,12},{... | collective-permute-start | bytes 344072 | tf_op jit(solution)/shard_map/ppermute | solution.py:131
  136.4 1.0 copy-start
  137.5 12.8 %collective-permute-start.34 = (bf16[512,256]{1,0:T(8,128)(2,1)S(1)}, bf16[512,256]{1,0:T(8,128)(2,1)S(1)}, u32[]{:S(2)}, u32[]{:S(2)}) collective-permute-start(bf16[512,256]{1,0:T(8,128)(2,1)S(1)} %get-tuple-element.163), channel_id=1, source_target_pairs={{0,8},{4,12},{8,0},{12,4},{16,24},{20,28},{24,16},{28,20},{1,9},{5... | collective-permute-start | bytes 786440 | tf_op jit(solution)/shard_map/ppermute | solution.py:47
  140.1 4.3 %collective-permute-start.23 = (bf16[64,256]{1,0:T(8,128)(2,1)S(1)}, bf16[64,256]{1,0:T(8,128)(2,1)S(1)}, u32[]{:S(2)}, u32[]{:S(2)}) collective-permute-start(bf16[64,256]{1,0:T(8,128)(2,1)S(1)} %get-tuple-element.147), channel_id=1, source_target_pairs={{0,1},{1,0},{2,3},{3,2},{4,5},{5,4},{6,7},{7,6},{8,9},{9,8},{10,11... | collective-permute-start | bytes 98312 | tf_op jit(solution)/shard_map/ppermute | solution.py:47
  144.4 4.0 %collective-permute-start.24 = (bf16[64,256]{1,0:T(8,128)(2,1)S(1)}, bf16[64,256]{1,0:T(8,128)(2,1)S(1)}, u32[]{:S(2)}, u32[]{:S(2)}) collective-permute-start(bf16[64,256]{1,0:T(8,128)(2,1)S(1)} %add.23.refs_2_), channel_id=1, source_target_pairs={{0,4},{4,0},{8,12},{12,8},{16,20},{20,16},{24,28},{28,24},{1,5},{5... | collective-permute-start | bytes 98312 | tf_op jit(solution)/shard_map/ppermute | solution.py:47
  144.6 20.9 %collective-permute-start.29 = (bf16[624,256]{1,0:T(8,128)(2,1)S(1)}, bf16[624,256]{1,0:T(8,128)(2,1)S(1)}, u32[]{:S(2)}, u32[]{:S(2)}) collective-permute-start(bf16[624,256]{1,0:T(8,128)(2,1)S(1)} %get-tuple-element.144.refs_3_), channel_id=1, source_target_pairs={{0,16},{4,20},{8,24},{12,28},{16,0},{20,4},{24,8},{28,12},{1,17},{... | collective-permute-start | bytes 958472 | tf_op jit(solution)/shard_map/ppermute | solution.py:47
  148.4 1.0 copy-start.1
  149.5 18.0 %collective-permute-start.25 = (bf16[576,256]{1,0:T(8,128)(2,1)S(1)}, bf16[576,256]{1,0:T(8,128)(2,1)S(1)}, u32[]{:S(2)}, u32[]{:S(2)}) collective-permute-start(bf16[576,256]{1,0:T(8,128)(2,1)S(1)} %get-tuple-element.149), channel_id=1, source_target_pairs={{0,8},{4,12},{8,0},{12,4},{16,24},{20,28},{24,16},{28,20},{1,9},{5... | collective-permute-start | bytes 884744 | tf_op jit(solution)/shard_map/ppermute | solution.py:47
  150.4 17.9 %collective-permute-start.35 = (bf16[256,256]{1,0:T(8,128)(2,1)S(1)}, bf16[256,256]{1,0:T(8,128)(2,1)S(1)}, u32[]{:S(2)}, u32[]{:S(2)}) collective-permute-start(bf16[256,256]{1,0:T(8,128)(2,1)S(1)} %get-tuple-element.165), channel_id=1, source_target_pairs={{0,16},{4,20},{8,24},{12,28},{16,0},{20,4},{24,8},{28,12},{1,17},{... | collective-permute-start | bytes 393224 | tf_op jit(solution)/shard_map/ppermute | solution.py:47
  165.6 5.6 %collective-permute-start.30 = (bf16[368,256]{1,0:T(8,128)(2,1)S(1)}, bf16[368,256]{1,0:T(8,128)(2,1)S(1)}, u32[]{:S(2)}, u32[]{:S(2)}) collective-permute-start(bf16[368,256]{1,0:T(8,128)(2,1)S(1)} %get-tuple-element.157), channel_id=1, source_target_pairs={{0,4},{4,0},{8,12},{12,8},{16,20},{20,16},{24,28},{28,24},{1,5},{5... | collective-permute-start | bytes 565256 | tf_op jit(solution)/shard_map/ppermute | solution.py:47
  167.6 7.2 %collective-permute-start.26 = (bf16[320,256]{1,0:T(8,128)(2,1)S(1)}, bf16[320,256]{1,0:T(8,128)(2,1)S(1)}, u32[]{:S(2)}, u32[]{:S(2)}) collective-permute-start(bf16[320,256]{1,0:T(8,128)(2,1)S(1)} %get-tuple-element.151), channel_id=1, source_target_pairs={{0,16},{4,20},{8,24},{12,28},{16,0},{20,4},{24,8},{28,12},{1,17},{... | collective-permute-start | bytes 491528 | tf_op jit(solution)/shard_map/ppermute | solution.py:47
  168.3 6.6 %collective-permute-start.36 = (bf16[1,256,256]{2,1,0:T(8,128)(2,1)S(1)}, bf16[1,256,256]{2,1,0:T(8,128)(2,1)S(1)}, u32[]{:S(2)}, u32[]{:S(2)}) collective-permute-start(bf16[1,256,256]{2,1,0:T(8,128)(2,1)S(1)} %add_bitcast_fusion), channel_id=1, source_target_pairs={{0,2},{1,3},{2,0},{3,1},{4,6},{5,7},{6,4},{7,5},{8,10},{9,11},{10,... | collective-permute-start | bytes 393224 | tf_op jit(solution)/shard_map/ppermute | solution.py:47
  171.3 6.5 %collective-permute-start.31 = (bf16[368,256]{1,0:T(8,128)(2,1)S(1)}, bf16[368,256]{1,0:T(8,128)(2,1)S(1)}, u32[]{:S(2)}, u32[]{:S(2)}) collective-permute-start(bf16[368,256]{1,0:T(8,128)(2,1)S(1)} %add.26), channel_id=1, source_target_pairs={{0,2},{1,3},{2,0},{3,1},{4,6},{5,7},{6,4},{7,5},{8,10},{9,11},{10,... | collective-permute-start | bytes 565256 | tf_op jit(solution)/shard_map/ppermute | solution.py:47
  174.8 5.6 %collective-permute-start.27 = (bf16[320,256]{1,0:T(8,128)(2,1)S(1)}, bf16[320,256]{1,0:T(8,128)(2,1)S(1)}, u32[]{:S(2)}, u32[]{:S(2)}) collective-permute-start(bf16[320,256]{1,0:T(8,128)(2,1)S(1)} %add.24), channel_id=1, source_target_pairs={{0,2},{1,3},{2,0},{3,1},{4,6},{5,7},{6,4},{7,5},{8,10},{9,11},{10,... | collective-permute-start | bytes 491528 | tf_op jit(solution)/shard_map/ppermute | solution.py:47
  175.0 7.8 %collective-permute-start.37 = (bf16[2,256,256]{2,1,0:T(8,128)(2,1)S(1)}, bf16[2,256,256]{2,1,0:T(8,128)(2,1)S(1)}, u32[]{:S(2)}, u32[]{:S(2)}) collective-permute-start(bf16[2,256,256]{2,1,0:T(8,128)(2,1)S(1)} %maximum_bitcast_fusion.refs_0_), channel_id=1, source_target_pairs={{0,1},{1,0},{2,3},{3,2},{4,5},{5,4},{6,7},{7,6},{8,9},{9,8},{10,11... | collective-permute-start | bytes 786440 | tf_op jit(solution)/shard_map/ppermute | solution.py:47
  177.8 2.7 %collective-permute-start.32 = (bf16[368,256]{1,0:T(8,128)(2,1)S(1)}, bf16[368,256]{1,0:T(8,128)(2,1)S(1)}, u32[]{:S(2)}, u32[]{:S(2)}) collective-permute-start(bf16[368,256]{1,0:T(8,128)(2,1)S(1)} %add.27.refs_0_), channel_id=1, source_target_pairs={{0,1},{1,0},{2,3},{3,2},{4,5},{5,4},{6,7},{7,6},{8,9},{9,8},{10,11... | collective-permute-start | bytes 565256 | tf_op jit(solution)/shard_map/ppermute | solution.py:47
  180.5 1.5 collective-permute-start.28

commit v11 on v9

--- a/solution.py
+++ b/solution.py
@@ -70,7 +70,7 @@
             "sum_step",
             (keep, received, *grown),
             (out, out),
-            after=after if place == 0 else (),
+            after=after if place == (1 if extra else 0) else (),
             limit=8,
             us=0.2,
         )

time: 172 us -> 179 us (1.041)
  waiting for transfers between devices: 48.8 us -> 62 us
  starting transfers between devices: 63.9 us -> 58.2 us
    ppermute x22, waiting for transfers between devices: 31.3 us -> 41.8 us  [swap(): lax.ppermute(values, axis, [(i, i ^ bit) for i in range(lax.axis_size(axi...]
    ppermute x22, starting transfers between devices: 23.8 us -> 18.8 us  [swap(): lax.ppermute(values, axis, [(i, i ^ bit) for i in range(lax.axis_size(axi...]
    ppermute x8, waiting for transfers between devices: 14.8 us -> 17.5 us  [neighbours(): lax.ppermute(first, axis, backward)]
  transfers between devices with their start and end apart: 38 -> 38, of which waited for: 17 -> 23; matrix products, arithmetic and copies ran while one was open for 0% -> 0% of each run, Pallas kernels for 16% -> 16%
where the time goes in v11:
time: 179 us
  waiting for transfers between devices  62 us (35%)
  starting transfers between devices  58.2 us (33%)
  Pallas kernels  51.1 us (29%)
  local copies, waits for them, and re-layouts  5.87 us (3%)
    pallas_call x26, Pallas kernels, run(): pl.pallas_call(inner, name=name, out_shape=outs, in_specs=[spec(i) for i...  51.1 us
    ppermute x22, waiting for transfers between devices, swap(): lax.ppermute(values, axis, [(i, i ^ bit) for i in range(lax.axis_size(axi...  41.8 us
    ppermute x8, starting transfers between devices, neighbours(): lax.ppermute(last, axis, forward)  29 us
    ppermute x22, starting transfers between devices, swap(): lax.ppermute(values, axis, [(i, i ^ bit) for i in range(lax.axis_size(axi...  18.8 us
    ppermute x8, waiting for transfers between devices, neighbours(): lax.ppermute(first, axis, backward)  17.5 us
    ppermute x8, starting transfers between devices, neighbours(): lax.ppermute(first, axis, backward)  10.5 us
    unnamed x26, local copies, waits for them, and re-layouts  4.87 us
  transfers between devices with their start and end apart: 38, of which 23 were waited for; matrix products, arithmetic and copies ran while one was open for 0% of the time, Pallas kernels for 16%

profile of v11, /device:TPU:0, one launch (start us, length us, event | category | flops | bytes accessed | tf_op | source)
XLA Modules:
  0.0 178.5 jit_solution(920469470654859286)
XLA Ops:
  0.7 1.0 slice_bitcast_fusion
  1.7 4.8 %collective-permute-start = (bf16[3,32,512]{2,1,0:T(8,128)(2,1)S(1)}, bf16[3,32,512]{2,1,0:T(8,128)(2,1)S(1)}, u32[]{:S(2)}, u32[]{:S(2)}) collective-permute-start(bf16[3,32,512]{2,1,0:T(8,128)(2,1)S(1)} %get-tuple-element.171), channel_id=1, source_target_pairs={{0,4},{4,8},{8,12},{12,16},{16,20},{20,24},{24,28},{1,5},{5,9},{9,... | collective-permute-start | bytes 294920 | tf_op jit(solution)/shard_map/ppermute | solution.py:120
  6.5 1.3 collective-permute-start.1
  7.8 0.9 collective-permute-done.refs_5_.refs_1_
  8.7 0.9 copy-done.1
  9.7 0.9 copy-done.8
  13.1 1.6 collective-permute-start.2
  14.6 1.4 collective-permute-start.3
  16.1 3.5 %collective-permute-done.3.refs_4_ = bf16[14,8,512]{2,1,0:T(8,128)(2,1)S(1)} collective-permute-done((bf16[14,8,512]{2,1,0:T(8,128)(2,1)S(1)}, bf16[14,8,512]{2,1,0:T(8,128)(2,1)S(1)}, u32[]{:S(2)}, u32[]{:S(2)}) %collective-permute-start.3) | collective-permute-done | bytes 114720 | tf_op jit(solution)/shard_map/ppermute | solution.py:120
  19.6 12.8 %front.1 = (bf16[256,3072]{1,0:T(8,128)(2,1)S(1)}, f32[256,512]{1,0:T(8,128)S(1)}, f32[256,1]{1,0:T(8,128)S(1)}, bf16[256,2048]{1,0:T(8,128)(2,1)S(1)}, f32[256,...) custom-call(bf16[8,32,512]{2,1,0:T(8,128)(2,1)S(1)} %get-tuple-eleme, ...), custom_call_target="tpu_custom_call" | custom-call | flops 13200001024 | bytes 1000 | tf_op jit(solution)/shard_map/front/pallas_call | solution.py:33
  32.5 4.4 %collective-permute-start.4 = (bf16[3,16,1024]{2,1,0:T(8,128)(2,1)S(1)}, bf16[3,16,1024]{2,1,0:T(8,128)(2,1)S(1)}, u32[]{:S(2)}, u32[]{:S(2)}) collective-permute-start(bf16[3,16,1024]{2,1,0:T(8,128)(2,1)S(1)} %get-tuple-element.97), channel_id=1, source_target_pairs={{0,4},{4,8},{8,12},{12,16},{16,20},{20,24},{24,28},{1,5},{5,9},{9,... | collective-permute-start | bytes 294920 | tf_op jit(solution)/shard_map/ppermute | solution.py:120
  36.8 1.3 collective-permute-start.5
  38.1 0.9 collective-permute-done.4.refs_1_
  39.0 4.5 %collective-permute-done.5.refs_2_ = bf16[3,16,1024]{2,1,0:T(8,128)(2,1)S(1)} collective-permute-done((bf16[3,16,1024]{2,1,0:T(8,128)(2,1)S(1)}, bf16[3,16,1024]{2,1,0:T(8,128)(2,1)S(1)}, u32[]{:S(2)}, u32[]{:S(2)}) %collective-permute-start.5) | collective-permute-done | bytes 98336 | tf_op jit(solution)/shard_map/ppermute | solution.py:120
  43.6 4.2 %collective-permute-start.6 = (bf16[10,8,1024]{2,1,0:T(8,128)(2,1)S(1)}, bf16[10,8,1024]{2,1,0:T(8,128)(2,1)S(1)}, u32[]{:S(2)}, u32[]{:S(2)}) collective-permute-start(bf16[10,8,1024]{2,1,0:T(8,128)(2,1)S(1)} %get-tuple-element.99), channel_id=1, source_target_pairs={{0,1},{1,2},{2,3},{4,5},{5,6},{6,7},{8,9},{9,10},{10,11},{12,13},{... | collective-permute-start | bytes 491528 | tf_op jit(solution)/shard_map/ppermute | solution.py:120
  47.8 1.3 collective-permute-start.7
  49.1 2.5 %collective-permute-done.7.refs_4_ = bf16[10,8,1024]{2,1,0:T(8,128)(2,1)S(1)} collective-permute-done((bf16[10,8,1024]{2,1,0:T(8,128)(2,1)S(1)}, bf16[10,8,1024]{2,1,0:T(8,128)(2,1)S(1)}, u32[]{:S(2)}, u32[]{:S(2)}) %collective-permute-start.7) | collective-permute-done | bytes 163872 | tf_op jit(solution)/shard_map/ppermute | solution.py:120
  51.6 3.3 %mixer.1 = (f32[4,16,1024]{2,1,0:T(8,128)S(1)}, bf16[4,16,1024]{2,1,0:T(8,128)(2,1)S(1)}, bf16[3,16,1024]{2,1,0:T(8,128)(2,1)S(1)}, bf16[3,16,1024]{2,1,0:T(8,128)(2,1)S(1)}, f32[1,1024]{1,0:T(1,128)S(1)}) custom-call(bf16[4,16,1024]{2,1,0:T(8,128)(2,1)S(1)} %get-tuple-element.96.refs_0_, bf16[3,16,1024]{2,1,0:T(8,128)(2,1)S(1)} %collective-permute-done.4.refs_1_, ...), custom_call_target="tpu_custom_call" | custom-call | flops 3300001024 | bytes 1000 | tf_op jit(solution)/shard_map/mixer/pallas_call | solution.py:33
  54.9 4.8 %collective-permute-start.8 = (bf16[3,16,1024]{2,1,0:T(8,128)(2,1)S(1)}, bf16[3,16,1024]{2,1,0:T(8,128)(2,1)S(1)}, u32[]{:S(2)}, u32[]{:S(2)}) collective-permute-start(bf16[3,16,1024]{2,1,0:T(8,128)(2,1)S(1)} %get-tuple-element.105), channel_id=1, source_target_pairs={{0,4},{4,8},{8,12},{12,16},{16,20},{20,24},{24,28},{1,5},{5,9},{9,... | collective-permute-start | bytes 294920 | tf_op jit(solution)/shard_map/ppermute | solution.py:120
  59.7 1.3 collective-permute-start.9
  61.0 0.9 collective-permute-done.8.refs_6_.refs_1_
  61.9 2.9 %mixer_weights.1.refs_3_.refs_7_ = f32[49,1024]{1,0:T(8,128)S(1)} custom-call(bf16[4,16,1024]{2,1,0:T(8,128)(2,1)S(1)} %get-tuple-element.96.refs_0_, bf16[3,16,1024]{2,1,0:T(8,128)(2,1)S(1)} %collective-permute-done.4.refs_1_, bf16[3,16,1024]{2,1,0:T(8,128)(2,1)S(1)} %collective-permute-done.5.refs_2_, ...), custom_call_target="tpu_custom_call" | custom-call | flops 3300001024 | bytes 1000 | tf_op jit(solution)/shard_map/mixer_weights/pallas_call | solution.py:33
  64.8 1.4 collective-permute-done.9.refs_2_
  66.3 4.5 %collective-permute-start.10 = (bf16[10,8,1024]{2,1,0:T(8,128)(2,1)S(1)}, bf16[10,8,1024]{2,1,0:T(8,128)(2,1)S(1)}, u32[]{:S(2)}, u32[]{:S(2)}) collective-permute-start(bf16[10,8,1024]{2,1,0:T(8,128)(2,1)S(1)} %get-tuple-element.108), channel_id=1, source_target_pairs={{0,1},{1,2},{2,3},{4,5},{5,6},{6,7},{8,9},{9,10},{10,11},{12,13},{... | collective-permute-start | bytes 491528 | tf_op jit(solution)/shard_map/ppermute | solution.py:120
  70.8 1.3 collective-permute-start.11
  72.1 2.6 %collective-permute-done.11.refs_4_ = bf16[10,8,1024]{2,1,0:T(8,128)(2,1)S(1)} collective-permute-done((bf16[10,8,1024]{2,1,0:T(8,128)(2,1)S(1)}, bf16[10,8,1024]{2,1,0:T(8,128)(2,1)S(1)}, u32[]{:S(2)}, u32[]{:S(2)}) %collective-permute-start.11) | collective-permute-done | bytes 163872 | tf_op jit(solution)/shard_map/ppermute | solution.py:120
  74.7 3.1 %section_grad.1 = (bf16[64,1024]{1,0:T(8,128)(2,1)S(1)}, bf16[2,64,256]{2,1,0:T(8,128)(2,1)S(1)}, bf16[2,64,256]{2,1,0:T(8,128)(2,1)S(1)}, bf16[256,3072]{1,0:T(8,128)(2,1)S(1)}) custom-call(bf16[4,16,1024]{2,1,0:T(8,128)(2,1)S(1)} %get-tuple-element.104.refs_0_, ...), custom_call_target="tpu_custom_call", output_to_operand_aliasing={{3}: (7, {})} | custom-call | flops 3300001024 | bytes 1000 | tf_op jit(solution)/shard_map/section_grad/pallas_call | solution.py:33
  77.8 3.9 %collective-permute-start.12 = (bf16[256,3072]{1,0:T(8,128)(2,1)S(1)}, bf16[256,3072]{1,0:T(8,128)(2,1)S(1)}, u32[]{:S(2)}, u32[]{:S(2)}) collective-permute-start(bf16[256,3072]{1,0:T(8,128)(2,1)S(1)} %get-tuple-element.124.refs_0_), channel_id=1, source_target_pairs={{0,1},{1,0},{2,3},{3,2},{4,5},{5,4},{6,7},{7,6},{8,9},{9,8},{10,11... | collective-permute-start | bytes 4718600 | tf_op jit(solution)/shard_map/ppermute | solution.py:47
  81.8 3.1 %collective-permute-done.13.refs_3_ = bf16[2,64,256]{2,1,0:T(8,128)(2,1)S(1)} collective-permute-done((bf16[2,64,256]{2,1,0:T(8,128)(2,1)S(1)}, bf16[2,64,256]{2,1,0:T(8,128)(2,1)S(1)}, u32[]{:S(2)}, u32[]{:S(2)}) %collective-permute-start.13) | collective-permute-done | bytes 65568 | tf_op jit(solution)/shard_map/ppermute | solution.py:47
  84.8 2.6 %patch_product.1 = (bf16[2048,256]{1,0:T(8,128)(2,1)S(1)}, bf16[2048,256]{1,0:T(8,128)(2,1)S(1)}) custom-call(bf16[256,3072]{1,0:T(8,128)(2,1)S(1)} %get-tuple-element.124.refs_0_, bf16[256,3072]{1,0:T(8,128)(2,1)S(1)} %collective-permute-done.12.refs_1_, bf16[2,64,256]{2,1,0:T(8,128)(2,1)S(1)} %get-tuple-element.125.refs_2_, ...), custom_call_target="tpu_custom_call" | custom-call | flops 990001024 | bytes 1000 | tf_op jit(solution)/shard_map/patch_product/pallas_call | solution.py:33
  87.6 2.5 %merge_back.1 = (f32[256,512]{1,0:T(8,128)S(1)}, bf16[256,512]{1,0:T(8,128)(2,1)S(1)}, bf16[368,256]{1,0:T(8,128)(2,1)S(1)}, bf16[368,256]{1,0:T(8,128)(2,1)S(1)}) custom-call(bf16[64,1024]{1,0:T(8,128)(2,1)S(1)} %get-tuple-element.112.refs_0_, bf16[2048,1024]{1,0:T(8,128)(2,1)S(1)} %get-tuple-element.113.refs_1_, ...), custom_call_target="tpu_custom_call" | custom-call | flops 880001024 | bytes 1000 | tf_op jit(solution)/shard_map/merge_back/pallas_call | solution.py:33
  90.1 3.2 %mlp_back.1 = (bf16[256,1024]{1,0:T(8,128)(2,1)S(1)}, bf16[256,1024]{1,0:T(8,128)(2,1)S(1)}, bf16[8,32,512]{2,1,0:T(8,128)(2,1)S(1)}, bf16[3,32,512]{2,1,0:T(8,1...) custom-call(bf16[256,512]{1,0:T(8,128)(2,1)S(1)} %get-tuple-element.118.refs_0_, ...), custom_call_target="tpu_custom_call" | custom-call | flops 1320001024 | bytes 1000 | tf_op jit(solution)/shard_map/mlp_back/pallas_call | solution.py:33
  93.8 3.0 %collective-permute-start.14 = (bf16[3,32,512]{2,1,0:T(8,128)(2,1)S(1)}, bf16[3,32,512]{2,1,0:T(8,128)(2,1)S(1)}, u32[]{:S(2)}, u32[]{:S(2)}) collective-permute-start(bf16[3,32,512]{2,1,0:T(8,128)(2,1)S(1)} %get-tuple-element.129), channel_id=1, source_target_pairs={{0,4},{4,8},{8,12},{12,16},{16,20},{20,24},{24,28},{1,5},{5,9},{9,... | collective-permute-start | bytes 294920 | tf_op jit(solution)/shard_map/ppermute | solution.py:120
  96.8 1.3 collective-permute-start.15
  98.1 2.8 %project_product.1 = (bf16[1136,256]{1,0:T(8,128)(2,1)S(1)}, bf16[1136,256]{1,0:T(8,128)(2,1)S(1)}) custom-call(bf16[256,3072]{1,0:T(8,128)(2,1)S(1)} %get-tuple-element.124.refs_0_, bf16[256,3072]{1,0:T(8,128)(2,1)S(1)} %collective-permute-done.12.refs_1_, bf16[368,256]{1,0:T(8,128)(2,1)S(1)} %get-tuple-element.133.refs_2_, ...), custom_call_target="tpu_custom_call" | custom-call | flops 990001024 | bytes 1000 | tf_op jit(solution)/shard_map/project_product/pallas_call | solution.py:33
  100.9 2.7 %collective-permute-done.15.refs_6_.refs_2_.refs_8_ = bf16[3,32,512]{2,1,0:T(8,128)(2,1)S(1)} collective-permute-done((bf16[3,32,512]{2,1,0:T(8,128)(2,1)S(1)}, bf16[3,32,512]{2,1,0:T(8,128)(2,1)S(1)}, u32[]{:S(2)}, u32[]{:S(2)}) %collective-permute-start.15) | collective-permute-done | bytes 98336 | tf_op jit(solution)/shard_map/ppermute | solution.py:120
  103.6 1.9 %expand_product.1 = (bf16[1024,256]{1,0:T(8,128)(2,1)S(1)}, bf16[1024,256]{1,0:T(8,128)(2,1)S(1)}) custom-call(bf16[256,3072]{1,0:T(8,128)(2,1)S(1)} %get-tuple-element.124.refs_0_, bf16[256,3072]{1,0:T(8,128)(2,1)S(1)} %collective-permute-done.12.refs_1_, bf16[256,1024]{1,0:T(8,128)(2,1)S(1)} %get-tuple-element.131.refs_2_, ...), custom_call_target="tpu_custom_call" | custom-call | flops 660001024 | bytes 1000 | tf_op jit(solution)/shard_map/expand_product/pallas_call | solution.py:33
  105.5 5.4 %block_weights.1 = (bf16[64,256]{1,0:T(8,128)(2,1)S(1)}, bf16[64,256]{1,0:T(8,128)(2,1)S(1)}) custom-call(bf16[8,32,512]{2,1,0:T(8,128)(2,1)S(1)} %get-tuple-element.89.refs_0_, bf16[3,32,512]{2,1,0:T(8,128)(2,1)S(1)} %collective-permute-done.refs_5_.refs_1_, bf16[3,32,512]{2,1,0:T(8,128)(2,1)S(1)} %collective-permute-done.1.refs_2_, ...), custom_call_target="tpu_custom_call" | custom-call | flops 1980001024 | bytes 1000 | tf_op jit(solution)/shard_map/block_weights/pallas_call | solution.py:33
  110.9 2.0 %collective-permute-done.32.refs_1_ = bf16[2048,256]{1,0:T(8,128)(2,1)S(1)} collective-permute-done((bf16[2048,256]{1,0:T(8,128)(2,1)S(1)}, bf16[2048,256]{1,0:T(8,128)(2,1)S(1)}, u32[]{:S(2)}, u32[]{:S(2)}) %collective-permute-start.32) | collective-permute-done | bytes 1048608 | tf_op jit(solution)/shard_map/ppermute | solution.py:47
  113.1 1.1 collective-permute-start.33
  114.3 1.6 collective-permute-start.27
  115.8 1.0 collective-permute-start.20
  116.8 11.2 %collective-permute-done.33.refs_1_ = bf16[1024,256]{1,0:T(8,128)(2,1)S(1)} collective-permute-done((bf16[1024,256]{1,0:T(8,128)(2,1)S(1)}, bf16[1024,256]{1,0:T(8,128)(2,1)S(1)}, u32[]{:S(2)}, u32[]{:S(2)}) %collective-permute-start.33) | collective-permute-done | bytes 524320 | tf_op jit(solution)/shard_map/ppermute | solution.py:47
  128.2 1.6 collective-permute-start.34
  129.8 1.2 collective-permute-done.21
  131.0 1.1 collective-permute-start.22
  132.2 1.8 %collective-permute-start.18 = (bf16[14,8,512]{2,1,0:T(8,128)(2,1)S(1)}, bf16[14,8,512]{2,1,0:T(8,128)(2,1)S(1)}, u32[]{:S(2)}, u32[]{:S(2)}) collective-permute-start(bf16[14,8,512]{2,1,0:T(8,128)(2,1)S(1)} %get-tuple-element.137), channel_id=1, source_target_pairs={{0,1},{1,2},{2,3},{4,5},{5,6},{6,7},{8,9},{9,10},{10,11},{12,13},{... | collective-permute-start | bytes 344072 | tf_op jit(solution)/shard_map/ppermute | solution.py:120
  134.0 1.3 collective-permute-start.19
  135.5 3.1 %collective-permute-done.22.refs_3_ = bf16[64,256]{1,0:T(8,128)(2,1)S(1)} collective-permute-done((bf16[64,256]{1,0:T(8,128)(2,1)S(1)}, bf16[64,256]{1,0:T(8,128)(2,1)S(1)}, u32[]{:S(2)}, u32[]{:S(2)}) %collective-permute-start.22) | collective-permute-done | bytes 32800 | tf_op jit(solution)/shard_map/ppermute | solution.py:47
  138.5 2.6 %collective-permute-start.28 = (bf16[624,256]{1,0:T(8,128)(2,1)S(1)}, bf16[624,256]{1,0:T(8,128)(2,1)S(1)}, u32[]{:S(2)}, u32[]{:S(2)}) collective-permute-start(bf16[624,256]{1,0:T(8,128)(2,1)S(1)} %get-tuple-element.153), channel_id=1, source_target_pairs={{0,16},{4,20},{8,24},{12,28},{16,0},{20,4},{24,8},{28,12},{1,17},{... | collective-permute-start | bytes 958472 | tf_op jit(solution)/shard_map/ppermute | solution.py:47
  141.9 1.5 collective-permute-start.35
  143.4 6.6 %input_grad.1.refs_2_ = bf16[8,32,512]{2,1,0:T(8,128)(2,1)} custom-call(bf16[8,32,512]{2,1,0:T(8,128)(2,1)S(1)} %get-tuple-element.128.refs_0_.refs_5_, bf16[3,32,512]{2,1,0:T(8,128)(2,1)S(1)} %collective-permute-done.14.refs_5_.refs_1_.refs_7_, bf16[3,32,512]{2,1,0:T(8,128)(2,1)S(1)} %collective-permute-done.15.refs_6_.refs_2_.refs_8_, ...), custom_call_target="tpu_custom_call" | custom-call | flops 2200001024 | bytes 1000 | tf_op jit(solution)/shard_map/input_grad/pallas_call | solution.py:33
  150.0 8.4 %collective-permute-done.28.refs_1_ = bf16[624,256]{1,0:T(8,128)(2,1)S(1)} collective-permute-done((bf16[624,256]{1,0:T(8,128)(2,1)S(1)}, bf16[624,256]{1,0:T(8,128)(2,1)S(1)}, u32[]{:S(2)}, u32[]{:S(2)}) %collective-permute-start.28) | collective-permute-done | bytes 319520 | tf_op jit(solution)/shard_map/ppermute | solution.py:47
  158.4 1.1 collective-permute-start.29
  159.6 0.9 copy-done
  160.7 2.3 %collective-permute-done.35 = bf16[256,256]{1,0:T(8,128)(2,1)S(1)} collective-permute-done((bf16[256,256]{1,0:T(8,128)(2,1)S(1)}, bf16[256,256]{1,0:T(8,128)(2,1)S(1)}, u32[]{:S(2)}, u32[]{:S(2)}) %collective-permute-start.35) | collective-permute-done | bytes 131104 | tf_op jit(solution)/shard_map/ppermute | solution.py:47
  163.1 1.0 collective-permute-done.29
  164.1 1.0 collective-permute-start.30
  165.2 2.8 %collective-permute-done.24 = bf16[320,256]{1,0:T(8,128)(2,1)S(1)} collective-permute-done((bf16[320,256]{1,0:T(8,128)(2,1)S(1)}, bf16[320,256]{1,0:T(8,128)(2,1)S(1)}, u32[]{:S(2)}, u32[]{:S(2)}) %collective-permute-start.24) | collective-permute-done | bytes 163872 | tf_op jit(solution)/shard_map/ppermute | solution.py:47
  168.5 1.0 collective-permute-done.36
  169.6 3.8 %collective-permute-done.30 = bf16[368,256]{1,0:T(8,128)(2,1)S(1)} collective-permute-done((bf16[368,256]{1,0:T(8,128)(2,1)S(1)}, bf16[368,256]{1,0:T(8,128)(2,1)S(1)}, u32[]{:S(2)}, u32[]{:S(2)}) %collective-permute-start.30) | collective-permute-done | bytes 188448 | tf_op jit(solution)/shard_map/ppermute | solution.py:47
  173.5 1.6 collective-permute-done.25
  175.2 1.0 finish_project.1
  177.5 1.0 finish_patch.1
  (73 shorter events, 7.2 us)
Async XLA Ops:
  0.6 19.0 %copy-start.6 = (bf16[1,4,16,1024]{3,2,1,0:T(8,128)(2,1)S(1)}, bf16[1,4,16,1024]{3,2,1,0:T(8,128)(2,1)}, u32[]{:S(2)}) copy-start(bf16[1,4,16,1024]{3,2,1,0:T(8,128)(2,1)} %param.22) | copy-start | bytes 393220
  0.7 19.0 %copy-start.7 = (bf16[1,4,16,1024]{3,2,1,0:T(8,128)(2,1)S(1)}, bf16[1,4,16,1024]{3,2,1,0:T(8,128)(2,1)}, u32[]{:S(2)}) copy-start(bf16[1,4,16,1024]{3,2,1,0:T(8,128)(2,1)} %param.23) | copy-start | bytes 393220
  0.7 18.9 %copy-start.9 = (f32[1024]{0:T(1024)S(1)}, f32[1024]{0:T(1024)}, u32[]{:S(2)}) copy-start(f32[1024]{0:T(1024)} %param.21) | copy-start | bytes 12292
  1.7 7.0 %collective-permute-start = (bf16[3,32,512]{2,1,0:T(8,128)(2,1)S(1)}, bf16[3,32,512]{2,1,0:T(8,128)(2,1)S(1)}, u32[]{:S(2)}, u32[]{:S(2)}) collective-permute-start(bf16[3,32,512]{2,1,0:T(8,128)(2,1)S(1)} %get-tuple-element.171), channel_id=1, source_target_pairs={{0,4},{4,8},{8,12},{12,16},{16,20},{20,24},{24,28},{1,5},{5,9},{9,... | collective-permute-start | bytes 294920 | tf_op jit(solution)/shard_map/ppermute | solution.py:120
  6.5 6.5 %collective-permute-start.1 = (bf16[3,32,512]{2,1,0:T(8,128)(2,1)S(1)}, bf16[3,32,512]{2,1,0:T(8,128)(2,1)S(1)}, u32[]{:S(2)}, u32[]{:S(2)}) collective-permute-start(bf16[3,32,512]{2,1,0:T(8,128)(2,1)S(1)} %get-tuple-element.170), channel_id=1, source_target_pairs={{4,0},{8,4},{12,8},{16,12},{20,16},{24,20},{28,24},{5,1},{9,5},{13... | collective-permute-start | bytes 294920 | tf_op jit(solution)/shard_map/ppermute | solution.py:120
  8.7 0.9 copy-start.1
  9.7 0.9 copy-start.8
  10.6 0.7 copy-start.10
  11.3 0.7 copy-start.11
  11.9 0.7 copy-start.12
  12.6 7.0 %copy-start.2 = (bf16[2048,1024]{1,0:T(8,128)(2,1)S(1)}, bf16[2048,1024]{1,0:T(8,128)(2,1)}, u32[]{:S(2)}) copy-start(bf16[2048,1024]{1,0:T(8,128)(2,1)} %refs_11_.1) | copy-start | bytes 12582916
  12.6 7.0 %copy-start.3 = (bf16[512,2048]{1,0:T(8,128)(2,1)S(1)}, bf16[512,2048]{1,0:T(8,128)(2,1)}, u32[]{:S(2)}) copy-start(bf16[512,2048]{1,0:T(8,128)(2,1)} %refs_9_.1) | copy-start | bytes 6291460
  12.6 7.0 %copy-start.4 = (bf16[2048,512]{1,0:T(8,128)(2,1)S(1)}, bf16[2048,512]{1,0:T(8,128)(2,1)}, u32[]{:S(2)}) copy-start(bf16[2048,512]{1,0:T(8,128)(2,1)} %refs_10_.1) | copy-start | bytes 6291460
  12.6 7.0 %copy-start.5 = (f32[7,7,1024]{2,1,0:T(8,128)S(1)}, f32[7,7,1024]{2,1,0:T(8,128)}, u32[]{:S(2)}) copy-start(f32[7,7,1024]{2,1,0:T(8,128)} %refs_12_.1) | copy-start | bytes 602116
  13.1 3.0 %collective-permute-start.2 = (bf16[14,8,512]{2,1,0:T(8,128)(2,1)S(1)}, bf16[14,8,512]{2,1,0:T(8,128)(2,1)S(1)}, u32[]{:S(2)}, u32[]{:S(2)}) collective-permute-start(bf16[14,8,512]{2,1,0:T(8,128)(2,1)S(1)} %get-tuple-element.90), channel_id=1, source_target_pairs={{0,1},{1,2},{2,3},{4,5},{5,6},{6,7},{8,9},{9,10},{10,11},{12,13},{... | collective-permute-start | bytes 344072 | tf_op jit(solution)/shard_map/ppermute | solution.py:120
  14.6 5.0 %collective-permute-start.3 = (bf16[14,8,512]{2,1,0:T(8,128)(2,1)S(1)}, bf16[14,8,512]{2,1,0:T(8,128)(2,1)S(1)}, u32[]{:S(2)}, u32[]{:S(2)}) collective-permute-start(bf16[14,8,512]{2,1,0:T(8,128)(2,1)S(1)} %get-tuple-element.91), channel_id=1, source_target_pairs={{1,0},{2,1},{3,2},{5,4},{6,5},{7,6},{9,8},{10,9},{11,10},{13,12},{... | collective-permute-start | bytes 344072 | tf_op jit(solution)/shard_map/ppermute | solution.py:120
  32.5 6.6 %collective-permute-start.4 = (bf16[3,16,1024]{2,1,0:T(8,128)(2,1)S(1)}, bf16[3,16,1024]{2,1,0:T(8,128)(2,1)S(1)}, u32[]{:S(2)}, u32[]{:S(2)}) collective-permute-start(bf16[3,16,1024]{2,1,0:T(8,128)(2,1)S(1)} %get-tuple-element.97), channel_id=1, source_target_pairs={{0,4},{4,8},{8,12},{12,16},{16,20},{20,24},{24,28},{1,5},{5,9},{9,... | collective-permute-start | bytes 294920 | tf_op jit(solution)/shard_map/ppermute | solution.py:120
  36.8 6.7 %collective-permute-start.5 = (bf16[3,16,1024]{2,1,0:T(8,128)(2,1)S(1)}, bf16[3,16,1024]{2,1,0:T(8,128)(2,1)S(1)}, u32[]{:S(2)}, u32[]{:S(2)}) collective-permute-start(bf16[3,16,1024]{2,1,0:T(8,128)(2,1)S(1)} %get-tuple-element.98), channel_id=1, source_target_pairs={{4,0},{8,4},{12,8},{16,12},{20,16},{24,20},{28,24},{5,1},{9,5},{13... | collective-permute-start | bytes 294920 | tf_op jit(solution)/shard_map/ppermute | solution.py:120
  43.6 5.5 %collective-permute-start.6 = (bf16[10,8,1024]{2,1,0:T(8,128)(2,1)S(1)}, bf16[10,8,1024]{2,1,0:T(8,128)(2,1)S(1)}, u32[]{:S(2)}, u32[]{:S(2)}) collective-permute-start(bf16[10,8,1024]{2,1,0:T(8,128)(2,1)S(1)} %get-tuple-element.99), channel_id=1, source_target_pairs={{0,1},{1,2},{2,3},{4,5},{5,6},{6,7},{8,9},{9,10},{10,11},{12,13},{... | collective-permute-start | bytes 491528 | tf_op jit(solution)/shard_map/ppermute | solution.py:120
  47.8 3.8 %collective-permute-start.7 = (bf16[10,8,1024]{2,1,0:T(8,128)(2,1)S(1)}, bf16[10,8,1024]{2,1,0:T(8,128)(2,1)S(1)}, u32[]{:S(2)}, u32[]{:S(2)}) collective-permute-start(bf16[10,8,1024]{2,1,0:T(8,128)(2,1)S(1)} %get-tuple-element.100), channel_id=1, source_target_pairs={{1,0},{2,1},{3,2},{5,4},{6,5},{7,6},{9,8},{10,9},{11,10},{13,12},{... | collective-permute-start | bytes 491528 | tf_op jit(solution)/shard_map/ppermute | solution.py:120
  54.9 7.0 %collective-permute-start.8 = (bf16[3,16,1024]{2,1,0:T(8,128)(2,1)S(1)}, bf16[3,16,1024]{2,1,0:T(8,128)(2,1)S(1)}, u32[]{:S(2)}, u32[]{:S(2)}) collective-permute-start(bf16[3,16,1024]{2,1,0:T(8,128)(2,1)S(1)} %get-tuple-element.105), channel_id=1, source_target_pairs={{0,4},{4,8},{8,12},{12,16},{16,20},{20,24},{24,28},{1,5},{5,9},{9,... | collective-permute-start | bytes 294920 | tf_op jit(solution)/shard_map/ppermute | solution.py:120
  59.7 6.5 %collective-permute-start.9 = (bf16[3,16,1024]{2,1,0:T(8,128)(2,1)S(1)}, bf16[3,16,1024]{2,1,0:T(8,128)(2,1)S(1)}, u32[]{:S(2)}, u32[]{:S(2)}) collective-permute-start(bf16[3,16,1024]{2,1,0:T(8,128)(2,1)S(1)} %get-tuple-element.106), channel_id=1, source_target_pairs={{4,0},{8,4},{12,8},{16,12},{20,16},{24,20},{28,24},{5,1},{9,5},{13... | collective-permute-start | bytes 294920 | tf_op jit(solution)/shard_map/ppermute | solution.py:120
  66.3 5.8 %collective-permute-start.10 = (bf16[10,8,1024]{2,1,0:T(8,128)(2,1)S(1)}, bf16[10,8,1024]{2,1,0:T(8,128)(2,1)S(1)}, u32[]{:S(2)}, u32[]{:S(2)}) collective-permute-start(bf16[10,8,1024]{2,1,0:T(8,128)(2,1)S(1)} %get-tuple-element.108), channel_id=1, source_target_pairs={{0,1},{1,2},{2,3},{4,5},{5,6},{6,7},{8,9},{9,10},{10,11},{12,13},{... | collective-permute-start | bytes 491528 | tf_op jit(solution)/shard_map/ppermute | solution.py:120
  70.8 3.9 %collective-permute-start.11 = (bf16[10,8,1024]{2,1,0:T(8,128)(2,1)S(1)}, bf16[10,8,1024]{2,1,0:T(8,128)(2,1)S(1)}, u32[]{:S(2)}, u32[]{:S(2)}) collective-permute-start(bf16[10,8,1024]{2,1,0:T(8,128)(2,1)S(1)} %get-tuple-element.109), channel_id=1, source_target_pairs={{1,0},{2,1},{3,2},{5,4},{6,5},{7,6},{9,8},{10,9},{11,10},{13,12},{... | collective-permute-start | bytes 491528 | tf_op jit(solution)/shard_map/ppermute | solution.py:120
  77.8 7.0 %collective-permute-start.12 = (bf16[256,3072]{1,0:T(8,128)(2,1)S(1)}, bf16[256,3072]{1,0:T(8,128)(2,1)S(1)}, u32[]{:S(2)}, u32[]{:S(2)}) collective-permute-start(bf16[256,3072]{1,0:T(8,128)(2,1)S(1)} %get-tuple-element.124.refs_0_), channel_id=1, source_target_pairs={{0,1},{1,0},{2,3},{3,2},{4,5},{5,4},{6,7},{7,6},{8,9},{9,8},{10,11... | collective-permute-start | bytes 4718600 | tf_op jit(solution)/shard_map/ppermute | solution.py:47
  81.7 3.1 %collective-permute-start.13 = (bf16[2,64,256]{2,1,0:T(8,128)(2,1)S(1)}, bf16[2,64,256]{2,1,0:T(8,128)(2,1)S(1)}, u32[]{:S(2)}, u32[]{:S(2)}) collective-permute-start(bf16[2,64,256]{2,1,0:T(8,128)(2,1)S(1)} %get-tuple-element.126), channel_id=1, source_target_pairs={{0,1},{1,0},{2,3},{3,2},{4,5},{5,4},{6,7},{7,6},{8,9},{9,8},{10,11... | collective-permute-start | bytes 196616 | tf_op jit(solution)/shard_map/ppermute | solution.py:47
  87.4 25.5 %collective-permute-start.32 = (bf16[2048,256]{1,0:T(8,128)(2,1)S(1)}, bf16[2048,256]{1,0:T(8,128)(2,1)S(1)}, u32[]{:S(2)}, u32[]{:S(2)}) collective-permute-start(bf16[2048,256]{1,0:T(8,128)(2,1)S(1)} %get-tuple-element.127.refs_7_), channel_id=1, source_target_pairs={{0,2},{1,3},{2,0},{3,1},{4,6},{5,7},{6,4},{7,5},{8,10},{9,11},{10,... | collective-permute-start | bytes 3145736 | tf_op jit(solution)/shard_map/ppermute | solution.py:47
  93.2 10.4 %collective-permute-start.16 = (bf16[256,1024]{1,0:T(8,128)(2,1)S(1)}, bf16[256,1024]{1,0:T(8,128)(2,1)S(1)}, u32[]{:S(2)}, u32[]{:S(2)}) collective-permute-start(bf16[256,1024]{1,0:T(8,128)(2,1)S(1)} %get-tuple-element.132.refs_4_), channel_id=1, source_target_pairs={{0,1},{1,0},{2,3},{3,2},{4,5},{5,4},{6,7},{7,6},{8,9},{9,8},{10,11... | collective-permute-start | bytes 1572872 | tf_op jit(solution)/shard_map/ppermute | solution.py:47
  93.6 4.5 %collective-permute-start.17 = (bf16[368,256]{1,0:T(8,128)(2,1)S(1)}, bf16[368,256]{1,0:T(8,128)(2,1)S(1)}, u32[]{:S(2)}, u32[]{:S(2)}) collective-permute-start(bf16[368,256]{1,0:T(8,128)(2,1)S(1)} %get-tuple-element.134), channel_id=1, source_target_pairs={{0,1},{1,0},{2,3},{3,2},{4,5},{5,4},{6,7},{7,6},{8,9},{9,8},{10,11... | collective-permute-start | bytes 565256 | tf_op jit(solution)/shard_map/ppermute | solution.py:47
  93.8 7.1 %collective-permute-start.14 = (bf16[3,32,512]{2,1,0:T(8,128)(2,1)S(1)}, bf16[3,32,512]{2,1,0:T(8,128)(2,1)S(1)}, u32[]{:S(2)}, u32[]{:S(2)}) collective-permute-start(bf16[3,32,512]{2,1,0:T(8,128)(2,1)S(1)} %get-tuple-element.129), channel_id=1, source_target_pairs={{0,4},{4,8},{8,12},{12,16},{16,20},{20,24},{24,28},{1,5},{5,9},{9,... | collective-permute-start | bytes 294920 | tf_op jit(solution)/shard_map/ppermute | solution.py:120
  96.8 6.8 %collective-permute-start.15 = (bf16[3,32,512]{2,1,0:T(8,128)(2,1)S(1)}, bf16[3,32,512]{2,1,0:T(8,128)(2,1)S(1)}, u32[]{:S(2)}, u32[]{:S(2)}) collective-permute-start(bf16[3,32,512]{2,1,0:T(8,128)(2,1)S(1)} %get-tuple-element.130), channel_id=1, source_target_pairs={{4,0},{8,4},{12,8},{16,12},{20,16},{24,20},{28,24},{5,1},{9,5},{13... | collective-permute-start | bytes 294920 | tf_op jit(solution)/shard_map/ppermute | solution.py:120
  113.1 14.9 %collective-permute-start.33 = (bf16[1024,256]{1,0:T(8,128)(2,1)S(1)}, bf16[1024,256]{1,0:T(8,128)(2,1)S(1)}, u32[]{:S(2)}, u32[]{:S(2)}) collective-permute-start(bf16[1024,256]{1,0:T(8,128)(2,1)S(1)} %get-tuple-element.161), channel_id=1, source_target_pairs={{0,4},{4,0},{8,12},{12,8},{16,20},{20,16},{24,28},{28,24},{1,5},{5... | collective-permute-start | bytes 1572872 | tf_op jit(solution)/shard_map/ppermute | solution.py:47
  114.3 19.7 %collective-permute-start.27 = (bf16[1136,256]{1,0:T(8,128)(2,1)S(1)}, bf16[1136,256]{1,0:T(8,128)(2,1)S(1)}, u32[]{:S(2)}, u32[]{:S(2)}) collective-permute-start(bf16[1136,256]{1,0:T(8,128)(2,1)S(1)} %get-tuple-element.135.refs_4_), channel_id=1, source_target_pairs={{0,8},{4,12},{8,0},{12,4},{16,24},{20,28},{24,16},{28,20},{1,9},{5... | collective-permute-start | bytes 1744904 | tf_op jit(solution)/shard_map/ppermute | solution.py:47
  115.8 25.3 %collective-permute-start.20 = (bf16[1024,256]{1,0:T(8,128)(2,1)S(1)}, bf16[1024,256]{1,0:T(8,128)(2,1)S(1)}, u32[]{:S(2)}, u32[]{:S(2)}) collective-permute-start(bf16[1024,256]{1,0:T(8,128)(2,1)S(1)} %get-tuple-element.136.refs_3_.refs_9_), channel_id=1, source_target_pairs={{0,4},{4,0},{8,12},{12,8},{16,20},{20,16},{24,28},{28,24},{1,5},{5... | collective-permute-start | bytes 1572872 | tf_op jit(solution)/shard_map/ppermute | solution.py:47
  128.2 13.6 %collective-permute-start.34 = (bf16[512,256]{1,0:T(8,128)(2,1)S(1)}, bf16[512,256]{1,0:T(8,128)(2,1)S(1)}, u32[]{:S(2)}, u32[]{:S(2)}) collective-permute-start(bf16[512,256]{1,0:T(8,128)(2,1)S(1)} %get-tuple-element.163), channel_id=1, source_target_pairs={{0,8},{4,12},{8,0},{12,4},{16,24},{20,28},{24,16},{28,20},{1,9},{5... | collective-permute-start | bytes 786440 | tf_op jit(solution)/shard_map/ppermute | solution.py:47
  129.8 1.2 collective-permute-start.21
  131.0 7.5 %collective-permute-start.22 = (bf16[64,256]{1,0:T(8,128)(2,1)S(1)}, bf16[64,256]{1,0:T(8,128)(2,1)S(1)}, u32[]{:S(2)}, u32[]{:S(2)}) collective-permute-start(bf16[64,256]{1,0:T(8,128)(2,1)S(1)} %add.23.refs_2_), channel_id=1, source_target_pairs={{0,4},{4,0},{8,12},{12,8},{16,20},{20,16},{24,28},{28,24},{1,5},{5... | collective-permute-start | bytes 98312 | tf_op jit(solution)/shard_map/ppermute | solution.py:47
  132.2 11.2 %collective-permute-start.18 = (bf16[14,8,512]{2,1,0:T(8,128)(2,1)S(1)}, bf16[14,8,512]{2,1,0:T(8,128)(2,1)S(1)}, u32[]{:S(2)}, u32[]{:S(2)}) collective-permute-start(bf16[14,8,512]{2,1,0:T(8,128)(2,1)S(1)} %get-tuple-element.137), channel_id=1, source_target_pairs={{0,1},{1,2},{2,3},{4,5},{5,6},{6,7},{8,9},{9,10},{10,11},{12,13},{... | collective-permute-start | bytes 344072 | tf_op jit(solution)/shard_map/ppermute | solution.py:120
  134.0 9.4 %collective-permute-start.19 = (bf16[14,8,512]{2,1,0:T(8,128)(2,1)S(1)}, bf16[14,8,512]{2,1,0:T(8,128)(2,1)S(1)}, u32[]{:S(2)}, u32[]{:S(2)}) collective-permute-start(bf16[14,8,512]{2,1,0:T(8,128)(2,1)S(1)} %get-tuple-element.138), channel_id=1, source_target_pairs={{1,0},{2,1},{3,2},{5,4},{6,5},{7,6},{9,8},{10,9},{11,10},{13,12},{... | collective-permute-start | bytes 344072 | tf_op jit(solution)/shard_map/ppermute | solution.py:120
  138.5 19.8 %collective-permute-start.28 = (bf16[624,256]{1,0:T(8,128)(2,1)S(1)}, bf16[624,256]{1,0:T(8,128)(2,1)S(1)}, u32[]{:S(2)}, u32[]{:S(2)}) collective-permute-start(bf16[624,256]{1,0:T(8,128)(2,1)S(1)} %get-tuple-element.153), channel_id=1, source_target_pairs={{0,16},{4,20},{8,24},{12,28},{16,0},{20,4},{24,8},{28,12},{1,17},{... | collective-permute-start | bytes 958472 | tf_op jit(solution)/shard_map/ppermute | solution.py:47
  141.3 18.3 %collective-permute-start.23 = (bf16[576,256]{1,0:T(8,128)(2,1)S(1)}, bf16[576,256]{1,0:T(8,128)(2,1)S(1)}, u32[]{:S(2)}, u32[]{:S(2)}) collective-permute-start(bf16[576,256]{1,0:T(8,128)(2,1)S(1)} %get-tuple-element.145), channel_id=1, source_target_pairs={{0,8},{4,12},{8,0},{12,4},{16,24},{20,28},{24,16},{28,20},{1,9},{5... | collective-permute-start | bytes 884744 | tf_op jit(solution)/shard_map/ppermute | solution.py:47
  141.9 21.1 %collective-permute-start.35 = (bf16[256,256]{1,0:T(8,128)(2,1)S(1)}, bf16[256,256]{1,0:T(8,128)(2,1)S(1)}, u32[]{:S(2)}, u32[]{:S(2)}) collective-permute-start(bf16[256,256]{1,0:T(8,128)(2,1)S(1)} %get-tuple-element.165), channel_id=1, source_target_pairs={{0,16},{4,20},{8,24},{12,28},{16,0},{20,4},{24,8},{28,12},{1,17},{... | collective-permute-start | bytes 393224 | tf_op jit(solution)/shard_map/ppermute | solution.py:47
  158.4 5.6 %collective-permute-start.29 = (bf16[368,256]{1,0:T(8,128)(2,1)S(1)}, bf16[368,256]{1,0:T(8,128)(2,1)S(1)}, u32[]{:S(2)}, u32[]{:S(2)}) collective-permute-start(bf16[368,256]{1,0:T(8,128)(2,1)S(1)} %get-tuple-element.155), channel_id=1, source_target_pairs={{0,4},{4,0},{8,12},{12,8},{16,20},{20,16},{24,28},{28,24},{1,5},{5... | collective-permute-start | bytes 565256 | tf_op jit(solution)/shard_map/ppermute | solution.py:47
  159.6 1.0 copy-start
  160.6 7.4 %collective-permute-start.24 = (bf16[320,256]{1,0:T(8,128)(2,1)S(1)}, bf16[320,256]{1,0:T(8,128)(2,1)S(1)}, u32[]{:S(2)}, u32[]{:S(2)}) collective-permute-start(bf16[320,256]{1,0:T(8,128)(2,1)S(1)} %get-tuple-element.147), channel_id=1, source_target_pairs={{0,16},{4,20},{8,24},{12,28},{16,0},{20,4},{24,8},{28,12},{1,17},{... | collective-permute-start | bytes 491528 | tf_op jit(solution)/shard_map/ppermute | solution.py:47
  162.9 6.5 %collective-permute-start.36 = (bf16[1,256,256]{2,1,0:T(8,128)(2,1)S(1)}, bf16[1,256,256]{2,1,0:T(8,128)(2,1)S(1)}, u32[]{:S(2)}, u32[]{:S(2)}) collective-permute-start(bf16[1,256,256]{2,1,0:T(8,128)(2,1)S(1)} %add_bitcast_fusion), channel_id=1, source_target_pairs={{0,2},{1,3},{2,0},{3,1},{4,6},{5,7},{6,4},{7,5},{8,10},{9,11},{10,... | collective-permute-start | bytes 393224 | tf_op jit(solution)/shard_map/ppermute | solution.py:47
  164.1 9.2 %collective-permute-start.30 = (bf16[368,256]{1,0:T(8,128)(2,1)S(1)}, bf16[368,256]{1,0:T(8,128)(2,1)S(1)}, u32[]{:S(2)}, u32[]{:S(2)}) collective-permute-start(bf16[368,256]{1,0:T(8,128)(2,1)S(1)} %add.26), channel_id=1, source_target_pairs={{0,2},{1,3},{2,0},{3,1},{4,6},{5,7},{6,4},{7,5},{8,10},{9,11},{10,... | collective-permute-start | bytes 565256 | tf_op jit(solution)/shard_map/ppermute | solution.py:47
  168.0 7.1 %collective-permute-start.25 = (bf16[320,256]{1,0:T(8,128)(2,1)S(1)}, bf16[320,256]{1,0:T(8,128)(2,1)S(1)}, u32[]{:S(2)}, u32[]{:S(2)}) collective-permute-start(bf16[320,256]{1,0:T(8,128)(2,1)S(1)} %add.24), channel_id=1, source_target_pairs={{0,2},{1,3},{2,0},{3,1},{4,6},{5,7},{6,4},{7,5},{8,10},{9,11},{10,... | collective-permute-start | bytes 491528 | tf_op jit(solution)/shard_map/ppermute | solution.py:47
  169.5 8.0 %collective-permute-start.37 = (bf16[2,256,256]{2,1,0:T(8,128)(2,1)S(1)}, bf16[2,256,256]{2,1,0:T(8,128)(2,1)S(1)}, u32[]{:S(2)}, u32[]{:S(2)}) collective-permute-start(bf16[2,256,256]{2,1,0:T(8,128)(2,1)S(1)} %maximum_bitcast_fusion.refs_0_), channel_id=1, source_target_pairs={{0,1},{1,0},{2,3},{3,2},{4,5},{5,4},{6,7},{7,6},{8,9},{9,8},{10,11... | collective-permute-start | bytes 786440 | tf_op jit(solution)/shard_map/ppermute | solution.py:47
  173.4 1.8 %collective-permute-start.31 = (bf16[368,256]{1,0:T(8,128)(2,1)S(1)}, bf16[368,256]{1,0:T(8,128)(2,1)S(1)}, u32[]{:S(2)}, u32[]{:S(2)}) collective-permute-start(bf16[368,256]{1,0:T(8,128)(2,1)S(1)} %add.27.refs_0_), channel_id=1, source_target_pairs={{0,1},{1,0},{2,3},{3,2},{4,5},{5,4},{6,7},{7,6},{8,9},{9,8},{10,11... | collective-permute-start | bytes 565256 | tf_op jit(solution)/shard_map/ppermute | solution.py:47
  175.1 1.5 collective-permute-start.26
